TPU v7x, 32 devices: a whole 2x2x4 slice. The times are simulated.
32 devices in a mesh: members: 2 (over x), band: 16 (over z, y, core).
Axes of the slice: x: 2, y: 2, z: 4, core: 2. Of those that a mesh axis runs over, the one named last changes fastest.
Arguments:
- queries: bfloat16 [8192, 1024], P(('members', 'band')), parts along dimension 0, may hold values from -32 to 32
- keys: bfloat16 [8192, 1024], P(('members', 'band')), parts along dimension 0, may hold values from -16 to 16
- values: bfloat16 [8192, 1024], P(('members', 'band')), parts along dimension 0, may hold values from -6 to 6
- grad_out: bfloat16 [8192, 1024], P(('members', 'band')), parts along dimension 0, may hold values from -6 to 6
- windows: int32 [4096, 2], P('band'), may hold values from 0 to 4096, as said below
Outputs:
- attended: bfloat16 [8192, 1024], P(('members', 'band')), parts along dimension 0
- grad_queries: bfloat16 [8192, 1024], P(('members', 'band')), parts along dimension 0
- grad_keys: bfloat16 [8192, 1024], P(('members', 'band')), parts along dimension 0
- grad_values: bfloat16 [8192, 1024], P(('members', 'band')), parts along dimension 0
There are 2 independent parts, one for each index of `members`. A program takes and returns all parts, laid end to end along the dimension named above; an argument that names none is the same for every part. Nothing has to cross between parts.
Inputs may be any that keep to these rules, and one draw needn't show every extreme that they name: `windows`: points are ordered by latitude rows of 1 to 100 points, growing from each pole toward the middle of the grid. A point's window runs from the first point of the row before its own to the last point of the row after its own (only its own row's side where it lies in the first or last row); so every window holds its own point, and no key lies more than 199 points before or after the point; both distances are reached.
All inputs are finite; a program needn't handle non-finite values.
Results may differ from a plain program's by a relative error of at most 0.018.
Values may be sent and summed in bfloat16 or wider, within the bound.
No kernel may reach another device: no remote copies, remote signals or barrier semaphores. Data moves between devices by JAX's collectives and lax.ppermute only.
A program may use at most 128 MiB of HBM per device.

v0:
```python
import jax
import jax.numpy as jnp
from jax import lax
from jax.sharding import PartitionSpec as P

HEADS = 16
HEAD_DIM = 64
ROWMIN = 20
STEP = 4


head_group = 4


def passed_along(value, axis, steps):
    count = lax.axis_size(axis)
    initial, last = (max(0, -steps), min(count, count - steps))
    return lax.ppermute(value, axis, [(source, source + steps) for source in range(initial, last)])


def reach_sizes(points, count):
    area_rows = points * count // STEP
    root_bound = min(((area_rows + 2 * 4**power) // (3 * 2**power) for power in range(3, 9)))
    grow_rows = root_bound - ROWMIN // STEP - 6
    row_longest = ROWMIN + STEP * (grow_rows - 1)
    rim_width = 2 * row_longest
    return (rim_width, (rim_width + points - 1) // points)


def surround(field, reach, rim_width, fetch_low, fetch_high):
    below = [fetch_low(field, offset) for offset in range(reach, 0, -1)]
    above = [fetch_high(field, -offset) for offset in range(1, reach + 1)]
    low_part = jnp.concatenate(below, axis=1)
    high_part = jnp.concatenate(above, axis=1)
    length = low_part.shape[1]
    low_part = lax.slice_in_dim(low_part, length - rim_width, length, axis=1)
    high_part = lax.slice_in_dim(high_part, 0, rim_width, axis=1)
    return jnp.concatenate([low_part, field, high_part], axis=1)


def window_scores(q_heads, k_heads, lower, upper, key_first, scale):
    scores = (
        jnp.einsum("rhe,che->hrc", q_heads, k_heads, preferred_element_type=jnp.float32) * scale
    )
    cols = key_first + lax.iota(jnp.int32, k_heads.shape[0])
    inside = (cols[None, :] >= lower[:, None]) & (cols[None, :] < upper[:, None])
    return jnp.where(inside[None], scores, -jnp.inf)


def query_pass(q_grp, k_grp, v_grp, g_grp, lower, upper, key_first):
    rows, width = q_grp.shape
    cols_n = k_grp.shape[0]
    scale = HEAD_DIM ** (-0.5)
    q_heads = q_grp.reshape(rows, head_group, HEAD_DIM)
    k_heads = k_grp.reshape(cols_n, head_group, HEAD_DIM)
    v_heads = v_grp.reshape(cols_n, head_group, HEAD_DIM)
    g_heads = g_grp.reshape(rows, head_group, HEAD_DIM)
    scores = window_scores(q_heads, k_heads, lower, upper, key_first, scale)
    top = jnp.max(scores, axis=-1, keepdims=True)
    totals = top + jnp.log(jnp.sum(jnp.exp(scores - top), axis=-1, keepdims=True))
    probs = jnp.exp(scores - totals)
    probs_low = probs.astype(jnp.bfloat16)
    attended = jnp.einsum(
        "hrc,che->rhe", probs_low, v_heads, preferred_element_type=jnp.float32
    ).astype(jnp.bfloat16)
    delta = jnp.einsum("rhe,rhe->hr", g_heads, attended, preferred_element_type=jnp.float32)
    dprobs = jnp.einsum("rhe,che->hrc", g_heads, v_heads, preferred_element_type=jnp.float32)
    dscores = (probs * (dprobs - delta[:, :, None])).astype(jnp.bfloat16)
    grad_q = (
        jnp.einsum("hrc,che->rhe", dscores, k_heads, preferred_element_type=jnp.float32) * scale
    ).astype(jnp.bfloat16)
    grad_k = (
        jnp.einsum("hrc,rhe->che", dscores, q_heads, preferred_element_type=jnp.float32) * scale
    )
    grad_v = jnp.einsum("hrc,rhe->che", probs_low, g_heads, preferred_element_type=jnp.float32)
    return (
        attended.reshape(rows, width),
        grad_q.reshape(rows, width),
        grad_k.reshape(cols_n, width),
        grad_v.reshape(cols_n, width),
        totals[:, :, 0],
        delta,
    )


def make_carry(points, width_all, key_cols):
    return (
        jnp.zeros((points, width_all), jnp.bfloat16),
        jnp.zeros((points, width_all), jnp.bfloat16),
        jnp.zeros((key_cols, width_all), jnp.float32),
        jnp.zeros((key_cols, width_all), jnp.float32),
        jnp.zeros((HEADS, points), jnp.float32),
        jnp.zeros((HEADS, points), jnp.float32),
    )


def per_device(queries, keys, values, grad_out, windows):
    points = queries.shape[0]
    width_all = queries.shape[1]
    width = head_group * HEAD_DIM
    groups = HEADS // head_group
    rim_width, reach = reach_sizes(points, lax.axis_size("band"))
    start = lax.axis_index("band") * points
    lower = windows[:, 0]
    upper = windows[:, 1]
    both = surround(
        jnp.stack([keys, values]),
        reach,
        rim_width,
        lambda field, offset: passed_along(field, "band", offset),
        lambda field, offset: passed_along(field, "band", offset),
    )
    keys_wide = both[0]
    values_wide = both[1]
    span = keys_wide.shape[0]

    def group_step(index, carry):
        attended, grad_q, key_acc, value_acc, totals, deltas = carry
        offset = index * width
        pieces = query_pass(
            lax.dynamic_slice_in_dim(queries, offset, width, 1),
            lax.dynamic_slice_in_dim(keys_wide, offset, width, 1),
            lax.dynamic_slice_in_dim(values_wide, offset, width, 1),
            lax.dynamic_slice_in_dim(grad_out, offset, width, 1),
            lower,
            upper,
            start - rim_width,
        )
        attended = lax.dynamic_update_slice_in_dim(attended, pieces[0], offset, 1)
        grad_q = lax.dynamic_update_slice_in_dim(grad_q, pieces[1], offset, 1)
        key_acc = lax.dynamic_update_slice_in_dim(key_acc, pieces[2], offset, 1)
        value_acc = lax.dynamic_update_slice_in_dim(value_acc, pieces[3], offset, 1)
        totals = lax.dynamic_update_slice_in_dim(totals, pieces[4], index * head_group, 0)
        deltas = lax.dynamic_update_slice_in_dim(deltas, pieces[5], index * head_group, 0)
        return (attended, grad_q, key_acc, value_acc, totals, deltas)

    start_carry = make_carry(points, width_all, span)
    attended, grad_q, key_acc, value_acc, totals, deltas = lax.fori_loop(
        0, groups, group_step, start_carry
    )
    terms = jnp.stack([key_acc, value_acc])
    filler = jnp.zeros((2, reach * points - rim_width, width_all), jnp.float32)
    low_full = jnp.concatenate([filler, terms[:, :rim_width]], axis=1)
    high_full = jnp.concatenate([terms[:, rim_width + points :], filler], axis=1)
    own = terms[:, rim_width : rim_width + points]
    for offset in range(1, reach + 1):
        upward = low_full[:, (reach - offset) * points : (reach - offset + 1) * points]
        own = own + passed_along(upward, "band", -offset)
        downward = high_full[:, (offset - 1) * points : offset * points]
        own = own + passed_along(downward.astype(jnp.bfloat16), "band", offset).astype(
            downward.dtype
        )
    grad_k = own[0].astype(jnp.bfloat16)
    grad_v = own[1].astype(jnp.bfloat16)
    return (attended, grad_q, grad_k, grad_v)


def solution(mesh):
    in_specs = (
        P(("members", "band"), None),
        P(("members", "band"), None),
        P(("members", "band"), None),
        P(("members", "band"), None),
        P("band", None),
    )
    out_specs = (
        P(("members", "band"), None),
        P(("members", "band"), None),
        P(("members", "band"), None),
        P(("members", "band"), None),
    )
    return jax.shard_map(
        per_device, mesh=mesh, in_specs=in_specs, out_specs=out_specs, check_vma=False
    )
```

profile of v0, /device:TPU:9, one launch (start us, length us, event | category | flops | bytes accessed | tf_op | source)
XLA Modules:
  0.0 141.7 jit_solution(12272181469505870669)
XLA Ops:
  0.6 1.2 copy.10
  1.9 1.2 copy.9
  3.3 3.7 %collective-permute-start = (bf16[2,256,1024]{1,2,0:T(8,128)(2,1)S(1)}, bf16[2,256,1024]{1,2,0:T(8,128)(2,1)S(1)}, u32[]{:S(2)}, u32[]{:S(2)}) collective-permute-start(bf16[2,256,1024]{1,2,0:T(8,128)(2,1)S(1)} %pad_maximum_fusion.2), channel_id=1, source_target_pairs={{0,1},{1,2},{2,3},{3,4},{4,5},{5,6},{6,7},{7,8},{8,9},{9,10},{10,1... | collective-permute-start | bytes 3145736 | tf_op jit(solution)/shard_map/ppermute | solution.py:18
  7.0 1.9 %collective-permute-start.1 = (bf16[2,256,1024]{1,2,0:T(8,128)(2,1)S(1)}, bf16[2,256,1024]{1,2,0:T(8,128)(2,1)}, u32[]{:S(2)}, u32[]{:S(2)}) collective-permute-start(bf16[2,256,1024]{1,2,0:T(8,128)(2,1)S(1)} %pad_maximum_fusion.2), channel_id=1, source_target_pairs={{1,0},{2,1},{3,2},{4,3},{5,4},{6,5},{7,6},{8,7},{9,8},{10,9},{11,1... | collective-permute-start | bytes 3145736 | tf_op jit(solution)/shard_map/ppermute | solution.py:18
  8.9 21.0 %collective-permute-done = bf16[2,256,1024]{1,2,0:T(8,128)(2,1)S(1)} collective-permute-done((bf16[2,256,1024]{1,2,0:T(8,128)(2,1)S(1)}, bf16[2,256,1024]{1,2,0:T(8,128)(2,1)S(1)}, u32[]{:S(2)}, u32[]{:S(2)}) %collective-permute-start) | collective-permute-done | bytes 1048608 | tf_op jit(solution)/shard_map/ppermute | solution.py:18
  30.4 1.2 collective-permute-done.1
  31.6 3.1 %pad_maximum_fusion = bf16[2,656,1024]{1,2,0:T(8,128)(2,1)S(1)} fusion(bf16[2,200,1024]{1,2,0:T(8,128)(2,1)} %bitcast.46, bf16[1,256,1024]{1,2,0:T(8,128)(2,1)S(1)} %bitcast.110, bf16[1,256,1024]{1,2,0:T(8,128)(2,1)S(1)} %bitcast.112, bf16[2,200,1024]{1,2,0:T(8,128)(2,1)S(1)} %slice.47), kind=kLoop, calls=%fused_computation.27 | loop fusion | flops 10747904 | bytes 5373952 | tf_op jit(solution)/shard_map/concatenate | solution.py:38
  34.7 1.9 %slice_bitcast_fusion = (bf16[656,1024]{0,1:T(8,128)(2,1)}, bf16[656,1024]{0,1:T(8,128)(2,1)}) fusion(bf16[2,656,1024]{1,2,0:T(8,128)(2,1)S(1)} %pad_maximum_fusion), kind=kLoop, calls=%fused_computation.35 | loop fusion | bytes 5373952 | tf_op jit(solution)/shard_map/squeeze | solution.py:113
  36.6 0.9 broadcast.101.clone
  37.4 0.9 broadcast.101.clone2
  38.3 1.9 %broadcast.102.clone = f32[656,1024]{1,0:T(8,128)} broadcast(f32[]{:T(128)} %constant.84.clone.1), dimensions={} | broadcast | bytes 2686980 | tf_op jit(solution)/shard_map/broadcast.8
  40.1 1.9 %broadcast.102.clone2 = f32[656,1024]{1,0:T(8,128)} broadcast(f32[]{:T(128)} %constant.84.clone.1), dimensions={} | broadcast | bytes 2686980 | tf_op jit(solution)/shard_map/broadcast.8
  42.0 57.3 %while.21 = (s32[]{:T(128)}, bf16[256,1024]{1,0:T(8,128)(2,1)}, bf16[256,1024]{1,0:T(8,128)(2,1)}, f32[656,1024]{1,0:T(8,128)}, f32[656,1024]{1,0:T(8,128)}, /*i...) while((s32[]{:T(128)}, bf16[256,1024]{1,0:T(8,128)(2,1)}, ...), condition=%wide.region_3.4_spmd, body=%wide.region_0.3_spmd.sunk | while | flops 525761184 | bytes 36695484 | solution.py:138
  42.0 1.0 constant_dynamic-slice_fusion.8
  43.0 0.9 constant_dynamic-slice_fusion.9
  44.3 0.7 fusion.50
  45.0 0.9 constant_dynamic-slice_fusion.10
  46.0 1.1 constant_dynamic-slice_fusion.11
  48.0 0.7 multiply_convert_fusion.2
  48.8 1.2 copy-done
  50.5 0.7 constant_dynamic-update-slice_fusion.6
  51.2 1.4 %fusion.53 = f32[4,64,656]{2,1,0:T(8,128)S(1)} fusion(bf16[256,4,64]{0,2,1:T(8,128)(2,1)} %bitcast.98, f32[4,256,656]{1,2,0:T(8,128)S(1)} %get-tuple-element.422, f32[4,256]{1,0:T(4,128)S(1)} %log_add_fusion.2), kind=kOutput, calls=%fused_computation.10.clone.1 | convolution fusion | flops 87326720 | bytes 3493888 | tf_op jit(solution)/shard_map/while/body/eval_jaxpr/hrc,rhe->che/dot_general | solution.py:75
  52.9 1.9 %convolution_multiply_fusion.3 = f32[4,64,656]{2,1,0:T(8,128)S(1)} fusion(bf16[256,4,64]{0,2,1:T(8,128)(2,1)} %bitcast.106, bf16[4,256,656]{1,2,0:T(8,128)(2,1)} %copy-done), kind=kOutput, calls=%fused_computation.5.clone.1 | convolution fusion | flops 86151168 | bytes 2146304 | tf_op jit(solution)/shard_map/while/body/eval_jaxpr/hrc,rhe->che/dot_general | solution.py:73
  55.1 1.3 constant_dynamic-update-slice_fusion.7
  56.4 1.0 constant_dynamic-slice_fusion.8
  57.4 0.9 constant_dynamic-slice_fusion.9
  58.6 0.7 fusion.50
  59.3 0.9 constant_dynamic-slice_fusion.10
  60.3 1.1 constant_dynamic-slice_fusion.11
  62.4 0.7 multiply_convert_fusion.2
  63.1 1.2 copy-done
  64.9 0.7 constant_dynamic-update-slice_fusion.6
  65.6 1.4 %fusion.53 = f32[4,64,656]{2,1,0:T(8,128)S(1)} fusion(bf16[256,4,64]{0,2,1:T(8,128)(2,1)} %bitcast.98, f32[4,256,656]{1,2,0:T(8,128)S(1)} %get-tuple-element.422, f32[4,256]{1,0:T(4,128)S(1)} %log_add_fusion.2), kind=kOutput, calls=%fused_computation.10.clone.1 | convolution fusion | flops 87326720 | bytes 3493888 | tf_op jit(solution)/shard_map/while/body/eval_jaxpr/hrc,rhe->che/dot_general | solution.py:75
  67.3 1.9 %convolution_multiply_fusion.3 = f32[4,64,656]{2,1,0:T(8,128)S(1)} fusion(bf16[256,4,64]{0,2,1:T(8,128)(2,1)} %bitcast.106, bf16[4,256,656]{1,2,0:T(8,128)(2,1)} %copy-done), kind=kOutput, calls=%fused_computation.5.clone.1 | convolution fusion | flops 86151168 | bytes 2146304 | tf_op jit(solution)/shard_map/while/body/eval_jaxpr/hrc,rhe->che/dot_general | solution.py:73
  69.4 1.2 constant_dynamic-update-slice_fusion.7
  70.7 1.0 constant_dynamic-slice_fusion.8
  71.7 0.9 constant_dynamic-slice_fusion.9
  73.0 0.7 fusion.50
  73.6 0.9 constant_dynamic-slice_fusion.10
  74.7 1.1 constant_dynamic-slice_fusion.11
  76.7 0.7 multiply_convert_fusion.2
  77.4 1.2 copy-done
  79.2 0.7 constant_dynamic-update-slice_fusion.6
  79.9 1.4 %fusion.53 = f32[4,64,656]{2,1,0:T(8,128)S(1)} fusion(bf16[256,4,64]{0,2,1:T(8,128)(2,1)} %bitcast.98, f32[4,256,656]{1,2,0:T(8,128)S(1)} %get-tuple-element.422, f32[4,256]{1,0:T(4,128)S(1)} %log_add_fusion.2), kind=kOutput, calls=%fused_computation.10.clone.1 | convolution fusion | flops 87326720 | bytes 3493888 | tf_op jit(solution)/shard_map/while/body/eval_jaxpr/hrc,rhe->che/dot_general | solution.py:75
  81.6 1.9 %convolution_multiply_fusion.3 = f32[4,64,656]{2,1,0:T(8,128)S(1)} fusion(bf16[256,4,64]{0,2,1:T(8,128)(2,1)} %bitcast.106, bf16[4,256,656]{1,2,0:T(8,128)(2,1)} %copy-done), kind=kOutput, calls=%fused_computation.5.clone.1 | convolution fusion | flops 86151168 | bytes 2146304 | tf_op jit(solution)/shard_map/while/body/eval_jaxpr/hrc,rhe->che/dot_general | solution.py:73
  83.8 1.2 constant_dynamic-update-slice_fusion.7
  85.0 1.0 constant_dynamic-slice_fusion.8
  86.0 0.9 constant_dynamic-slice_fusion.9
  87.3 0.7 fusion.50
  87.9 0.9 constant_dynamic-slice_fusion.10
  89.0 1.1 constant_dynamic-slice_fusion.11
  91.0 0.7 multiply_convert_fusion.2
  91.8 1.2 copy-done
  93.5 0.7 constant_dynamic-update-slice_fusion.6
  94.2 1.4 %fusion.53 = f32[4,64,656]{2,1,0:T(8,128)S(1)} fusion(bf16[256,4,64]{0,2,1:T(8,128)(2,1)} %bitcast.98, f32[4,256,656]{1,2,0:T(8,128)S(1)} %get-tuple-element.422, f32[4,256]{1,0:T(4,128)S(1)} %log_add_fusion.2), kind=kOutput, calls=%fused_computation.10.clone.1 | convolution fusion | flops 87326720 | bytes 3493888 | tf_op jit(solution)/shard_map/while/body/eval_jaxpr/hrc,rhe->che/dot_general | solution.py:75
  95.9 1.9 %convolution_multiply_fusion.3 = f32[4,64,656]{2,1,0:T(8,128)S(1)} fusion(bf16[256,4,64]{0,2,1:T(8,128)(2,1)} %bitcast.106, bf16[4,256,656]{1,2,0:T(8,128)(2,1)} %copy-done), kind=kOutput, calls=%fused_computation.5.clone.1 | convolution fusion | flops 86151168 | bytes 2146304 | tf_op jit(solution)/shard_map/while/body/eval_jaxpr/hrc,rhe->che/dot_general | solution.py:73
  98.1 1.2 constant_dynamic-update-slice_fusion.7
  99.3 1.6 %fusion.10 = f32[2,200,1024]{2,1,0:T(8,128)S(1)} fusion(f32[1,656,1024]{2,1,0:T(8,128)} %bitcast.99, f32[1,656,1024]{2,1,0:T(8,128)} %bitcast.102), kind=kLoop, calls=%fused_computation.32 | loop fusion | flops 409600 | bytes 7012352 | tf_op jit(solution)/shard_map/stack | solution.py:141
  101.3 2.1 %collective-permute-start.2 = (f32[2,256,1024]{2,1,0:T(8,128)S(1)}, f32[2,256,1024]{2,1,0:T(8,128)S(1)}, u32[]{:S(2)}, u32[]{:S(2)}) collective-permute-start(f32[2,256,1024]{2,1,0:T(8,128)S(1)} %concatenate.10), channel_id=1, source_target_pairs={{1,0},{2,1},{3,2},{4,3},{5,4},{6,5},{7,6},{8,7},{9,8},{10,9},{11,1... | collective-permute-start | bytes 6291464 | tf_op jit(solution)/shard_map/ppermute | solution.py:18
  103.6 3.6 %collective-permute-start.3 = (bf16[2,256,1024]{2,1,0:T(8,128)(2,1)S(1)}, bf16[2,256,1024]{2,1,0:T(8,128)(2,1)S(1)}, u32[]{:S(2)}, u32[]{:S(2)}) collective-permute-start(bf16[2,256,1024]{2,1,0:T(8,128)(2,1)S(1)} %concatenate.11), channel_id=1, source_target_pairs={{0,1},{1,2},{2,3},{3,4},{4,5},{5,6},{6,7},{7,8},{8,9},{9,10},{10,1... | collective-permute-start | bytes 3145736 | tf_op jit(solution)/shard_map/ppermute | solution.py:18
  107.2 25.6 %collective-permute-done.3 = bf16[2,256,1024]{2,1,0:T(8,128)(2,1)S(1)} collective-permute-done((bf16[2,256,1024]{2,1,0:T(8,128)(2,1)S(1)}, bf16[2,256,1024]{2,1,0:T(8,128)(2,1)S(1)}, u32[]{:S(2)}, u32[]{:S(2)}) %collective-permute-start.3) | collective-permute-done | bytes 1048608 | tf_op jit(solution)/shard_map/ppermute | solution.py:18
  132.8 7.2 %collective-permute-done.2 = f32[2,256,1024]{2,1,0:T(8,128)S(1)} collective-permute-done((f32[2,256,1024]{2,1,0:T(8,128)S(1)}, f32[2,256,1024]{2,1,0:T(8,128)S(1)}, u32[]{:S(2)}, u32[]{:S(2)}) %collective-permute-start.2) | collective-permute-done | bytes 2097184 | tf_op jit(solution)/shard_map/ppermute | solution.py:18
  140.0 0.6 fusion.9
  140.6 1.0 slice_bitcast_fusion.2
  (80 shorter events, 10.6 us)
Async XLA Ops:
  0.6 8.3 %copy-start.5 = (s32[256,2]{0,1:T(2,128)S(1)}, s32[256,2]{0,1:T(2,128)}, u32[]{:S(2)}) copy-start(s32[256,2]{0,1:T(2,128)} %param.11) | copy-start | bytes 6148
  3.3 26.7 %collective-permute-start = (bf16[2,256,1024]{1,2,0:T(8,128)(2,1)S(1)}, bf16[2,256,1024]{1,2,0:T(8,128)(2,1)S(1)}, u32[]{:S(2)}, u32[]{:S(2)}) collective-permute-start(bf16[2,256,1024]{1,2,0:T(8,128)(2,1)S(1)} %pad_maximum_fusion.2), channel_id=1, source_target_pairs={{0,1},{1,2},{2,3},{3,4},{4,5},{5,6},{6,7},{7,8},{8,9},{9,10},{10,1... | collective-permute-start | bytes 3145736 | tf_op jit(solution)/shard_map/ppermute | solution.py:18
  7.0 24.6 %collective-permute-start.1 = (bf16[2,256,1024]{1,2,0:T(8,128)(2,1)S(1)}, bf16[2,256,1024]{1,2,0:T(8,128)(2,1)}, u32[]{:S(2)}, u32[]{:S(2)}) collective-permute-start(bf16[2,256,1024]{1,2,0:T(8,128)(2,1)S(1)} %pad_maximum_fusion.2), channel_id=1, source_target_pairs={{1,0},{2,1},{3,2},{4,3},{5,4},{6,5},{7,6},{8,7},{9,8},{10,9},{11,1... | collective-permute-start | bytes 3145736 | tf_op jit(solution)/shard_map/ppermute | solution.py:18
  44.1 0.9 copy-start.4
  46.0 5.2 %copy-start.1 = (bf16[256,256]{0,1:T(8,128)(2,1)}, bf16[256,256]{0,1:T(8,128)(2,1)S(1)}, u32[]{:S(2)}) copy-start(bf16[256,256]{0,1:T(8,128)(2,1)S(1)} %copy.43) | copy-start | bytes 393220 | tf_op jit(solution)/shard_map/while
  48.8 1.2 copy-start
  58.4 0.9 copy-start.4
  60.3 5.2 %copy-start.1 = (bf16[256,256]{0,1:T(8,128)(2,1)}, bf16[256,256]{0,1:T(8,128)(2,1)S(1)}, u32[]{:S(2)}) copy-start(bf16[256,256]{0,1:T(8,128)(2,1)S(1)} %copy.43) | copy-start | bytes 393220 | tf_op jit(solution)/shard_map/while
  63.1 1.2 copy-start
  72.7 0.9 copy-start.4
  74.6 5.2 %copy-start.1 = (bf16[256,256]{0,1:T(8,128)(2,1)}, bf16[256,256]{0,1:T(8,128)(2,1)S(1)}, u32[]{:S(2)}) copy-start(bf16[256,256]{0,1:T(8,128)(2,1)S(1)} %copy.43) | copy-start | bytes 393220 | tf_op jit(solution)/shard_map/while
  77.4 1.2 copy-start
  87.0 0.9 copy-start.4
  89.0 5.2 %copy-start.1 = (bf16[256,256]{0,1:T(8,128)(2,1)}, bf16[256,256]{0,1:T(8,128)(2,1)S(1)}, u32[]{:S(2)}) copy-start(bf16[256,256]{0,1:T(8,128)(2,1)S(1)} %copy.43) | copy-start | bytes 393220 | tf_op jit(solution)/shard_map/while
  91.8 1.2 copy-start
  99.3 4.0 %copy-start.3 = (f32[656,1024]{1,0:T(8,128)S(1)}, f32[656,1024]{1,0:T(8,128)}, u32[]{:S(2)}) copy-start(f32[656,1024]{1,0:T(8,128)} %get-tuple-element.286) | copy-start | bytes 8060932
  101.0 2.4 %copy-start.2 = (f32[656,1024]{1,0:T(8,128)S(1)}, f32[656,1024]{1,0:T(8,128)}, u32[]{:S(2)}) copy-start(f32[656,1024]{1,0:T(8,128)} %get-tuple-element.285) | copy-start | bytes 8060932
  101.3 38.7 %collective-permute-start.2 = (f32[2,256,1024]{2,1,0:T(8,128)S(1)}, f32[2,256,1024]{2,1,0:T(8,128)S(1)}, u32[]{:S(2)}, u32[]{:S(2)}) collective-permute-start(f32[2,256,1024]{2,1,0:T(8,128)S(1)} %concatenate.10), channel_id=1, source_target_pairs={{1,0},{2,1},{3,2},{4,3},{5,4},{6,5},{7,6},{8,7},{9,8},{10,9},{11,1... | collective-permute-start | bytes 6291464 | tf_op jit(solution)/shard_map/ppermute | solution.py:18
  103.6 29.2 %collective-permute-start.3 = (bf16[2,256,1024]{2,1,0:T(8,128)(2,1)S(1)}, bf16[2,256,1024]{2,1,0:T(8,128)(2,1)S(1)}, u32[]{:S(2)}, u32[]{:S(2)}) collective-permute-start(bf16[2,256,1024]{2,1,0:T(8,128)(2,1)S(1)} %concatenate.11), channel_id=1, source_target_pairs={{0,1},{1,2},{2,3},{3,4},{4,5},{5,6},{6,7},{7,8},{8,9},{9,10},{10,1... | collective-permute-start | bytes 3145736 | tf_op jit(solution)/shard_map/ppermute | solution.py:18
where the time goes:
time: 143 us; the launch traced here: 142 us
  waiting for transfers between devices  55 us (38%)
  local copies, waits for them, and re-layouts  43.4 us (30%)
  matrix products  22.6 us (16%)
  starting transfers between devices  11.3 us (8%)
  other arithmetic  7.92 us (6%)
    ppermute x4, waiting for transfers between devices, passed_along(): lax.ppermute(value, axis, [(source, source + steps) for source in range(i...  55 us
    ppermute x4, starting transfers between devices, passed_along(): lax.ppermute(value, axis, [(source, source + steps) for source in range(i...  11.3 us
    dot_general x4, matrix products, query_pass(): jnp.einsum('hrc,rhe->che', dscores, q_heads, preferred_element_type=jnp.f...  7.7 us
    dynamic_update_slice x8, local copies, waits for them, and re-layouts, group_step(): value_acc = lax.dynamic_update_slice_in_dim(value_acc, pieces[3], offset, 1)  5.93 us
    dot_general x4, matrix products, query_pass(): jnp.einsum('hrc,rhe->che', probs_low, g_heads, preferred_element_type=jnp...  5.76 us
    another operation x4, local copies, waits for them, and re-layouts  5.43 us
    while x24, local copies, waits for them, and re-layouts  4.67 us
    dynamic_slice x4, local copies, waits for them, and re-layouts, group_step(): lax.dynamic_slice_in_dim(values_wide, offset, width, 1)  4.3 us
  transfers between devices with their start and end apart: 4, of which 4 were waited for; matrix products, arithmetic and copies ran while one was open for 0% of the time, Pallas kernels for 0%

commit v1 on v0

v1 whole, which is shorter than its diff:
```python
import functools
import math

import jax
import jax.numpy as jnp
from jax import lax
from jax.experimental import pallas as pl
from jax.experimental.pallas import tpu as pltpu
from jax.sharding import PartitionSpec as P

HEADS = 16
HEAD_DIM = 64
ROWMIN = 20
STEP = 4
PAIR = 2 * HEAD_DIM
PAIRS = HEADS // 2
SCALE = HEAD_DIM**-0.5
EXP2_SCALE = SCALE * math.log2(math.e)
OUTSIDE = -1e30
QG_CHUNKS = (0, 4, 8)
VMEM_BYTES = 40 * 2**20


def passed_along(value, steps):
    count = lax.axis_size("band")
    initial, last = (max(0, -steps), min(count, count - steps))
    return lax.ppermute(value, "band", [(source, source + steps) for source in range(initial, last)])


def reach_sizes(points, count):
    area_rows = points * count // STEP
    root_bound = min(((area_rows + 2 * 4**power) // (3 * 2**power) for power in range(3, 9)))
    grow_rows = root_bound - ROWMIN // STEP - 6
    row_longest = ROWMIN + STEP * (grow_rows - 1)
    rim_width = (2 * row_longest + 15) // 16 * 16
    return (rim_width, (rim_width + points - 1) // points)


def dot_nt(left, right):
    return lax.dot_general(
        left, right, (((1,), (1,)), ((), ())), preferred_element_type=jnp.float32
    )


def dot_nn(left, right):
    return jnp.dot(left, right, preferred_element_type=jnp.float32)


def head_masks():
    lanes = lax.broadcasted_iota(jnp.int32, (1, PAIR), 1)
    first = (lanes < HEAD_DIM).astype(jnp.float32).astype(jnp.bfloat16)
    return (first, (1.0 - first.astype(jnp.float32)).astype(jnp.bfloat16))


def own_kernel(firsts, lengths, points, *refs):
    count = len(firsts)
    win_ref, q_ref, g_ref, k_ref, v_ref = refs[:5]
    halo_refs = refs[5 : 5 + count - 1]
    att_ref, dq_ref, dk_ref, dv_ref = refs[5 + count - 1 : 9 + count - 1]
    stat_refs = refs[9 + count - 1 : 9 + 2 * (count - 1)]
    bias_ref = refs[-1]
    own = count // 2
    rows = [sum(lengths[:at]) for at in range(count)]

    @pl.when(pl.program_id(0) == 0)
    def _():
        lower = win_ref[0:1, :]
        upper = win_ref[1:2, :]
        for at in range(count):
            keys = firsts[at] + lax.broadcasted_iota(jnp.int32, (lengths[at], points), 0)
            inside = (keys >= lower) & (keys < upper)
            bias_ref[rows[at] : rows[at] + lengths[at], :] = jnp.where(inside, 0.0, OUTSIDE)

    q = q_ref[...]
    g = g_ref[...]
    ks, vs = [], []
    for at in range(count):
        if at == own:
            ks.append(k_ref[...])
            vs.append(v_ref[...])
        else:
            ref = halo_refs[at if at < own else at - 1]
            ks.append(ref[0])
            vs.append(ref[1])
    k_all = jnp.concatenate(ks, axis=0)
    v_all = jnp.concatenate(vs, axis=0)
    k_turned = k_all.T
    v_turned = v_all.T
    g_turned = g.T
    own_rows = slice(rows[own], rows[own] + points)
    att, dq, stats = [], [], []
    dk = dv = None
    for head, mask in enumerate(head_masks()):
        part = slice(head * HEAD_DIM, (head + 1) * HEAD_DIM)
        q_head = q * mask
        g_head = g * mask
        scores = dot_nt(k_all, q_head) + bias_ref[...]
        top = jnp.max(scores, axis=0, keepdims=True)
        probs = jnp.exp2((scores - top) * EXP2_SCALE)
        total = jnp.sum(probs, axis=0, keepdims=True)
        probs = probs * (1.0 / total)
        stats.append(top + jnp.log(total) * (1.0 / SCALE))
        probs_low = probs.astype(jnp.bfloat16)
        att_head = dot_nn(v_turned[part], probs_low).astype(jnp.bfloat16)
        delta = jnp.sum(
            g_turned[part].astype(jnp.float32) * att_head.astype(jnp.float32), axis=0, keepdims=True
        )
        stats.append(delta)
        dscores = (probs * (dot_nt(v_all, g_head) - delta)).astype(jnp.bfloat16)
        dq_head = (dot_nn(k_turned[part], dscores) * SCALE).astype(jnp.bfloat16)
        att.append(att_head)
        dq.append(dq_head)
        dk_head = dot_nn(dscores[own_rows], q_head)
        dv_head = dot_nn(probs_low[own_rows], g_head)
        dk = dk_head if dk is None else dk + dk_head
        dv = dv_head if dv is None else dv + dv_head
    att_ref[...] = jnp.concatenate(att, axis=0).T
    dq_ref[...] = jnp.concatenate(dq, axis=0).T
    dk_ref[...] = dk
    dv_ref[...] = dv
    stats = jnp.concatenate(stats, axis=0)
    for ref, at in zip(stat_refs, [at for at in range(count) if at != own]):
        ref[0] = stats[:, points - lengths[at] :] if at < own else stats[:, : lengths[at]]


def halo_kernel(firsts, lengths, points, *refs):
    count = len(firsts)
    win_ref, k_ref, v_ref, dk_part_ref, dv_part_ref = refs[:5]
    qg_refs = refs[5 : 5 + count]
    stat_refs = refs[5 + count : 5 + 2 * count]
    dk_ref, dv_ref = refs[-2 - count : -count]
    bias_refs = refs[-count:]
    lows = [first < 0 for first in firsts]
    starts = [0 if low else points - length for low, length in zip(lows, lengths)]

    @pl.when(pl.program_id(0) == 0)
    def _():
        for at in range(count):
            part = slice(starts[at], starts[at] + lengths[at])
            queries = firsts[at] + lax.broadcasted_iota(jnp.int32, (lengths[at], lengths[at]), 1)
            inside = (queries >= win_ref[part, 0:1]) & (queries < win_ref[part, 1:2])
            bias_refs[at][...] = jnp.where(inside, 0.0, OUTSIDE)

    dk_ref_sum = dk_part_ref[...]
    dv_ref_sum = dv_part_ref[...]
    for at in range(count):
        part = slice(starts[at], starts[at] + lengths[at])
        k = k_ref[part, :]
        v = v_ref[part, :]
        q = qg_refs[at][0]
        g = qg_refs[at][1]
        stats = stat_refs[at][0]
        dk = dv = None
        for head, mask in enumerate(head_masks()):
            q_head = q * mask
            g_head = g * mask
            lse = stats[2 * head : 2 * head + 1]
            delta = stats[2 * head + 1 : 2 * head + 2]
            scores = dot_nt(k, q_head) + bias_refs[at][...]
            probs = jnp.exp2((scores - lse) * EXP2_SCALE)
            dscores = (probs * (dot_nt(v, g_head) - delta)).astype(jnp.bfloat16)
            dk_head = dot_nn(dscores, q_head)
            dv_head = dot_nn(probs.astype(jnp.bfloat16), g_head)
            dk = dk_head if dk is None else dk + dk_head
            dv = dv_head if dv is None else dv + dv_head
        if lengths[at] < points:
            blank = jnp.zeros((points - lengths[at], PAIR), jnp.float32)
            order = (lambda x: [x, blank]) if lows[at] else (lambda x: [blank, x])
            dk = jnp.concatenate(order(dk), axis=0)
            dv = jnp.concatenate(order(dv), axis=0)
        dk_ref_sum = dk_ref_sum + dk
        dv_ref_sum = dv_ref_sum + dv
    dk_ref[...] = (dk_ref_sum * SCALE).astype(jnp.bfloat16)
    dv_ref[...] = dv_ref_sum.astype(jnp.bfloat16)


def compiler_params():
    return pltpu.CompilerParams(
        vmem_limit_bytes=VMEM_BYTES, dimension_semantics=("arbitrary",)
    )


def per_device(queries, keys, values, grad_out, windows):
    points, width = queries.shape
    rim_width, reach = reach_sizes(points, lax.axis_size("band"))
    offsets = [d for d in range(-reach, reach + 1) if d != 0]
    sizes = [min(points, rim_width - (abs(d) - 1) * points) for d in offsets]
    firsts = [(d + 1) * points - n if d < 0 else d * points for d, n in zip(offsets, sizes)]
    relative = windows - lax.axis_index("band") * points

    def edge(field, offset, size):
        return field[points - size :] if offset < 0 else field[:size]

    def fetch(fields, columns):
        return [
            passed_along(
                jnp.stack([edge(field, d, n)[:, columns] for field in fields]), -d
            )
            for d, n in zip(offsets, sizes)
        ]

    kv_halo = fetch([keys, values], slice(0, width))
    qg_halo = [
        fetch([queries, grad_out], slice(low * PAIR, high * PAIR))
        for low, high in zip(QG_CHUNKS[:-1], QG_CHUNKS[1:])
    ]

    pair_block = pl.BlockSpec((points, PAIR), lambda i: (0, i))
    own_count = len(offsets) + 1
    own_at = own_count // 2
    all_sizes = sizes[:own_at] + [points] + sizes[own_at:]
    all_firsts = firsts[:own_at] + [0] + firsts[own_at:]
    wide = sum(all_sizes)
    outs = pl.pallas_call(
        functools.partial(own_kernel, all_firsts, all_sizes, points),
        grid=(PAIRS,),
        in_specs=[pl.BlockSpec((2, points), lambda i: (0, 0))]
        + [pair_block] * 4
        + [pl.BlockSpec((2, n, PAIR), lambda i: (0, 0, i)) for n in sizes],
        out_specs=[pair_block] * 4 + [pl.BlockSpec((1, 4, n), lambda i: (i, 0, 0)) for n in sizes],
        out_shape=[
            jax.ShapeDtypeStruct((points, width), jnp.bfloat16),
            jax.ShapeDtypeStruct((points, width), jnp.bfloat16),
            jax.ShapeDtypeStruct((points, width), jnp.float32),
            jax.ShapeDtypeStruct((points, width), jnp.float32),
        ]
        + [jax.ShapeDtypeStruct((PAIRS, 4, n), jnp.float32) for n in sizes],
        scratch_shapes=[pltpu.VMEM((wide, points), jnp.float32)],
        compiler_params=compiler_params(),
        cost_estimate=pl.CostEstimate(
            flops=HEADS * 8 * points * wide * PAIR,
            bytes_accessed=2 * width * (6 * points + 2 * wide) + 8 * points * width,
            transcendentals=HEADS * points * wide,
        ),
        name="own_queries",
    )(relative.T, queries, grad_out, keys, values, *kv_halo)
    attended, grad_q, dk_part, dv_part = outs[:4]
    stats_halo = [passed_along(stat, -d) for stat, d in zip(outs[4:], offsets)]

    grads = None
    for chunk, (low, high) in enumerate(zip(QG_CHUNKS[:-1], QG_CHUNKS[1:])):
        from_low = functools.partial(lambda low, i: (0, i + low), low)
        block = pl.BlockSpec((points, PAIR), from_low)
        carried = [] if grads is None else list(grads)
        kernel = functools.partial(halo_kernel, firsts, sizes, points)
        args = [relative, keys, values, dk_part, dv_part, *qg_halo[chunk], *stats_halo]
        if carried:
            inner = kernel
            kernel = functools.partial(
                lambda inner, at, *refs: inner(*refs[:at], *refs[at + 2 :]), inner, len(args)
            )
        grads = pl.pallas_call(
            kernel,
            grid=(high - low,),
            in_specs=[pl.BlockSpec((points, 2), lambda i: (0, 0))]
            + [block] * 4
            + [pl.BlockSpec((2, n, PAIR), lambda i: (0, 0, i)) for n in sizes]
            + [
                pl.BlockSpec((1, 4, n), functools.partial(lambda low, i: (i + low, 0, 0), low))
                for n in sizes
            ]
            + [pl.BlockSpec(memory_space=pl.ANY)] * len(carried),
            out_specs=[block] * 2,
            out_shape=[jax.ShapeDtypeStruct((points, width), jnp.bfloat16)] * 2,
            input_output_aliases={len(args) + at: at for at in range(len(carried))},
            scratch_shapes=[pltpu.VMEM((n, n), jnp.float32) for n in sizes],
            compiler_params=compiler_params(),
            cost_estimate=pl.CostEstimate(
                flops=(high - low) * 2 * sum(8 * n * n * PAIR for n in sizes),
                bytes_accessed=(high - low) * PAIR * 20 * points,
                transcendentals=(high - low) * 2 * sum(n * n for n in sizes),
            ),
            name=f"halo_queries_{chunk}",
        )(*args, *carried)
    return (attended, grad_q, grads[0], grads[1])


def solution(mesh):
    spread = P(("members", "band"), None)
    return jax.shard_map(
        per_device,
        mesh=mesh,
        in_specs=(spread, spread, spread, spread, P("band", None)),
        out_specs=(spread, spread, spread, spread),
        check_vma=False,
    )
```

time: 143 us -> 73.7 us (0.52)
  waiting for transfers between devices: 55 us -> 12.2 us
  local copies, waits for them, and re-layouts: 43.4 us -> 3.64 us
  Pallas kernels: 0 us -> 29.4 us
  matrix products: 22.6 us -> 0 us
  starting transfers between devices: 11.3 us -> 21 us
  other arithmetic: 7.92 us -> 6.16 us
    ppermute x4 -> x8, waiting for transfers between devices: 55 us -> 12.2 us  [passed_along(): lax.ppermute(value, 'band', [(source, source + steps) for source in range...]
    pallas_call x0 -> x3, Pallas kernels: none -> 29.4 us  [the longest x1 19.8 us: per_device(): pl.pallas_call(functools.partial(own_kernel, all_firsts, all_sizes, point...]
    dot_general x24 -> x0, matrix products: 22.6 us -> none  [the longest x4 7.7 us: query_pass(): jnp.einsum('hrc,rhe->che', dscores, q_heads, preferred_element_type=jnp.f...]
    dynamic_slice x24 -> x0, local copies, waits for them, and re-layouts: 16.5 us -> none  [the longest x4 4.3 us: group_step(): lax.dynamic_slice_in_dim(values_wide, offset, width, 1)]
    dynamic_update_slice x24 -> x0, local copies, waits for them, and re-layouts: 10.5 us -> none  [the longest x8 5.93 us: group_step(): value_acc = lax.dynamic_update_slice_in_dim(value_acc, pieces[3], offset, 1)]
    ppermute x4 -> x8, starting transfers between devices: 11.3 us -> 21 us  [passed_along(): lax.ppermute(value, 'band', [(source, source + steps) for source in range...]
    while x24 -> x0, local copies, waits for them, and re-layouts: 4.67 us -> none
    concatenate x1 -> x0, other arithmetic: 3.1 us -> none  [surround(): return jnp.concatenate([low_part, field, high_part], axis=1)]
  transfers between devices with their start and end apart: 4 -> 8, of which waited for: 4 -> 3; matrix products, arithmetic and copies ran while one was open for 0% -> 10% of each run, Pallas kernels for 0% -> 34%
where the time goes in v1:
time: 73.7 us; the launch traced here: 73.3 us
  Pallas kernels  29.4 us (40%)
  starting transfers between devices  21 us (28%)
  waiting for transfers between devices  12.2 us (17%)
  other arithmetic  6.16 us (8%)
  local copies, waits for them, and re-layouts  3.64 us (5%)
  between operations  0.81 us (1%)
    ppermute x8, starting transfers between devices, passed_along(): lax.ppermute(value, 'band', [(source, source + steps) for source in range...  21 us
    pallas_call x1, Pallas kernels, per_device(): pl.pallas_call(functools.partial(own_kernel, all_firsts, all_sizes, point...  19.8 us
    ppermute x8, waiting for transfers between devices, passed_along(): lax.ppermute(value, 'band', [(source, source + steps) for source in range...  12.2 us
    pallas_call x2, Pallas kernels, per_device(): pl.pallas_call(kernel, grid=(high - low,), in_specs=[pl.BlockSpec((points...  9.65 us
    another operation x6, other arithmetic, fetch(): jnp.stack([edge(field, d, n)[:, columns] for field in fields])  5.48 us
    another operation x2, local copies, waits for them, and re-layouts, fetch(): jnp.stack([edge(field, d, n)[:, columns] for field in fields])  2.44 us
  transfers between devices with their start and end apart: 8, of which 3 were waited for; matrix products, arithmetic and copies ran while one was open for 10% of the time, Pallas kernels for 34%

profile of v1, /device:TPU:9, one launch (start us, length us, event | category | flops | bytes accessed | tf_op | source)
XLA Modules:
  0.0 73.3 jit_solution(3784407758238996828)
XLA Ops:
  0.6 1.6 %slice_bitcast_fusion = (bf16[1,208,1024]{2,1,0:T(8,128)(2,1)S(1)}, bf16[1,208,1024]{2,1,0:T(8,128)(2,1)S(1)}, bf16[1,208,1024]{2,1,0:T(8,128)(2,1)S(1)}, bf16[1,208,1024]{2,1,0:T(8,128)(2,1)S(1)}) fusion(bf16[256,1024]{1,0:T(8,128)(2,1)} %refs_2_.5, bf16[256,1024]{1,0:T(8,128)(2,1)} %refs_1_.5), kind=kLoop, calls=%fused_computation.6 | loop fusion | bytes 3407872 | tf_op jit(solution)/shard_map/stack | solution.py:197
  2.2 1.0 %pad_maximum_fusion = bf16[2,208,1024]{2,1,0:T(8,128)(2,1)} fusion(bf16[1,208,1024]{2,1,0:T(8,128)(2,1)S(1)} %get-tuple-element.35, bf16[1,208,1024]{2,1,0:T(8,128)(2,1)S(1)} %get-tuple-element.36), kind=kLoop, calls=%fused_computation | loop fusion | flops 425984 | bytes 1703936 | tf_op jit(solution)/shard_map/stack | solution.py:197
  3.2 3.7 %collective-permute-start = (bf16[2,208,1024]{2,1,0:T(8,128)(2,1)}, bf16[2,208,1024]{2,1,0:T(8,128)(2,1)}, u32[]{:S(2)}, u32[]{:S(2)}) collective-permute-start(bf16[2,208,1024]{2,1,0:T(8,128)(2,1)} %pad_maximum_fusion), channel_id=1, source_target_pairs={{0,1},{1,2},{2,3},{3,4},{4,5},{5,6},{6,7},{7,8},{8,9},{9,10},{10,1... | collective-permute-start | bytes 2555912 | tf_op jit(solution)/shard_map/ppermute | solution.py:27
  6.9 0.0 copy-start.2
  6.9 0.0 copy-start.3
  6.9 1.0 %pad_maximum_fusion.1 = bf16[2,208,1024]{2,1,0:T(8,128)(2,1)} fusion(bf16[1,208,1024]{2,1,0:T(8,128)(2,1)S(1)} %get-tuple-element.34, bf16[1,208,1024]{2,1,0:T(8,128)(2,1)S(1)} %get-tuple-element.37), kind=kLoop, calls=%fused_computation.1 | loop fusion | flops 425984 | bytes 1703936 | tf_op jit(solution)/shard_map/stack | solution.py:197
  7.9 1.9 %collective-permute-start.1 = (bf16[2,208,1024]{2,1,0:T(8,128)(2,1)}, bf16[2,208,1024]{2,1,0:T(8,128)(2,1)}, u32[]{:S(2)}, u32[]{:S(2)}) collective-permute-start(bf16[2,208,1024]{2,1,0:T(8,128)(2,1)} %pad_maximum_fusion.1), channel_id=1, source_target_pairs={{1,0},{2,1},{3,2},{4,3},{5,4},{6,5},{7,6},{8,7},{9,8},{10,9},{11,1... | collective-permute-start | bytes 2555912 | tf_op jit(solution)/shard_map/ppermute | solution.py:27
  9.8 0.0 copy-done.2
  9.8 0.0 copy-done.3
  9.9 0.9 %slice_bitcast_fusion.4 = (bf16[1,208,512]{2,1,0:T(8,128)(2,1)}, bf16[1,208,512]{2,1,0:T(8,128)(2,1)S(1)}, bf16[1,208,512]{2,1,0:T(8,128)(2,1)S(1)}, bf16[1,208,...) fusion(bf16[256,1024]{1,0:T(8,128)(2,1)S(1)} %copy-done.3, ...), kind=kLoop, calls=%fused_computation.10 | loop fusion | bytes 3407872 | tf_op jit(solution)/shard_map/stack | solution.py:197
  10.7 0.8 %pad_maximum_fusion.2 = bf16[2,208,512]{2,1,0:T(8,128)(2,1)} fusion(bf16[1,208,512]{2,1,0:T(8,128)(2,1)S(1)} %get-tuple-element.30, bf16[1,208,512]{2,1,0:T(8,128)(2,1)S(1)} %get-tuple-element.39), kind=kLoop, calls=%fused_computation.2 | loop fusion | flops 212992 | bytes 851968 | tf_op jit(solution)/shard_map/stack | solution.py:197
  11.5 3.6 %collective-permute-start.2 = (bf16[2,208,512]{2,1,0:T(8,128)(2,1)}, bf16[2,208,512]{2,1,0:T(8,128)(2,1)S(1)}, u32[]{:S(2)}, u32[]{:S(2)}) collective-permute-start(bf16[2,208,512]{2,1,0:T(8,128)(2,1)} %pad_maximum_fusion.2), channel_id=1, source_target_pairs={{0,1},{1,2},{2,3},{3,4},{4,5},{5,6},{6,7},{7,8},{8,9},{9,10},{10,1... | collective-permute-start | bytes 1277960 | tf_op jit(solution)/shard_map/ppermute | solution.py:27
  15.2 0.8 %pad_maximum_fusion.3 = bf16[2,208,512]{2,1,0:T(8,128)(2,1)} fusion(bf16[1,208,512]{2,1,0:T(8,128)(2,1)S(1)} %get-tuple-element.29, bf16[1,208,512]{2,1,0:T(8,128)(2,1)S(1)} %get-tuple-element.40), kind=kLoop, calls=%fused_computation.3 | loop fusion | flops 212992 | bytes 851968 | tf_op jit(solution)/shard_map/stack | solution.py:197
  16.0 1.9 %collective-permute-start.3 = (bf16[2,208,512]{2,1,0:T(8,128)(2,1)}, bf16[2,208,512]{2,1,0:T(8,128)(2,1)S(1)}, u32[]{:S(2)}, u32[]{:S(2)}) collective-permute-start(bf16[2,208,512]{2,1,0:T(8,128)(2,1)} %pad_maximum_fusion.3), channel_id=1, source_target_pairs={{1,0},{2,1},{3,2},{4,3},{5,4},{6,5},{7,6},{8,7},{9,8},{10,9},{11,1... | collective-permute-start | bytes 1277960 | tf_op jit(solution)/shard_map/ppermute | solution.py:27
  17.9 0.0 copy-start.4
  17.9 0.8 %pad_maximum_fusion.4 = bf16[2,208,512]{2,1,0:T(8,128)(2,1)} fusion(bf16[1,208,512]{2,1,0:T(8,128)(2,1)S(1)} %get-tuple-element.31, bf16[1,208,512]{2,1,0:T(8,128)(2,1)S(1)} %get-tuple-element.38), kind=kLoop, calls=%fused_computation.4 | loop fusion | flops 212992 | bytes 851968 | tf_op jit(solution)/shard_map/stack | solution.py:197
  18.7 3.6 %collective-permute-start.6 = (bf16[2,208,512]{2,1,0:T(8,128)(2,1)}, bf16[2,208,512]{2,1,0:T(8,128)(2,1)S(1)}, u32[]{:S(2)}, u32[]{:S(2)}) collective-permute-start(bf16[2,208,512]{2,1,0:T(8,128)(2,1)} %pad_maximum_fusion.4), channel_id=1, source_target_pairs={{0,1},{1,2},{2,3},{3,4},{4,5},{5,6},{6,7},{7,8},{8,9},{9,10},{10,1... | collective-permute-start | bytes 1277960 | tf_op jit(solution)/shard_map/ppermute | solution.py:27
  22.3 0.0 copy-done.4
  22.4 0.1 copy.11
  22.5 0.0 copy-start.1
  22.5 0.7 fusion
  23.2 0.0 copy-start
  23.2 1.0 %copy.12.refs_0_ = s32[2,256]{1,0:T(2,128)S(1)} copy(s32[2,256]{0,1:T(8,128)} %fusion) | data formatting | bytes 4096 | tf_op jit(solution)/shard_map/transpose | solution.py:236
  24.2 1.1 %pad_maximum_fusion.5 = bf16[2,208,512]{2,1,0:T(8,128)(2,1)S(1)} fusion(bf16[1,208,512]{2,1,0:T(8,128)(2,1)} %get-tuple-element.28, bf16[1,208,512]{2,1,0:T(8,128)(2,1)} %get-tuple-element.41), kind=kLoop, calls=%fused_computation.5 | loop fusion | flops 212992 | bytes 851968 | tf_op jit(solution)/shard_map/stack | solution.py:197
  25.3 5.2 %collective-permute-done.refs_5_ = bf16[2,208,1024]{2,1,0:T(8,128)(2,1)} collective-permute-done((bf16[2,208,1024]{2,1,0:T(8,128)(2,1)}, bf16[2,208,1024]{2,1,0:T(8,128)(2,1)}, u32[]{:S(2)}, u32[]{:S(2)}) %collective-permute-start) | collective-permute-done | bytes 852000 | tf_op jit(solution)/shard_map/ppermute | solution.py:27
  30.5 1.9 %collective-permute-start.7 = (bf16[2,208,512]{2,1,0:T(8,128)(2,1)S(1)}, bf16[2,208,512]{2,1,0:T(8,128)(2,1)S(1)}, u32[]{:S(2)}, u32[]{:S(2)}) collective-permute-start(bf16[2,208,512]{2,1,0:T(8,128)(2,1)S(1)} %pad_maximum_fusion.5), channel_id=1, source_target_pairs={{1,0},{2,1},{3,2},{4,3},{5,4},{6,5},{7,6},{8,7},{9,8},{10,9},{11,1... | collective-permute-start | bytes 1277960 | tf_op jit(solution)/shard_map/ppermute | solution.py:27
  32.5 4.2 %collective-permute-done.1.refs_6_ = bf16[2,208,1024]{2,1,0:T(8,128)(2,1)} collective-permute-done((bf16[2,208,1024]{2,1,0:T(8,128)(2,1)}, bf16[2,208,1024]{2,1,0:T(8,128)(2,1)}, u32[]{:S(2)}, u32[]{:S(2)}) %collective-permute-start.1) | collective-permute-done | bytes 852000 | tf_op jit(solution)/shard_map/ppermute | solution.py:27
  36.7 0.0 copy-done.1
  36.7 0.0 copy-done
  36.7 19.8 %own_queries.1 = (bf16[256,1024]{1,0:T(8,128)(2,1)}, bf16[256,1024]{1,0:T(8,128)(2,1)}, f32[256,1024]{1,0:T(8,128)S(1)}, f32[256,1024]{1,0:T(8,128)S(1)}, f32[8,...) custom-call(s32[2,256]{1,0:T(2,128)S(1)} %copy.12.refs_0_, bf16[256,1024]{1,0:T(8,128)(2,1)S(1)} %copy-done.2, ...), custom_call_target="tpu_custom_call" | custom-call | flops 2818572288 | bytes 7995392 | tf_op jit(solution)/shard_map/own_queries/pallas_call | solution.py:214
  56.5 1.9 %collective-permute-start.4 = (f32[8,4,208]{2,1,0:T(4,128)S(1)}, f32[8,4,208]{2,1,0:T(4,128)S(1)}, u32[]{:S(2)}, u32[]{:S(2)}) collective-permute-start(f32[8,4,208]{2,1,0:T(4,128)S(1)} %get-tuple-element.18), channel_id=1, source_target_pairs={{0,1},{1,2},{2,3},{3,4},{4,5},{5,6},{6,7},{7,8},{8,9},{9,10},{10,1... | collective-permute-start | bytes 79880 | tf_op jit(solution)/shard_map/ppermute | solution.py:27
  58.4 0.0 collective-permute-done.6.refs_5_
  58.4 2.4 %collective-permute-start.5 = (f32[8,4,208]{2,1,0:T(4,128)S(1)}, f32[8,4,208]{2,1,0:T(4,128)S(1)}, u32[]{:S(2)}, u32[]{:S(2)}) collective-permute-start(f32[8,4,208]{2,1,0:T(4,128)S(1)} %get-tuple-element.19), channel_id=1, source_target_pairs={{1,0},{2,1},{3,2},{4,3},{5,4},{6,5},{7,6},{8,7},{9,8},{10,9},{11,1... | collective-permute-start | bytes 79880 | tf_op jit(solution)/shard_map/ppermute | solution.py:27
  60.8 0.0 collective-permute-done.7.refs_6_
  60.8 0.0 collective-permute-done.4.refs_7_
  60.8 2.8 %collective-permute-done.5.refs_8_ = f32[8,4,208]{2,1,0:T(4,128)S(1)} collective-permute-done((f32[8,4,208]{2,1,0:T(4,128)S(1)}, f32[8,4,208]{2,1,0:T(4,128)S(1)}, u32[]{:S(2)}, u32[]{:S(2)}) %collective-permute-start.5) | collective-permute-done | bytes 26656 | tf_op jit(solution)/shard_map/ppermute | solution.py:27
  63.6 4.8 %halo_queries_0.1 = (bf16[256,1024]{1,0:T(8,128)(2,1)}, bf16[256,1024]{1,0:T(8,128)(2,1)}) custom-call(s32[256,2]{1,0:T(8,128)S(1)} %broadcast_subtract_fusion.refs_0_, bf16[256,1024]{1,0:T(8,128)(2,1)S(1)} %copy-done, bf16[256,1024]{1,0:T(8,128)(2,1)S(1)} %copy-done.1, f32[256,1024]{1,0:T(8,128)S(1)} %get-tuple-element.16.refs_3_, ...), custom_call_target="tpu_custom_call" | custom-call | flops 708837376 | bytes 2621440 | tf_op jit(solution)/shard_map/halo_queries_0/pallas_call | solution.py:252
  68.4 0.0 collective-permute-done.2.refs_5_
  68.4 0.0 collective-permute-done.3.refs_6_
  68.4 4.8 %halo_queries_1.1 = (bf16[256,1024]{1,0:T(8,128)(2,1)}, bf16[256,1024]{1,0:T(8,128)(2,1)}) custom-call(s32[256,2]{1,0:T(8,128)S(1)} %broadcast_subtract_fusion.refs_0_, bf16[256,1024]{1,0:T(8,128)(2,1)S(1)} %copy-done, bf16[256,1024]{1,0:T(8,128)(2,1)S(1)} %copy-done.1, ...), custom_call_target="tpu_custom_call", output_to_operand_aliasing={{0}: (9, {}), {1}: (10, {})} | custom-call | flops 708837376 | bytes 2621440 | tf_op jit(solution)/shard_map/halo_queries_1/pallas_call | solution.py:252
  (1 shorter events, 0.0 us)
Async XLA Ops:
  3.2 27.3 %collective-permute-start = (bf16[2,208,1024]{2,1,0:T(8,128)(2,1)}, bf16[2,208,1024]{2,1,0:T(8,128)(2,1)}, u32[]{:S(2)}, u32[]{:S(2)}) collective-permute-start(bf16[2,208,1024]{2,1,0:T(8,128)(2,1)} %pad_maximum_fusion), channel_id=1, source_target_pairs={{0,1},{1,2},{2,3},{3,4},{4,5},{5,6},{6,7},{7,8},{8,9},{9,10},{10,1... | collective-permute-start | bytes 2555912 | tf_op jit(solution)/shard_map/ppermute | solution.py:27
  6.9 2.9 %copy-start.2 = (bf16[256,1024]{1,0:T(8,128)(2,1)S(1)}, bf16[256,1024]{1,0:T(8,128)(2,1)}, u32[]{:S(2)}) copy-start(bf16[256,1024]{1,0:T(8,128)(2,1)} %refs_1_.3) | copy-start | bytes 1572868
  6.9 2.9 %copy-start.3 = (bf16[256,1024]{1,0:T(8,128)(2,1)S(1)}, bf16[256,1024]{1,0:T(8,128)(2,1)}, u32[]{:S(2)}) copy-start(bf16[256,1024]{1,0:T(8,128)(2,1)} %refs_2_.3) | copy-start | bytes 1572868
  7.9 28.8 %collective-permute-start.1 = (bf16[2,208,1024]{2,1,0:T(8,128)(2,1)}, bf16[2,208,1024]{2,1,0:T(8,128)(2,1)}, u32[]{:S(2)}, u32[]{:S(2)}) collective-permute-start(bf16[2,208,1024]{2,1,0:T(8,128)(2,1)} %pad_maximum_fusion.1), channel_id=1, source_target_pairs={{1,0},{2,1},{3,2},{4,3},{5,4},{6,5},{7,6},{8,7},{9,8},{10,9},{11,1... | collective-permute-start | bytes 2555912 | tf_op jit(solution)/shard_map/ppermute | solution.py:27
  11.5 56.9 %collective-permute-start.2 = (bf16[2,208,512]{2,1,0:T(8,128)(2,1)}, bf16[2,208,512]{2,1,0:T(8,128)(2,1)S(1)}, u32[]{:S(2)}, u32[]{:S(2)}) collective-permute-start(bf16[2,208,512]{2,1,0:T(8,128)(2,1)} %pad_maximum_fusion.2), channel_id=1, source_target_pairs={{0,1},{1,2},{2,3},{3,4},{4,5},{5,6},{6,7},{7,8},{8,9},{9,10},{10,1... | collective-permute-start | bytes 1277960 | tf_op jit(solution)/shard_map/ppermute | solution.py:27
  16.0 52.5 %collective-permute-start.3 = (bf16[2,208,512]{2,1,0:T(8,128)(2,1)}, bf16[2,208,512]{2,1,0:T(8,128)(2,1)S(1)}, u32[]{:S(2)}, u32[]{:S(2)}) collective-permute-start(bf16[2,208,512]{2,1,0:T(8,128)(2,1)} %pad_maximum_fusion.3), channel_id=1, source_target_pairs={{1,0},{2,1},{3,2},{4,3},{5,4},{6,5},{7,6},{8,7},{9,8},{10,9},{11,1... | collective-permute-start | bytes 1277960 | tf_op jit(solution)/shard_map/ppermute | solution.py:27
  17.9 4.5 %copy-start.4 = (s32[256,2]{0,1:T(2,128)S(1)}, s32[256,2]{0,1:T(2,128)}, u32[]{:S(2)}) copy-start(s32[256,2]{0,1:T(2,128)} %param.9) | copy-start | bytes 6148
  18.7 39.7 %collective-permute-start.6 = (bf16[2,208,512]{2,1,0:T(8,128)(2,1)}, bf16[2,208,512]{2,1,0:T(8,128)(2,1)S(1)}, u32[]{:S(2)}, u32[]{:S(2)}) collective-permute-start(bf16[2,208,512]{2,1,0:T(8,128)(2,1)} %pad_maximum_fusion.4), channel_id=1, source_target_pairs={{0,1},{1,2},{2,3},{3,4},{4,5},{5,6},{6,7},{7,8},{8,9},{9,10},{10,1... | collective-permute-start | bytes 1277960 | tf_op jit(solution)/shard_map/ppermute | solution.py:27
  22.5 14.2 %copy-start.1 = (bf16[256,1024]{1,0:T(8,128)(2,1)S(1)}, bf16[256,1024]{1,0:T(8,128)(2,1)}, u32[]{:S(2)}) copy-start(bf16[256,1024]{1,0:T(8,128)(2,1)} %refs_2_.5) | copy-start | bytes 1572868
  23.2 13.5 %copy-start = (bf16[256,1024]{1,0:T(8,128)(2,1)S(1)}, bf16[256,1024]{1,0:T(8,128)(2,1)}, u32[]{:S(2)}) copy-start(bf16[256,1024]{1,0:T(8,128)(2,1)} %refs_1_.5) | copy-start | bytes 1572868
  30.5 30.3 %collective-permute-start.7 = (bf16[2,208,512]{2,1,0:T(8,128)(2,1)S(1)}, bf16[2,208,512]{2,1,0:T(8,128)(2,1)S(1)}, u32[]{:S(2)}, u32[]{:S(2)}) collective-permute-start(bf16[2,208,512]{2,1,0:T(8,128)(2,1)S(1)} %pad_maximum_fusion.5), channel_id=1, source_target_pairs={{1,0},{2,1},{3,2},{4,3},{5,4},{6,5},{7,6},{8,7},{9,8},{10,9},{11,1... | collective-permute-start | bytes 1277960 | tf_op jit(solution)/shard_map/ppermute | solution.py:27
  56.5 4.4 %collective-permute-start.4 = (f32[8,4,208]{2,1,0:T(4,128)S(1)}, f32[8,4,208]{2,1,0:T(4,128)S(1)}, u32[]{:S(2)}, u32[]{:S(2)}) collective-permute-start(f32[8,4,208]{2,1,0:T(4,128)S(1)} %get-tuple-element.18), channel_id=1, source_target_pairs={{0,1},{1,2},{2,3},{3,4},{4,5},{5,6},{6,7},{7,8},{8,9},{9,10},{10,1... | collective-permute-start | bytes 79880 | tf_op jit(solution)/shard_map/ppermute | solution.py:27
  58.4 5.2 %collective-permute-start.5 = (f32[8,4,208]{2,1,0:T(4,128)S(1)}, f32[8,4,208]{2,1,0:T(4,128)S(1)}, u32[]{:S(2)}, u32[]{:S(2)}) collective-permute-start(f32[8,4,208]{2,1,0:T(4,128)S(1)} %get-tuple-element.19), channel_id=1, source_target_pairs={{1,0},{2,1},{3,2},{4,3},{5,4},{6,5},{7,6},{8,7},{9,8},{10,9},{11,1... | collective-permute-start | bytes 79880 | tf_op jit(solution)/shard_map/ppermute | solution.py:27

commit v2 on v1

v2 whole, which is shorter than its diff:
```python
import functools
import math

import jax
import jax.numpy as jnp
from jax import lax
from jax.experimental import pallas as pl
from jax.experimental.pallas import tpu as pltpu
from jax.sharding import PartitionSpec as P

HEADS = 16
HEAD_DIM = 64
ROWMIN = 20
STEP = 4
PAIR = 2 * HEAD_DIM
PAIRS = HEADS // 2
SCALE = HEAD_DIM**-0.5
EXP2_SCALE = SCALE * math.log2(math.e)
OUTSIDE = -1e30
KV_CHUNKS = (0, 4, 8)
QG_CHUNKS = (0, 4, 8)
VMEM_BYTES = 40 * 2**20


def reach_sizes(points, count):
    area_rows = points * count // STEP
    root_bound = min(((area_rows + 2 * 4**power) // (3 * 2**power) for power in range(3, 9)))
    grow_rows = root_bound - ROWMIN // STEP - 6
    row_longest = ROWMIN + STEP * (grow_rows - 1)
    rim_width = (2 * row_longest + 15) // 16 * 16
    return (rim_width, (rim_width + points - 1) // points)


def spans(bounds):
    return list(zip(bounds[:-1], bounds[1:]))


def passed_along(value, steps):
    count = lax.axis_size("band")
    initial, last = (max(0, -steps), min(count, count - steps))
    pairs = [(source, source + steps) for source in range(initial, last)]
    return lax.ppermute(value, "band", pairs)[None]


def swapped(value, first):
    count = lax.axis_size("band")
    groups = [sorted([at, (at + 1) % count]) for at in range(first, count, 2)]
    return lax.all_gather(value, "band", axis_index_groups=groups)


def dot_nt(left, right):
    return lax.dot_general(
        left, right, (((1,), (1,)), ((), ())), preferred_element_type=jnp.float32
    )


def dot_nn(left, right):
    return jnp.dot(left, right, preferred_element_type=jnp.float32)


def head_masks():
    lanes = lax.broadcasted_iota(jnp.int32, (1, PAIR), 1)
    first = (lanes < HEAD_DIM).astype(jnp.float32)
    return (first.astype(jnp.bfloat16), (1.0 - first).astype(jnp.bfloat16))


def pack_kernel(plan, inputs, info_ref, *refs):
    sources, targets, sems = refs[:inputs], refs[inputs:-1], refs[-1]
    copies = []
    for at, (source, start_at, columns, target, slot) in enumerate(plan):
        rows = targets[target].shape[1]
        start = pl.multiple_of(info_ref[start_at], 16)
        copies.append(
            pltpu.make_async_copy(
                sources[source].at[pl.ds(start, rows), columns], targets[target].at[slot], sems.at[at]
            )
        )
    for copy in copies:
        copy.start()
    for copy in copies:
        copy.wait()


def pack(sources, starts, buffers, name):
    plan, shapes = [], []
    for target, (rows, parts) in enumerate(buffers):
        for slot, (source, start_at, columns) in enumerate(parts):
            plan.append((source, start_at, columns, target, slot))
        width = parts[0][2].stop - parts[0][2].start
        shapes.append(jax.ShapeDtypeStruct((len(parts), rows, width), jnp.bfloat16))
    return pl.pallas_call(
        functools.partial(pack_kernel, plan, len(sources)),
        in_specs=[pl.BlockSpec(memory_space=pltpu.SMEM)]
        + [pl.BlockSpec(memory_space=pl.ANY)] * len(sources),
        out_specs=[pl.BlockSpec(memory_space=pl.ANY)] * len(shapes),
        out_shape=shapes,
        scratch_shapes=[pltpu.SemaphoreType.DMA((len(plan),))],
        cost_estimate=pl.CostEstimate(
            flops=0, bytes_accessed=sum(4 * math.prod(s.shape) for s in shapes), transcendentals=0
        ),
        name=name,
    )(starts, *sources)


def own_kernel(lengths, points, carried, info_ref, *refs):
    count = len(lengths)
    win_ref, q_ref, g_ref, k_ref, v_ref = refs[:5]
    halo_refs = refs[5 : 5 + count]
    att_ref, dq_ref, dk_ref, dv_ref, stat_ref, bias_ref = refs[5 + count + carried :]
    sizes = [points, *lengths]
    rows = [sum(sizes[:at]) for at in range(count + 1)]

    @pl.when(pl.program_id(0) == 0)
    def _():
        lower = win_ref[0:1, :]
        upper = win_ref[1:2, :]
        for at in range(count + 1):
            first = 0 if at == 0 else info_ref[2 * at - 2]
            keys = first + lax.broadcasted_iota(jnp.int32, (sizes[at], points), 0)
            inside = (keys >= lower) & (keys < upper)
            bias_ref[rows[at] : rows[at] + sizes[at], :] = jnp.where(inside, 0.0, OUTSIDE)

    q = q_ref[...]
    g = g_ref[...]
    k_all = jnp.concatenate([k_ref[...]] + [ref[0, 0] for ref in halo_refs], axis=0)
    v_all = jnp.concatenate([v_ref[...]] + [ref[0, 1] for ref in halo_refs], axis=0)
    k_turned = k_all.T
    v_turned = v_all.T
    g_turned = g.T
    att, dq, stats = [], [], []
    dk = dv = None
    for head, mask in enumerate(head_masks()):
        part = slice(head * HEAD_DIM, (head + 1) * HEAD_DIM)
        q_head = q * mask
        g_head = g * mask
        scores = dot_nt(k_all, q_head) + bias_ref[...]
        top = jnp.max(scores, axis=0, keepdims=True)
        probs = jnp.exp2((scores - top) * EXP2_SCALE)
        total = jnp.sum(probs, axis=0, keepdims=True)
        probs = probs * (1.0 / total)
        stats.append(top + jnp.log(total) * (1.0 / SCALE))
        probs_low = probs.astype(jnp.bfloat16)
        att_head = dot_nn(v_turned[part], probs_low).astype(jnp.bfloat16)
        delta = jnp.sum(
            g_turned[part].astype(jnp.float32) * att_head.astype(jnp.float32), axis=0, keepdims=True
        )
        stats.append(delta)
        dscores = (probs * (dot_nt(v_all, g_head) - delta)).astype(jnp.bfloat16)
        dq_head = (dot_nn(k_turned[part], dscores) * SCALE).astype(jnp.bfloat16)
        att.append(att_head)
        dq.append(dq_head)
        dk_head = dot_nn(dscores[:points], q_head)
        dv_head = dot_nn(probs_low[:points], g_head)
        dk = dk_head if dk is None else dk + dk_head
        dv = dv_head if dv is None else dv + dv_head
    att_ref[...] = jnp.concatenate(att, axis=0).T
    dq_ref[...] = jnp.concatenate(dq, axis=0).T
    dk_ref[...] = dk
    dv_ref[...] = dv
    stat_ref[0] = jnp.concatenate(stats, axis=0)


def halo_kernel(lengths, points, carried, info_ref, *refs):
    count = len(lengths)
    win_ref, k_ref, v_ref, dk_part_ref, dv_part_ref = refs[:5]
    qg_refs = refs[5 : 5 + count]
    stat_refs = refs[5 + count : 5 + 2 * count]
    refs = refs[5 + 2 * count + carried :]
    dk_ref, dv_ref, dk_sum, dv_sum = refs[:4]
    bias_refs = refs[4:]
    firsts = [info_ref[2 * at] for at in range(count)]
    parts = [
        pl.ds(pl.multiple_of(jnp.where(first < 0, 0, points - length), 16), length)
        for first, length in zip(firsts, lengths)
    ]

    @pl.when(pl.program_id(0) == 0)
    def _():
        for at in range(count):
            queries = firsts[at] + lax.broadcasted_iota(jnp.int32, (lengths[at], lengths[at]), 1)
            window = win_ref[parts[at], :]
            inside = (queries >= window[:, 0:1]) & (queries < window[:, 1:2])
            bias_refs[at][...] = jnp.where(inside, 0.0, OUTSIDE)

    dk_sum[...] = dk_part_ref[...]
    dv_sum[...] = dv_part_ref[...]
    for at in range(count):
        k = k_ref[parts[at], :]
        v = v_ref[parts[at], :]
        q = qg_refs[at][0, 0]
        g = qg_refs[at][0, 1]
        stats = stat_refs[at][0, 0]
        stats = jnp.where(firsts[at] < 0, stats[:, points - lengths[at] :], stats[:, : lengths[at]])
        dk = dv = None
        for head, mask in enumerate(head_masks()):
            q_head = q * mask
            g_head = g * mask
            lse = stats[2 * head : 2 * head + 1]
            delta = stats[2 * head + 1 : 2 * head + 2]
            scores = dot_nt(k, q_head) + bias_refs[at][...]
            probs = jnp.exp2((scores - lse) * EXP2_SCALE)
            dscores = (probs * (dot_nt(v, g_head) - delta)).astype(jnp.bfloat16)
            dk_head = dot_nn(dscores, q_head)
            dv_head = dot_nn(probs.astype(jnp.bfloat16), g_head)
            dk = dk_head if dk is None else dk + dk_head
            dv = dv_head if dv is None else dv + dv_head
        dk_sum[parts[at], :] += dk
        dv_sum[parts[at], :] += dv
    dk_ref[...] = (dk_sum[...] * SCALE).astype(jnp.bfloat16)
    dv_ref[...] = dv_sum[...].astype(jnp.bfloat16)


def chunk_call(kernel, info, args, in_specs, carried, out_specs, out_shape, **options):
    in_specs = in_specs + [pl.BlockSpec(memory_space=pl.ANY)] * len(carried)
    grid, scratch = options.pop("grid"), options.pop("scratch_shapes")
    return pl.pallas_call(
        functools.partial(kernel, len(carried)),
        grid_spec=pltpu.PrefetchScalarGridSpec(
            num_scalar_prefetch=1,
            grid=grid,
            in_specs=in_specs,
            out_specs=out_specs,
            scratch_shapes=scratch,
        ),
        out_shape=out_shape,
        input_output_aliases={1 + len(args) + at: at for at in range(len(carried))},
        compiler_params=pltpu.CompilerParams(
            vmem_limit_bytes=VMEM_BYTES, dimension_semantics=("arbitrary",)
        ),
        **options,
    )(info, *args, *carried)


def chunk_of(chunks, pair):
    return next(at for at, (low, high) in enumerate(spans(chunks)) if low <= pair < high)


def per_device(queries, keys, values, grad_out, windows):
    points, width = queries.shape
    rim_width, reach = reach_sizes(points, lax.axis_size("band"))
    band = lax.axis_index("band")
    parity = band % 2
    near = min(points, rim_width)
    relative = windows - band * points
    columns = [slice(low * PAIR, high * PAIR) for low, high in spans(KV_CHUNKS)]
    g_columns = [slice(low * PAIR, high * PAIR) for low, high in spans(QG_CHUNKS)]
    every = slice(0, width)

    starts = jnp.stack([(1 - parity) * (points - near), parity * (points - near)])
    next_kv = pack(
        [keys, values], starts, [(near, [(0, 1, c), (1, 1, c)]) for c in columns], "pack_next_kv"
    )
    other = pack(
        [keys, values, queries, grad_out],
        starts,
        [(near, [(at, 0, every) for at in range(4)])]
        + [(near, [(2, 1, c), (3, 1, c)]) for c in g_columns],
        "pack_other",
    )
    next_kv = [swapped(piece, 1) for piece in next_kv]
    partner = swapped(other[0], 0)
    next_qg = [swapped(piece, 1) for piece in other[1:]]
    partner_first = jnp.where(parity == 0, points, -near)
    next_first = jnp.where(parity == 0, -near, points)
    sizes = [near, near]
    info = [partner_first, 1 - parity, next_first, parity]
    far = [d for d in range(-reach, reach + 1) if abs(d) > 1]
    far_kvqg = []
    for d in far:
        size = min(points, rim_width - (abs(d) - 1) * points)
        part = slice(points - size, points) if d < 0 else slice(0, size)
        both = jnp.stack([field[part] for field in (keys, values, queries, grad_out)])
        far_kvqg.append(passed_along(both, -d))
        sizes.append(size)
        info += [(d + 1) * points - size if d < 0 else d * points, 0]
    info = jnp.stack([jnp.asarray(x, jnp.int32) for x in info])
    wide = points + sum(sizes)

    def offset_block(low):
        return pl.BlockSpec((points, PAIR), lambda i, info: (0, i + low))

    def piece_block(at, rows, half, low):
        return pl.BlockSpec(
            (1, 2, rows, PAIR), lambda i, info: (info[2 * at + 1], half, 0, i + low)
        )

    whole_shape = jax.ShapeDtypeStruct((points, width), jnp.bfloat16)
    own_outs, dk_parts, dv_parts, stats = [], [], [], []
    for chunk, (low, high) in enumerate(spans(KV_CHUNKS)):
        block, local = offset_block(low), offset_block(0)
        count = high - low
        own_outs = chunk_call(
            lambda carried, *refs: own_kernel(sizes, points, carried, *refs),
            info,
            [relative.T, queries, grad_out, keys, values, partner, next_kv[chunk], *far_kvqg],
            [pl.BlockSpec((2, points), lambda i, info: (0, 0))]
            + [block] * 4
            + [piece_block(0, near, 0, low), piece_block(1, near, 0, 0)]
            + [piece_block(2 + at, sizes[2 + at], 0, low) for at in range(len(far))],
            own_outs[:2],
            [block, block, local, local, pl.BlockSpec((1, 4, points), lambda i, info: (i, 0, 0))],
            [whole_shape] * 2
            + [jax.ShapeDtypeStruct((points, count * PAIR), jnp.float32)] * 2
            + [jax.ShapeDtypeStruct((count, 4, points), jnp.float32)],
            grid=(count,),
            scratch_shapes=[pltpu.VMEM((wide, points), jnp.float32)],
            cost_estimate=pl.CostEstimate(
                flops=count * 16 * points * wide * PAIR,
                bytes_accessed=count * PAIR * (12 * points + 4 * wide + 8 * points),
                transcendentals=2 * count * points * wide,
            ),
            name=f"own_queries_{chunk}",
        )
        dk_parts.append(own_outs[2])
        dv_parts.append(own_outs[3])
        stats.append(own_outs[4])
    stats = jnp.concatenate(stats, axis=0)
    stats = [swapped(stats, 0), swapped(stats, 1)] + [passed_along(stats, -d) for d in far]

    grads = []
    for chunk, (low, high) in enumerate(spans(QG_CHUNKS)):
        block = offset_block(low)
        count = high - low
        of_own = chunk_of(KV_CHUNKS, low)
        part_block = offset_block(low - KV_CHUNKS[of_own])

        def stat_block(at, low=low):
            return pl.BlockSpec(
                (1, 1, 4, points), lambda i, info: (info[2 * at + 1], i + low, 0, 0)
            )

        grads = chunk_call(
            lambda carried, *refs: halo_kernel(sizes, points, carried, *refs),
            info,
            [relative, keys, values, dk_parts[of_own], dv_parts[of_own]]
            + [partner, next_qg[chunk], *far_kvqg, *stats],
            [pl.BlockSpec((points, 2), lambda i, info: (0, 0)), block, block]
            + [part_block] * 2
            + [piece_block(0, near, 1, low), piece_block(1, near, 0, 0)]
            + [piece_block(2 + at, sizes[2 + at], 1, low) for at in range(len(far))]
            + [stat_block(at) for at in range(len(sizes))],
            grads,
            [block] * 2,
            [whole_shape] * 2,
            grid=(count,),
            scratch_shapes=[pltpu.VMEM((points, PAIR), jnp.float32)] * 2
            + [pltpu.VMEM((n, n), jnp.float32) for n in sizes],
            cost_estimate=pl.CostEstimate(
                flops=count * 2 * sum(8 * n * n * PAIR for n in sizes),
                bytes_accessed=count * PAIR * 20 * points,
                transcendentals=count * 2 * sum(n * n for n in sizes),
            ),
            name=f"halo_queries_{chunk}",
        )
    return (own_outs[0], own_outs[1], grads[0], grads[1])


def solution(mesh):
    spread = P(("members", "band"), None)
    return jax.shard_map(
        per_device,
        mesh=mesh,
        in_specs=(spread, spread, spread, spread, P("band", None)),
        out_specs=(spread, spread, spread, spread),
        check_vma=False,
    )
```

time: 73.7 us -> 225 us (3.05)
  the two profiles are of different devices: /device:TPU:9 before, /device:TPU:0 now
where the time goes in v2:
time: 225 us; the launch traced here: 224 us
  Pallas kernels  139 us (62%)
  blocking collectives  67.3 us (30%)
  between operations  14.2 us (6%)
    pallas_call x2, Pallas kernels, pack(): pl.pallas_call(functools.partial(pack_kernel, plan, len(sources)), in_spe...  107 us
    all_gather x6, blocking collectives, swapped(): return lax.all_gather(value, 'band', axis_index_groups=groups)  67.3 us
    pallas_call x4, Pallas kernels, chunk_call(): pl.pallas_call(functools.partial(kernel, len(carried)), grid_spec=pltpu.P...  32.5 us
  transfers between devices with their start and end apart: 1, of which 0 were waited for; matrix products, arithmetic and copies ran while one was open for 0% of the time, Pallas kernels for 12%

profile of v2, /device:TPU:0, one launch (start us, length us, event | category | flops | bytes accessed | tf_op | source)
XLA Modules:
  0.0 224.0 jit_solution(1579866896389676213)
XLA Ops:
  7.2 0.0 copy-start.9
  7.2 0.0 all-gather.9.cloned.1.call-start
  7.2 0.6 pad_add_fusion.1.info_ref
  7.8 79.3 %pack_other.1 = (bf16[4,208,1024]{2,1,0:T(8,128)(2,1)}, bf16[2,208,512]{2,1,0:T(8,128)(2,1)}, bf16[2,208,512]{2,1,0:T(8,128)(2,1)}) custom-call(s32[2]{0:T(128)} %pad_add_fusion.1.info_ref, bf16[256,1024]{1,0:T(8,128)(2,1)} %refs_2_.9, bf16[256,1024]{1,0:T(8,128)(2,1)} %refs_3_.9, bf16[256,1024]{1,0:T(8,128)(2,1)} %refs_2_.7, bf16[256,1024]{1,0:T(8,128)(2,1)} %refs_3_.7), custom_call_target="tpu_custom_call" | custom-call | bytes 5111808 | tf_op jit(solution)/shard_map/pack_other/pallas_call | solution.py:91
  87.1 0.0 all-gather.9.cloned.1.call-update
  87.1 0.0 copy-start.2
  87.2 0.0 copy-start.3
  87.2 0.0 copy-start.4
  87.2 0.0 copy-start.5
  87.2 27.7 %pack_next_kv.1 = (bf16[2,208,512]{2,1,0:T(8,128)(2,1)}, bf16[2,208,512]{2,1,0:T(8,128)(2,1)}) custom-call(s32[2]{0:T(128)} %pad_add_fusion.1.info_ref, bf16[256,1024]{1,0:T(8,128)(2,1)} %refs_2_.9, bf16[256,1024]{1,0:T(8,128)(2,1)} %refs_3_.9), custom_call_target="tpu_custom_call" | custom-call | bytes 1703936 | tf_op jit(solution)/shard_map/pack_next_kv/pallas_call | solution.py:91
  114.9 0.0 copy-done.9
  115.0 0.1 copy.16
  115.1 0.1 copy.18.refs_1_
  115.2 0.1 pad_add_fusion.refs_0_
  115.3 12.3 %all-gather.2 = bf16[4,208,512]{2,1,0:T(8,128)(2,1)S(1)} all-gather(bf16[2,208,512]{2,1,0:T(8,128)(2,1)} %get-tuple-element.25), channel_id=4, replica_groups={{1,2},{3,4},{5,6},{7,8},{9,10},{11,12},{13,14},{0,15},{17,18},{19,20},{..., dimensions={0}, use_global_device_ids=true | all-gather | bytes 1277952 | tf_op jit(solution)/shard_map/all_gather | solution.py:48
  127.6 15.6 %all-gather.1 = bf16[4,208,512]{2,1,0:T(8,128)(2,1)} all-gather(bf16[2,208,512]{2,1,0:T(8,128)(2,1)} %get-tuple-element.24), channel_id=3, replica_groups={{1,2},{3,4},{5,6},{7,8},{9,10},{11,12},{13,14},{0,15},{17,18},{19,20},{..., dimensions={0}, use_global_device_ids=true | all-gather | bytes 1277952 | tf_op jit(solution)/shard_map/all_gather | solution.py:48
  143.1 11.3 %all-gather.6 = bf16[4,208,512]{2,1,0:T(8,128)(2,1)} all-gather(bf16[2,208,512]{2,1,0:T(8,128)(2,1)} %get-tuple-element.37), channel_id=8, replica_groups={{1,2},{3,4},{5,6},{7,8},{9,10},{11,12},{13,14},{0,15},{17,18},{19,20},{..., dimensions={0}, use_global_device_ids=true | all-gather | bytes 1277952 | tf_op jit(solution)/shard_map/all_gather | solution.py:48
  154.5 15.5 %all-gather.3 = bf16[4,208,512]{2,1,0:T(8,128)(2,1)} all-gather(bf16[2,208,512]{2,1,0:T(8,128)(2,1)} %get-tuple-element.32), channel_id=5, replica_groups={{1,2},{3,4},{5,6},{7,8},{9,10},{11,12},{13,14},{0,15},{17,18},{19,20},{..., dimensions={0}, use_global_device_ids=true | all-gather | bytes 1277952 | tf_op jit(solution)/shard_map/all_gather | solution.py:48
  170.0 0.0 all-gather.9.cloned.1.call-done
  170.0 0.0 copy-done.2
  170.1 0.0 copy-done.3
  170.1 0.0 copy-done.4
  170.1 0.0 copy-done.5
  170.1 0.0 copy-start
  170.1 2.0 copy-done
  172.0 0.0 copy-start.7
  172.0 10.6 %own_queries_0.1 = (bf16[256,1024]{1,0:T(8,128)(2,1)}, bf16[256,1024]{1,0:T(8,128)(2,1)}, f32[256,512]{1,0:T(8,128)S(1)}, f32[256,512]{1,0:T(8,128)S(1)}, f32[4,4,256]{2,1,0:T(4,128)S(1)}) custom-call(s32[4]{0:T(128)S(1)} %pad_add_fusion.refs_0_, s32[2,256]{1,0:T(2,128)S(1)} %copy.18.refs_1_, bf16[256,1024]{1,0:T(8,128)(2,1)S(1)} %copy-done.4, ...), custom_call_target="tpu_custom_call" | custom-call | flops 1409286144 | bytes 3997696 | tf_op jit(solution)/shard_map/own_queries_0/pallas_call | solution.py:216
  182.6 0.0 copy-done.7
  182.6 0.0 copy-start.1
  182.6 0.0 copy-start.6
  182.6 10.6 %own_queries_1.1 = (bf16[256,1024]{1,0:T(8,128)(2,1)}, bf16[256,1024]{1,0:T(8,128)(2,1)}, f32[256,512]{1,0:T(8,128)S(1)}, f32[256,512]{1,0:T(8,128)S(1)}, f32[4,4,256]{2,1,0:T(4,128)S(1)}) custom-call(s32[4]{0:T(128)S(1)} %pad_add_fusion.refs_0_, s32[2,256]{1,0:T(2,128)S(1)} %copy.18.refs_1_, ...), custom_call_target="tpu_custom_call", output_to_operand_aliasing={{0}: (8, {}), {1}: (9, {})} | custom-call | flops 1409286144 | bytes 3997696 | tf_op jit(solution)/shard_map/own_queries_1/pallas_call | solution.py:216
  193.2 0.0 copy-start.8
  193.3 5.9 %all-gather.4 = f32[16,4,256]{2,1,0:T(4,128)S(1)} all-gather(f32[8,4,256]{2,1,0:T(4,128)S(1)} %constant_dynamic-update-slice_fusion), channel_id=6, replica_groups={{0,1},{2,3},{4,5},{6,7},{8,9},{10,11},{12,13},{14,15},{16,17},{18,19},{..., dimensions={0}, use_global_device_ids=true | all-gather | bytes 98304 | tf_op jit(solution)/shard_map/all_gather | solution.py:48
  199.2 6.7 %all-gather.5 = f32[16,4,256]{2,1,0:T(4,128)S(1)} all-gather(f32[8,4,256]{2,1,0:T(4,128)S(1)} %constant_dynamic-update-slice_fusion), channel_id=7, replica_groups={{1,2},{3,4},{5,6},{7,8},{9,10},{11,12},{13,14},{0,15},{17,18},{19,20},{..., dimensions={0}, use_global_device_ids=true | all-gather | bytes 98304 | tf_op jit(solution)/shard_map/all_gather | solution.py:48
  205.9 0.0 copy-done.1
  205.9 0.0 copy-done.6
  205.9 5.6 %halo_queries_0.1 = (bf16[256,1024]{1,0:T(8,128)(2,1)}, bf16[256,1024]{1,0:T(8,128)(2,1)}) custom-call(s32[4]{0:T(128)S(1)} %pad_add_fusion.refs_0_, s32[256,2]{1,0:T(8,128)S(1)} %broadcast_subtract_fusion.refs_1_, bf16[256,1024]{1,0:T(8,128)(2,1)S(1)} %copy-done.2, bf16[256,1024]{1,0:T(8,128)(2,1)S(1)} %copy-done.3, ...), custom_call_target="tpu_custom_call" | custom-call | flops 708837376 | bytes 2621440 | tf_op jit(solution)/shard_map/halo_queries_0/pallas_call | solution.py:216
  211.5 0.0 copy-done.8
  211.5 5.6 %halo_queries_1.1 = (bf16[256,1024]{1,0:T(8,128)(2,1)}, bf16[256,1024]{1,0:T(8,128)(2,1)}) custom-call(s32[4]{0:T(128)S(1)} %pad_add_fusion.refs_0_, s32[256,2]{1,0:T(8,128)S(1)} %broadcast_subtract_fusion.refs_1_, bf16[256,1024]{1,0:T(8,128)(2,1)S(1)} %copy-done.2, bf16[256,1024]{1,0:T(8,128)(2,1)S(1)} %copy-done.3, ...), custom_call_target="tpu_custom_call", output_to_operand_aliasing={{0}: (10, {}), {1}: (11, {})} | custom-call | flops 708837376 | bytes 2621440 | tf_op jit(solution)/shard_map/halo_queries_1/pallas_call | solution.py:216
  (4 shorter events, 0.0 us)
Async XLA Ops:
  7.2 107.8 %copy-start.9 = (s32[256,2]{0,1:T(2,128)S(1)}, s32[256,2]{0,1:T(2,128)}, u32[]{:S(2)}) copy-start(s32[256,2]{0,1:T(2,128)} %param.9) | copy-start | bytes 6148
  7.2 162.9 %all-gather.9.cloned.1.call-start = ((), (), s32[]{:S(2)}) async-start(), calls=%async_computation | async-start | bytes 5111808 | tf_op jit(solution)/shard_map/all_gather | solution.py:48
  87.1 82.9 %copy-start.2 = (bf16[256,1024]{1,0:T(8,128)(2,1)S(1)}, bf16[256,1024]{1,0:T(8,128)(2,1)}, u32[]{:S(2)}) copy-start(bf16[256,1024]{1,0:T(8,128)(2,1)} %refs_2_.9) | copy-start | bytes 1572868
  87.2 82.9 %copy-start.3 = (bf16[256,1024]{1,0:T(8,128)(2,1)S(1)}, bf16[256,1024]{1,0:T(8,128)(2,1)}, u32[]{:S(2)}) copy-start(bf16[256,1024]{1,0:T(8,128)(2,1)} %refs_3_.9) | copy-start | bytes 1572868
  87.2 82.9 %copy-start.4 = (bf16[256,1024]{1,0:T(8,128)(2,1)S(1)}, bf16[256,1024]{1,0:T(8,128)(2,1)}, u32[]{:S(2)}) copy-start(bf16[256,1024]{1,0:T(8,128)(2,1)} %refs_2_.7) | copy-start | bytes 1572868
  87.2 82.9 %copy-start.5 = (bf16[256,1024]{1,0:T(8,128)(2,1)S(1)}, bf16[256,1024]{1,0:T(8,128)(2,1)}, u32[]{:S(2)}) copy-start(bf16[256,1024]{1,0:T(8,128)(2,1)} %refs_3_.7) | copy-start | bytes 1572868
  170.1 2.0 copy-start
  172.0 10.6 %copy-start.7 = (bf16[4,208,512]{2,1,0:T(8,128)(2,1)S(1)}, bf16[4,208,512]{2,1,0:T(8,128)(2,1)}, u32[]{:S(2)}) copy-start(bf16[4,208,512]{2,1,0:T(8,128)(2,1)} %all-gather.1) | copy-start | bytes 2555908
  182.6 23.2 %copy-start.1 = (bf16[8,208,1024]{2,1,0:T(8,128)(2,1)S(1)}, bf16[8,208,1024]{2,1,0:T(8,128)(2,1)}, u32[]{:S(2)}) copy-start(bf16[8,208,1024]{2,1,0:T(8,128)(2,1)} %all-gather.9.cloned.1.call-done) | copy-start | bytes 10223620
  182.6 23.2 %copy-start.6 = (bf16[4,208,512]{2,1,0:T(8,128)(2,1)S(1)}, bf16[4,208,512]{2,1,0:T(8,128)(2,1)}, u32[]{:S(2)}) copy-start(bf16[4,208,512]{2,1,0:T(8,128)(2,1)} %all-gather.6) | copy-start | bytes 2555908
  193.2 18.3 %copy-start.8 = (bf16[4,208,512]{2,1,0:T(8,128)(2,1)S(1)}, bf16[4,208,512]{2,1,0:T(8,128)(2,1)}, u32[]{:S(2)}) copy-start(bf16[4,208,512]{2,1,0:T(8,128)(2,1)} %all-gather.3) | copy-start | bytes 2555908
Sparse Core Ops, SparseCore 0:
  87.3 15.2 all-gather.8

commit v3 on v0

v3 whole, which is shorter than its diff:
```python
import functools
import math

import jax
import jax.numpy as jnp
from jax import lax
from jax.experimental import pallas as pl
from jax.experimental.pallas import tpu as pltpu
from jax.sharding import PartitionSpec as P

HEADS = 16
HEAD_DIM = 64
ROWMIN = 20
STEP = 4
PAIR = 2 * HEAD_DIM
PAIRS = HEADS // 2
SCALE = HEAD_DIM**-0.5
EXP2_SCALE = SCALE * math.log2(math.e)
OUTSIDE = -1e30
CHUNKS = (0, 4, 8)
VMEM_BYTES = 40 * 2**20


def reach_sizes(points, count):
    area_rows = points * count // STEP
    root_bound = min(((area_rows + 2 * 4**power) // (3 * 2**power) for power in range(3, 9)))
    grow_rows = root_bound - ROWMIN // STEP - 6
    row_longest = ROWMIN + STEP * (grow_rows - 1)
    rim_width = (2 * row_longest + 15) // 16 * 16
    return (rim_width, (rim_width + points - 1) // points)


def spans(bounds):
    return list(zip(bounds[:-1], bounds[1:]))


def passed_along(value, steps):
    count = lax.axis_size("band")
    initial, last = (max(0, -steps), min(count, count - steps))
    return lax.ppermute(value, "band", [(source, source + steps) for source in range(initial, last)])


def swapped(value, first):
    count = lax.axis_size("band")
    pairs = [(at, at + 1) for at in range(first, count - 1, 2)]
    return lax.ppermute(value, "band", pairs + [(high, low) for low, high in pairs])


def dot_nt(left, right):
    return lax.dot_general(
        left, right, (((1,), (1,)), ((), ())), preferred_element_type=jnp.float32
    )


def dot_nn(left, right):
    return jnp.dot(left, right, preferred_element_type=jnp.float32)


def head_masks():
    lanes = lax.broadcasted_iota(jnp.int32, (1, PAIR), 1)
    first = (lanes < HEAD_DIM).astype(jnp.float32)
    return (first.astype(jnp.bfloat16), (1.0 - first).astype(jnp.bfloat16))


def pack_kernel(plan, inputs, start_ref, *refs):
    for source, start_at, target, slot in plan:
        out_ref = refs[inputs + target]
        start = pl.multiple_of(start_ref[start_at], 16)
        out_ref[slot] = refs[source][pl.ds(start, out_ref.shape[1]), :]


def pack(sources, starts, buffers, low, high, name):
    points = sources[0].shape[0]
    width = (high - low) * PAIR
    plan = [
        (source, start_at, target, source)
        for target, (rows, start_at) in enumerate(buffers)
        for source in range(len(sources))
    ]
    return pl.pallas_call(
        functools.partial(pack_kernel, plan, len(sources)),
        grid=(1,),
        in_specs=[pl.BlockSpec(memory_space=pltpu.SMEM)]
        + [pl.BlockSpec((points, width), lambda i: (0, low * PAIR // width))] * len(sources),
        out_specs=[pl.BlockSpec((len(sources), rows, width), lambda i: (0, 0, 0)) for rows, _ in buffers],
        out_shape=[
            jax.ShapeDtypeStruct((len(sources), rows, width), jnp.bfloat16) for rows, _ in buffers
        ],
        cost_estimate=pl.CostEstimate(
            flops=0, bytes_accessed=4 * len(sources) * points * width, transcendentals=0
        ),
        name=name,
    )(starts, *sources)


def attention_kernel(rim, lengths, points, carried, parity_ref, *refs):
    far = len(lengths) // 2 - 1
    near = lengths[far]
    half = points // 2
    reached = half + 2 * rim
    win_ref, q_ref, g_ref, k_ref, v_ref, partner_ref, next_ref = refs[:7]
    far_refs = refs[7 : 7 + 2 * far]
    outs = refs[7 + 2 * far + carried :]
    att_ref, dq_ref, to_partner_ref, dk_ref, dv_ref, to_next_ref = outs[:6]
    to_far_refs = outs[6 : 6 + 2 * far]
    bias_ref = outs[-1]
    even = parity_ref[0] == 0

    @pl.when(pl.program_id(0) == 0)
    def _():
        for part in range(2):
            own = slice(part * half, (part + 1) * half)
            lower = jnp.concatenate([win_ref[0:1, own]] * 2, axis=1)
            upper = jnp.concatenate([win_ref[1:2, own]] * 2, axis=1)
            keys = part * half - rim + lax.broadcasted_iota(jnp.int32, (reached, points), 0)
            bias_ref[part] = jnp.where((keys >= lower) & (keys < upper), 0.0, OUTSIDE)

    def all_keys(slot, own):
        near_low = jnp.where(even, next_ref[slot], partner_ref[slot])
        near_high = jnp.where(even, partner_ref[slot], next_ref[slot])
        lows = [ref[slot] for ref in far_refs[:far]] + [near_low]
        highs = [near_high] + [ref[slot] for ref in far_refs[far:]]
        return jnp.concatenate(lows + [own] + highs, axis=0)

    k_all = all_keys(0, k_ref[...])
    v_all = all_keys(1, v_ref[...])
    k_turned = k_all.T
    v_turned = v_all.T
    g_turned = g_ref[...].T
    masks = head_masks()

    def both(turned):
        return [turned[:HEAD_DIM, :half], turned[HEAD_DIM:, half:]]

    dks, dvs = [], []
    for part in range(2):
        own = slice(part * half, (part + 1) * half)
        span = slice(part * half, part * half + reached)
        q_both = jnp.concatenate([q_ref[own, :] * mask for mask in masks], axis=0)
        g_both = jnp.concatenate([g_ref[own, :] * mask for mask in masks], axis=0)
        scores = dot_nt(k_all[span], q_both) + bias_ref[part]
        top = jnp.max(scores, axis=0, keepdims=True)
        probs = jnp.exp2((scores - top) * EXP2_SCALE)
        probs = probs * (1.0 / jnp.sum(probs, axis=0, keepdims=True))
        probs_low = probs.astype(jnp.bfloat16)
        att = [x.astype(jnp.bfloat16) for x in both(dot_nn(v_turned[:, span], probs_low))]
        delta = [
            jnp.sum(
                g_turned[head * HEAD_DIM : (head + 1) * HEAD_DIM, own].astype(jnp.float32)
                * att[head].astype(jnp.float32),
                axis=0,
                keepdims=True,
            )
            for head in range(2)
        ]
        dprobs = dot_nt(v_all[span], g_both)
        dscores = (probs * (dprobs - jnp.concatenate(delta, axis=1))).astype(jnp.bfloat16)
        dq = [(x * SCALE).astype(jnp.bfloat16) for x in both(dot_nn(k_turned[:, span], dscores))]
        att_ref[own, :] = jnp.concatenate(att, axis=0).T
        dq_ref[own, :] = jnp.concatenate(dq, axis=0).T
        dks.append(dot_nn(dscores, q_both) * SCALE)
        dvs.append(dot_nn(probs_low, g_both))

    def rows_of(sums, start, stop):
        low, high = sums
        cuts = sorted({start, stop} | {x for x in (half, reached) if start < x < stop})
        pieces = []
        for first, last in spans(cuts):
            if last <= half:
                pieces.append(low[first:last])
            elif first >= reached:
                pieces.append(high[first - half : last - half])
            else:
                pieces.append(low[first:last] + high[first - half : last - half])
        return jnp.concatenate(pieces, axis=0)

    for slot, (sums, own_ref) in enumerate([(dks, dk_ref), (dvs, dv_ref)]):
        own_ref[...] = rows_of(sums, rim, rim + points)
        near_low = rows_of(sums, rim - near, rim).astype(jnp.bfloat16)
        near_high = rows_of(sums, rim + points, rim + points + near).astype(jnp.bfloat16)
        to_partner_ref[slot] = jnp.where(even, near_high, near_low)
        to_next_ref[slot] = jnp.where(even, near_low, near_high)
        start = 0
        for at in range(far):
            ref = to_far_refs[at]
            ref[slot] = rows_of(sums, start, start + lengths[at]).astype(jnp.bfloat16)
            start += lengths[at]
        start = rim + points + near
        for at in range(far, 2 * far):
            ref = to_far_refs[at]
            ref[slot] = rows_of(sums, start, start + lengths[at + 2]).astype(jnp.bfloat16)
            start += lengths[at + 2]


def sum_kernel(far_lengths, points, carried, start_ref, *refs):
    far = len(far_lengths) // 2
    dk_ref, dv_ref, partner_ref, next_ref = refs[:4]
    far_refs = refs[4 : 4 + 2 * far]
    outs = refs[4 + 2 * far + carried :]
    total = outs[-1]
    near = partner_ref.shape[1]
    for slot, (own_ref, out_ref) in enumerate([(dk_ref, outs[0]), (dv_ref, outs[1])]):
        total[...] = own_ref[...]
        for at, ref in enumerate((partner_ref, next_ref)):
            rows = pl.ds(pl.multiple_of(start_ref[at], 16), near)
            total[rows, :] += ref[slot].astype(jnp.float32)
        for at, (ref, length) in enumerate(zip(far_refs, far_lengths)):
            rows = slice(points - length, points) if at < far else slice(0, length)
            total[rows, :] += ref[slot].astype(jnp.float32)
        out_ref[...] = total[...].astype(jnp.bfloat16)


def chunk_call(kernel, scalars, args, in_specs, carried, out_specs, out_shape, **options):
    return pl.pallas_call(
        functools.partial(kernel, len(carried)),
        in_specs=[pl.BlockSpec(memory_space=pltpu.SMEM)]
        + in_specs
        + [pl.BlockSpec(memory_space=pl.ANY)] * len(carried),
        out_specs=out_specs,
        out_shape=out_shape,
        input_output_aliases={1 + len(args) + at: at for at in range(len(carried))},
        compiler_params=pltpu.CompilerParams(
            vmem_limit_bytes=VMEM_BYTES, dimension_semantics=("arbitrary",)
        ),
        **options,
    )(scalars, *args, *carried)


def per_device(queries, keys, values, grad_out, windows):
    points, width = queries.shape
    rim_width, reach = reach_sizes(points, lax.axis_size("band"))
    band = lax.axis_index("band")
    parity = band % 2
    near = min(points, rim_width)
    far = [d for d in range(-reach, reach + 1) if abs(d) > 1]
    far_sizes = [min(points, rim_width - (abs(d) - 1) * points) for d in far]
    lows = len(far) // 2
    lengths = far_sizes[:lows] + [near, near] + far_sizes[lows:]
    wide = points + 2 * rim_width
    relative = (windows - band * points).T
    parities = parity.astype(jnp.int32).reshape(1)
    starts = jnp.stack([(1 - parity) * (points - near), parity * (points - near)]).astype(jnp.int32)

    to_next, from_next = [], []
    ready = (keys, values)
    for chunk, (low, high) in enumerate(spans(CHUNKS)):
        to_next.append(pack(ready, starts, [(near, 1)], low, high, f"pack_next_{chunk}")[0])
        from_next.append(swapped(to_next[chunk], 1))
        if chunk == 0:
            to_partner = pack(
                lax.optimization_barrier((keys, values, to_next[0]))[:2],
                starts,
                [(near, 0)],
                0,
                PAIRS,
                "pack_partner",
            )[0]
            from_partner = swapped(to_partner, 0)
            ready = lax.optimization_barrier((keys, values, from_partner))[:2]
    from_far = []
    for d, size in zip(far, far_sizes):
        part = slice(points - size, points) if d < 0 else slice(0, size)
        from_far.append(passed_along(jnp.stack([keys[part], values[part]]), -d))

    def columns(rows, low):
        return pl.BlockSpec((rows, PAIR), lambda i: (0, i + low))

    def piece(rows, low):
        return pl.BlockSpec((2, rows, PAIR), lambda i: (0, 0, i + low))

    whole = jax.ShapeDtypeStruct((points, width), jnp.bfloat16)
    reached = points // 2 + 2 * rim_width
    outs, own_terms, back_next, back_far = [], [], [], []
    for chunk, (low, high) in enumerate(spans(CHUNKS)):
        count = high - low
        chunk_width = count * PAIR
        outs = chunk_call(
            lambda carried, *refs: attention_kernel(rim_width, lengths, points, carried, *refs),
            parities,
            [relative, queries, grad_out, keys, values, from_partner, from_next[chunk], *from_far],
            [pl.BlockSpec((2, points), lambda i: (0, 0))]
            + [columns(points, low)] * 4
            + [piece(near, low), piece(near, 0)]
            + [piece(size, low) for size in far_sizes],
            outs[:3],
            [columns(points, low)] * 2
            + [piece(near, low)]
            + [columns(points, 0)] * 2
            + [piece(near, 0)]
            + [piece(size, 0) for size in far_sizes],
            [whole] * 2
            + [jax.ShapeDtypeStruct((2, near, width), jnp.bfloat16)]
            + [jax.ShapeDtypeStruct((points, chunk_width), jnp.float32)] * 2
            + [
                jax.ShapeDtypeStruct((2, size, chunk_width), jnp.bfloat16)
                for size in [near] + far_sizes
            ],
            grid=(count,),
            scratch_shapes=[pltpu.VMEM((2, reached, points), jnp.float32)],
            cost_estimate=pl.CostEstimate(
                flops=count * 24 * reached * points * PAIR,
                bytes_accessed=count * PAIR * (20 * points + 8 * wide),
                transcendentals=2 * count * points * reached,
            ),
            name=f"attention_{chunk}",
        )
        own_terms.append(outs[3:5])
        back_next.append(swapped(outs[5], 1))
        back_far.append([passed_along(term, d) for term, d in zip(outs[6:], far)])
    back_partner = swapped(outs[2], 0)

    grads = []
    for chunk, (low, high) in enumerate(spans(CHUNKS)):
        chunk_width = (high - low) * PAIR
        step = 2 * PAIR

        def sums(rows, low):
            return pl.BlockSpec((rows, step), lambda i: (0, i + low * PAIR // step))

        def terms(rows, low):
            return pl.BlockSpec((2, rows, step), lambda i: (0, 0, i + low * PAIR // step))

        grads = chunk_call(
            lambda carried, *refs: sum_kernel(far_sizes, points, carried, *refs),
            starts,
            [*own_terms[chunk], back_partner, back_next[chunk], *back_far[chunk]],
            [sums(points, 0)] * 2
            + [terms(near, low), terms(near, 0)]
            + [terms(size, 0) for size in far_sizes],
            grads,
            [sums(points, low)] * 2,
            [whole] * 2,
            grid=(chunk_width // step,),
            scratch_shapes=[pltpu.VMEM((points, step), jnp.float32)],
            cost_estimate=pl.CostEstimate(
                flops=6 * points * chunk_width,
                bytes_accessed=20 * points * chunk_width,
                transcendentals=0,
            ),
            name=f"gradient_sums_{chunk}",
        )
    return (outs[0], outs[1], grads[0], grads[1])


def solution(mesh):
    spread = P(("members", "band"), None)
    return jax.shard_map(
        per_device,
        mesh=mesh,
        in_specs=(spread, spread, spread, spread, P("band", None)),
        out_specs=(spread, spread, spread, spread),
        check_vma=False,
    )
```

time: 143 us -> 71.2 us (0.50)
  local copies, waits for them, and re-layouts: 43.4 us -> 0.62 us
  Pallas kernels: 0 us -> 30.4 us
  waiting for transfers between devices: 55 us -> 26.8 us
  matrix products: 22.6 us -> 0 us
  other arithmetic: 7.92 us -> 0.58 us
    pallas_call x0 -> x7, Pallas kernels: none -> 30.4 us  [the longest x4 24.5 us: chunk_call(): pl.pallas_call(functools.partial(kernel, len(carried)), in_specs=[pl.Bloc...]
    ppermute x4 -> x6, waiting for transfers between devices: 55 us -> 26.8 us  [swapped(): lax.ppermute(value, 'band', pairs + [(high, low) for low, high in pairs])]
    dot_general x24 -> x0, matrix products: 22.6 us -> none  [the longest x4 7.7 us: query_pass(): jnp.einsum('hrc,rhe->che', dscores, q_heads, preferred_element_type=jnp.f...]
    dynamic_slice x24 -> x0, local copies, waits for them, and re-layouts: 16.5 us -> none  [the longest x4 4.3 us: group_step(): lax.dynamic_slice_in_dim(values_wide, offset, width, 1)]
    dynamic_update_slice x24 -> x0, local copies, waits for them, and re-layouts: 10.5 us -> none  [the longest x8 5.93 us: group_step(): value_acc = lax.dynamic_update_slice_in_dim(value_acc, pieces[3], offset, 1)]
    another operation x4 -> x0, local copies, waits for them, and re-layouts: 5.43 us -> none
    while x24 -> x0, local copies, waits for them, and re-layouts: 4.67 us -> none
    concatenate x1 -> x0, other arithmetic: 3.1 us -> none  [surround(): return jnp.concatenate([low_part, field, high_part], axis=1)]
  transfers between devices with their start and end apart: 4 -> 6, of which waited for: 4 -> 3; matrix products, arithmetic and copies ran while one was open for 0% -> 0% of each run, Pallas kernels for 0% -> 20%
where the time goes in v3:
time: 71.2 us; the launch traced here: 70.9 us
  Pallas kernels  30.4 us (43%)
  waiting for transfers between devices  26.8 us (38%)
  starting transfers between devices  11.8 us (17%)
  between operations  0.73 us (1%)
    ppermute x6, waiting for transfers between devices, swapped(): lax.ppermute(value, 'band', pairs + [(high, low) for low, high in pairs])  26.8 us
    pallas_call x4, Pallas kernels, chunk_call(): pl.pallas_call(functools.partial(kernel, len(carried)), in_specs=[pl.Bloc...  24.5 us
    ppermute x6, starting transfers between devices, swapped(): lax.ppermute(value, 'band', pairs + [(high, low) for low, high in pairs])  11.8 us
    pallas_call x3, Pallas kernels, pack(): pl.pallas_call(functools.partial(pack_kernel, plan, len(sources)), grid=(...  5.92 us
  transfers between devices with their start and end apart: 6, of which 3 were waited for; matrix products, arithmetic and copies ran while one was open for 0% of the time, Pallas kernels for 20%

profile of v3, /device:TPU:9, one launch (start us, length us, event | category | flops | bytes accessed | tf_op | source)
XLA Modules:
  0.0 70.9 jit_solution(4741616600261840397)
XLA Ops:
  0.6 0.6 pad_add_fusion.start_ref.refs_0_
  1.2 1.8 %pack_next_0.1 = bf16[2,208,512]{2,1,0:T(8,128)(2,1)} custom-call(s32[2]{0:T(128)} %pad_add_fusion.start_ref.refs_0_, bf16[256,1024]{1,0:T(8,128)(2,1)} %refs_4_.3, bf16[256,1024]{1,0:T(8,128)(2,1)} %refs_5_.3), custom_call_target="tpu_custom_call" | custom-call | bytes 1048576 | tf_op jit(solution)/shard_map/pack_next_0/pallas_call | solution.py:80
  3.0 0.0 copy-start.3
  3.1 0.0 copy-start.4
  3.1 2.3 %pack_partner.1 = bf16[2,208,1024]{2,1,0:T(8,128)(2,1)} custom-call(s32[2]{0:T(128)} %pad_add_fusion.start_ref.refs_0_, bf16[256,1024]{1,0:T(8,128)(2,1)} %refs_4_.3, bf16[256,1024]{1,0:T(8,128)(2,1)} %refs_5_.3), custom_call_target="tpu_custom_call" | custom-call | bytes 2097152 | tf_op jit(solution)/shard_map/pack_partner/pallas_call | solution.py:80
  5.3 0.0 copy-start
  5.3 0.0 copy-start.1
  5.3 0.7 collective-permute-start
  6.0 3.2 %collective-permute-start.2 = (bf16[2,208,512]{2,1,0:T(8,128)(2,1)}, bf16[2,208,512]{2,1,0:T(8,128)(2,1)}, u32[]{:S(2)}, u32[]{:S(2)}) collective-permute-start(bf16[2,208,512]{2,1,0:T(8,128)(2,1)} %pack_next_0.1), channel_id=1, source_target_pairs={{1,2},{3,4},{5,6},{7,8},{9,10},{11,12},{13,14},{2,1},{4,3},{6,5},{... | collective-permute-start | bytes 1277960 | tf_op jit(solution)/shard_map/ppermute | solution.py:46
  9.2 0.0 collective-permute-done.refs_6_
  9.2 0.0 copy-start.5
  9.2 1.8 %pack_next_1.1 = bf16[2,208,512]{2,1,0:T(8,128)(2,1)} custom-call(s32[2]{0:T(128)} %pad_add_fusion.start_ref.refs_0_, bf16[256,1024]{1,0:T(8,128)(2,1)} %refs_4_.3, bf16[256,1024]{1,0:T(8,128)(2,1)} %refs_5_.3), custom_call_target="tpu_custom_call" | custom-call | bytes 1048576 | tf_op jit(solution)/shard_map/pack_next_1/pallas_call | solution.py:80
  11.0 2.4 %collective-permute-start.1 = (bf16[2,208,512]{2,1,0:T(8,128)(2,1)}, bf16[2,208,512]{2,1,0:T(8,128)(2,1)S(1)}, u32[]{:S(2)}, u32[]{:S(2)}) collective-permute-start(bf16[2,208,512]{2,1,0:T(8,128)(2,1)} %pack_next_1.1), channel_id=1, source_target_pairs={{1,2},{3,4},{5,6},{7,8},{9,10},{11,12},{13,14},{2,1},{4,3},{6,5},{... | collective-permute-start | bytes 1277960 | tf_op jit(solution)/shard_map/ppermute | solution.py:46
  13.5 0.0 copy-done.5
  13.5 11.4 %collective-permute-done.2.refs_7_ = bf16[2,208,512]{2,1,0:T(8,128)(2,1)} collective-permute-done((bf16[2,208,512]{2,1,0:T(8,128)(2,1)}, bf16[2,208,512]{2,1,0:T(8,128)(2,1)}, u32[]{:S(2)}, u32[]{:S(2)}) %collective-permute-start.2) | collective-permute-done | bytes 426016 | tf_op jit(solution)/shard_map/ppermute | solution.py:46
  24.9 0.0 copy-done.3
  24.9 0.0 copy-done.4
  24.9 0.0 copy-done
  24.9 0.0 copy-done.1
  24.9 11.0 %attention_0.1 = (bf16[256,1024]{1,0:T(8,128)(2,1)}, bf16[256,1024]{1,0:T(8,128)(2,1)}, bf16[2,208,1024]{2,1,0:T(8,128)(2,1)S(1)}, f32[256,512]{1,0:T(8,128)S(1)...) custom-call(s32[1]{0:T(128)} %bitcast.refs_0_, s32[2,256]{1,0:T(2,128)S(1)} %subtract_bitcast_fusion.refs_1_, ...), custom_call_target="tpu_custom_call" | custom-call | flops 1711276032 | bytes 5373952 | tf_op jit(solution)/shard_map/attention_0/pallas_call | solution.py:214
  35.9 0.0 collective-permute-done.1.refs_7_
  35.9 10.3 %attention_1.1 = (bf16[256,1024]{1,0:T(8,128)(2,1)}, bf16[256,1024]{1,0:T(8,128)(2,1)}, bf16[2,208,1024]{2,1,0:T(8,128)(2,1)S(1)}, f32[256,512]{1,0:T(8,128)S(1)...) custom-call(s32[1]{0:T(128)} %bitcast.refs_0_, ...), custom_call_target="tpu_custom_call", output_to_operand_aliasing={{0}: (8, {}), {1}: (9, {}), {2}: (10, {})} | custom-call | flops 1711276032 | bytes 5373952 | tf_op jit(solution)/shard_map/attention_1/pallas_call | solution.py:214
  46.2 0.0 collective-permute-start.3
  46.2 3.2 %collective-permute-start.5 = (bf16[2,208,512]{2,1,0:T(8,128)(2,1)S(1)}, bf16[2,208,512]{2,1,0:T(8,128)(2,1)S(1)}, u32[]{:S(2)}, u32[]{:S(2)}) collective-permute-start(bf16[2,208,512]{2,1,0:T(8,128)(2,1)S(1)} %get-tuple-element.39), channel_id=1, source_target_pairs={{1,2},{3,4},{5,6},{7,8},{9,10},{11,12},{13,14},{2,1},{4,3},{6,5},{... | collective-permute-start | bytes 1277960 | tf_op jit(solution)/shard_map/ppermute | solution.py:46
  49.3 2.4 %collective-permute-start.4 = (bf16[2,208,512]{2,1,0:T(8,128)(2,1)S(1)}, bf16[2,208,512]{2,1,0:T(8,128)(2,1)S(1)}, u32[]{:S(2)}, u32[]{:S(2)}) collective-permute-start(bf16[2,208,512]{2,1,0:T(8,128)(2,1)S(1)} %get-tuple-element.36), channel_id=1, source_target_pairs={{1,2},{3,4},{5,6},{7,8},{9,10},{11,12},{13,14},{2,1},{4,3},{6,5},{... | collective-permute-start | bytes 1277960 | tf_op jit(solution)/shard_map/ppermute | solution.py:46
  51.7 13.0 %collective-permute-done.5.refs_4_ = bf16[2,208,512]{2,1,0:T(8,128)(2,1)S(1)} collective-permute-done((bf16[2,208,512]{2,1,0:T(8,128)(2,1)S(1)}, bf16[2,208,512]{2,1,0:T(8,128)(2,1)S(1)}, u32[]{:S(2)}, u32[]{:S(2)}) %collective-permute-start.5) | collective-permute-done | bytes 426016 | tf_op jit(solution)/shard_map/ppermute | solution.py:46
  64.7 0.0 collective-permute-done.3.refs_3_
  64.7 0.0 copy-start.2
  64.7 0.6 copy-done.2
  65.3 1.6 %gradient_sums_0.1 = (bf16[256,1024]{1,0:T(8,128)(2,1)}, bf16[256,1024]{1,0:T(8,128)(2,1)}) custom-call(s32[2]{0:T(128)S(1)} %copy-done.2, f32[256,512]{1,0:T(8,128)S(1)} %get-tuple-element.37.refs_1_, f32[256,512]{1,0:T(8,128)S(1)} %get-tuple-element.38.refs_2_, bf16[2,208,1024]{2,1,0:T(8,128)(2,1)S(1)} %collective-permute-done.3.refs_3_, ...), custom_call_target="tpu_custom_call" | custom-call | flops 786432 | bytes 2621440 | tf_op jit(solution)/shard_map/gradient_sums_0/pallas_call | solution.py:214
  66.9 2.4 %collective-permute-done.4.refs_4_ = bf16[2,208,512]{2,1,0:T(8,128)(2,1)S(1)} collective-permute-done((bf16[2,208,512]{2,1,0:T(8,128)(2,1)S(1)}, bf16[2,208,512]{2,1,0:T(8,128)(2,1)S(1)}, u32[]{:S(2)}, u32[]{:S(2)}) %collective-permute-start.4) | collective-permute-done | bytes 426016 | tf_op jit(solution)/shard_map/ppermute | solution.py:46
  69.3 1.6 %gradient_sums_1.1 = (bf16[256,1024]{1,0:T(8,128)(2,1)}, bf16[256,1024]{1,0:T(8,128)(2,1)}) custom-call(s32[2]{0:T(128)S(1)} %copy-done.2, f32[256,512]{1,0:T(8,128)S(1)} %get-tuple-element.33.refs_1_, f32[256,512]{1,0:T(8,128)S(1)} %get-tuple-element.34.refs_2_, ...), custom_call_target="tpu_custom_call", output_to_operand_aliasing={{0}: (5, {}), {1}: (6, {})} | custom-call | flops 786432 | bytes 2621440 | tf_op jit(solution)/shard_map/gradient_sums_1/pallas_call | solution.py:214
  (1 shorter events, 0.0 us)
Async XLA Ops:
  3.0 21.8 %copy-start.3 = (bf16[256,1024]{1,0:T(8,128)(2,1)S(1)}, bf16[256,1024]{1,0:T(8,128)(2,1)}, u32[]{:S(2)}) copy-start(bf16[256,1024]{1,0:T(8,128)(2,1)} %refs_2_.3) | copy-start | bytes 1572868
  3.1 21.8 %copy-start.4 = (bf16[256,1024]{1,0:T(8,128)(2,1)S(1)}, bf16[256,1024]{1,0:T(8,128)(2,1)}, u32[]{:S(2)}) copy-start(bf16[256,1024]{1,0:T(8,128)(2,1)} %refs_3_.3) | copy-start | bytes 1572868
  5.3 19.6 %copy-start = (bf16[256,1024]{1,0:T(8,128)(2,1)S(1)}, bf16[256,1024]{1,0:T(8,128)(2,1)}, u32[]{:S(2)}) copy-start(bf16[256,1024]{1,0:T(8,128)(2,1)} %refs_4_.3) | copy-start | bytes 1572868
  5.3 19.6 %copy-start.1 = (bf16[256,1024]{1,0:T(8,128)(2,1)S(1)}, bf16[256,1024]{1,0:T(8,128)(2,1)}, u32[]{:S(2)}) copy-start(bf16[256,1024]{1,0:T(8,128)(2,1)} %refs_5_.3) | copy-start | bytes 1572868
  5.3 3.9 %collective-permute-start = (bf16[2,208,1024]{2,1,0:T(8,128)(2,1)}, bf16[2,208,1024]{2,1,0:T(8,128)(2,1)S(1)}, u32[]{:S(2)}, u32[]{:S(2)}) collective-permute-start(bf16[2,208,1024]{2,1,0:T(8,128)(2,1)} %pack_partner.1), channel_id=1, source_target_pairs={{0,1},{2,3},{4,5},{6,7},{8,9},{10,11},{12,13},{14,15},{1,0},{3,2},... | collective-permute-start | bytes 2555912 | tf_op jit(solution)/shard_map/ppermute | solution.py:46
  6.0 18.9 %collective-permute-start.2 = (bf16[2,208,512]{2,1,0:T(8,128)(2,1)}, bf16[2,208,512]{2,1,0:T(8,128)(2,1)}, u32[]{:S(2)}, u32[]{:S(2)}) collective-permute-start(bf16[2,208,512]{2,1,0:T(8,128)(2,1)} %pack_next_0.1), channel_id=1, source_target_pairs={{1,2},{3,4},{5,6},{7,8},{9,10},{11,12},{13,14},{2,1},{4,3},{6,5},{... | collective-permute-start | bytes 1277960 | tf_op jit(solution)/shard_map/ppermute | solution.py:46
  9.2 4.3 %copy-start.5 = (s32[256,2]{0,1:T(2,128)S(1)}, s32[256,2]{0,1:T(2,128)}, u32[]{:S(2)}) copy-start(s32[256,2]{0,1:T(2,128)} %param.9) | copy-start | bytes 6148
  11.0 24.8 %collective-permute-start.1 = (bf16[2,208,512]{2,1,0:T(8,128)(2,1)}, bf16[2,208,512]{2,1,0:T(8,128)(2,1)S(1)}, u32[]{:S(2)}, u32[]{:S(2)}) collective-permute-start(bf16[2,208,512]{2,1,0:T(8,128)(2,1)} %pack_next_1.1), channel_id=1, source_target_pairs={{1,2},{3,4},{5,6},{7,8},{9,10},{11,12},{13,14},{2,1},{4,3},{6,5},{... | collective-permute-start | bytes 1277960 | tf_op jit(solution)/shard_map/ppermute | solution.py:46
  46.2 18.6 %collective-permute-start.3 = (bf16[2,208,1024]{2,1,0:T(8,128)(2,1)S(1)}, bf16[2,208,1024]{2,1,0:T(8,128)(2,1)S(1)}, u32[]{:S(2)}, u32[]{:S(2)}) collective-permute-start(bf16[2,208,1024]{2,1,0:T(8,128)(2,1)S(1)} %get-tuple-element.35), channel_id=1, source_target_pairs={{0,1},{2,3},{4,5},{6,7},{8,9},{10,11},{12,13},{14,15},{1,0},{3,2},... | collective-permute-start | bytes 2555912 | tf_op jit(solution)/shard_map/ppermute | solution.py:46
  46.2 18.6 %collective-permute-start.5 = (bf16[2,208,512]{2,1,0:T(8,128)(2,1)S(1)}, bf16[2,208,512]{2,1,0:T(8,128)(2,1)S(1)}, u32[]{:S(2)}, u32[]{:S(2)}) collective-permute-start(bf16[2,208,512]{2,1,0:T(8,128)(2,1)S(1)} %get-tuple-element.39), channel_id=1, source_target_pairs={{1,2},{3,4},{5,6},{7,8},{9,10},{11,12},{13,14},{2,1},{4,3},{6,5},{... | collective-permute-start | bytes 1277960 | tf_op jit(solution)/shard_map/ppermute | solution.py:46
  49.3 20.0 %collective-permute-start.4 = (bf16[2,208,512]{2,1,0:T(8,128)(2,1)S(1)}, bf16[2,208,512]{2,1,0:T(8,128)(2,1)S(1)}, u32[]{:S(2)}, u32[]{:S(2)}) collective-permute-start(bf16[2,208,512]{2,1,0:T(8,128)(2,1)S(1)} %get-tuple-element.36), channel_id=1, source_target_pairs={{1,2},{3,4},{5,6},{7,8},{9,10},{11,12},{13,14},{2,1},{4,3},{6,5},{... | collective-permute-start | bytes 1277960 | tf_op jit(solution)/shard_map/ppermute | solution.py:46
  64.7 0.6 copy-start.2

commit v4 on v3

v4 whole, which is shorter than its diff:
```python
import functools
import math

import jax
import jax.numpy as jnp
from jax import lax
from jax.experimental import pallas as pl
from jax.experimental.pallas import tpu as pltpu
from jax.sharding import PartitionSpec as P

HEADS = 16
HEAD_DIM = 64
ROWMIN = 20
STEP = 4
PAIR = 2 * HEAD_DIM
PAIRS = HEADS // 2
SCALE = HEAD_DIM**-0.5
LOG2_E = math.log2(math.e)
BLOCK = 32
OUTSIDE = -1e30
CHUNKS = (0, 4, 8)
VMEM_BYTES = 40 * 2**20


def reach_sizes(points, count):
    area_rows = points * count // STEP
    root_bound = min(((area_rows + 2 * 4**power) // (3 * 2**power) for power in range(3, 9)))
    grow_rows = root_bound - ROWMIN // STEP - 6
    row_longest = ROWMIN + STEP * (grow_rows - 1)
    rim_width = (2 * row_longest + 15) // 16 * 16
    return (rim_width, (rim_width + points - 1) // points)


def spans(bounds):
    return list(zip(bounds[:-1], bounds[1:]))


def passed_along(value, steps):
    count = lax.axis_size("band")
    initial, last = (max(0, -steps), min(count, count - steps))
    return lax.ppermute(value, "band", [(source, source + steps) for source in range(initial, last)])


def swapped(value, first):
    count = lax.axis_size("band")
    pairs = [(at, at + 1) for at in range(first, count - 1, 2)]
    return lax.ppermute(value, "band", pairs + [(high, low) for low, high in pairs])


def dot_nt(left, right):
    return lax.dot_general(
        left, right, (((1,), (1,)), ((), ())), preferred_element_type=jnp.float32
    )


def dot_nn(left, right):
    return jnp.dot(left, right, preferred_element_type=jnp.float32)


def head_masks():
    lanes = lax.broadcasted_iota(jnp.int32, (1, PAIR), 1)
    first = (lanes < HEAD_DIM).astype(jnp.float32)
    return (first.astype(jnp.bfloat16), (1.0 - first).astype(jnp.bfloat16))


def is_even():
    return lax.axis_index("band") % 2 == 0


def pack_kernel(points, columns, *refs):
    sources, out_ref, sems = refs[:-2], refs[-2], refs[-1]
    rows = out_ref.shape[1]
    start = pl.multiple_of(jnp.where(is_even(), 0, points - rows), 16)
    copies = [
        pltpu.make_async_copy(
            source.at[pl.ds(start, rows), columns], out_ref.at[at], sems.at[at]
        )
        for at, source in enumerate(sources)
    ]
    for copy in copies:
        copy.start()
    for copy in copies:
        copy.wait()


def pack(sources, rows, low, high, name):
    points = sources[0].shape[0]
    width = (high - low) * PAIR
    return pl.pallas_call(
        functools.partial(pack_kernel, points, slice(low * PAIR, high * PAIR)),
        in_specs=[pl.BlockSpec(memory_space=pl.ANY)] * len(sources),
        out_specs=pl.BlockSpec(memory_space=pltpu.VMEM),
        out_shape=jax.ShapeDtypeStruct((len(sources), rows, width), jnp.bfloat16),
        scratch_shapes=[pltpu.SemaphoreType.DMA((len(sources),))],
        cost_estimate=pl.CostEstimate(
            flops=0, bytes_accessed=4 * len(sources) * rows * width, transcendentals=0
        ),
        name=name,
    )(*sources)


def attention_kernel(rim, lengths, points, carried, *refs):
    far = len(lengths) // 2 - 1
    near = lengths[far]
    half = points // 2
    reached = half + 2 * rim
    win_ref, q_ref, g_ref, k_ref, v_ref, partner_k_ref, partner_v_ref, next_ref = refs[:8]
    far_refs = refs[8 : 8 + 2 * far]
    outs = refs[8 + 2 * far + carried :]
    att_ref, dq_ref, to_partner_ref, dk_ref, dv_ref, to_next_ref = outs[:6]
    to_far_refs = outs[6 : 6 + 2 * far]
    bias_ref, keys_ref, turned_ref, exps_ref, probs_ref, dscores_ref = outs[-6:]
    even = is_even()

    @pl.when(pl.program_id(0) == 0)
    def _():
        for part in range(2):
            own = slice(part * half, (part + 1) * half)
            lower = jnp.concatenate([win_ref[0:1, own]] * 2, axis=1)
            upper = jnp.concatenate([win_ref[1:2, own]] * 2, axis=1)
            keys = part * half - rim + lax.broadcasted_iota(jnp.int32, (reached, points), 0)
            bias_ref[part] = jnp.where((keys >= lower) & (keys < upper), 0.0, OUTSIDE)

    for slot, (own_ref, partner_ref) in enumerate([(k_ref, partner_k_ref), (v_ref, partner_v_ref)]):
        start = 0
        for at in range(far):
            keys_ref[slot, start : start + lengths[at], :] = far_refs[at][slot]
            start += lengths[at]
        keys_ref[slot, start : start + near, :] = jnp.where(
            even, next_ref[slot], partner_ref[points - near :, :]
        )
        keys_ref[slot, rim : rim + points, :] = own_ref[...]
        start = rim + points
        keys_ref[slot, start : start + near, :] = jnp.where(
            even, partner_ref[:near, :], next_ref[slot]
        )
        start += near
        for at in range(far, 2 * far):
            keys_ref[slot, start : start + lengths[at + 2], :] = far_refs[at][slot]
            start += lengths[at + 2]
        turned_ref[slot] = keys_ref[slot].T
    g_turned = g_ref[...].T
    masks = head_masks()
    spans_of = [slice(part * half, part * half + reached) for part in range(2)]
    owns = [slice(part * half, (part + 1) * half) for part in range(2)]
    q_both = [
        jnp.concatenate([q_ref[own, :] * (mask * SCALE) for mask in masks], axis=0) for own in owns
    ]
    g_both = [jnp.concatenate([g_ref[own, :] * mask for mask in masks], axis=0) for own in owns]
    blocks = [slice(row, row + BLOCK) for row in range(0, reached, BLOCK)]

    def fold(op, total, block):
        for row in range(0, BLOCK, 8):
            total = op(total, block[row : row + 8])
        return total

    def both(turned):
        return [turned[:HEAD_DIM, :half], turned[HEAD_DIM:, half:]]

    def forward_scores(part):
        scores = dot_nt(keys_ref[0, spans_of[part], :], q_both[part])
        top = jnp.full((8, points), OUTSIDE, jnp.float32)
        for block in blocks:
            biased = scores[block] + bias_ref[part, block, :]
            exps_ref[part, block, :] = biased
            top = fold(jnp.maximum, top, biased)
        return jnp.max(top, axis=0, keepdims=True)

    def forward_probs(part, top):
        total = jnp.zeros((8, points), jnp.float32)
        for block in blocks:
            exps = jnp.exp2((exps_ref[part, block, :] - top) * LOG2_E)
            exps_ref[part, block, :] = exps
            total = fold(jnp.add, total, exps)
        inverse = 1.0 / jnp.sum(total, axis=0, keepdims=True)
        for block in blocks:
            probs_ref[part, block, :] = (exps_ref[part, block, :] * inverse).astype(jnp.bfloat16)
        return inverse

    def forward_outputs(part):
        own = owns[part]
        att = [
            x.astype(jnp.bfloat16) for x in both(dot_nn(turned_ref[1, :, spans_of[part]], probs_ref[part]))
        ]
        att_ref[own, :] = jnp.concatenate(att, axis=0).T
        return jnp.concatenate(
            [
                jnp.sum(
                    g_turned[head * HEAD_DIM : (head + 1) * HEAD_DIM, own].astype(jnp.float32)
                    * att[head].astype(jnp.float32),
                    axis=0,
                    keepdims=True,
                )
                for head in range(2)
            ],
            axis=1,
        )

    def backward_scores(part, inverse, delta):
        dprobs = dot_nt(keys_ref[1, spans_of[part], :], g_both[part])
        for block in blocks:
            probs = exps_ref[part, block, :] * inverse
            dscores_ref[part, block, :] = (probs * (dprobs[block] - delta)).astype(jnp.bfloat16)

    def backward_outputs(part):
        own = owns[part]
        dq = both(dot_nn(turned_ref[0, :, spans_of[part]], dscores_ref[part]))
        dq_ref[own, :] = jnp.concatenate([(x * SCALE).astype(jnp.bfloat16) for x in dq], axis=0).T
        return (
            dot_nn(dscores_ref[part], q_both[part]),
            dot_nn(probs_ref[part], g_both[part]),
        )

    top_0 = forward_scores(0)
    top_1 = forward_scores(1)
    inverse_0 = forward_probs(0, top_0)
    delta_0 = forward_outputs(0)
    inverse_1 = forward_probs(1, top_1)
    backward_scores(0, inverse_0, delta_0)
    delta_1 = forward_outputs(1)
    sums_0 = backward_outputs(0)
    backward_scores(1, inverse_1, delta_1)
    sums_1 = backward_outputs(1)

    def rows_of(low, high, start, stop):
        cuts = sorted({start, stop} | {x for x in (half, reached) if start < x < stop})
        pieces = []
        for first, last in spans(cuts):
            if last <= half:
                pieces.append(low[first:last])
            elif first >= reached:
                pieces.append(high[first - half : last - half])
            else:
                pieces.append(low[first:last] + high[first - half : last - half])
        return jnp.concatenate(pieces, axis=0)

    for slot, own_ref in enumerate([dk_ref, dv_ref]):
        low, high = sums_0[slot], sums_1[slot]
        own_ref[...] = rows_of(low, high, rim, rim + points)
        near_low = rows_of(low, high, rim - near, rim).astype(jnp.bfloat16)
        near_high = rows_of(low, high, rim + points, rim + points + near).astype(jnp.bfloat16)
        to_partner_ref[slot] = jnp.where(even, near_high, near_low)
        to_next_ref[slot] = jnp.where(even, near_low, near_high)
        start = 0
        for at in range(far):
            ref = to_far_refs[at]
            ref[slot] = rows_of(low, high, start, start + lengths[at]).astype(jnp.bfloat16)
            start += lengths[at]
        start = rim + points + near
        for at in range(far, 2 * far):
            ref = to_far_refs[at]
            ref[slot] = rows_of(low, high, start, start + lengths[at + 2]).astype(jnp.bfloat16)
            start += lengths[at + 2]


def sum_kernel(far_lengths, points, carried, *refs):
    far = len(far_lengths) // 2
    dk_ref, dv_ref, partner_ref, next_ref = refs[:4]
    far_refs = refs[4 : 4 + 2 * far]
    outs = refs[4 + 2 * far + carried :]
    total = outs[-1]
    near = partner_ref.shape[1]
    high = pl.multiple_of(jnp.where(is_even(), points - near, 0), 16)
    starts = (high, points - near - high)
    for slot, (own_ref, out_ref) in enumerate([(dk_ref, outs[0]), (dv_ref, outs[1])]):
        total[...] = own_ref[...]
        for at, ref in enumerate((partner_ref, next_ref)):
            rows = pl.ds(pl.multiple_of(starts[at], 16), near)
            total[rows, :] += ref[slot].astype(jnp.float32)
        for at, (ref, length) in enumerate(zip(far_refs, far_lengths)):
            rows = slice(points - length, points) if at < far else slice(0, length)
            total[rows, :] += ref[slot].astype(jnp.float32)
        out_ref[...] = total[...].astype(jnp.bfloat16)


def chunk_call(kernel, args, in_specs, carried, out_specs, out_shape, **options):
    return pl.pallas_call(
        functools.partial(kernel, len(carried)),
        in_specs=in_specs + [pl.BlockSpec(memory_space=pl.ANY)] * len(carried),
        out_specs=out_specs,
        out_shape=out_shape,
        input_output_aliases={len(args) + at: at for at in range(len(carried))},
        compiler_params=pltpu.CompilerParams(
            vmem_limit_bytes=VMEM_BYTES, dimension_semantics=("arbitrary",)
        ),
        **options,
    )(*args, *carried)


def per_device(queries, keys, values, grad_out, windows):
    points, width = queries.shape
    rim_width, reach = reach_sizes(points, lax.axis_size("band"))
    band = lax.axis_index("band")
    near = min(points, rim_width)
    far = [d for d in range(-reach, reach + 1) if abs(d) > 1]
    far_sizes = [min(points, rim_width - (abs(d) - 1) * points) for d in far]
    lows = len(far) // 2
    lengths = far_sizes[:lows] + [near, near] + far_sizes[lows:]
    wide = points + 2 * rim_width
    relative = (windows - band * points).T

    to_next, from_next = [], []
    ready = (keys, values)
    for chunk, (low, high) in enumerate(spans(CHUNKS)):
        to_next.append(pack(ready, near, low, high, f"pack_next_{chunk}"))
        ready = lax.optimization_barrier((keys, values, to_next[chunk]))[:2]
    from_next.append(swapped(to_next[0], 1))
    from_partner = [swapped(field, 0) for field in ready]
    for piece in to_next[1:]:
        from_next.append(swapped(lax.optimization_barrier((piece, *from_partner))[0], 1))
    from_far = []
    for d, size in zip(far, far_sizes):
        part = slice(points - size, points) if d < 0 else slice(0, size)
        from_far.append(passed_along(jnp.stack([keys[part], values[part]]), -d))

    def columns(rows, low):
        return pl.BlockSpec((rows, PAIR), lambda i: (0, i + low))

    def piece(rows, low):
        return pl.BlockSpec((2, rows, PAIR), lambda i: (0, 0, i + low))

    whole = jax.ShapeDtypeStruct((points, width), jnp.bfloat16)
    reached = points // 2 + 2 * rim_width
    outs, own_terms, back_next, back_far = [], [], [], []
    for chunk, (low, high) in enumerate(spans(CHUNKS)):
        count = high - low
        chunk_width = count * PAIR
        outs = chunk_call(
            lambda carried, *refs: attention_kernel(rim_width, lengths, points, carried, *refs),
            [relative, queries, grad_out, keys, values, *from_partner, from_next[chunk], *from_far],
            [pl.BlockSpec((2, points), lambda i: (0, 0))]
            + [columns(points, low)] * 6
            + [piece(near, 0)]
            + [piece(size, low) for size in far_sizes],
            outs[:3],
            [columns(points, low)] * 2
            + [piece(near, low)]
            + [columns(points, 0)] * 2
            + [piece(near, 0)]
            + [piece(size, 0) for size in far_sizes],
            [whole] * 2
            + [jax.ShapeDtypeStruct((2, near, width), jnp.bfloat16)]
            + [jax.ShapeDtypeStruct((points, chunk_width), jnp.float32)] * 2
            + [
                jax.ShapeDtypeStruct((2, size, chunk_width), jnp.bfloat16)
                for size in [near] + far_sizes
            ],
            grid=(count,),
            scratch_shapes=[
                pltpu.VMEM((2, reached, points), jnp.float32),
                pltpu.VMEM((2, wide, PAIR), jnp.bfloat16),
                pltpu.VMEM((2, PAIR, wide), jnp.bfloat16),
                pltpu.VMEM((2, reached, points), jnp.float32),
                pltpu.VMEM((2, reached, points), jnp.bfloat16),
                pltpu.VMEM((2, reached, points), jnp.bfloat16),
            ],
            cost_estimate=pl.CostEstimate(
                flops=count * 24 * reached * points * PAIR,
                bytes_accessed=count * PAIR * (20 * points + 8 * wide),
                transcendentals=2 * count * points * reached,
            ),
            name=f"attention_{chunk}",
        )
        own_terms.append(outs[3:5])
        to_back = outs[5]
        if back_next:
            to_back = lax.optimization_barrier((to_back, back_next[-1]))[0]
        back_next.append(swapped(to_back, 1))
        back_far.append([passed_along(term, d) for term, d in zip(outs[6:], far)])
    back_partner = swapped(outs[2], 0)

    grads = []
    for chunk, (low, high) in enumerate(spans(CHUNKS)):
        chunk_width = (high - low) * PAIR
        step = 2 * PAIR

        def sums(rows, low):
            return pl.BlockSpec((rows, step), lambda i: (0, i + low * PAIR // step))

        def terms(rows, low):
            return pl.BlockSpec((2, rows, step), lambda i: (0, 0, i + low * PAIR // step))

        grads = chunk_call(
            lambda carried, *refs: sum_kernel(far_sizes, points, carried, *refs),
            [*own_terms[chunk], back_partner, back_next[chunk], *back_far[chunk]],
            [sums(points, 0)] * 2
            + [terms(near, low), terms(near, 0)]
            + [terms(size, 0) for size in far_sizes],
            grads,
            [sums(points, low)] * 2,
            [whole] * 2,
            grid=(chunk_width // step,),
            scratch_shapes=[pltpu.VMEM((points, step), jnp.float32)],
            cost_estimate=pl.CostEstimate(
                flops=6 * points * chunk_width,
                bytes_accessed=20 * points * chunk_width,
                transcendentals=0,
            ),
            name=f"gradient_sums_{chunk}",
        )
    return (outs[0], outs[1], grads[0], grads[1])


def solution(mesh):
    spread = P(("members", "band"), None)
    return jax.shard_map(
        per_device,
        mesh=mesh,
        in_specs=(spread, spread, spread, spread, P("band", None)),
        out_specs=(spread, spread, spread, spread),
        check_vma=False,
    )
```

time: 71.2 us -> 60.3 us (0.85)
  Pallas kernels: 30.4 us -> 23.2 us
  waiting for transfers between devices: 26.8 us -> 23.3 us
    pallas_call x7 -> x6, Pallas kernels: 30.4 us -> 23.2 us  [the longest x4 19.4 us: chunk_call(): pl.pallas_call(functools.partial(kernel, len(carried)), in_specs=in_specs...]
    ppermute x6 -> x7, waiting for transfers between devices: 26.8 us -> 23.3 us  [swapped(): lax.ppermute(value, 'band', pairs + [(high, low) for low, high in pairs])]
    ppermute x6 -> x7, starting transfers between devices: 11.8 us -> 12 us  [swapped(): lax.ppermute(value, 'band', pairs + [(high, low) for low, high in pairs])]
  transfers between devices with their start and end apart: 6 -> 7, of which waited for: 3 -> 3; matrix products, arithmetic and copies ran while one was open for 0% -> 0% of each run, Pallas kernels for 20% -> 30%
where the time goes in v4:
time: 60.3 us; the launch traced here: 59.9 us
  waiting for transfers between devices  23.3 us (39%)
  Pallas kernels  23.2 us (38%)
  starting transfers between devices  12 us (20%)
  between operations  0.76 us (1%)
  local copies, waits for them, and re-layouts  0.7 us (1%)
    ppermute x7, waiting for transfers between devices, swapped(): lax.ppermute(value, 'band', pairs + [(high, low) for low, high in pairs])  23.3 us
    pallas_call x4, Pallas kernels, chunk_call(): pl.pallas_call(functools.partial(kernel, len(carried)), in_specs=in_specs...  19.4 us
    ppermute x7, starting transfers between devices, swapped(): lax.ppermute(value, 'band', pairs + [(high, low) for low, high in pairs])  12 us
    pallas_call x2, Pallas kernels, pack(): pl.pallas_call(functools.partial(pack_kernel, points, slice(low * PAIR, h...  3.81 us
  transfers between devices with their start and end apart: 7, of which 3 were waited for; matrix products, arithmetic and copies ran while one was open for 0% of the time, Pallas kernels for 30%

profile of v4, /device:TPU:9, one launch (start us, length us, event | category | flops | bytes accessed | tf_op | source)
XLA Modules:
  0.0 59.9 jit_solution(75235924040041423)
XLA Ops:
  0.6 0.0 copy-start.2
  0.6 0.0 copy-start.3
  0.7 1.9 %pack_next_0.1 = bf16[2,208,512]{2,1,0:T(8,128)(2,1)} custom-call(bf16[256,1024]{1,0:T(8,128)(2,1)} %refs_3_.3, bf16[256,1024]{1,0:T(8,128)(2,1)} %refs_4_.3), custom_call_target="tpu_custom_call" | custom-call | bytes 851968 | tf_op jit(solution)/shard_map/pack_next_0/pallas_call | solution.py:89
  2.6 0.0 copy-start
  2.6 0.0 copy-start.1
  2.6 1.9 %pack_next_1.1 = bf16[2,208,512]{2,1,0:T(8,128)(2,1)} custom-call(bf16[256,1024]{1,0:T(8,128)(2,1)} %refs_3_.3, bf16[256,1024]{1,0:T(8,128)(2,1)} %refs_4_.3), custom_call_target="tpu_custom_call" | custom-call | bytes 851968 | tf_op jit(solution)/shard_map/pack_next_1/pallas_call | solution.py:89
  4.5 0.0 copy-done
  4.5 0.7 %collective-permute-start = (bf16[256,1024]{1,0:T(8,128)(2,1)S(1)}, bf16[256,1024]{1,0:T(8,128)(2,1)S(1)}, u32[]{:S(2)}, u32[]{:S(2)}) collective-permute-start(bf16[256,1024]{1,0:T(8,128)(2,1)S(1)} %copy-done), channel_id=1, source_target_pairs={{0,1},{2,3},{4,5},{6,7},{8,9},{10,11},{12,13},{14,15},{1,0},{3,2},... | collective-permute-start | bytes 1572872 | tf_op jit(solution)/shard_map/ppermute | solution.py:47
  5.2 0.0 copy-done.1
  5.3 0.1 collective-permute-start.1
  5.3 3.4 %collective-permute-start.3 = (bf16[2,208,512]{2,1,0:T(8,128)(2,1)}, bf16[2,208,512]{2,1,0:T(8,128)(2,1)}, u32[]{:S(2)}, u32[]{:S(2)}) collective-permute-start(bf16[2,208,512]{2,1,0:T(8,128)(2,1)} %pack_next_0.1), channel_id=1, source_target_pairs={{1,2},{3,4},{5,6},{7,8},{9,10},{11,12},{13,14},{2,1},{4,3},{6,5},{... | collective-permute-start | bytes 1277960 | tf_op jit(solution)/shard_map/ppermute | solution.py:47
  8.8 0.0 collective-permute-done.refs_5_
  8.8 0.0 collective-permute-done.1.refs_6_
  8.8 2.1 %collective-permute-start.2 = (bf16[2,208,512]{2,1,0:T(8,128)(2,1)}, bf16[2,208,512]{2,1,0:T(8,128)(2,1)}, u32[]{:S(2)}, u32[]{:S(2)}) collective-permute-start(bf16[2,208,512]{2,1,0:T(8,128)(2,1)} %pack_next_1.1), channel_id=1, source_target_pairs={{1,2},{3,4},{5,6},{7,8},{9,10},{11,12},{13,14},{2,1},{4,3},{6,5},{... | collective-permute-start | bytes 1277960 | tf_op jit(solution)/shard_map/ppermute | solution.py:47
  10.9 0.0 copy-start.4
  11.0 0.7 %copy-done.4 = s32[256,2]{0,1:T(2,128)S(1)} copy-done((s32[256,2]{0,1:T(2,128)S(1)}, s32[256,2]{0,1:T(2,128)}, u32[]{:S(2)}) %copy-start.4) | copy-done | bytes 2072
  11.6 12.6 %collective-permute-done.3.refs_7_ = bf16[2,208,512]{2,1,0:T(8,128)(2,1)} collective-permute-done((bf16[2,208,512]{2,1,0:T(8,128)(2,1)}, bf16[2,208,512]{2,1,0:T(8,128)(2,1)}, u32[]{:S(2)}, u32[]{:S(2)}) %collective-permute-start.3) | collective-permute-done | bytes 426016 | tf_op jit(solution)/shard_map/ppermute | solution.py:47
  24.2 0.0 copy-done.2
  24.2 0.0 copy-done.3
  24.2 8.5 %attention_0.1 = (bf16[256,1024]{1,0:T(8,128)(2,1)}, bf16[256,1024]{1,0:T(8,128)(2,1)}, bf16[2,208,1024]{2,1,0:T(8,128)(2,1)S(1)}, f32[256,512]{1,0:T(8,128)S(1)...) custom-call(s32[2,256]{1,0:T(2,128)S(1)} %subtract_bitcast_fusion.refs_0_, bf16[256,1024]{1,0:T(8,128)(2,1)S(1)} %copy-done.2, ...), custom_call_target="tpu_custom_call" | custom-call | flops 1711276032 | bytes 5373952 | tf_op jit(solution)/shard_map/attention_0/pallas_call | solution.py:277
  32.7 3.4 %collective-permute-start.5 = (bf16[2,208,512]{2,1,0:T(8,128)(2,1)S(1)}, bf16[2,208,512]{2,1,0:T(8,128)(2,1)S(1)}, u32[]{:S(2)}, u32[]{:S(2)}) collective-permute-start(bf16[2,208,512]{2,1,0:T(8,128)(2,1)S(1)} %get-tuple-element.40), channel_id=1, source_target_pairs={{1,2},{3,4},{5,6},{7,8},{9,10},{11,12},{13,14},{2,1},{4,3},{6,5},{... | collective-permute-start | bytes 1277960 | tf_op jit(solution)/shard_map/ppermute | solution.py:47
  36.2 0.0 collective-permute-done.2.refs_7_
  36.2 8.5 %attention_1.1 = (bf16[256,1024]{1,0:T(8,128)(2,1)}, bf16[256,1024]{1,0:T(8,128)(2,1)}, bf16[2,208,1024]{2,1,0:T(8,128)(2,1)S(1)}, f32[256,512]{1,0:T(8,128)S(1)...) custom-call(s32[2,256]{1,0:T(2,128)S(1)} %subtract_bitcast_fusion.re, ...), custom_call_target="tpu_custom_call", output_to_operand_aliasing={{0}: (8, {}), {1}: (9, {}), {2}: (10, {})} | custom-call | flops 1711276032 | bytes 5373952 | tf_op jit(solution)/shard_map/attention_1/pallas_call | solution.py:277
  44.7 0.0 collective-permute-start.4
  44.7 0.0 collective-permute-done.5.refs_3_
  44.7 2.1 %collective-permute-start.6 = (bf16[2,208,512]{2,1,0:T(8,128)(2,1)S(1)}, bf16[2,208,512]{2,1,0:T(8,128)(2,1)S(1)}, u32[]{:S(2)}, u32[]{:S(2)}) collective-permute-start(bf16[2,208,512]{2,1,0:T(8,128)(2,1)S(1)} %get-tuple-element.41), channel_id=1, source_target_pairs={{1,2},{3,4},{5,6},{7,8},{9,10},{11,12},{13,14},{2,1},{4,3},{6,5},{... | collective-permute-start | bytes 1277960 | tf_op jit(solution)/shard_map/ppermute | solution.py:47
  46.9 0.2 collective-permute-done.4.refs_2_
  47.1 1.2 %gradient_sums_0.1 = (bf16[256,1024]{1,0:T(8,128)(2,1)}, bf16[256,1024]{1,0:T(8,128)(2,1)}) custom-call(f32[256,512]{1,0:T(8,128)S(1)} %get-tuple-element.42.refs_0_, f32[256,512]{1,0:T(8,128)S(1)} %get-tuple-element.43.refs_1_, bf16[2,208,1024]{2,1,0:T(8,128)(2,1)S(1)} %collective-permute-done.4.refs_2_, bf16[2,208,512]{2,1,0:T(8,128)(2,1)S(1)} %collective-permute-done.5.refs_3_), custom_call_target="tpu_custom_call" | custom-call | flops 786432 | bytes 2621440 | tf_op jit(solution)/shard_map/gradient_sums_0/pallas_call | solution.py:277
  48.3 10.4 %collective-permute-done.6.refs_3_ = bf16[2,208,512]{2,1,0:T(8,128)(2,1)S(1)} collective-permute-done((bf16[2,208,512]{2,1,0:T(8,128)(2,1)S(1)}, bf16[2,208,512]{2,1,0:T(8,128)(2,1)S(1)}, u32[]{:S(2)}, u32[]{:S(2)}) %collective-permute-start.6) | collective-permute-done | bytes 426016 | tf_op jit(solution)/shard_map/ppermute | solution.py:47
  58.8 1.2 %gradient_sums_1.1 = (bf16[256,1024]{1,0:T(8,128)(2,1)}, bf16[256,1024]{1,0:T(8,128)(2,1)}) custom-call(f32[256,512]{1,0:T(8,128)S(1)} %get-tuple-element.36.refs_0_, f32[256,512]{1,0:T(8,128)S(1)} %get-tuple-element.37.refs_1_, bf16[2,208,1024]{2,1,0:T(8,128)(2,1)S(1)} %collective-permute-done.4.refs_2_, ...), custom_call_target="tpu_custom_call", output_to_operand_aliasing={{0}: (4, {}), {1}: (5, {})} | custom-call | flops 786432 | bytes 2621440 | tf_op jit(solution)/shard_map/gradient_sums_1/pallas_call | solution.py:277
  (1 shorter events, 0.0 us)
Async XLA Ops:
  0.6 23.6 %copy-start.2 = (bf16[256,1024]{1,0:T(8,128)(2,1)S(1)}, bf16[256,1024]{1,0:T(8,128)(2,1)}, u32[]{:S(2)}) copy-start(bf16[256,1024]{1,0:T(8,128)(2,1)} %refs_1_.6) | copy-start | bytes 1572868
  0.6 23.6 %copy-start.3 = (bf16[256,1024]{1,0:T(8,128)(2,1)S(1)}, bf16[256,1024]{1,0:T(8,128)(2,1)}, u32[]{:S(2)}) copy-start(bf16[256,1024]{1,0:T(8,128)(2,1)} %refs_2_.3) | copy-start | bytes 1572868
  2.6 1.9 %copy-start = (bf16[256,1024]{1,0:T(8,128)(2,1)S(1)}, bf16[256,1024]{1,0:T(8,128)(2,1)}, u32[]{:S(2)}) copy-start(bf16[256,1024]{1,0:T(8,128)(2,1)} %refs_3_.3) | copy-start | bytes 1572868
  2.6 2.7 %copy-start.1 = (bf16[256,1024]{1,0:T(8,128)(2,1)S(1)}, bf16[256,1024]{1,0:T(8,128)(2,1)}, u32[]{:S(2)}) copy-start(bf16[256,1024]{1,0:T(8,128)(2,1)} %refs_4_.3) | copy-start | bytes 1572868
  4.5 4.3 %collective-permute-start = (bf16[256,1024]{1,0:T(8,128)(2,1)S(1)}, bf16[256,1024]{1,0:T(8,128)(2,1)S(1)}, u32[]{:S(2)}, u32[]{:S(2)}) collective-permute-start(bf16[256,1024]{1,0:T(8,128)(2,1)S(1)} %copy-done), channel_id=1, source_target_pairs={{0,1},{2,3},{4,5},{6,7},{8,9},{10,11},{12,13},{14,15},{1,0},{3,2},... | collective-permute-start | bytes 1572872 | tf_op jit(solution)/shard_map/ppermute | solution.py:47
  5.3 3.6 %collective-permute-start.1 = (bf16[256,1024]{1,0:T(8,128)(2,1)S(1)}, bf16[256,1024]{1,0:T(8,128)(2,1)S(1)}, u32[]{:S(2)}, u32[]{:S(2)}) collective-permute-start(bf16[256,1024]{1,0:T(8,128)(2,1)S(1)} %copy-done.1), channel_id=1, source_target_pairs={{0,1},{2,3},{4,5},{6,7},{8,9},{10,11},{12,13},{14,15},{1,0},{3,2},... | collective-permute-start | bytes 1572872 | tf_op jit(solution)/shard_map/ppermute | solution.py:47
  5.3 18.9 %collective-permute-start.3 = (bf16[2,208,512]{2,1,0:T(8,128)(2,1)}, bf16[2,208,512]{2,1,0:T(8,128)(2,1)}, u32[]{:S(2)}, u32[]{:S(2)}) collective-permute-start(bf16[2,208,512]{2,1,0:T(8,128)(2,1)} %pack_next_0.1), channel_id=1, source_target_pairs={{1,2},{3,4},{5,6},{7,8},{9,10},{11,12},{13,14},{2,1},{4,3},{6,5},{... | collective-permute-start | bytes 1277960 | tf_op jit(solution)/shard_map/ppermute | solution.py:47
  8.8 27.4 %collective-permute-start.2 = (bf16[2,208,512]{2,1,0:T(8,128)(2,1)}, bf16[2,208,512]{2,1,0:T(8,128)(2,1)}, u32[]{:S(2)}, u32[]{:S(2)}) collective-permute-start(bf16[2,208,512]{2,1,0:T(8,128)(2,1)} %pack_next_1.1), channel_id=1, source_target_pairs={{1,2},{3,4},{5,6},{7,8},{9,10},{11,12},{13,14},{2,1},{4,3},{6,5},{... | collective-permute-start | bytes 1277960 | tf_op jit(solution)/shard_map/ppermute | solution.py:47
  10.9 0.7 %copy-start.4 = (s32[256,2]{0,1:T(2,128)S(1)}, s32[256,2]{0,1:T(2,128)}, u32[]{:S(2)}) copy-start(s32[256,2]{0,1:T(2,128)} %param.9) | copy-start | bytes 6148
  32.7 12.0 %collective-permute-start.5 = (bf16[2,208,512]{2,1,0:T(8,128)(2,1)S(1)}, bf16[2,208,512]{2,1,0:T(8,128)(2,1)S(1)}, u32[]{:S(2)}, u32[]{:S(2)}) collective-permute-start(bf16[2,208,512]{2,1,0:T(8,128)(2,1)S(1)} %get-tuple-element.40), channel_id=1, source_target_pairs={{1,2},{3,4},{5,6},{7,8},{9,10},{11,12},{13,14},{2,1},{4,3},{6,5},{... | collective-permute-start | bytes 1277960 | tf_op jit(solution)/shard_map/ppermute | solution.py:47
  44.7 2.4 %collective-permute-start.4 = (bf16[2,208,1024]{2,1,0:T(8,128)(2,1)S(1)}, bf16[2,208,1024]{2,1,0:T(8,128)(2,1)S(1)}, u32[]{:S(2)}, u32[]{:S(2)}) collective-permute-start(bf16[2,208,1024]{2,1,0:T(8,128)(2,1)S(1)} %get-tuple-element.38), channel_id=1, source_target_pairs={{0,1},{2,3},{4,5},{6,7},{8,9},{10,11},{12,13},{14,15},{1,0},{3,2},... | collective-permute-start | bytes 2555912 | tf_op jit(solution)/shard_map/ppermute | solution.py:47
  44.7 14.0 %collective-permute-start.6 = (bf16[2,208,512]{2,1,0:T(8,128)(2,1)S(1)}, bf16[2,208,512]{2,1,0:T(8,128)(2,1)S(1)}, u32[]{:S(2)}, u32[]{:S(2)}) collective-permute-start(bf16[2,208,512]{2,1,0:T(8,128)(2,1)S(1)} %get-tuple-element.41), channel_id=1, source_target_pairs={{1,2},{3,4},{5,6},{7,8},{9,10},{11,12},{13,14},{2,1},{4,3},{6,5},{... | collective-permute-start | bytes 1277960 | tf_op jit(solution)/shard_map/ppermute | solution.py:47

commit v5 on v4

v5 whole, which is shorter than its diff:
```python
import functools
import math

import jax
import jax.numpy as jnp
from jax import lax
from jax.experimental import pallas as pl
from jax.experimental.pallas import tpu as pltpu
from jax.sharding import PartitionSpec as P

HEADS = 16
HEAD_DIM = 64
ROWMIN = 20
STEP = 4
PAIR = 2 * HEAD_DIM
PAIRS = HEADS // 2
SCALE = HEAD_DIM**-0.5
LOG2_E = math.log2(math.e)
BLOCK = 32
OUTSIDE = -1e30
CHUNKS = (0, 4, 8)
NEXT_CHUNKS = (0, 4, 8)
VMEM_BYTES = 40 * 2**20


def reach_sizes(points, count):
    area_rows = points * count // STEP
    root_bound = min(((area_rows + 2 * 4**power) // (3 * 2**power) for power in range(3, 9)))
    grow_rows = root_bound - ROWMIN // STEP - 6
    row_longest = ROWMIN + STEP * (grow_rows - 1)
    rim_width = (2 * row_longest + 15) // 16 * 16
    return (rim_width, (rim_width + points - 1) // points)


def spans(bounds):
    return list(zip(bounds[:-1], bounds[1:]))


def passed_along(value, steps):
    count = lax.axis_size("band")
    initial, last = (max(0, -steps), min(count, count - steps))
    return lax.ppermute(value, "band", [(source, source + steps) for source in range(initial, last)])


def swapped(value, first):
    count = lax.axis_size("band")
    pairs = [(at, at + 1) for at in range(first, count - 1, 2)]
    return lax.ppermute(value, "band", pairs + [(high, low) for low, high in pairs])


def dot_nt(left, right):
    return lax.dot_general(
        left, right, (((1,), (1,)), ((), ())), preferred_element_type=jnp.float32
    )


def dot_nn(left, right):
    return jnp.dot(left, right, preferred_element_type=jnp.float32)


def head_masks():
    lanes = lax.broadcasted_iota(jnp.int32, (1, PAIR), 1)
    first = (lanes < HEAD_DIM).astype(jnp.float32)
    return (first.astype(jnp.bfloat16), (1.0 - first).astype(jnp.bfloat16))


def is_even():
    return lax.axis_index("band") % 2 == 0


def pack_kernel(points, columns, *refs):
    sources, out_ref, sems = refs[:-2], refs[-2], refs[-1]
    rows = out_ref.shape[1]
    start = pl.multiple_of(jnp.where(is_even(), 0, points - rows), 16)
    copies = [
        pltpu.make_async_copy(
            source.at[pl.ds(start, rows), columns], out_ref.at[at], sems.at[at]
        )
        for at, source in enumerate(sources)
    ]
    for copy in copies:
        copy.start()
    for copy in copies:
        copy.wait()


def pack(sources, rows, low, high, name):
    points = sources[0].shape[0]
    width = (high - low) * PAIR
    return pl.pallas_call(
        functools.partial(pack_kernel, points, slice(low * PAIR, high * PAIR)),
        in_specs=[pl.BlockSpec(memory_space=pl.ANY)] * len(sources),
        out_specs=pl.BlockSpec(memory_space=pltpu.VMEM),
        out_shape=jax.ShapeDtypeStruct((len(sources), rows, width), jnp.bfloat16),
        scratch_shapes=[pltpu.SemaphoreType.DMA((len(sources),))],
        cost_estimate=pl.CostEstimate(
            flops=0, bytes_accessed=4 * len(sources) * rows * width, transcendentals=0
        ),
        name=name,
    )(*sources)


def attention_kernel(rim, lengths, points, low_pair, next_pairs, carried, *refs):
    far = len(lengths) // 2 - 1
    near = lengths[far]
    half = points // 2
    reached = half + 2 * rim
    wide = points + 2 * rim
    pairs = sum(next_pairs)
    win_ref, q_ref, g_ref, k_ref, v_ref, partner_k_ref, partner_v_ref = refs[:7]
    next_refs = refs[7 : 7 + len(next_pairs)]
    refs = refs[7 + len(next_pairs) :]
    far_refs = refs[: 2 * far]
    outs = refs[2 * far + carried :]
    att_out, dq_out, to_partner_ref, to_next_ref, dk_ref, dv_ref = outs[:6]
    to_far_refs = outs[6 : 6 + 2 * far]
    (bias_ref, keys_ref, turned_ref, exps_ref, probs_ref, dscores_ref, sums_ref, att_ref, dq_ref, sems) = outs[-10:]
    even = is_even()
    owns = [slice(part * half, (part + 1) * half) for part in range(2)]
    spans_of = [slice(part * half, part * half + reached) for part in range(2)]
    blocks = [slice(row, row + BLOCK) for row in range(0, reached, BLOCK)]
    masks = head_masks()

    for part, own in enumerate(owns):
        lower = jnp.concatenate([win_ref[0:1, own]] * 2, axis=1)
        upper = jnp.concatenate([win_ref[1:2, own]] * 2, axis=1)
        for block in blocks:
            keys = lax.broadcasted_iota(jnp.int32, (BLOCK, points), 0) + (part * half - rim + block.start)
            inside = (keys >= lower) & (keys < upper)
            bias_ref[part, block, :] = jnp.where(inside, 0.0, OUTSIDE)

    where_next = [
        (chunk, at) for chunk, count in enumerate(next_pairs) for at in range(count)
    ]

    def columns_of(pair):
        return slice((low_pair + pair) * PAIR, (low_pair + pair + 1) * PAIR)

    def local_columns(pair):
        return slice(pair * PAIR, (pair + 1) * PAIR)

    def gather_keys(pair):
        columns = columns_of(pair)
        chunk, at = where_next[pair]
        next_columns = local_columns(at)
        into = keys_ref.at[pair % 2]
        for slot, (own_ref, partner_ref) in enumerate([(k_ref, partner_k_ref), (v_ref, partner_v_ref)]):
            start = 0
            for at in range(far):
                into[slot, start : start + lengths[at], :] = far_refs[at][slot, :, columns]
                start += lengths[at]
            into[slot, start : start + near, :] = jnp.where(
                even, next_refs[chunk][slot, :, next_columns], partner_ref[points - near :, columns]
            )
            into[slot, rim : rim + points, :] = own_ref[:, columns]
            start = rim + points
            into[slot, start : start + near, :] = jnp.where(
                even, partner_ref[:near, columns], next_refs[chunk][slot, :, next_columns]
            )
            start += near
            for at in range(far, 2 * far):
                into[slot, start : start + lengths[at + 2], :] = far_refs[at][slot, :, columns]
                start += lengths[at + 2]
            turned_ref[pair % 2, slot] = into[slot].T

    def fold(op, total, block):
        for row in range(0, BLOCK, 8):
            total = op(total, block[row : row + 8])
        return total

    def both(turned):
        return [turned[:HEAD_DIM, :half], turned[HEAD_DIM:, half:]]

    def q_both(pair, part):
        q = q_ref[owns[part], columns_of(pair)]
        return jnp.concatenate([q * (mask * SCALE) for mask in masks], axis=0)

    def g_both(pair, part):
        g = g_ref[owns[part], columns_of(pair)]
        return jnp.concatenate([g * mask for mask in masks], axis=0)

    def forward_scores(pair, part):
        exps = exps_ref.at[pair % 2, part]
        scores = dot_nt(keys_ref[pair % 2, 0, spans_of[part], :], q_both(pair, part))
        top = jnp.full((8, points), OUTSIDE, jnp.float32)
        for block in blocks:
            biased = scores[block] + bias_ref[part, block, :]
            exps[block, :] = biased
            top = fold(jnp.maximum, top, biased)
        return jnp.max(top, axis=0, keepdims=True)

    def forward_probs(pair, part, top):
        exps = exps_ref.at[pair % 2, part]
        total = jnp.zeros((8, points), jnp.float32)
        for block in blocks:
            values = jnp.exp2((exps[block, :] - top) * LOG2_E)
            exps[block, :] = values
            total = fold(jnp.add, total, values)
        inverse = 1.0 / jnp.sum(total, axis=0, keepdims=True)
        for block in blocks:
            probs_ref[pair % 2, part, block, :] = (exps[block, :] * inverse).astype(jnp.bfloat16)
        return inverse

    def forward_outputs(pair, part):
        own = owns[part]
        att = [
            x.astype(jnp.bfloat16)
            for x in both(
                dot_nn(turned_ref[pair % 2, 1, :, spans_of[part]], probs_ref[pair % 2, part])
            )
        ]
        att_ref[pair, own, :] = jnp.concatenate(att, axis=0).T
        g_turned = g_ref[own, columns_of(pair)].T
        return jnp.concatenate(
            [
                jnp.sum(
                    g_turned[head * HEAD_DIM : (head + 1) * HEAD_DIM].astype(jnp.float32)
                    * att[head].astype(jnp.float32),
                    axis=0,
                    keepdims=True,
                )
                for head in range(2)
            ],
            axis=1,
        )

    def backward_scores(pair, part, inverse, delta):
        dprobs = dot_nt(keys_ref[pair % 2, 1, spans_of[part], :], g_both(pair, part))
        for block in blocks:
            probs = exps_ref[pair % 2, part, block, :] * inverse
            dscores_ref[pair % 2, part, block, :] = (probs * (dprobs[block] - delta)).astype(jnp.bfloat16)

    def backward_outputs(pair, part):
        dscores = dscores_ref[pair % 2, part]
        dq = both(dot_nn(turned_ref[pair % 2, 0, :, spans_of[part]], dscores))
        dq_ref[pair, owns[part], :] = jnp.concatenate(
            [(x * SCALE).astype(jnp.bfloat16) for x in dq], axis=0
        ).T
        terms = (dot_nn(dscores, q_both(pair, part)), dot_nn(probs_ref[pair % 2, part], g_both(pair, part)))
        for slot, term in enumerate(terms):
            into = sums_ref.at[pair % 2, slot]
            if part == 0:
                into[:reached, :] = term
            else:
                into[half:reached, :] += term[: reached - half]
                into[reached:, :] = term[reached - half :]

    copies = []

    def send_out(pair):
        columns = local_columns(pair)
        for slot, own_ref in enumerate([dk_ref, dv_ref]):
            sums = sums_ref.at[pair % 2, slot]
            own_ref[:, columns] = sums[rim : rim + points, :]
            near_low = sums[rim - near : rim, :].astype(jnp.bfloat16)
            near_high = sums[rim + points : rim + points + near, :].astype(jnp.bfloat16)
            to_partner_ref[slot, :, columns] = jnp.where(even, near_high, near_low)
            to_next_ref[slot, :, columns] = jnp.where(even, near_low, near_high)
            start = 0
            for at in range(far):
                size = lengths[at]
                to_far_refs[at][slot, :, columns] = sums[start : start + size, :].astype(jnp.bfloat16)
                start += size
            start = rim + points + near
            for at in range(far, 2 * far):
                size = lengths[at + 2]
                to_far_refs[at][slot, :, columns] = sums[start : start + size, :].astype(jnp.bfloat16)
                start += size
        for at, (ref, out) in enumerate([(att_ref, att_out), (dq_ref, dq_out)]):
            copy = pltpu.make_async_copy(ref.at[pair], out.at[:, columns_of(pair)], sems.at[at, pair])
            copy.start()
            copies.append(copy)

    units = [(pair, part) for pair in range(pairs) for part in range(2)]
    gather_keys(0)
    tops = {units[0]: forward_scores(*units[0])}
    for at, unit in enumerate(units):
        if at + 1 < len(units):
            following = units[at + 1]
            if following[1] == 0:
                gather_keys(following[0])
            tops[following] = forward_scores(*following)
        if at > 0:
            backward_outputs(*units[at - 1])
            if units[at - 1][1] == 1:
                send_out(units[at - 1][0])
        inverse = forward_probs(*unit, tops.pop(unit))
        delta = forward_outputs(*unit)
        backward_scores(*unit, inverse, delta)
    backward_outputs(*units[-1])
    send_out(units[-1][0])
    for copy in copies:
        copy.wait()


def sum_kernel(far_lengths, points, low, high, carried, *refs):
    far = len(far_lengths) // 2
    own_refs, partner_ref, next_ref = refs[:2], refs[2], refs[3]
    far_refs = refs[4 : 4 + 2 * far]
    outs = refs[4 + 2 * far + carried :]
    total, low_ref, sems = outs[-3:]
    near = partner_ref.shape[1]
    first = pl.multiple_of(jnp.where(is_even(), points - near, 0), 16)
    starts = (first, points - near - first)
    copies = []
    for slot in range(2):
        total[...] = own_refs[slot][...]
        for at, ref in enumerate((partner_ref, next_ref)):
            rows = pl.ds(pl.multiple_of(starts[at], 16), near)
            total[rows, :] += ref[slot].astype(jnp.float32)
        for at, (ref, length) in enumerate(zip(far_refs, far_lengths)):
            rows = slice(points - length, points) if at < far else slice(0, length)
            total[rows, :] += ref[slot].astype(jnp.float32)
        low_ref[slot] = total[...].astype(jnp.bfloat16)
        copy = pltpu.make_async_copy(
            low_ref.at[slot], outs[slot].at[:, low * PAIR : high * PAIR], sems.at[slot]
        )
        copy.start()
        copies.append(copy)
    for copy in copies:
        copy.wait()


def chunk_call(kernel, args, carried, count, out_shape, **options):
    vmem = pl.BlockSpec(memory_space=pltpu.VMEM)
    anywhere = pl.BlockSpec(memory_space=pl.ANY)
    return pl.pallas_call(
        functools.partial(kernel, len(carried)),
        in_specs=[vmem] * len(args) + [anywhere] * len(carried),
        out_specs=[anywhere] * count + [vmem] * (len(out_shape) - count),
        out_shape=out_shape,
        input_output_aliases={len(args) + at: at for at in range(len(carried))},
        compiler_params=pltpu.CompilerParams(vmem_limit_bytes=VMEM_BYTES),
        **options,
    )(*args, *carried)


def per_device(queries, keys, values, grad_out, windows):
    points, width = queries.shape
    rim_width, reach = reach_sizes(points, lax.axis_size("band"))
    band = lax.axis_index("band")
    near = min(points, rim_width)
    far = [d for d in range(-reach, reach + 1) if abs(d) > 1]
    far_sizes = [min(points, rim_width - (abs(d) - 1) * points) for d in far]
    lows = len(far) // 2
    lengths = far_sizes[:lows] + [near, near] + far_sizes[lows:]
    wide = points + 2 * rim_width
    reached = points // 2 + 2 * rim_width
    relative = (windows - band * points).T

    to_next, from_next, from_partner = [], [], []
    ready = (keys, values)
    for chunk, (low, high) in enumerate(spans(NEXT_CHUNKS)):
        to_next.append(pack(ready, near, low, high, f"pack_next_{chunk}"))
        from_next.append(swapped(to_next[chunk], 1))
        if chunk == 0:
            ready = lax.optimization_barrier((keys, values, to_next[0]))[:2]
            from_partner = [swapped(field, 0) for field in ready]
            ready = lax.optimization_barrier((keys, values, *from_partner))[:2]
        else:
            ready = lax.optimization_barrier((*ready, to_next[chunk], from_next[chunk - 1]))[:2]
    from_far = []
    for d, size in zip(far, far_sizes):
        part = slice(points - size, points) if d < 0 else slice(0, size)
        from_far.append(passed_along(jnp.stack([keys[part], values[part]]), -d))

    whole = jax.ShapeDtypeStruct((points, width), jnp.bfloat16)
    outs, own_terms, back_partner, back_next, back_far = [], [], [], [], []
    for chunk, (low, high) in enumerate(spans(CHUNKS)):
        count = high - low
        chunk_width = count * PAIR
        parts = [
            (at, last - first)
            for at, (first, last) in enumerate(spans(NEXT_CHUNKS))
            if low <= first and last <= high
        ]
        next_pairs = [size for _, size in parts]
        assert sum(next_pairs) == count
        outs = chunk_call(
            functools.partial(attention_kernel, rim_width, lengths, points, low, next_pairs),
            [relative, queries, grad_out, keys, values, *from_partner]
            + [from_next[at] for at, _ in parts]
            + from_far,
            outs[:2],
            2,
            [whole] * 2
            + [jax.ShapeDtypeStruct((2, near, chunk_width), jnp.bfloat16)] * 2
            + [jax.ShapeDtypeStruct((points, chunk_width), jnp.float32)] * 2
            + [jax.ShapeDtypeStruct((2, size, chunk_width), jnp.bfloat16) for size in far_sizes],
            scratch_shapes=[
                pltpu.VMEM((2, reached, points), jnp.float32),
                pltpu.VMEM((2, 2, wide, PAIR), jnp.bfloat16),
                pltpu.VMEM((2, 2, PAIR, wide), jnp.bfloat16),
                pltpu.VMEM((2, 2, reached, points), jnp.float32),
                pltpu.VMEM((2, 2, reached, points), jnp.bfloat16),
                pltpu.VMEM((2, 2, reached, points), jnp.bfloat16),
                pltpu.VMEM((2, 2, wide, PAIR), jnp.float32),
                pltpu.VMEM((count, points, PAIR), jnp.bfloat16),
                pltpu.VMEM((count, points, PAIR), jnp.bfloat16),
                pltpu.SemaphoreType.DMA((2, count)),
            ],
            cost_estimate=pl.CostEstimate(
                flops=count * 24 * reached * points * PAIR,
                bytes_accessed=count * PAIR * (20 * points + 8 * wide),
                transcendentals=2 * count * points * reached,
            ),
            name=f"attention_{chunk}",
        )
        own_terms.append(outs[4:6])
        back_partner.append(swapped(outs[2], 0))
        back_next.append(swapped(outs[3], 1))
        back_far.append([passed_along(term, d) for term, d in zip(outs[6:], far)])

    grads = []
    for chunk, (low, high) in enumerate(spans(CHUNKS)):
        chunk_width = (high - low) * PAIR
        grads = chunk_call(
            functools.partial(sum_kernel, far_sizes, points, low, high),
            [*own_terms[chunk], back_partner[chunk], back_next[chunk], *back_far[chunk]],
            grads,
            2,
            [whole] * 2,
            scratch_shapes=[
                pltpu.VMEM((points, chunk_width), jnp.float32),
                pltpu.VMEM((2, points, chunk_width), jnp.bfloat16),
                pltpu.SemaphoreType.DMA((2,)),
            ],
            cost_estimate=pl.CostEstimate(
                flops=6 * points * chunk_width,
                bytes_accessed=20 * points * chunk_width,
                transcendentals=0,
            ),
            name=f"gradient_sums_{chunk}",
        )
    return (outs[0], outs[1], grads[0], grads[1])


def solution(mesh):
    spread = P(("members", "band"), None)
    return jax.shard_map(
        per_device,
        mesh=mesh,
        in_specs=(spread, spread, spread, spread, P("band", None)),
        out_specs=(spread, spread, spread, spread),
        check_vma=False,
    )
```

time: 60.3 us -> 56.7 us (0.940)
  Pallas kernels: 23.2 us -> 18.6 us
  waiting for transfers between devices: 23.3 us -> 19.6 us
  local copies, waits for them, and re-layouts: 0.7 us -> 3.58 us
  starting transfers between devices: 12 us -> 13.6 us
    pallas_call x4, Pallas kernels: 19.4 us -> 14.9 us  [chunk_call(): pl.pallas_call(functools.partial(kernel, len(carried)), in_specs=[vmem] *...]
    ppermute x7 -> x8, waiting for transfers between devices: 23.3 us -> 19.6 us  [swapped(): lax.ppermute(value, 'band', pairs + [(high, low) for low, high in pairs])]
    unnamed x10 -> x22, local copies, waits for them, and re-layouts: 0.7 us -> 3.58 us
    ppermute x7 -> x8, starting transfers between devices: 12 us -> 13.6 us  [swapped(): lax.ppermute(value, 'band', pairs + [(high, low) for low, high in pairs])]
  transfers between devices with their start and end apart: 7 -> 8, of which waited for: 3 -> 3; matrix products, arithmetic and copies ran while one was open for 0% -> 0% of each run, Pallas kernels for 30% -> 28%
where the time goes in v5:
time: 56.7 us; the launch traced here: 56.3 us
  waiting for transfers between devices  19.6 us (35%)
  Pallas kernels  18.6 us (33%)
  starting transfers between devices  13.6 us (24%)
  local copies, waits for them, and re-layouts  3.58 us (6%)
  between operations  0.85 us (1%)
    ppermute x8, waiting for transfers between devices, swapped(): lax.ppermute(value, 'band', pairs + [(high, low) for low, high in pairs])  19.6 us
    pallas_call x4, Pallas kernels, chunk_call(): pl.pallas_call(functools.partial(kernel, len(carried)), in_specs=[vmem] *...  14.9 us
    ppermute x8, starting transfers between devices, swapped(): lax.ppermute(value, 'band', pairs + [(high, low) for low, high in pairs])  13.6 us
    pallas_call x2, Pallas kernels, pack(): pl.pallas_call(functools.partial(pack_kernel, points, slice(low * PAIR, h...  3.74 us
    unnamed x22, local copies, waits for them, and re-layouts  3.58 us
  transfers between devices with their start and end apart: 8, of which 3 were waited for; matrix products, arithmetic and copies ran while one was open for 0% of the time, Pallas kernels for 28%

profile of v5, /device:TPU:9, one launch (start us, length us, event | category | flops | bytes accessed | tf_op | source)
XLA Modules:
  0.0 56.3 jit_solution(9423867796904191585)
XLA Ops:
  0.6 0.0 copy-start
  0.6 0.0 copy-start.2
  0.7 0.0 copy-start.4
  0.7 1.9 %pack_next_0.1 = bf16[2,208,512]{2,1,0:T(8,128)(2,1)} custom-call(bf16[256,1024]{1,0:T(8,128)(2,1)} %refs_3_.3, bf16[256,1024]{1,0:T(8,128)(2,1)} %refs_4_.3), custom_call_target="tpu_custom_call" | custom-call | bytes 851968 | tf_op jit(solution)/shard_map/pack_next_0/pallas_call | solution.py:90
  2.6 0.0 copy-done
  2.6 0.0 copy-start.1
  2.6 0.0 copy-start.3
  2.6 0.7 %collective-permute-start = (bf16[256,1024]{1,0:T(8,128)(2,1)S(1)}, bf16[256,1024]{1,0:T(8,128)(2,1)S(1)}, u32[]{:S(2)}, u32[]{:S(2)}) collective-permute-start(bf16[256,1024]{1,0:T(8,128)(2,1)S(1)} %copy-done), channel_id=1, source_target_pairs={{0,1},{2,3},{4,5},{6,7},{8,9},{10,11},{12,13},{14,15},{1,0},{3,2},... | collective-permute-start | bytes 1572872 | tf_op jit(solution)/shard_map/ppermute | solution.py:48
  3.4 0.0 copy-done.2
  3.4 0.1 collective-permute-start.1
  3.5 3.4 %collective-permute-start.3 = (bf16[2,208,512]{2,1,0:T(8,128)(2,1)}, bf16[2,208,512]{2,1,0:T(8,128)(2,1)}, u32[]{:S(2)}, u32[]{:S(2)}) collective-permute-start(bf16[2,208,512]{2,1,0:T(8,128)(2,1)} %pack_next_0.1), channel_id=1, source_target_pairs={{1,2},{3,4},{5,6},{7,8},{9,10},{11,12},{13,14},{2,1},{4,3},{6,5},{... | collective-permute-start | bytes 1277960 | tf_op jit(solution)/shard_map/ppermute | solution.py:48
  6.9 0.0 collective-permute-done.refs_5_
  6.9 0.0 collective-permute-done.1.refs_6_
  6.9 0.0 copy-start.7
  7.0 0.8 %copy-done.7 = bf16[256,1024]{1,0:T(8,128)(2,1)} copy-done((bf16[256,1024]{1,0:T(8,128)(2,1)}, bf16[256,1024]{1,0:T(8,128)(2,1)S(1)}, u32[]{:S(2)}) %copy-start.7) | copy-done | bytes 524312
  7.7 1.8 %pack_next_1.1 = bf16[2,208,512]{2,1,0:T(8,128)(2,1)} custom-call(bf16[256,1024]{1,0:T(8,128)(2,1)} %refs_3_.3, bf16[256,1024]{1,0:T(8,128)(2,1)} %refs_4_.3), custom_call_target="tpu_custom_call" | custom-call | bytes 851968 | tf_op jit(solution)/shard_map/pack_next_1/pallas_call | solution.py:90
  9.6 2.1 %collective-permute-start.2 = (bf16[2,208,512]{2,1,0:T(8,128)(2,1)}, bf16[2,208,512]{2,1,0:T(8,128)(2,1)S(1)}, u32[]{:S(2)}, u32[]{:S(2)}) collective-permute-start(bf16[2,208,512]{2,1,0:T(8,128)(2,1)} %pack_next_1.1), channel_id=1, source_target_pairs={{1,2},{3,4},{5,6},{7,8},{9,10},{11,12},{13,14},{2,1},{4,3},{6,5},{... | collective-permute-start | bytes 1277960 | tf_op jit(solution)/shard_map/ppermute | solution.py:48
  11.7 0.0 copy-start.10
  11.7 0.7 %copy-done.10 = s32[256,2]{0,1:T(2,128)S(1)} copy-done((s32[256,2]{0,1:T(2,128)S(1)}, s32[256,2]{0,1:T(2,128)}, u32[]{:S(2)}) %copy-start.10) | copy-done | bytes 2072
  12.4 10.0 %collective-permute-done.3.refs_7_ = bf16[2,208,512]{2,1,0:T(8,128)(2,1)} collective-permute-done((bf16[2,208,512]{2,1,0:T(8,128)(2,1)}, bf16[2,208,512]{2,1,0:T(8,128)(2,1)}, u32[]{:S(2)}, u32[]{:S(2)}) %collective-permute-start.3) | collective-permute-done | bytes 426016 | tf_op jit(solution)/shard_map/ppermute | solution.py:48
  22.3 0.0 copy-done.4
  22.4 0.0 copy-done.1
  22.4 0.0 copy-done.3
  22.4 0.0 copy-start.5
  22.4 1.0 %copy-done.5 = bf16[256,1024]{1,0:T(8,128)(2,1)S(1)} copy-done((bf16[256,1024]{1,0:T(8,128)(2,1)S(1)}, bf16[256,1024]{1,0:T(8,128)(2,1)}, u32[]{:S(2)}) %copy-start.5) | copy-done | bytes 524312
  23.4 0.0 copy-start.8
  23.4 1.0 %copy-done.8 = bf16[256,1024]{1,0:T(8,128)(2,1)S(1)} copy-done((bf16[256,1024]{1,0:T(8,128)(2,1)S(1)}, bf16[256,1024]{1,0:T(8,128)(2,1)}, u32[]{:S(2)}) %copy-start.8) | copy-done | bytes 524312
  24.4 0.0 copy-start.6
  24.4 0.0 copy-start.9
  24.5 6.9 %attention_0.1 = (bf16[256,1024]{1,0:T(8,128)(2,1)}, bf16[256,1024]{1,0:T(8,128)(2,1)}, bf16[2,208,512]{2,1,0:T(8,128)(2,1)S(1)}, bf16[2,208,512]{2,1,0:T(8,128)...) custom-call(s32[2,256]{1,0:T(2,128)S(1)} %subtract_bitcast_fusion.refs_0_, bf16[256,1024]{1,0:T(8,128)(2,1)S(1)} %copy-done.4, ...), custom_call_target="tpu_custom_call" | custom-call | flops 1711276032 | bytes 5373952 | tf_op jit(solution)/shard_map/attention_0/pallas_call | solution.py:327
  31.4 0.1 collective-permute-start.6
  31.4 3.5 %collective-permute-start.7 = (bf16[2,208,512]{2,1,0:T(8,128)(2,1)S(1)}, bf16[2,208,512]{2,1,0:T(8,128)(2,1)S(1)}, u32[]{:S(2)}, u32[]{:S(2)}) collective-permute-start(bf16[2,208,512]{2,1,0:T(8,128)(2,1)S(1)} %get-tuple-element.39), channel_id=1, source_target_pairs={{1,2},{3,4},{5,6},{7,8},{9,10},{11,12},{13,14},{2,1},{4,3},{6,5},{... | collective-permute-start | bytes 1277960 | tf_op jit(solution)/shard_map/ppermute | solution.py:48
  34.9 0.0 collective-permute-done.2.refs_7_
  34.9 0.0 copy-done.6
  34.9 0.0 copy-done.9
  34.9 5.8 %attention_1.1 = (bf16[256,1024]{1,0:T(8,128)(2,1)}, bf16[256,1024]{1,0:T(8,128)(2,1)}, bf16[2,208,512]{2,1,0:T(8,128)(2,1)S(1)}, bf16[2,208,512]{2,1,0:T(8,128)...) custom-call(s32[2,256]{1,0:T(2,128)S(1)} %subtract_bitcast_fusion.refs_0_, ...), custom_call_target="tpu_custom_call", output_to_operand_aliasing={{0}: (8, {}), {1}: (9, {})} | custom-call | flops 1711276032 | bytes 5373952 | tf_op jit(solution)/shard_map/attention_1/pallas_call | solution.py:327
  40.8 0.4 collective-permute-start.4
  41.2 3.2 %collective-permute-start.5 = (bf16[2,208,512]{2,1,0:T(8,128)(2,1)S(1)}, bf16[2,208,512]{2,1,0:T(8,128)(2,1)S(1)}, u32[]{:S(2)}, u32[]{:S(2)}) collective-permute-start(bf16[2,208,512]{2,1,0:T(8,128)(2,1)S(1)} %get-tuple-element.35), channel_id=1, source_target_pairs={{1,2},{3,4},{5,6},{7,8},{9,10},{11,12},{13,14},{2,1},{4,3},{6,5},{... | collective-permute-start | bytes 1277960 | tf_op jit(solution)/shard_map/ppermute | solution.py:48
  44.4 0.0 collective-permute-done.6.refs_2_
  44.5 1.0 %collective-permute-done.7.refs_3_ = bf16[2,208,512]{2,1,0:T(8,128)(2,1)S(1)} collective-permute-done((bf16[2,208,512]{2,1,0:T(8,128)(2,1)S(1)}, bf16[2,208,512]{2,1,0:T(8,128)(2,1)S(1)}, u32[]{:S(2)}, u32[]{:S(2)}) %collective-permute-start.7) | collective-permute-done | bytes 426016 | tf_op jit(solution)/shard_map/ppermute | solution.py:48
  45.4 1.1 %gradient_sums_0.1 = (bf16[256,1024]{1,0:T(8,128)(2,1)}, bf16[256,1024]{1,0:T(8,128)(2,1)}) custom-call(f32[256,512]{1,0:T(8,128)S(1)} %get-tuple-element.36.refs_0_, f32[256,512]{1,0:T(8,128)S(1)} %get-tuple-element.37.refs_1_, bf16[2,208,512]{2,1,0:T(8,128)(2,1)S(1)} %collective-permute-done.6.refs_2_, bf16[2,208,512]{2,1,0:T(8,128)(2,1)S(1)} %collective-permute-done.7.refs_3_), custom_call_target="tpu_custom_call" | custom-call | flops 786432 | bytes 2621440 | tf_op jit(solution)/shard_map/gradient_sums_0/pallas_call | solution.py:327
  46.5 0.0 collective-permute-done.4.refs_2_
  46.5 8.7 %collective-permute-done.5.refs_3_ = bf16[2,208,512]{2,1,0:T(8,128)(2,1)S(1)} collective-permute-done((bf16[2,208,512]{2,1,0:T(8,128)(2,1)S(1)}, bf16[2,208,512]{2,1,0:T(8,128)(2,1)S(1)}, u32[]{:S(2)}, u32[]{:S(2)}) %collective-permute-start.5) | collective-permute-done | bytes 426016 | tf_op jit(solution)/shard_map/ppermute | solution.py:48
  55.2 1.1 %gradient_sums_1.1 = (bf16[256,1024]{1,0:T(8,128)(2,1)}, bf16[256,1024]{1,0:T(8,128)(2,1)}) custom-call(f32[256,512]{1,0:T(8,128)S(1)} %get-tuple-element.32.refs_0_, f32[256,512]{1,0:T(8,128)S(1)} %get-tuple-element.33.refs_1_, bf16[2,208,512]{2,1,0:T(8,128)(2,1)S(1)} %collective-permute-done.4.refs_2_, ...), custom_call_target="tpu_custom_call", output_to_operand_aliasing={{0}: (4, {}), {1}: (5, {})} | custom-call | flops 786432 | bytes 2621440 | tf_op jit(solution)/shard_map/gradient_sums_1/pallas_call | solution.py:327
  (1 shorter events, 0.0 us)
Async XLA Ops:
  0.6 2.0 %copy-start = (bf16[256,1024]{1,0:T(8,128)(2,1)S(1)}, bf16[256,1024]{1,0:T(8,128)(2,1)}, u32[]{:S(2)}) copy-start(bf16[256,1024]{1,0:T(8,128)(2,1)} %refs_3_.3) | copy-start | bytes 1572868
  0.6 2.7 %copy-start.2 = (bf16[256,1024]{1,0:T(8,128)(2,1)S(1)}, bf16[256,1024]{1,0:T(8,128)(2,1)}, u32[]{:S(2)}) copy-start(bf16[256,1024]{1,0:T(8,128)(2,1)} %refs_4_.3) | copy-start | bytes 1572868
  0.7 21.7 %copy-start.4 = (bf16[256,1024]{1,0:T(8,128)(2,1)S(1)}, bf16[256,1024]{1,0:T(8,128)(2,1)}, u32[]{:S(2)}) copy-start(bf16[256,1024]{1,0:T(8,128)(2,1)} %refs_1_.6) | copy-start | bytes 1572868
  2.6 19.7 %copy-start.1 = (bf16[256,1024]{1,0:T(8,128)(2,1)S(1)}, bf16[256,1024]{1,0:T(8,128)(2,1)}, u32[]{:S(2)}) copy-start(bf16[256,1024]{1,0:T(8,128)(2,1)} %refs_3_.3) | copy-start | bytes 1572868
  2.6 19.7 %copy-start.3 = (bf16[256,1024]{1,0:T(8,128)(2,1)S(1)}, bf16[256,1024]{1,0:T(8,128)(2,1)}, u32[]{:S(2)}) copy-start(bf16[256,1024]{1,0:T(8,128)(2,1)} %refs_4_.3) | copy-start | bytes 1572868
  2.6 4.3 %collective-permute-start = (bf16[256,1024]{1,0:T(8,128)(2,1)S(1)}, bf16[256,1024]{1,0:T(8,128)(2,1)S(1)}, u32[]{:S(2)}, u32[]{:S(2)}) collective-permute-start(bf16[256,1024]{1,0:T(8,128)(2,1)S(1)} %copy-done), channel_id=1, source_target_pairs={{0,1},{2,3},{4,5},{6,7},{8,9},{10,11},{12,13},{14,15},{1,0},{3,2},... | collective-permute-start | bytes 1572872 | tf_op jit(solution)/shard_map/ppermute | solution.py:48
  3.4 3.6 %collective-permute-start.1 = (bf16[256,1024]{1,0:T(8,128)(2,1)S(1)}, bf16[256,1024]{1,0:T(8,128)(2,1)S(1)}, u32[]{:S(2)}, u32[]{:S(2)}) collective-permute-start(bf16[256,1024]{1,0:T(8,128)(2,1)S(1)} %copy-done.2), channel_id=1, source_target_pairs={{0,1},{2,3},{4,5},{6,7},{8,9},{10,11},{12,13},{14,15},{1,0},{3,2},... | collective-permute-start | bytes 1572872 | tf_op jit(solution)/shard_map/ppermute | solution.py:48
  3.5 18.9 %collective-permute-start.3 = (bf16[2,208,512]{2,1,0:T(8,128)(2,1)}, bf16[2,208,512]{2,1,0:T(8,128)(2,1)}, u32[]{:S(2)}, u32[]{:S(2)}) collective-permute-start(bf16[2,208,512]{2,1,0:T(8,128)(2,1)} %pack_next_0.1), channel_id=1, source_target_pairs={{1,2},{3,4},{5,6},{7,8},{9,10},{11,12},{13,14},{2,1},{4,3},{6,5},{... | collective-permute-start | bytes 1277960 | tf_op jit(solution)/shard_map/ppermute | solution.py:48
  6.9 0.8 %copy-start.7 = (bf16[256,1024]{1,0:T(8,128)(2,1)}, bf16[256,1024]{1,0:T(8,128)(2,1)S(1)}, u32[]{:S(2)}) copy-start(bf16[256,1024]{1,0:T(8,128)(2,1)S(1)} %collective-permute-done.1.refs_6_) | copy-start | bytes 1572868
  9.6 25.3 %collective-permute-start.2 = (bf16[2,208,512]{2,1,0:T(8,128)(2,1)}, bf16[2,208,512]{2,1,0:T(8,128)(2,1)S(1)}, u32[]{:S(2)}, u32[]{:S(2)}) collective-permute-start(bf16[2,208,512]{2,1,0:T(8,128)(2,1)} %pack_next_1.1), channel_id=1, source_target_pairs={{1,2},{3,4},{5,6},{7,8},{9,10},{11,12},{13,14},{2,1},{4,3},{6,5},{... | collective-permute-start | bytes 1277960 | tf_op jit(solution)/shard_map/ppermute | solution.py:48
  11.7 0.7 %copy-start.10 = (s32[256,2]{0,1:T(2,128)S(1)}, s32[256,2]{0,1:T(2,128)}, u32[]{:S(2)}) copy-start(s32[256,2]{0,1:T(2,128)} %param.9) | copy-start | bytes 6148
  22.4 1.0 %copy-start.5 = (bf16[256,1024]{1,0:T(8,128)(2,1)S(1)}, bf16[256,1024]{1,0:T(8,128)(2,1)}, u32[]{:S(2)}) copy-start(bf16[256,1024]{1,0:T(8,128)(2,1)} %refs_2_.3) | copy-start | bytes 1572868
  23.4 1.0 %copy-start.8 = (bf16[256,1024]{1,0:T(8,128)(2,1)S(1)}, bf16[256,1024]{1,0:T(8,128)(2,1)}, u32[]{:S(2)}) copy-start(bf16[256,1024]{1,0:T(8,128)(2,1)} %copy-done.7) | copy-start | bytes 1572868
  24.4 10.5 %copy-start.6 = (bf16[256,1024]{1,0:T(8,128)(2,1)S(1)}, bf16[256,1024]{1,0:T(8,128)(2,1)}, u32[]{:S(2)}) copy-start(bf16[256,1024]{1,0:T(8,128)(2,1)} %refs_2_.3) | copy-start | bytes 1572868
  24.4 10.5 %copy-start.9 = (bf16[256,1024]{1,0:T(8,128)(2,1)S(1)}, bf16[256,1024]{1,0:T(8,128)(2,1)}, u32[]{:S(2)}) copy-start(bf16[256,1024]{1,0:T(8,128)(2,1)} %copy-done.7) | copy-start | bytes 1572868
  31.4 13.1 %collective-permute-start.6 = (bf16[2,208,512]{2,1,0:T(8,128)(2,1)S(1)}, bf16[2,208,512]{2,1,0:T(8,128)(2,1)S(1)}, u32[]{:S(2)}, u32[]{:S(2)}) collective-permute-start(bf16[2,208,512]{2,1,0:T(8,128)(2,1)S(1)} %get-tuple-element.38), channel_id=1, source_target_pairs={{0,1},{2,3},{4,5},{6,7},{8,9},{10,11},{12,13},{14,15},{1,0},{3,2},... | collective-permute-start | bytes 1277960 | tf_op jit(solution)/shard_map/ppermute | solution.py:48
  31.4 14.0 %collective-permute-start.7 = (bf16[2,208,512]{2,1,0:T(8,128)(2,1)S(1)}, bf16[2,208,512]{2,1,0:T(8,128)(2,1)S(1)}, u32[]{:S(2)}, u32[]{:S(2)}) collective-permute-start(bf16[2,208,512]{2,1,0:T(8,128)(2,1)S(1)} %get-tuple-element.39), channel_id=1, source_target_pairs={{1,2},{3,4},{5,6},{7,8},{9,10},{11,12},{13,14},{2,1},{4,3},{6,5},{... | collective-permute-start | bytes 1277960 | tf_op jit(solution)/shard_map/ppermute | solution.py:48
  40.8 5.8 %collective-permute-start.4 = (bf16[2,208,512]{2,1,0:T(8,128)(2,1)S(1)}, bf16[2,208,512]{2,1,0:T(8,128)(2,1)S(1)}, u32[]{:S(2)}, u32[]{:S(2)}) collective-permute-start(bf16[2,208,512]{2,1,0:T(8,128)(2,1)S(1)} %get-tuple-element.34), channel_id=1, source_target_pairs={{0,1},{2,3},{4,5},{6,7},{8,9},{10,11},{12,13},{14,15},{1,0},{3,2},... | collective-permute-start | bytes 1277960 | tf_op jit(solution)/shard_map/ppermute | solution.py:48
  41.2 14.0 %collective-permute-start.5 = (bf16[2,208,512]{2,1,0:T(8,128)(2,1)S(1)}, bf16[2,208,512]{2,1,0:T(8,128)(2,1)S(1)}, u32[]{:S(2)}, u32[]{:S(2)}) collective-permute-start(bf16[2,208,512]{2,1,0:T(8,128)(2,1)S(1)} %get-tuple-element.35), channel_id=1, source_target_pairs={{1,2},{3,4},{5,6},{7,8},{9,10},{11,12},{13,14},{2,1},{4,3},{6,5},{... | collective-permute-start | bytes 1277960 | tf_op jit(solution)/shard_map/ppermute | solution.py:48

commit v6 on v5

--- a/solution.py
+++ b/solution.py
@@ -19,8 +19,7 @@
 BLOCK = 32
 OUTSIDE = -1e30
 CHUNKS = (0, 4, 8)
-NEXT_CHUNKS = (0, 4, 8)
-VMEM_BYTES = 40 * 2**20
+NEXT_CHUNKS = (0, 2, 4, 8)
 
 
 def reach_sizes(points, count):
@@ -321,7 +320,7 @@
         copy.wait()
 
 
-def chunk_call(kernel, args, carried, count, out_shape, **options):
+def chunk_call(kernel, args, carried, count, out_shape, vmem_bytes, **options):
     vmem = pl.BlockSpec(memory_space=pltpu.VMEM)
     anywhere = pl.BlockSpec(memory_space=pl.ANY)
     return pl.pallas_call(
@@ -330,7 +329,7 @@
         out_specs=[anywhere] * count + [vmem] * (len(out_shape) - count),
         out_shape=out_shape,
         input_output_aliases={len(args) + at: at for at in range(len(carried))},
-        compiler_params=pltpu.CompilerParams(vmem_limit_bytes=VMEM_BYTES),
+        compiler_params=pltpu.CompilerParams(vmem_limit_bytes=vmem_bytes),
         **options,
     )(*args, *carried)
 
@@ -387,6 +386,7 @@
             + [jax.ShapeDtypeStruct((2, near, chunk_width), jnp.bfloat16)] * 2
             + [jax.ShapeDtypeStruct((points, chunk_width), jnp.float32)] * 2
             + [jax.ShapeDtypeStruct((2, size, chunk_width), jnp.bfloat16) for size in far_sizes],
+            48 * wide * points + 12 * 2**20,
             scratch_shapes=[
                 pltpu.VMEM((2, reached, points), jnp.float32),
                 pltpu.VMEM((2, 2, wide, PAIR), jnp.bfloat16),
@@ -400,7 +400,7 @@
                 pltpu.SemaphoreType.DMA((2, count)),
             ],
             cost_estimate=pl.CostEstimate(
-                flops=count * 24 * reached * points * PAIR,
+                flops=count * 120 * reached * points * PAIR,
                 bytes_accessed=count * PAIR * (20 * points + 8 * wide),
                 transcendentals=2 * count * points * reached,
             ),
@@ -420,6 +420,7 @@
             grads,
             2,
             [whole] * 2,
+            12 * 2**20,
             scratch_shapes=[
                 pltpu.VMEM((points, chunk_width), jnp.float32),
                 pltpu.VMEM((2, points, chunk_width), jnp.bfloat16),

time: 56.7 us -> 50.1 us (0.88)
  waiting for transfers between devices: 19.6 us -> 12.1 us
  local copies, waits for them, and re-layouts: 3.58 us -> 0.04 us
  starting transfers between devices: 13.6 us -> 16.7 us
  Pallas kernels: 18.6 us -> 20 us
    ppermute x8 -> x9, waiting for transfers between devices: 19.6 us -> 12.1 us  [swapped(): lax.ppermute(value, 'band', pairs + [(high, low) for low, high in pairs])]
    unnamed x22 -> x14, local copies, waits for them, and re-layouts: 3.58 us -> 0.04 us
    ppermute x8 -> x9, starting transfers between devices: 13.6 us -> 16.7 us  [swapped(): lax.ppermute(value, 'band', pairs + [(high, low) for low, high in pairs])]
    pallas_call x2 -> x3, Pallas kernels: 3.74 us -> 5.29 us  [pack(): pl.pallas_call(functools.partial(pack_kernel, points, slice(low * PAIR, h...]
  transfers between devices with their start and end apart: 8 -> 9, of which waited for: 3 -> 5; matrix products, arithmetic and copies ran while one was open for 0% -> 0% of each run, Pallas kernels for 28% -> 35%
where the time goes in v6:
time: 50.1 us; the launch traced here: 49.7 us
  Pallas kernels  20 us (40%)
  starting transfers between devices  16.7 us (33%)
  waiting for transfers between devices  12.1 us (24%)
  between operations  0.86 us (2%)
    ppermute x9, starting transfers between devices, swapped(): lax.ppermute(value, 'band', pairs + [(high, low) for low, high in pairs])  16.7 us
    pallas_call x4, Pallas kernels, chunk_call(): pl.pallas_call(functools.partial(kernel, len(carried)), in_specs=[vmem] *...  14.7 us
    ppermute x9, waiting for transfers between devices, swapped(): lax.ppermute(value, 'band', pairs + [(high, low) for low, high in pairs])  12.1 us
    pallas_call x3, Pallas kernels, pack(): pl.pallas_call(functools.partial(pack_kernel, points, slice(low * PAIR, h...  5.29 us
  transfers between devices with their start and end apart: 9, of which 5 were waited for; matrix products, arithmetic and copies ran while one was open for 0% of the time, Pallas kernels for 35%

profile of v6, /device:TPU:9, one launch (start us, length us, event | category | flops | bytes accessed | tf_op | source)
XLA Modules:
  0.0 49.7 jit_solution(16619707815254697599)
XLA Ops:
  0.6 0.0 copy-start
  0.6 0.0 copy-start.2
  0.7 1.7 %pack_next_0.1 = bf16[2,208,256]{2,1,0:T(8,128)(2,1)} custom-call(bf16[256,1024]{1,0:T(8,128)(2,1)} %refs_3_.3, bf16[256,1024]{1,0:T(8,128)(2,1)} %refs_4_.3), custom_call_target="tpu_custom_call" | custom-call | bytes 425984 | tf_op jit(solution)/shard_map/pack_next_0/pallas_call | solution.py:89
  2.4 0.0 copy-done
  2.4 0.7 %collective-permute-start = (bf16[256,1024]{1,0:T(8,128)(2,1)S(1)}, bf16[256,1024]{1,0:T(8,128)(2,1)S(1)}, u32[]{:S(2)}, u32[]{:S(2)}) collective-permute-start(bf16[256,1024]{1,0:T(8,128)(2,1)S(1)} %copy-done), channel_id=1, source_target_pairs={{0,1},{2,3},{4,5},{6,7},{8,9},{10,11},{12,13},{14,15},{1,0},{3,2},... | collective-permute-start | bytes 1572872 | tf_op jit(solution)/shard_map/ppermute | solution.py:47
  3.2 0.0 copy-done.2
  3.2 0.1 collective-permute-start.1
  3.2 3.4 %collective-permute-start.2 = (bf16[2,208,256]{2,1,0:T(8,128)(2,1)}, bf16[2,208,256]{2,1,0:T(8,128)(2,1)S(1)}, u32[]{:S(2)}, u32[]{:S(2)}) collective-permute-start(bf16[2,208,256]{2,1,0:T(8,128)(2,1)} %pack_next_0.1), channel_id=1, source_target_pairs={{1,2},{3,4},{5,6},{7,8},{9,10},{11,12},{13,14},{2,1},{4,3},{6,5},{... | collective-permute-start | bytes 638984 | tf_op jit(solution)/shard_map/ppermute | solution.py:47
  6.7 0.0 copy-start.6
  6.7 0.0 collective-permute-done.refs_5_
  6.7 0.0 collective-permute-done.1.refs_6_
  6.7 0.0 copy-start.4
  6.7 0.0 copy-start.5
  6.8 1.7 %pack_next_1.1 = bf16[2,208,256]{2,1,0:T(8,128)(2,1)} custom-call(bf16[256,1024]{1,0:T(8,128)(2,1)} %refs_3_.3, bf16[256,1024]{1,0:T(8,128)(2,1)} %refs_4_.3), custom_call_target="tpu_custom_call" | custom-call | bytes 425984 | tf_op jit(solution)/shard_map/pack_next_1/pallas_call | solution.py:89
  8.5 2.1 %collective-permute-start.4 = (bf16[2,208,256]{2,1,0:T(8,128)(2,1)}, bf16[2,208,256]{2,1,0:T(8,128)(2,1)}, u32[]{:S(2)}, u32[]{:S(2)}) collective-permute-start(bf16[2,208,256]{2,1,0:T(8,128)(2,1)} %pack_next_1.1), channel_id=1, source_target_pairs={{1,2},{3,4},{5,6},{7,8},{9,10},{11,12},{13,14},{2,1},{4,3},{6,5},{... | collective-permute-start | bytes 638984 | tf_op jit(solution)/shard_map/ppermute | solution.py:47
  10.6 0.0 copy-done.6
  10.7 0.0 copy-start.1
  10.7 0.0 copy-start.3
  10.7 2.2 %collective-permute-done.2.refs_7_ = bf16[2,208,256]{2,1,0:T(8,128)(2,1)S(1)} collective-permute-done((bf16[2,208,256]{2,1,0:T(8,128)(2,1)}, bf16[2,208,256]{2,1,0:T(8,128)(2,1)S(1)}, u32[]{:S(2)}, u32[]{:S(2)}) %collective-permute-start.2) | collective-permute-done | bytes 213024 | tf_op jit(solution)/shard_map/ppermute | solution.py:47
  12.9 1.8 %pack_next_2.1 = bf16[2,208,512]{2,1,0:T(8,128)(2,1)} custom-call(bf16[256,1024]{1,0:T(8,128)(2,1)} %refs_3_.3, bf16[256,1024]{1,0:T(8,128)(2,1)} %refs_4_.3), custom_call_target="tpu_custom_call" | custom-call | bytes 851968 | tf_op jit(solution)/shard_map/pack_next_2/pallas_call | solution.py:89
  14.7 3.5 %collective-permute-start.3 = (bf16[2,208,512]{2,1,0:T(8,128)(2,1)}, bf16[2,208,512]{2,1,0:T(8,128)(2,1)S(1)}, u32[]{:S(2)}, u32[]{:S(2)}) collective-permute-start(bf16[2,208,512]{2,1,0:T(8,128)(2,1)} %pack_next_2.1), channel_id=1, source_target_pairs={{1,2},{3,4},{5,6},{7,8},{9,10},{11,12},{13,14},{2,1},{4,3},{6,5},{... | collective-permute-start | bytes 1277960 | tf_op jit(solution)/shard_map/ppermute | solution.py:47
  18.2 0.1 collective-permute-done.4.refs_8_
  18.3 0.0 copy-done.4
  18.3 0.0 copy-done.5
  18.3 0.0 copy-done.1
  18.3 0.0 copy-done.3
  18.3 6.8 %attention_0.1 = (bf16[256,1024]{1,0:T(8,128)(2,1)}, bf16[256,1024]{1,0:T(8,128)(2,1)}, bf16[2,208,512]{2,1,0:T(8,128)(2,1)S(1)}, bf16[2,208,512]{2,1,0:T(8,128)...) custom-call(s32[2,256]{1,0:T(2,128)S(1)} %subtract_bitcast_fusion.refs_0_, bf16[256,1024]{1,0:T(8,128)(2,1)S(1)} %copy-done.4, ...), custom_call_target="tpu_custom_call" | custom-call | flops 8556380160 | bytes 5373952 | tf_op jit(solution)/shard_map/attention_0/pallas_call | solution.py:326
  25.1 0.1 collective-permute-start.7
  25.1 2.7 %collective-permute-start.8 = (bf16[2,208,512]{2,1,0:T(8,128)(2,1)S(1)}, bf16[2,208,512]{2,1,0:T(8,128)(2,1)S(1)}, u32[]{:S(2)}, u32[]{:S(2)}) collective-permute-start(bf16[2,208,512]{2,1,0:T(8,128)(2,1)S(1)} %get-tuple-element.43), channel_id=1, source_target_pairs={{1,2},{3,4},{5,6},{7,8},{9,10},{11,12},{13,14},{2,1},{4,3},{6,5},{... | collective-permute-start | bytes 1277960 | tf_op jit(solution)/shard_map/ppermute | solution.py:47
  27.9 0.5 collective-permute-done.3.refs_7_
  28.4 5.8 %attention_1.1 = (bf16[256,1024]{1,0:T(8,128)(2,1)}, bf16[256,1024]{1,0:T(8,128)(2,1)}, bf16[2,208,512]{2,1,0:T(8,128)(2,1)S(1)}, bf16[2,208,512]{2,1,0:T(8,128)...) custom-call(s32[2,256]{1,0:T(2,128)S(1)} %subtract_bitcast_fusion.refs_0_, ...), custom_call_target="tpu_custom_call", output_to_operand_aliasing={{0}: (8, {}), {1}: (9, {})} | custom-call | flops 8556380160 | bytes 5373952 | tf_op jit(solution)/shard_map/attention_1/pallas_call | solution.py:326
  34.2 0.1 collective-permute-start.5
  34.3 4.0 %collective-permute-start.6 = (bf16[2,208,512]{2,1,0:T(8,128)(2,1)S(1)}, bf16[2,208,512]{2,1,0:T(8,128)(2,1)S(1)}, u32[]{:S(2)}, u32[]{:S(2)}) collective-permute-start(bf16[2,208,512]{2,1,0:T(8,128)(2,1)S(1)} %get-tuple-element.39), channel_id=1, source_target_pairs={{1,2},{3,4},{5,6},{7,8},{9,10},{11,12},{13,14},{2,1},{4,3},{6,5},{... | collective-permute-start | bytes 1277960 | tf_op jit(solution)/shard_map/ppermute | solution.py:47
  38.3 0.0 collective-permute-done.7.refs_2_
  38.3 0.9 %collective-permute-done.8.refs_3_ = bf16[2,208,512]{2,1,0:T(8,128)(2,1)S(1)} collective-permute-done((bf16[2,208,512]{2,1,0:T(8,128)(2,1)S(1)}, bf16[2,208,512]{2,1,0:T(8,128)(2,1)S(1)}, u32[]{:S(2)}, u32[]{:S(2)}) %collective-permute-start.8) | collective-permute-done | bytes 426016 | tf_op jit(solution)/shard_map/ppermute | solution.py:47
  39.1 1.1 %gradient_sums_0.1 = (bf16[256,1024]{1,0:T(8,128)(2,1)}, bf16[256,1024]{1,0:T(8,128)(2,1)}) custom-call(f32[256,512]{1,0:T(8,128)S(1)} %get-tuple-element.40.refs_0_, f32[256,512]{1,0:T(8,128)S(1)} %get-tuple-element.41.refs_1_, bf16[2,208,512]{2,1,0:T(8,128)(2,1)S(1)} %collective-permute-done.7.refs_2_, bf16[2,208,512]{2,1,0:T(8,128)(2,1)S(1)} %collective-permute-done.8.refs_3_), custom_call_target="tpu_custom_call" | custom-call | flops 786432 | bytes 2621440 | tf_op jit(solution)/shard_map/gradient_sums_0/pallas_call | solution.py:326
  40.2 0.0 collective-permute-done.5.refs_2_
  40.2 8.4 %collective-permute-done.6.refs_3_ = bf16[2,208,512]{2,1,0:T(8,128)(2,1)S(1)} collective-permute-done((bf16[2,208,512]{2,1,0:T(8,128)(2,1)S(1)}, bf16[2,208,512]{2,1,0:T(8,128)(2,1)S(1)}, u32[]{:S(2)}, u32[]{:S(2)}) %collective-permute-start.6) | collective-permute-done | bytes 426016 | tf_op jit(solution)/shard_map/ppermute | solution.py:47
  48.6 1.1 %gradient_sums_1.1 = (bf16[256,1024]{1,0:T(8,128)(2,1)}, bf16[256,1024]{1,0:T(8,128)(2,1)}) custom-call(f32[256,512]{1,0:T(8,128)S(1)} %get-tuple-element.36.refs_0_, f32[256,512]{1,0:T(8,128)S(1)} %get-tuple-element.37.refs_1_, bf16[2,208,512]{2,1,0:T(8,128)(2,1)S(1)} %collective-permute-done.5.refs_2_, ...), custom_call_target="tpu_custom_call", output_to_operand_aliasing={{0}: (4, {}), {1}: (5, {})} | custom-call | flops 786432 | bytes 2621440 | tf_op jit(solution)/shard_map/gradient_sums_1/pallas_call | solution.py:326
  (1 shorter events, 0.0 us)
Async XLA Ops:
  0.6 1.8 %copy-start = (bf16[256,1024]{1,0:T(8,128)(2,1)S(1)}, bf16[256,1024]{1,0:T(8,128)(2,1)}, u32[]{:S(2)}) copy-start(bf16[256,1024]{1,0:T(8,128)(2,1)} %refs_3_.3) | copy-start | bytes 1572868
  0.6 2.5 %copy-start.2 = (bf16[256,1024]{1,0:T(8,128)(2,1)S(1)}, bf16[256,1024]{1,0:T(8,128)(2,1)}, u32[]{:S(2)}) copy-start(bf16[256,1024]{1,0:T(8,128)(2,1)} %refs_4_.3) | copy-start | bytes 1572868
  2.4 4.3 %collective-permute-start = (bf16[256,1024]{1,0:T(8,128)(2,1)S(1)}, bf16[256,1024]{1,0:T(8,128)(2,1)S(1)}, u32[]{:S(2)}, u32[]{:S(2)}) collective-permute-start(bf16[256,1024]{1,0:T(8,128)(2,1)S(1)} %copy-done), channel_id=1, source_target_pairs={{0,1},{2,3},{4,5},{6,7},{8,9},{10,11},{12,13},{14,15},{1,0},{3,2},... | collective-permute-start | bytes 1572872 | tf_op jit(solution)/shard_map/ppermute | solution.py:47
  3.2 3.6 %collective-permute-start.1 = (bf16[256,1024]{1,0:T(8,128)(2,1)S(1)}, bf16[256,1024]{1,0:T(8,128)(2,1)S(1)}, u32[]{:S(2)}, u32[]{:S(2)}) collective-permute-start(bf16[256,1024]{1,0:T(8,128)(2,1)S(1)} %copy-done.2), channel_id=1, source_target_pairs={{0,1},{2,3},{4,5},{6,7},{8,9},{10,11},{12,13},{14,15},{1,0},{3,2},... | collective-permute-start | bytes 1572872 | tf_op jit(solution)/shard_map/ppermute | solution.py:47
  3.2 9.6 %collective-permute-start.2 = (bf16[2,208,256]{2,1,0:T(8,128)(2,1)}, bf16[2,208,256]{2,1,0:T(8,128)(2,1)S(1)}, u32[]{:S(2)}, u32[]{:S(2)}) collective-permute-start(bf16[2,208,256]{2,1,0:T(8,128)(2,1)} %pack_next_0.1), channel_id=1, source_target_pairs={{1,2},{3,4},{5,6},{7,8},{9,10},{11,12},{13,14},{2,1},{4,3},{6,5},{... | collective-permute-start | bytes 638984 | tf_op jit(solution)/shard_map/ppermute | solution.py:47
  6.7 3.9 %copy-start.6 = (s32[256,2]{0,1:T(2,128)S(1)}, s32[256,2]{0,1:T(2,128)}, u32[]{:S(2)}) copy-start(s32[256,2]{0,1:T(2,128)} %param.9) | copy-start | bytes 6148
  6.7 11.5 %copy-start.4 = (bf16[256,1024]{1,0:T(8,128)(2,1)S(1)}, bf16[256,1024]{1,0:T(8,128)(2,1)}, u32[]{:S(2)}) copy-start(bf16[256,1024]{1,0:T(8,128)(2,1)} %refs_1_.7) | copy-start | bytes 1572868
  6.7 11.5 %copy-start.5 = (bf16[256,1024]{1,0:T(8,128)(2,1)S(1)}, bf16[256,1024]{1,0:T(8,128)(2,1)}, u32[]{:S(2)}) copy-start(bf16[256,1024]{1,0:T(8,128)(2,1)} %refs_2_.3) | copy-start | bytes 1572868
  8.5 9.8 %collective-permute-start.4 = (bf16[2,208,256]{2,1,0:T(8,128)(2,1)}, bf16[2,208,256]{2,1,0:T(8,128)(2,1)}, u32[]{:S(2)}, u32[]{:S(2)}) collective-permute-start(bf16[2,208,256]{2,1,0:T(8,128)(2,1)} %pack_next_1.1), channel_id=1, source_target_pairs={{1,2},{3,4},{5,6},{7,8},{9,10},{11,12},{13,14},{2,1},{4,3},{6,5},{... | collective-permute-start | bytes 638984 | tf_op jit(solution)/shard_map/ppermute | solution.py:47
  10.7 7.6 %copy-start.1 = (bf16[256,1024]{1,0:T(8,128)(2,1)S(1)}, bf16[256,1024]{1,0:T(8,128)(2,1)}, u32[]{:S(2)}) copy-start(bf16[256,1024]{1,0:T(8,128)(2,1)} %refs_3_.3) | copy-start | bytes 1572868
  10.7 7.6 %copy-start.3 = (bf16[256,1024]{1,0:T(8,128)(2,1)S(1)}, bf16[256,1024]{1,0:T(8,128)(2,1)}, u32[]{:S(2)}) copy-start(bf16[256,1024]{1,0:T(8,128)(2,1)} %refs_4_.3) | copy-start | bytes 1572868
  14.7 13.7 %collective-permute-start.3 = (bf16[2,208,512]{2,1,0:T(8,128)(2,1)}, bf16[2,208,512]{2,1,0:T(8,128)(2,1)S(1)}, u32[]{:S(2)}, u32[]{:S(2)}) collective-permute-start(bf16[2,208,512]{2,1,0:T(8,128)(2,1)} %pack_next_2.1), channel_id=1, source_target_pairs={{1,2},{3,4},{5,6},{7,8},{9,10},{11,12},{13,14},{2,1},{4,3},{6,5},{... | collective-permute-start | bytes 1277960 | tf_op jit(solution)/shard_map/ppermute | solution.py:47
  25.1 13.2 %collective-permute-start.7 = (bf16[2,208,512]{2,1,0:T(8,128)(2,1)S(1)}, bf16[2,208,512]{2,1,0:T(8,128)(2,1)S(1)}, u32[]{:S(2)}, u32[]{:S(2)}) collective-permute-start(bf16[2,208,512]{2,1,0:T(8,128)(2,1)S(1)} %get-tuple-element.42), channel_id=1, source_target_pairs={{0,1},{2,3},{4,5},{6,7},{8,9},{10,11},{12,13},{14,15},{1,0},{3,2},... | collective-permute-start | bytes 1277960 | tf_op jit(solution)/shard_map/ppermute | solution.py:47
  25.1 14.0 %collective-permute-start.8 = (bf16[2,208,512]{2,1,0:T(8,128)(2,1)S(1)}, bf16[2,208,512]{2,1,0:T(8,128)(2,1)S(1)}, u32[]{:S(2)}, u32[]{:S(2)}) collective-permute-start(bf16[2,208,512]{2,1,0:T(8,128)(2,1)S(1)} %get-tuple-element.43), channel_id=1, source_target_pairs={{1,2},{3,4},{5,6},{7,8},{9,10},{11,12},{13,14},{2,1},{4,3},{6,5},{... | collective-permute-start | bytes 1277960 | tf_op jit(solution)/shard_map/ppermute | solution.py:47
  34.2 6.1 %collective-permute-start.5 = (bf16[2,208,512]{2,1,0:T(8,128)(2,1)S(1)}, bf16[2,208,512]{2,1,0:T(8,128)(2,1)S(1)}, u32[]{:S(2)}, u32[]{:S(2)}) collective-permute-start(bf16[2,208,512]{2,1,0:T(8,128)(2,1)S(1)} %get-tuple-element.38), channel_id=1, source_target_pairs={{0,1},{2,3},{4,5},{6,7},{8,9},{10,11},{12,13},{14,15},{1,0},{3,2},... | collective-permute-start | bytes 1277960 | tf_op jit(solution)/shard_map/ppermute | solution.py:47
  34.3 14.4 %collective-permute-start.6 = (bf16[2,208,512]{2,1,0:T(8,128)(2,1)S(1)}, bf16[2,208,512]{2,1,0:T(8,128)(2,1)S(1)}, u32[]{:S(2)}, u32[]{:S(2)}) collective-permute-start(bf16[2,208,512]{2,1,0:T(8,128)(2,1)S(1)} %get-tuple-element.39), channel_id=1, source_target_pairs={{1,2},{3,4},{5,6},{7,8},{9,10},{11,12},{13,14},{2,1},{4,3},{6,5},{... | collective-permute-start | bytes 1277960 | tf_op jit(solution)/shard_map/ppermute | solution.py:47

commit v7 on v6

--- a/solution.py
+++ b/solution.py
@@ -27,7 +27,7 @@
     root_bound = min(((area_rows + 2 * 4**power) // (3 * 2**power) for power in range(3, 9)))
     grow_rows = root_bound - ROWMIN // STEP - 6
     row_longest = ROWMIN + STEP * (grow_rows - 1)
-    rim_width = (2 * row_longest + 15) // 16 * 16
+    rim_width = 2 * row_longest
     return (rim_width, (rim_width + points - 1) // points)
 
 
@@ -67,42 +67,25 @@
     return lax.axis_index("band") % 2 == 0
 
 
-def pack_kernel(points, columns, *refs):
-    sources, out_ref, sems = refs[:-2], refs[-2], refs[-1]
-    rows = out_ref.shape[1]
-    start = pl.multiple_of(jnp.where(is_even(), 0, points - rows), 16)
-    copies = [
-        pltpu.make_async_copy(
-            source.at[pl.ds(start, rows), columns], out_ref.at[at], sems.at[at]
-        )
-        for at, source in enumerate(sources)
+def pack(sources, rows, low, high):
+    points = sources[0].shape[0]
+    columns = slice(low * PAIR, high * PAIR)
+    parts = [
+        jnp.where(is_even(), field[:rows, columns], field[points - rows :, columns])
+        for field in sources
     ]
-    for copy in copies:
-        copy.start()
-    for copy in copies:
-        copy.wait()
-
-
-def pack(sources, rows, low, high, name):
-    points = sources[0].shape[0]
-    width = (high - low) * PAIR
-    return pl.pallas_call(
-        functools.partial(pack_kernel, points, slice(low * PAIR, high * PAIR)),
-        in_specs=[pl.BlockSpec(memory_space=pl.ANY)] * len(sources),
-        out_specs=pl.BlockSpec(memory_space=pltpu.VMEM),
-        out_shape=jax.ShapeDtypeStruct((len(sources), rows, width), jnp.bfloat16),
-        scratch_shapes=[pltpu.SemaphoreType.DMA((len(sources),))],
-        cost_estimate=pl.CostEstimate(
-            flops=0, bytes_accessed=4 * len(sources) * rows * width, transcendentals=0
-        ),
-        name=name,
-    )(*sources)
-
-
-def attention_kernel(rim, lengths, points, low_pair, next_pairs, carried, *refs):
+    return jnp.stack(parts)
+
+
+def padded(rows):
+    return (rows + 15) // 16 * 16
+
+
+def attention_kernel(rim_width, lengths, points, low_pair, next_pairs, carried, *refs):
     far = len(lengths) // 2 - 1
     near = lengths[far]
     half = points // 2
+    rim = padded(rim_width)
     reached = half + 2 * rim
     wide = points + 2 * rim
     pairs = sum(next_pairs)
@@ -125,8 +108,15 @@
         upper = jnp.concatenate([win_ref[1:2, own]] * 2, axis=1)
         for block in blocks:
             keys = lax.broadcasted_iota(jnp.int32, (BLOCK, points), 0) + (part * half - rim + block.start)
+            if rim > rim_width:
+                below = jnp.where(keys < rim_width - rim, keys + (rim - rim_width), -wide)
+                keys = jnp.where(keys < 0, below, jnp.where(keys < points + rim_width, keys, 2 * wide))
             inside = (keys >= lower) & (keys < upper)
             bias_ref[part, block, :] = jnp.where(inside, 0.0, OUTSIDE)
+
+    if rim > rim_width:
+        for gap in (slice(rim - 16, rim), slice(wide - 16, wide)):
+            keys_ref[:, :, gap, :] = jnp.zeros((2, 2, 16, PAIR), jnp.bfloat16)
 
     where_next = [
         (chunk, at) for chunk, count in enumerate(next_pairs) for at in range(count)
@@ -251,7 +241,7 @@
         for slot, own_ref in enumerate([dk_ref, dv_ref]):
             sums = sums_ref.at[pair % 2, slot]
             own_ref[:, columns] = sums[rim : rim + points, :]
-            near_low = sums[rim - near : rim, :].astype(jnp.bfloat16)
+            near_low = sums[rim_width - near : rim_width, :].astype(jnp.bfloat16)
             near_high = sums[rim + points : rim + points + near, :].astype(jnp.bfloat16)
             to_partner_ref[slot, :, columns] = jnp.where(even, near_high, near_low)
             to_next_ref[slot, :, columns] = jnp.where(even, near_low, near_high)
@@ -299,13 +289,13 @@
     outs = refs[4 + 2 * far + carried :]
     total, low_ref, sems = outs[-3:]
     near = partner_ref.shape[1]
-    first = pl.multiple_of(jnp.where(is_even(), points - near, 0), 16)
+    first = pl.multiple_of(jnp.where(is_even(), points - near, 0), 8)
     starts = (first, points - near - first)
     copies = []
     for slot in range(2):
         total[...] = own_refs[slot][...]
         for at, ref in enumerate((partner_ref, next_ref)):
-            rows = pl.ds(pl.multiple_of(starts[at], 16), near)
+            rows = pl.ds(pl.multiple_of(starts[at], 8), near)
             total[rows, :] += ref[slot].astype(jnp.float32)
         for at, (ref, length) in enumerate(zip(far_refs, far_lengths)):
             rows = slice(points - length, points) if at < far else slice(0, length)
@@ -343,21 +333,23 @@
     far_sizes = [min(points, rim_width - (abs(d) - 1) * points) for d in far]
     lows = len(far) // 2
     lengths = far_sizes[:lows] + [near, near] + far_sizes[lows:]
-    wide = points + 2 * rim_width
-    reached = points // 2 + 2 * rim_width
+    wide = points + 2 * padded(rim_width)
+    reached = points // 2 + 2 * padded(rim_width)
     relative = (windows - band * points).T
 
     to_next, from_next, from_partner = [], [], []
     ready = (keys, values)
     for chunk, (low, high) in enumerate(spans(NEXT_CHUNKS)):
-        to_next.append(pack(ready, near, low, high, f"pack_next_{chunk}"))
-        from_next.append(swapped(to_next[chunk], 1))
+        piece = pack(ready, near, low, high)
+        to_next.append(piece)
+        ready = lax.optimization_barrier((*ready, piece))[:2]
+        if chunk > 1:
+            piece = lax.optimization_barrier((piece, from_next[chunk - 2]))[0]
+        from_next.append(swapped(piece, 1))
         if chunk == 0:
-            ready = lax.optimization_barrier((keys, values, to_next[0]))[:2]
             from_partner = [swapped(field, 0) for field in ready]
-            ready = lax.optimization_barrier((keys, values, *from_partner))[:2]
-        else:
-            ready = lax.optimization_barrier((*ready, to_next[chunk], from_next[chunk - 1]))[:2]
+        elif chunk == 1:
+            ready = lax.optimization_barrier((*ready, *from_partner))[:2]
     from_far = []
     for d, size in zip(far, far_sizes):
         part = slice(points - size, points) if d < 0 else slice(0, size)

time: 50.1 us -> 47.4 us (0.946)
  Pallas kernels: 20 us -> 13.9 us
  other arithmetic: 0.01 us -> 2.19 us
  starting transfers between devices: 16.7 us -> 18.2 us
    pallas_call x3 -> x0, Pallas kernels: 5.29 us -> none  [pack(): pl.pallas_call(functools.partial(pack_kernel, points, slice(low * PAIR, h...]
    another operation x0 -> x8, other arithmetic: none -> 2.19 us  [pack(): return jnp.stack(parts)]
    ppermute x9, starting transfers between devices: 16.7 us -> 18.2 us  [swapped(): lax.ppermute(value, 'band', pairs + [(high, low) for low, high in pairs])]
    pallas_call x4, Pallas kernels: 14.7 us -> 13.9 us  [chunk_call(): pl.pallas_call(functools.partial(kernel, len(carried)), in_specs=[vmem] *...]
  transfers between devices with their start and end apart: 9 -> 9, of which waited for: 5 -> 4; matrix products, arithmetic and copies ran while one was open for 0% -> 0% of each run, Pallas kernels for 35% -> 27%
where the time goes in v7:
time: 47.4 us; the launch traced here: 47.1 us
  starting transfers between devices  18.2 us (38%)
  Pallas kernels  13.9 us (29%)
  waiting for transfers between devices  11.9 us (25%)
  other arithmetic  2.19 us (5%)
  between operations  0.89 us (2%)
    ppermute x9, starting transfers between devices, swapped(): lax.ppermute(value, 'band', pairs + [(high, low) for low, high in pairs])  18.2 us
    pallas_call x4, Pallas kernels, chunk_call(): pl.pallas_call(functools.partial(kernel, len(carried)), in_specs=[vmem] *...  13.9 us
    ppermute x9, waiting for transfers between devices, swapped(): lax.ppermute(value, 'band', pairs + [(high, low) for low, high in pairs])  11.9 us
    another operation x8, other arithmetic, pack(): return jnp.stack(parts)  2.19 us
  transfers between devices with their start and end apart: 9, of which 4 were waited for; matrix products, arithmetic and copies ran while one was open for 0% of the time, Pallas kernels for 27%

profile of v7, /device:TPU:9, one launch (start us, length us, event | category | flops | bytes accessed | tf_op | source)
XLA Modules:
  0.0 47.1 jit_solution(5112177762900578294)
XLA Ops:
  0.6 0.0 copy-start
  0.6 0.0 copy-start.1
  0.7 1.0 %select_bitcast_fusion.4 = bf16[1,200,256]{2,1,0:T(8,128)(2,1)S(1)} fusion(bf16[256,1024]{1,0:T(8,128)(2,1)} %refs_4_.3, pred[]{:T(512)S(6)} %eq.15), kind=kLoop, calls=%fused_computation.7 | loop fusion | flops 51200 | bytes 307201 | tf_op jit(solution)/shard_map/stack | solution.py:77
  1.7 1.0 %select_bitcast_fusion.5 = bf16[1,200,256]{2,1,0:T(8,128)(2,1)S(1)} fusion(bf16[256,1024]{1,0:T(8,128)(2,1)} %refs_3_.3, pred[]{:T(512)S(6)} %eq.15), kind=kLoop, calls=%fused_computation.8 | loop fusion | flops 51200 | bytes 307201 | tf_op jit(solution)/shard_map/stack | solution.py:77
  2.7 3.7 %collective-permute-start.2 = (bf16[2,200,256]{2,1,0:T(8,128)(2,1)S(1)}, bf16[2,200,256]{2,1,0:T(8,128)(2,1)S(1)}, u32[]{:S(2)}, u32[]{:S(2)}) collective-permute-start(bf16[2,200,256]{2,1,0:T(8,128)(2,1)S(1)} %pad_maximum_fusion.1), channel_id=1, source_target_pairs={{1,2},{3,4},{5,6},{7,8},{9,10},{11,12},{13,14},{2,1},{4,3},{6,5},{... | collective-permute-start | bytes 614408 | tf_op jit(solution)/shard_map/ppermute | solution.py:47
  6.4 0.0 copy-done
  6.5 0.1 collective-permute-start
  6.5 0.0 copy-done.1
  6.5 0.5 %collective-permute-start.1 = (bf16[256,1024]{1,0:T(8,128)(2,1)S(1)}, bf16[256,1024]{1,0:T(8,128)(2,1)S(1)}, u32[]{:S(2)}, u32[]{:S(2)}) collective-permute-start(bf16[256,1024]{1,0:T(8,128)(2,1)S(1)} %copy-done.1), channel_id=1, source_target_pairs={{0,1},{2,3},{4,5},{6,7},{8,9},{10,11},{12,13},{14,15},{1,0},{3,2},... | collective-permute-start | bytes 1572872 | tf_op jit(solution)/shard_map/ppermute | solution.py:47
  7.1 0.0 copy-start.4
  7.1 3.1 %collective-permute-start.4 = (bf16[2,200,256]{2,1,0:T(8,128)(2,1)S(1)}, bf16[2,200,256]{2,1,0:T(8,128)(2,1)S(1)}, u32[]{:S(2)}, u32[]{:S(2)}) collective-permute-start(bf16[2,200,256]{2,1,0:T(8,128)(2,1)S(1)} %pad_maximum_fusion.2), channel_id=1, source_target_pairs={{1,2},{3,4},{5,6},{7,8},{9,10},{11,12},{13,14},{2,1},{4,3},{6,5},{... | collective-permute-start | bytes 614408 | tf_op jit(solution)/shard_map/ppermute | solution.py:47
  10.3 0.0 copy-done.4
  10.3 0.0 collective-permute-done.refs_5_
  10.3 0.0 collective-permute-done.1.refs_6_
  10.3 0.0 copy-start.3
  10.4 0.0 copy-start.2
  10.4 1.6 %collective-permute-done.2.refs_7_ = bf16[2,200,256]{2,1,0:T(8,128)(2,1)S(1)} collective-permute-done((bf16[2,200,256]{2,1,0:T(8,128)(2,1)S(1)}, bf16[2,200,256]{2,1,0:T(8,128)(2,1)S(1)}, u32[]{:S(2)}, u32[]{:S(2)}) %collective-permute-start.2) | collective-permute-done | bytes 204832 | tf_op jit(solution)/shard_map/ppermute | solution.py:47
  12.1 3.6 %collective-permute-start.3 = (bf16[2,200,512]{2,1,0:T(8,128)(2,1)S(1)}, bf16[2,200,512]{2,1,0:T(8,128)(2,1)S(1)}, u32[]{:S(2)}, u32[]{:S(2)}) collective-permute-start(bf16[2,200,512]{2,1,0:T(8,128)(2,1)S(1)} %pad_maximum_fusion), channel_id=1, source_target_pairs={{1,2},{3,4},{5,6},{7,8},{9,10},{11,12},{13,14},{2,1},{4,3},{6,5},{... | collective-permute-start | bytes 1228808 | tf_op jit(solution)/shard_map/ppermute | solution.py:47
  15.7 0.8 %collective-permute-done.4.refs_8_ = bf16[2,200,256]{2,1,0:T(8,128)(2,1)S(1)} collective-permute-done((bf16[2,200,256]{2,1,0:T(8,128)(2,1)S(1)}, bf16[2,200,256]{2,1,0:T(8,128)(2,1)S(1)}, u32[]{:S(2)}, u32[]{:S(2)}) %collective-permute-start.4) | collective-permute-done | bytes 204832 | tf_op jit(solution)/shard_map/ppermute | solution.py:47
  16.5 0.0 copy-done.3
  16.5 0.0 copy-done.2
  16.5 5.9 %attention_0.1 = (bf16[256,1024]{1,0:T(8,128)(2,1)}, bf16[256,1024]{1,0:T(8,128)(2,1)}, bf16[2,200,512]{2,1,0:T(8,128)(2,1)S(1)}, bf16[2,200,512]{2,1,0:T(8,128)...) custom-call(s32[2,256]{1,0:T(2,128)S(1)} %subtract_bitcast_fusion.refs_0_, bf16[256,1024]{1,0:T(8,128)(2,1)S(1)} %copy-done.2, ...), custom_call_target="tpu_custom_call" | custom-call | flops 8556380160 | bytes 5373952 | tf_op jit(solution)/shard_map/attention_0/pallas_call | solution.py:316
  22.3 0.1 collective-permute-start.7
  22.4 3.6 %collective-permute-start.8 = (bf16[2,200,512]{2,1,0:T(8,128)(2,1)S(1)}, bf16[2,200,512]{2,1,0:T(8,128)(2,1)S(1)}, u32[]{:S(2)}, u32[]{:S(2)}) collective-permute-start(bf16[2,200,512]{2,1,0:T(8,128)(2,1)S(1)} %get-tuple-element.45), channel_id=1, source_target_pairs={{1,2},{3,4},{5,6},{7,8},{9,10},{11,12},{13,14},{2,1},{4,3},{6,5},{... | collective-permute-start | bytes 1228808 | tf_op jit(solution)/shard_map/ppermute | solution.py:47
  26.1 0.0 collective-permute-done.3.refs_7_
  26.1 5.9 %attention_1.1 = (bf16[256,1024]{1,0:T(8,128)(2,1)}, bf16[256,1024]{1,0:T(8,128)(2,1)}, bf16[2,200,512]{2,1,0:T(8,128)(2,1)S(1)}, bf16[2,200,512]{2,1,0:T(8,128)...) custom-call(s32[2,256]{1,0:T(2,128)S(1)} %subtract_bitcast_fusion.refs_0_, ...), custom_call_target="tpu_custom_call", output_to_operand_aliasing={{0}: (8, {}), {1}: (9, {})} | custom-call | flops 8556380160 | bytes 5373952 | tf_op jit(solution)/shard_map/attention_1/pallas_call | solution.py:316
  31.9 0.4 collective-permute-start.5
  32.4 3.0 %collective-permute-start.6 = (bf16[2,200,512]{2,1,0:T(8,128)(2,1)S(1)}, bf16[2,200,512]{2,1,0:T(8,128)(2,1)S(1)}, u32[]{:S(2)}, u32[]{:S(2)}) collective-permute-start(bf16[2,200,512]{2,1,0:T(8,128)(2,1)S(1)} %get-tuple-element.41), channel_id=1, source_target_pairs={{1,2},{3,4},{5,6},{7,8},{9,10},{11,12},{13,14},{2,1},{4,3},{6,5},{... | collective-permute-start | bytes 1228808 | tf_op jit(solution)/shard_map/ppermute | solution.py:47
  35.4 0.0 collective-permute-done.7.refs_2_
  35.4 0.6 %collective-permute-done.8.refs_3_ = bf16[2,200,512]{2,1,0:T(8,128)(2,1)S(1)} collective-permute-done((bf16[2,200,512]{2,1,0:T(8,128)(2,1)S(1)}, bf16[2,200,512]{2,1,0:T(8,128)(2,1)S(1)}, u32[]{:S(2)}, u32[]{:S(2)}) %collective-permute-start.8) | collective-permute-done | bytes 409632 | tf_op jit(solution)/shard_map/ppermute | solution.py:47
  36.1 1.1 %gradient_sums_0.1 = (bf16[256,1024]{1,0:T(8,128)(2,1)}, bf16[256,1024]{1,0:T(8,128)(2,1)}) custom-call(f32[256,512]{1,0:T(8,128)S(1)} %get-tuple-element.42.refs_0_, f32[256,512]{1,0:T(8,128)S(1)} %get-tuple-element.43.refs_1_, bf16[2,200,512]{2,1,0:T(8,128)(2,1)S(1)} %collective-permute-done.7.refs_2_, bf16[2,200,512]{2,1,0:T(8,128)(2,1)S(1)} %collective-permute-done.8.refs_3_), custom_call_target="tpu_custom_call" | custom-call | flops 786432 | bytes 2621440 | tf_op jit(solution)/shard_map/gradient_sums_0/pallas_call | solution.py:316
  37.2 0.0 collective-permute-done.5.refs_2_
  37.2 8.9 %collective-permute-done.6.refs_3_ = bf16[2,200,512]{2,1,0:T(8,128)(2,1)S(1)} collective-permute-done((bf16[2,200,512]{2,1,0:T(8,128)(2,1)S(1)}, bf16[2,200,512]{2,1,0:T(8,128)(2,1)S(1)}, u32[]{:S(2)}, u32[]{:S(2)}) %collective-permute-start.6) | collective-permute-done | bytes 409632 | tf_op jit(solution)/shard_map/ppermute | solution.py:47
  46.0 1.1 %gradient_sums_1.1 = (bf16[256,1024]{1,0:T(8,128)(2,1)}, bf16[256,1024]{1,0:T(8,128)(2,1)}) custom-call(f32[256,512]{1,0:T(8,128)S(1)} %get-tuple-element.38.refs_0_, f32[256,512]{1,0:T(8,128)S(1)} %get-tuple-element.39.refs_1_, bf16[2,200,512]{2,1,0:T(8,128)(2,1)S(1)} %collective-permute-done.5.refs_2_, ...), custom_call_target="tpu_custom_call", output_to_operand_aliasing={{0}: (4, {}), {1}: (5, {})} | custom-call | flops 786432 | bytes 2621440 | tf_op jit(solution)/shard_map/gradient_sums_1/pallas_call | solution.py:316
  (7 shorter events, 0.2 us)
Async XLA Ops:
  0.6 5.8 %copy-start = (bf16[256,1024]{1,0:T(8,128)(2,1)S(1)}, bf16[256,1024]{1,0:T(8,128)(2,1)}, u32[]{:S(2)}) copy-start(bf16[256,1024]{1,0:T(8,128)(2,1)} %refs_3_.3) | copy-start | bytes 1572868
  0.6 5.9 %copy-start.1 = (bf16[256,1024]{1,0:T(8,128)(2,1)S(1)}, bf16[256,1024]{1,0:T(8,128)(2,1)}, u32[]{:S(2)}) copy-start(bf16[256,1024]{1,0:T(8,128)(2,1)} %refs_4_.3) | copy-start | bytes 1572868
  2.7 9.3 %collective-permute-start.2 = (bf16[2,200,256]{2,1,0:T(8,128)(2,1)S(1)}, bf16[2,200,256]{2,1,0:T(8,128)(2,1)S(1)}, u32[]{:S(2)}, u32[]{:S(2)}) collective-permute-start(bf16[2,200,256]{2,1,0:T(8,128)(2,1)S(1)} %pad_maximum_fusion.1), channel_id=1, source_target_pairs={{1,2},{3,4},{5,6},{7,8},{9,10},{11,12},{13,14},{2,1},{4,3},{6,5},{... | collective-permute-start | bytes 614408 | tf_op jit(solution)/shard_map/ppermute | solution.py:47
  6.5 3.8 %collective-permute-start = (bf16[256,1024]{1,0:T(8,128)(2,1)S(1)}, bf16[256,1024]{1,0:T(8,128)(2,1)S(1)}, u32[]{:S(2)}, u32[]{:S(2)}) collective-permute-start(bf16[256,1024]{1,0:T(8,128)(2,1)S(1)} %copy-done), channel_id=1, source_target_pairs={{0,1},{2,3},{4,5},{6,7},{8,9},{10,11},{12,13},{14,15},{1,0},{3,2},... | collective-permute-start | bytes 1572872 | tf_op jit(solution)/shard_map/ppermute | solution.py:47
  6.5 3.7 %collective-permute-start.1 = (bf16[256,1024]{1,0:T(8,128)(2,1)S(1)}, bf16[256,1024]{1,0:T(8,128)(2,1)S(1)}, u32[]{:S(2)}, u32[]{:S(2)}) collective-permute-start(bf16[256,1024]{1,0:T(8,128)(2,1)S(1)} %copy-done.1), channel_id=1, source_target_pairs={{0,1},{2,3},{4,5},{6,7},{8,9},{10,11},{12,13},{14,15},{1,0},{3,2},... | collective-permute-start | bytes 1572872 | tf_op jit(solution)/shard_map/ppermute | solution.py:47
  7.1 3.2 %copy-start.4 = (s32[256,2]{0,1:T(2,128)S(1)}, s32[256,2]{0,1:T(2,128)}, u32[]{:S(2)}) copy-start(s32[256,2]{0,1:T(2,128)} %param.9) | copy-start | bytes 6148
  7.1 9.3 %collective-permute-start.4 = (bf16[2,200,256]{2,1,0:T(8,128)(2,1)S(1)}, bf16[2,200,256]{2,1,0:T(8,128)(2,1)S(1)}, u32[]{:S(2)}, u32[]{:S(2)}) collective-permute-start(bf16[2,200,256]{2,1,0:T(8,128)(2,1)S(1)} %pad_maximum_fusion.2), channel_id=1, source_target_pairs={{1,2},{3,4},{5,6},{7,8},{9,10},{11,12},{13,14},{2,1},{4,3},{6,5},{... | collective-permute-start | bytes 614408 | tf_op jit(solution)/shard_map/ppermute | solution.py:47
  10.3 6.2 %copy-start.3 = (bf16[256,1024]{1,0:T(8,128)(2,1)S(1)}, bf16[256,1024]{1,0:T(8,128)(2,1)}, u32[]{:S(2)}) copy-start(bf16[256,1024]{1,0:T(8,128)(2,1)} %refs_2_.3) | copy-start | bytes 1572868
  10.4 6.1 %copy-start.2 = (bf16[256,1024]{1,0:T(8,128)(2,1)S(1)}, bf16[256,1024]{1,0:T(8,128)(2,1)}, u32[]{:S(2)}) copy-start(bf16[256,1024]{1,0:T(8,128)(2,1)} %refs_1_.3) | copy-start | bytes 1572868
  12.1 14.0 %collective-permute-start.3 = (bf16[2,200,512]{2,1,0:T(8,128)(2,1)S(1)}, bf16[2,200,512]{2,1,0:T(8,128)(2,1)S(1)}, u32[]{:S(2)}, u32[]{:S(2)}) collective-permute-start(bf16[2,200,512]{2,1,0:T(8,128)(2,1)S(1)} %pad_maximum_fusion), channel_id=1, source_target_pairs={{1,2},{3,4},{5,6},{7,8},{9,10},{11,12},{13,14},{2,1},{4,3},{6,5},{... | collective-permute-start | bytes 1228808 | tf_op jit(solution)/shard_map/ppermute | solution.py:47
  22.3 13.1 %collective-permute-start.7 = (bf16[2,200,512]{2,1,0:T(8,128)(2,1)S(1)}, bf16[2,200,512]{2,1,0:T(8,128)(2,1)S(1)}, u32[]{:S(2)}, u32[]{:S(2)}) collective-permute-start(bf16[2,200,512]{2,1,0:T(8,128)(2,1)S(1)} %get-tuple-element.44), channel_id=1, source_target_pairs={{0,1},{2,3},{4,5},{6,7},{8,9},{10,11},{12,13},{14,15},{1,0},{3,2},... | collective-permute-start | bytes 1228808 | tf_op jit(solution)/shard_map/ppermute | solution.py:47
  22.4 13.7 %collective-permute-start.8 = (bf16[2,200,512]{2,1,0:T(8,128)(2,1)S(1)}, bf16[2,200,512]{2,1,0:T(8,128)(2,1)S(1)}, u32[]{:S(2)}, u32[]{:S(2)}) collective-permute-start(bf16[2,200,512]{2,1,0:T(8,128)(2,1)S(1)} %get-tuple-element.45), channel_id=1, source_target_pairs={{1,2},{3,4},{5,6},{7,8},{9,10},{11,12},{13,14},{2,1},{4,3},{6,5},{... | collective-permute-start | bytes 1228808 | tf_op jit(solution)/shard_map/ppermute | solution.py:47
  31.9 5.2 %collective-permute-start.5 = (bf16[2,200,512]{2,1,0:T(8,128)(2,1)S(1)}, bf16[2,200,512]{2,1,0:T(8,128)(2,1)S(1)}, u32[]{:S(2)}, u32[]{:S(2)}) collective-permute-start(bf16[2,200,512]{2,1,0:T(8,128)(2,1)S(1)} %get-tuple-element.40), channel_id=1, source_target_pairs={{0,1},{2,3},{4,5},{6,7},{8,9},{10,11},{12,13},{14,15},{1,0},{3,2},... | collective-permute-start | bytes 1228808 | tf_op jit(solution)/shard_map/ppermute | solution.py:47
  32.4 13.6 %collective-permute-start.6 = (bf16[2,200,512]{2,1,0:T(8,128)(2,1)S(1)}, bf16[2,200,512]{2,1,0:T(8,128)(2,1)S(1)}, u32[]{:S(2)}, u32[]{:S(2)}) collective-permute-start(bf16[2,200,512]{2,1,0:T(8,128)(2,1)S(1)} %get-tuple-element.41), channel_id=1, source_target_pairs={{1,2},{3,4},{5,6},{7,8},{9,10},{11,12},{13,14},{2,1},{4,3},{6,5},{... | collective-permute-start | bytes 1228808 | tf_op jit(solution)/shard_map/ppermute | solution.py:47

commit v8 on v7

--- a/solution.py
+++ b/solution.py
@@ -70,11 +70,9 @@
 def pack(sources, rows, low, high):
     points = sources[0].shape[0]
     columns = slice(low * PAIR, high * PAIR)
-    parts = [
-        jnp.where(is_even(), field[:rows, columns], field[points - rows :, columns])
-        for field in sources
-    ]
-    return jnp.stack(parts)
+    first = jnp.stack([field[:rows, columns] for field in sources])
+    last = jnp.stack([field[points - rows :, columns] for field in sources])
+    return jnp.where(is_even(), first, last)
 
 
 def padded(rows):
@@ -96,7 +94,7 @@
     outs = refs[2 * far + carried :]
     att_out, dq_out, to_partner_ref, to_next_ref, dk_ref, dv_ref = outs[:6]
     to_far_refs = outs[6 : 6 + 2 * far]
-    (bias_ref, keys_ref, turned_ref, exps_ref, probs_ref, dscores_ref, sums_ref, att_ref, dq_ref, sems) = outs[-10:]
+    (bias_ref, keys_ref, turned_ref, exps_ref, probs_ref, dscores_ref, att_ref, dq_ref, sems) = outs[-9:]
     even = is_even()
     owns = [slice(part * half, (part + 1) * half) for part in range(2)]
     spans_of = [slice(part * half, part * half + reached) for part in range(2)]
@@ -219,42 +217,56 @@
             probs = exps_ref[pair % 2, part, block, :] * inverse
             dscores_ref[pair % 2, part, block, :] = (probs * (dprobs[block] - delta)).astype(jnp.bfloat16)
 
-    def backward_outputs(pair, part):
-        dscores = dscores_ref[pair % 2, part]
-        dq = both(dot_nn(turned_ref[pair % 2, 0, :, spans_of[part]], dscores))
-        dq_ref[pair, owns[part], :] = jnp.concatenate(
-            [(x * SCALE).astype(jnp.bfloat16) for x in dq], axis=0
-        ).T
-        terms = (dot_nn(dscores, q_both(pair, part)), dot_nn(probs_ref[pair % 2, part], g_both(pair, part)))
-        for slot, term in enumerate(terms):
-            into = sums_ref.at[pair % 2, slot]
-            if part == 0:
-                into[:reached, :] = term
-            else:
-                into[half:reached, :] += term[: reached - half]
-                into[reached:, :] = term[reached - half :]
-
     copies = []
 
-    def send_out(pair):
+    def backward_outputs(pair):
+        for part in range(2):
+            dq = both(dot_nn(turned_ref[pair % 2, 0, :, spans_of[part]], dscores_ref[pair % 2, part]))
+            dq_ref[pair, owns[part], :] = jnp.concatenate(
+                [(x * SCALE).astype(jnp.bfloat16) for x in dq], axis=0
+            ).T
+        for slot, (scores_ref, own_both, own_ref) in enumerate(
+            [(dscores_ref, q_both, dk_ref), (probs_ref, g_both, dv_ref)]
+        ):
+            low_scores, high_scores = (scores_ref.at[pair % 2, part] for part in range(2))
+            low, high = (own_both(pair, part) for part in range(2))
+            shared = jnp.concatenate([low_scores[half:, :], high_scores[: reached - half, :]], axis=1)
+            sums = [
+                dot_nn(low_scores[:half, :], low),
+                dot_nn(shared, jnp.concatenate([low, high], axis=0)),
+                dot_nn(high_scores[reached - half :, :], high),
+            ]
+            send_out(pair, slot, own_ref, sums)
+
+    def send_out(pair, slot, own_ref, sums):
         columns = local_columns(pair)
-        for slot, own_ref in enumerate([dk_ref, dv_ref]):
-            sums = sums_ref.at[pair % 2, slot]
-            own_ref[:, columns] = sums[rim : rim + points, :]
-            near_low = sums[rim_width - near : rim_width, :].astype(jnp.bfloat16)
-            near_high = sums[rim + points : rim + points + near, :].astype(jnp.bfloat16)
-            to_partner_ref[slot, :, columns] = jnp.where(even, near_high, near_low)
-            to_next_ref[slot, :, columns] = jnp.where(even, near_low, near_high)
-            start = 0
-            for at in range(far):
-                size = lengths[at]
-                to_far_refs[at][slot, :, columns] = sums[start : start + size, :].astype(jnp.bfloat16)
-                start += size
-            start = rim + points + near
-            for at in range(far, 2 * far):
-                size = lengths[at + 2]
-                to_far_refs[at][slot, :, columns] = sums[start : start + size, :].astype(jnp.bfloat16)
-                start += size
+        bounds = spans((0, half, reached, wide))
+
+        def rows(start, stop):
+            pieces = [
+                term[max(start, first) - first : min(stop, last) - first]
+                for term, (first, last) in zip(sums, bounds)
+                if start < last and stop > first
+            ]
+            return jnp.concatenate(pieces, axis=0)
+
+        own_ref[:, columns] = rows(rim, rim + points)
+        near_low = rows(rim_width - near, rim_width).astype(jnp.bfloat16)
+        near_high = rows(rim + points, rim + points + near).astype(jnp.bfloat16)
+        to_partner_ref[slot, :, columns] = jnp.where(even, near_high, near_low)
+        to_next_ref[slot, :, columns] = jnp.where(even, near_low, near_high)
+        start = 0
+        for at in range(far):
+            to_far_refs[at][slot, :, columns] = rows(start, start + lengths[at]).astype(jnp.bfloat16)
+            start += lengths[at]
+        start = rim + points + near
+        for at in range(far, 2 * far):
+            size = lengths[at + 2]
+            to_far_refs[at][slot, :, columns] = rows(start, start + size).astype(jnp.bfloat16)
+            start += size
+
+    def finish(pair):
+        backward_outputs(pair)
         for at, (ref, out) in enumerate([(att_ref, att_out), (dq_ref, dq_out)]):
             copy = pltpu.make_async_copy(ref.at[pair], out.at[:, columns_of(pair)], sems.at[at, pair])
             copy.start()
@@ -269,15 +281,12 @@
             if following[1] == 0:
                 gather_keys(following[0])
             tops[following] = forward_scores(*following)
-        if at > 0:
-            backward_outputs(*units[at - 1])
-            if units[at - 1][1] == 1:
-                send_out(units[at - 1][0])
+        if unit[1] == 0 and unit[0] > 0:
+            finish(unit[0] - 1)
         inverse = forward_probs(*unit, tops.pop(unit))
         delta = forward_outputs(*unit)
         backward_scores(*unit, inverse, delta)
-    backward_outputs(*units[-1])
-    send_out(units[-1][0])
+    finish(units[-1][0])
     for copy in copies:
         copy.wait()
 
@@ -386,7 +395,6 @@
                 pltpu.VMEM((2, 2, reached, points), jnp.float32),
                 pltpu.VMEM((2, 2, reached, points), jnp.bfloat16),
                 pltpu.VMEM((2, 2, reached, points), jnp.bfloat16),
-                pltpu.VMEM((2, 2, wide, PAIR), jnp.float32),
                 pltpu.VMEM((count, points, PAIR), jnp.bfloat16),
                 pltpu.VMEM((count, points, PAIR), jnp.bfloat16),
                 pltpu.SemaphoreType.DMA((2, count)),

time: 47.4 us -> 45.2 us (0.954)
  other arithmetic: 2.19 us -> 0.16 us
  Pallas kernels: 13.9 us -> 12.6 us
  local copies, waits for them, and re-layouts: 0.03 us -> 1.28 us
    another operation x8 -> x0, other arithmetic: 2.19 us -> none  [pack(): return jnp.stack(parts)]
    another operation x0 -> x5, local copies, waits for them, and re-layouts: none -> 1.26 us  [pack(): last = jnp.stack([field[points - rows:, columns] for field in sources])]
    pallas_call x4, Pallas kernels: 13.9 us -> 12.6 us  [chunk_call(): pl.pallas_call(functools.partial(kernel, len(carried)), in_specs=[vmem] *...]
  transfers between devices with their start and end apart: 9 -> 9, of which waited for: 4 -> 4; matrix products, arithmetic and copies ran while one was open for 0% -> 0% of each run, Pallas kernels for 27% -> 26%
where the time goes in v8:
time: 45.2 us; the launch traced here: 45 us
  starting transfers between devices  18.5 us (41%)
  Pallas kernels  12.6 us (28%)
  waiting for transfers between devices  11.6 us (26%)
  local copies, waits for them, and re-layouts  1.28 us (3%)
  between operations  0.89 us (2%)
    ppermute x9, starting transfers between devices, swapped(): lax.ppermute(value, 'band', pairs + [(high, low) for low, high in pairs])  18.5 us
    pallas_call x4, Pallas kernels, chunk_call(): pl.pallas_call(functools.partial(kernel, len(carried)), in_specs=[vmem] *...  12.6 us
    ppermute x9, waiting for transfers between devices, swapped(): lax.ppermute(value, 'band', pairs + [(high, low) for low, high in pairs])  11.6 us
    another operation x5, local copies, waits for them, and re-layouts, pack(): last = jnp.stack([field[points - rows:, columns] for field in sources])  1.26 us
  transfers between devices with their start and end apart: 9, of which 4 were waited for; matrix products, arithmetic and copies ran while one was open for 0% of the time, Pallas kernels for 26%

profile of v8, /device:TPU:9, one launch (start us, length us, event | category | flops | bytes accessed | tf_op | source)
XLA Modules:
  0.0 45.0 jit_solution(7131055456514546047)
XLA Ops:
  0.6 0.0 copy-start
  0.7 0.0 copy-start.1
  0.7 1.2 %slice_bitcast_fusion.8 = (bf16[1,200,256]{2,1,0:T(8,128)(2,1)S(1)}, bf16[1,200,256]{2,1,0:T(8,128)(2,1)S(1)}, bf16[1,200,256]{2,1,0:T(8,128)(2,1)S(1)}, bf16[1,200,256]{2,1,0:T(8,128)(2,1)S(1)}) fusion(bf16[256,1024]{1,0:T(8,128)(2,1)} %refs_4_.3, bf16[256,1024]{1,0:T(8,128)(2,1)} %refs_3_.3), kind=kLoop, calls=%fused_computation.11 | loop fusion | bytes 819200 | tf_op jit(solution)/shard_map/stack | solution.py:74
  1.9 3.7 %collective-permute-start.2 = (bf16[2,200,256]{2,1,0:T(8,128)(2,1)S(1)}, bf16[2,200,256]{2,1,0:T(8,128)(2,1)S(1)}, u32[]{:S(2)}, u32[]{:S(2)}) collective-permute-start(bf16[2,200,256]{2,1,0:T(8,128)(2,1)S(1)} %maximum_select_fusion.1), channel_id=1, source_target_pairs={{1,2},{3,4},{5,6},{7,8},{9,10},{11,12},{13,14},{2,1},{4,3},{6,5},{... | collective-permute-start | bytes 614408 | tf_op jit(solution)/shard_map/ppermute | solution.py:47
  5.6 0.0 copy-done
  5.6 0.1 collective-permute-start
  5.7 0.0 copy-done.1
  5.7 0.5 %collective-permute-start.1 = (bf16[256,1024]{1,0:T(8,128)(2,1)S(1)}, bf16[256,1024]{1,0:T(8,128)(2,1)S(1)}, u32[]{:S(2)}, u32[]{:S(2)}) collective-permute-start(bf16[256,1024]{1,0:T(8,128)(2,1)S(1)} %copy-done.1), channel_id=1, source_target_pairs={{0,1},{2,3},{4,5},{6,7},{8,9},{10,11},{12,13},{14,15},{1,0},{3,2},... | collective-permute-start | bytes 1572872 | tf_op jit(solution)/shard_map/ppermute | solution.py:47
  6.2 0.0 copy-start.4
  6.3 3.1 %collective-permute-start.4 = (bf16[2,200,256]{2,1,0:T(8,128)(2,1)S(1)}, bf16[2,200,256]{2,1,0:T(8,128)(2,1)S(1)}, u32[]{:S(2)}, u32[]{:S(2)}) collective-permute-start(bf16[2,200,256]{2,1,0:T(8,128)(2,1)S(1)} %maximum_select_fusion.2), channel_id=1, source_target_pairs={{1,2},{3,4},{5,6},{7,8},{9,10},{11,12},{13,14},{2,1},{4,3},{6,5},{... | collective-permute-start | bytes 614408 | tf_op jit(solution)/shard_map/ppermute | solution.py:47
  9.4 0.0 copy-done.4
  9.4 0.0 collective-permute-done.refs_5_
  9.4 0.0 collective-permute-done.1.refs_6_
  9.5 0.0 copy-start.2
  9.5 0.0 copy-start.3
  9.6 0.1 maximum_select_fusion
  9.6 1.6 %collective-permute-done.2.refs_7_ = bf16[2,200,256]{2,1,0:T(8,128)(2,1)S(1)} collective-permute-done((bf16[2,200,256]{2,1,0:T(8,128)(2,1)S(1)}, bf16[2,200,256]{2,1,0:T(8,128)(2,1)S(1)}, u32[]{:S(2)}, u32[]{:S(2)}) %collective-permute-start.2) | collective-permute-done | bytes 204832 | tf_op jit(solution)/shard_map/ppermute | solution.py:47
  11.2 3.6 %collective-permute-start.3 = (bf16[2,200,512]{2,1,0:T(8,128)(2,1)S(1)}, bf16[2,200,512]{2,1,0:T(8,128)(2,1)S(1)}, u32[]{:S(2)}, u32[]{:S(2)}) collective-permute-start(bf16[2,200,512]{2,1,0:T(8,128)(2,1)S(1)} %maximum_select_fusion), channel_id=1, source_target_pairs={{1,2},{3,4},{5,6},{7,8},{9,10},{11,12},{13,14},{2,1},{4,3},{6,5},{... | collective-permute-start | bytes 1228808 | tf_op jit(solution)/shard_map/ppermute | solution.py:47
  14.9 0.8 %collective-permute-done.4.refs_8_ = bf16[2,200,256]{2,1,0:T(8,128)(2,1)S(1)} collective-permute-done((bf16[2,200,256]{2,1,0:T(8,128)(2,1)S(1)}, bf16[2,200,256]{2,1,0:T(8,128)(2,1)S(1)}, u32[]{:S(2)}, u32[]{:S(2)}) %collective-permute-start.4) | collective-permute-done | bytes 204832 | tf_op jit(solution)/shard_map/ppermute | solution.py:47
  15.6 0.0 copy-done.2
  15.6 0.0 copy-done.3
  15.6 5.2 %attention_0.1 = (bf16[256,1024]{1,0:T(8,128)(2,1)}, bf16[256,1024]{1,0:T(8,128)(2,1)}, bf16[2,200,512]{2,1,0:T(8,128)(2,1)S(1)}, bf16[2,200,512]{2,1,0:T(8,128)...) custom-call(s32[2,256]{1,0:T(2,128)S(1)} %subtract_bitcast_fusion.refs_0_, bf16[256,1024]{1,0:T(8,128)(2,1)S(1)} %copy-done.2, ...), custom_call_target="tpu_custom_call" | custom-call | flops 8556380160 | bytes 5373952 | tf_op jit(solution)/shard_map/attention_0/pallas_call | solution.py:325
  20.8 0.1 collective-permute-start.7
  20.9 3.6 %collective-permute-start.8 = (bf16[2,200,512]{2,1,0:T(8,128)(2,1)S(1)}, bf16[2,200,512]{2,1,0:T(8,128)(2,1)S(1)}, u32[]{:S(2)}, u32[]{:S(2)}) collective-permute-start(bf16[2,200,512]{2,1,0:T(8,128)(2,1)S(1)} %get-tuple-element.45), channel_id=1, source_target_pairs={{1,2},{3,4},{5,6},{7,8},{9,10},{11,12},{13,14},{2,1},{4,3},{6,5},{... | collective-permute-start | bytes 1228808 | tf_op jit(solution)/shard_map/ppermute | solution.py:47
  24.6 0.0 collective-permute-done.3.refs_7_
  24.6 5.2 %attention_1.1 = (bf16[256,1024]{1,0:T(8,128)(2,1)}, bf16[256,1024]{1,0:T(8,128)(2,1)}, bf16[2,200,512]{2,1,0:T(8,128)(2,1)S(1)}, bf16[2,200,512]{2,1,0:T(8,128)...) custom-call(s32[2,256]{1,0:T(2,128)S(1)} %subtract_bitcast_fusion.refs_0_, ...), custom_call_target="tpu_custom_call", output_to_operand_aliasing={{0}: (8, {}), {1}: (9, {})} | custom-call | flops 8556380160 | bytes 5373952 | tf_op jit(solution)/shard_map/attention_1/pallas_call | solution.py:325
  29.8 0.4 collective-permute-start.5
  30.3 3.3 %collective-permute-start.6 = (bf16[2,200,512]{2,1,0:T(8,128)(2,1)S(1)}, bf16[2,200,512]{2,1,0:T(8,128)(2,1)S(1)}, u32[]{:S(2)}, u32[]{:S(2)}) collective-permute-start(bf16[2,200,512]{2,1,0:T(8,128)(2,1)S(1)} %get-tuple-element.41), channel_id=1, source_target_pairs={{1,2},{3,4},{5,6},{7,8},{9,10},{11,12},{13,14},{2,1},{4,3},{6,5},{... | collective-permute-start | bytes 1228808 | tf_op jit(solution)/shard_map/ppermute | solution.py:47
  33.6 0.0 collective-permute-done.7.refs_2_
  33.6 1.0 %collective-permute-done.8.refs_3_ = bf16[2,200,512]{2,1,0:T(8,128)(2,1)S(1)} collective-permute-done((bf16[2,200,512]{2,1,0:T(8,128)(2,1)S(1)}, bf16[2,200,512]{2,1,0:T(8,128)(2,1)S(1)}, u32[]{:S(2)}, u32[]{:S(2)}) %collective-permute-start.8) | collective-permute-done | bytes 409632 | tf_op jit(solution)/shard_map/ppermute | solution.py:47
  34.6 1.1 %gradient_sums_0.1 = (bf16[256,1024]{1,0:T(8,128)(2,1)}, bf16[256,1024]{1,0:T(8,128)(2,1)}) custom-call(f32[256,512]{1,0:T(8,128)S(1)} %get-tuple-element.42.refs_0_, f32[256,512]{1,0:T(8,128)S(1)} %get-tuple-element.43.refs_1_, bf16[2,200,512]{2,1,0:T(8,128)(2,1)S(1)} %collective-permute-done.7.refs_2_, bf16[2,200,512]{2,1,0:T(8,128)(2,1)S(1)} %collective-permute-done.8.refs_3_), custom_call_target="tpu_custom_call" | custom-call | flops 786432 | bytes 2621440 | tf_op jit(solution)/shard_map/gradient_sums_0/pallas_call | solution.py:325
  35.7 0.0 collective-permute-done.5.refs_2_
  35.7 8.2 %collective-permute-done.6.refs_3_ = bf16[2,200,512]{2,1,0:T(8,128)(2,1)S(1)} collective-permute-done((bf16[2,200,512]{2,1,0:T(8,128)(2,1)S(1)}, bf16[2,200,512]{2,1,0:T(8,128)(2,1)S(1)}, u32[]{:S(2)}, u32[]{:S(2)}) %collective-permute-start.6) | collective-permute-done | bytes 409632 | tf_op jit(solution)/shard_map/ppermute | solution.py:47
  43.9 1.1 %gradient_sums_1.1 = (bf16[256,1024]{1,0:T(8,128)(2,1)}, bf16[256,1024]{1,0:T(8,128)(2,1)}) custom-call(f32[256,512]{1,0:T(8,128)S(1)} %get-tuple-element.38.refs_0_, f32[256,512]{1,0:T(8,128)S(1)} %get-tuple-element.39.refs_1_, bf16[2,200,512]{2,1,0:T(8,128)(2,1)S(1)} %collective-permute-done.5.refs_2_, ...), custom_call_target="tpu_custom_call", output_to_operand_aliasing={{0}: (4, {}), {1}: (5, {})} | custom-call | flops 786432 | bytes 2621440 | tf_op jit(solution)/shard_map/gradient_sums_1/pallas_call | solution.py:325
  (7 shorter events, 0.2 us)
Async XLA Ops:
  0.6 4.9 %copy-start = (bf16[256,1024]{1,0:T(8,128)(2,1)S(1)}, bf16[256,1024]{1,0:T(8,128)(2,1)}, u32[]{:S(2)}) copy-start(bf16[256,1024]{1,0:T(8,128)(2,1)} %refs_3_.3) | copy-start | bytes 1572868
  0.7 5.0 %copy-start.1 = (bf16[256,1024]{1,0:T(8,128)(2,1)S(1)}, bf16[256,1024]{1,0:T(8,128)(2,1)}, u32[]{:S(2)}) copy-start(bf16[256,1024]{1,0:T(8,128)(2,1)} %refs_4_.3) | copy-start | bytes 1572868
  1.9 9.3 %collective-permute-start.2 = (bf16[2,200,256]{2,1,0:T(8,128)(2,1)S(1)}, bf16[2,200,256]{2,1,0:T(8,128)(2,1)S(1)}, u32[]{:S(2)}, u32[]{:S(2)}) collective-permute-start(bf16[2,200,256]{2,1,0:T(8,128)(2,1)S(1)} %maximum_select_fusion.1), channel_id=1, source_target_pairs={{1,2},{3,4},{5,6},{7,8},{9,10},{11,12},{13,14},{2,1},{4,3},{6,5},{... | collective-permute-start | bytes 614408 | tf_op jit(solution)/shard_map/ppermute | solution.py:47
  5.6 3.8 %collective-permute-start = (bf16[256,1024]{1,0:T(8,128)(2,1)S(1)}, bf16[256,1024]{1,0:T(8,128)(2,1)S(1)}, u32[]{:S(2)}, u32[]{:S(2)}) collective-permute-start(bf16[256,1024]{1,0:T(8,128)(2,1)S(1)} %copy-done), channel_id=1, source_target_pairs={{0,1},{2,3},{4,5},{6,7},{8,9},{10,11},{12,13},{14,15},{1,0},{3,2},... | collective-permute-start | bytes 1572872 | tf_op jit(solution)/shard_map/ppermute | solution.py:47
  5.7 3.8 %collective-permute-start.1 = (bf16[256,1024]{1,0:T(8,128)(2,1)S(1)}, bf16[256,1024]{1,0:T(8,128)(2,1)S(1)}, u32[]{:S(2)}, u32[]{:S(2)}) collective-permute-start(bf16[256,1024]{1,0:T(8,128)(2,1)S(1)} %copy-done.1), channel_id=1, source_target_pairs={{0,1},{2,3},{4,5},{6,7},{8,9},{10,11},{12,13},{14,15},{1,0},{3,2},... | collective-permute-start | bytes 1572872 | tf_op jit(solution)/shard_map/ppermute | solution.py:47
  6.2 3.2 %copy-start.4 = (s32[256,2]{0,1:T(2,128)S(1)}, s32[256,2]{0,1:T(2,128)}, u32[]{:S(2)}) copy-start(s32[256,2]{0,1:T(2,128)} %param.9) | copy-start | bytes 6148
  6.3 9.3 %collective-permute-start.4 = (bf16[2,200,256]{2,1,0:T(8,128)(2,1)S(1)}, bf16[2,200,256]{2,1,0:T(8,128)(2,1)S(1)}, u32[]{:S(2)}, u32[]{:S(2)}) collective-permute-start(bf16[2,200,256]{2,1,0:T(8,128)(2,1)S(1)} %maximum_select_fusion.2), channel_id=1, source_target_pairs={{1,2},{3,4},{5,6},{7,8},{9,10},{11,12},{13,14},{2,1},{4,3},{6,5},{... | collective-permute-start | bytes 614408 | tf_op jit(solution)/shard_map/ppermute | solution.py:47
  9.5 6.1 %copy-start.2 = (bf16[256,1024]{1,0:T(8,128)(2,1)S(1)}, bf16[256,1024]{1,0:T(8,128)(2,1)}, u32[]{:S(2)}) copy-start(bf16[256,1024]{1,0:T(8,128)(2,1)} %refs_1_.3) | copy-start | bytes 1572868
  9.5 6.1 %copy-start.3 = (bf16[256,1024]{1,0:T(8,128)(2,1)S(1)}, bf16[256,1024]{1,0:T(8,128)(2,1)}, u32[]{:S(2)}) copy-start(bf16[256,1024]{1,0:T(8,128)(2,1)} %refs_2_.3) | copy-start | bytes 1572868
  11.2 13.4 %collective-permute-start.3 = (bf16[2,200,512]{2,1,0:T(8,128)(2,1)S(1)}, bf16[2,200,512]{2,1,0:T(8,128)(2,1)S(1)}, u32[]{:S(2)}, u32[]{:S(2)}) collective-permute-start(bf16[2,200,512]{2,1,0:T(8,128)(2,1)S(1)} %maximum_select_fusion), channel_id=1, source_target_pairs={{1,2},{3,4},{5,6},{7,8},{9,10},{11,12},{13,14},{2,1},{4,3},{6,5},{... | collective-permute-start | bytes 1228808 | tf_op jit(solution)/shard_map/ppermute | solution.py:47
  20.8 12.7 %collective-permute-start.7 = (bf16[2,200,512]{2,1,0:T(8,128)(2,1)S(1)}, bf16[2,200,512]{2,1,0:T(8,128)(2,1)S(1)}, u32[]{:S(2)}, u32[]{:S(2)}) collective-permute-start(bf16[2,200,512]{2,1,0:T(8,128)(2,1)S(1)} %get-tuple-element.44), channel_id=1, source_target_pairs={{0,1},{2,3},{4,5},{6,7},{8,9},{10,11},{12,13},{14,15},{1,0},{3,2},... | collective-permute-start | bytes 1228808 | tf_op jit(solution)/shard_map/ppermute | solution.py:47
  20.9 13.7 %collective-permute-start.8 = (bf16[2,200,512]{2,1,0:T(8,128)(2,1)S(1)}, bf16[2,200,512]{2,1,0:T(8,128)(2,1)S(1)}, u32[]{:S(2)}, u32[]{:S(2)}) collective-permute-start(bf16[2,200,512]{2,1,0:T(8,128)(2,1)S(1)} %get-tuple-element.45), channel_id=1, source_target_pairs={{1,2},{3,4},{5,6},{7,8},{9,10},{11,12},{13,14},{2,1},{4,3},{6,5},{... | collective-permute-start | bytes 1228808 | tf_op jit(solution)/shard_map/ppermute | solution.py:47
  29.8 5.9 %collective-permute-start.5 = (bf16[2,200,512]{2,1,0:T(8,128)(2,1)S(1)}, bf16[2,200,512]{2,1,0:T(8,128)(2,1)S(1)}, u32[]{:S(2)}, u32[]{:S(2)}) collective-permute-start(bf16[2,200,512]{2,1,0:T(8,128)(2,1)S(1)} %get-tuple-element.40), channel_id=1, source_target_pairs={{0,1},{2,3},{4,5},{6,7},{8,9},{10,11},{12,13},{14,15},{1,0},{3,2},... | collective-permute-start | bytes 1228808 | tf_op jit(solution)/shard_map/ppermute | solution.py:47
  30.3 13.6 %collective-permute-start.6 = (bf16[2,200,512]{2,1,0:T(8,128)(2,1)S(1)}, bf16[2,200,512]{2,1,0:T(8,128)(2,1)S(1)}, u32[]{:S(2)}, u32[]{:S(2)}) collective-permute-start(bf16[2,200,512]{2,1,0:T(8,128)(2,1)S(1)} %get-tuple-element.41), channel_id=1, source_target_pairs={{1,2},{3,4},{5,6},{7,8},{9,10},{11,12},{13,14},{2,1},{4,3},{6,5},{... | collective-permute-start | bytes 1228808 | tf_op jit(solution)/shard_map/ppermute | solution.py:47

commit v9 on v8

--- a/solution.py
+++ b/solution.py
@@ -274,17 +274,16 @@
 
     units = [(pair, part) for pair in range(pairs) for part in range(2)]
     gather_keys(0)
-    tops = {units[0]: forward_scores(*units[0])}
+    top = forward_scores(*units[0])
     for at, unit in enumerate(units):
-        if at + 1 < len(units):
-            following = units[at + 1]
-            if following[1] == 0:
-                gather_keys(following[0])
-            tops[following] = forward_scores(*following)
         if unit[1] == 0 and unit[0] > 0:
             finish(unit[0] - 1)
-        inverse = forward_probs(*unit, tops.pop(unit))
+        inverse = forward_probs(*unit, top)
         delta = forward_outputs(*unit)
+        if at + 1 < len(units):
+            if units[at + 1][1] == 0:
+                gather_keys(units[at + 1][0])
+            top = forward_scores(*units[at + 1])
         backward_scores(*unit, inverse, delta)
     finish(units[-1][0])
     for copy in copies:

time: 45.2 us -> 47.2 us (1.044)
  Pallas kernels: 12.6 us -> 14.6 us
    pallas_call x4, Pallas kernels: 12.6 us -> 14.6 us  [chunk_call(): pl.pallas_call(functools.partial(kernel, len(carried)), in_specs=[vmem] *...]
  transfers between devices with their start and end apart: 9 -> 9, of which waited for: 4 -> 4; matrix products, arithmetic and copies ran while one was open for 0% -> 0% of each run, Pallas kernels for 26% -> 29%
where the time goes in v9:
time: 47.2 us; the launch traced here: 46.9 us
  starting transfers between devices  18.2 us (39%)
  Pallas kernels  14.6 us (31%)
  waiting for transfers between devices  11.8 us (25%)
  local copies, waits for them, and re-layouts  1.28 us (3%)
  between operations  0.89 us (2%)
    ppermute x9, starting transfers between devices, swapped(): lax.ppermute(value, 'band', pairs + [(high, low) for low, high in pairs])  18.2 us
    pallas_call x4, Pallas kernels, chunk_call(): pl.pallas_call(functools.partial(kernel, len(carried)), in_specs=[vmem] *...  14.6 us
    ppermute x9, waiting for transfers between devices, swapped(): lax.ppermute(value, 'band', pairs + [(high, low) for low, high in pairs])  11.8 us
    another operation x5, local copies, waits for them, and re-layouts, pack(): last = jnp.stack([field[points - rows:, columns] for field in sources])  1.26 us
  transfers between devices with their start and end apart: 9, of which 4 were waited for; matrix products, arithmetic and copies ran while one was open for 0% of the time, Pallas kernels for 29%

profile of v9, /device:TPU:9, one launch (start us, length us, event | category | flops | bytes accessed | tf_op | source)
XLA Modules:
  0.0 46.9 jit_solution(17771485139776687580)
XLA Ops:
  0.6 0.0 copy-start
  0.7 0.0 copy-start.1
  0.7 1.2 %slice_bitcast_fusion.8 = (bf16[1,200,256]{2,1,0:T(8,128)(2,1)S(1)}, bf16[1,200,256]{2,1,0:T(8,128)(2,1)S(1)}, bf16[1,200,256]{2,1,0:T(8,128)(2,1)S(1)}, bf16[1,200,256]{2,1,0:T(8,128)(2,1)S(1)}) fusion(bf16[256,1024]{1,0:T(8,128)(2,1)} %refs_4_.3, bf16[256,1024]{1,0:T(8,128)(2,1)} %refs_3_.3), kind=kLoop, calls=%fused_computation.11 | loop fusion | bytes 819200 | tf_op jit(solution)/shard_map/stack | solution.py:74
  1.9 3.7 %collective-permute-start.2 = (bf16[2,200,256]{2,1,0:T(8,128)(2,1)S(1)}, bf16[2,200,256]{2,1,0:T(8,128)(2,1)S(1)}, u32[]{:S(2)}, u32[]{:S(2)}) collective-permute-start(bf16[2,200,256]{2,1,0:T(8,128)(2,1)S(1)} %maximum_select_fusion.1), channel_id=1, source_target_pairs={{1,2},{3,4},{5,6},{7,8},{9,10},{11,12},{13,14},{2,1},{4,3},{6,5},{... | collective-permute-start | bytes 614408 | tf_op jit(solution)/shard_map/ppermute | solution.py:47
  5.6 0.0 copy-done
  5.6 0.1 collective-permute-start
  5.7 0.0 copy-done.1
  5.7 0.5 %collective-permute-start.1 = (bf16[256,1024]{1,0:T(8,128)(2,1)S(1)}, bf16[256,1024]{1,0:T(8,128)(2,1)S(1)}, u32[]{:S(2)}, u32[]{:S(2)}) collective-permute-start(bf16[256,1024]{1,0:T(8,128)(2,1)S(1)} %copy-done.1), channel_id=1, source_target_pairs={{0,1},{2,3},{4,5},{6,7},{8,9},{10,11},{12,13},{14,15},{1,0},{3,2},... | collective-permute-start | bytes 1572872 | tf_op jit(solution)/shard_map/ppermute | solution.py:47
  6.2 0.0 copy-start.4
  6.3 3.1 %collective-permute-start.4 = (bf16[2,200,256]{2,1,0:T(8,128)(2,1)S(1)}, bf16[2,200,256]{2,1,0:T(8,128)(2,1)S(1)}, u32[]{:S(2)}, u32[]{:S(2)}) collective-permute-start(bf16[2,200,256]{2,1,0:T(8,128)(2,1)S(1)} %maximum_select_fusion.2), channel_id=1, source_target_pairs={{1,2},{3,4},{5,6},{7,8},{9,10},{11,12},{13,14},{2,1},{4,3},{6,5},{... | collective-permute-start | bytes 614408 | tf_op jit(solution)/shard_map/ppermute | solution.py:47
  9.4 0.0 copy-done.4
  9.4 0.0 collective-permute-done.refs_5_
  9.4 0.0 collective-permute-done.1.refs_6_
  9.5 0.0 copy-start.2
  9.5 0.0 copy-start.3
  9.6 0.1 maximum_select_fusion
  9.6 1.6 %collective-permute-done.2.refs_7_ = bf16[2,200,256]{2,1,0:T(8,128)(2,1)S(1)} collective-permute-done((bf16[2,200,256]{2,1,0:T(8,128)(2,1)S(1)}, bf16[2,200,256]{2,1,0:T(8,128)(2,1)S(1)}, u32[]{:S(2)}, u32[]{:S(2)}) %collective-permute-start.2) | collective-permute-done | bytes 204832 | tf_op jit(solution)/shard_map/ppermute | solution.py:47
  11.2 3.6 %collective-permute-start.3 = (bf16[2,200,512]{2,1,0:T(8,128)(2,1)S(1)}, bf16[2,200,512]{2,1,0:T(8,128)(2,1)S(1)}, u32[]{:S(2)}, u32[]{:S(2)}) collective-permute-start(bf16[2,200,512]{2,1,0:T(8,128)(2,1)S(1)} %maximum_select_fusion), channel_id=1, source_target_pairs={{1,2},{3,4},{5,6},{7,8},{9,10},{11,12},{13,14},{2,1},{4,3},{6,5},{... | collective-permute-start | bytes 1228808 | tf_op jit(solution)/shard_map/ppermute | solution.py:47
  14.9 0.8 %collective-permute-done.4.refs_8_ = bf16[2,200,256]{2,1,0:T(8,128)(2,1)S(1)} collective-permute-done((bf16[2,200,256]{2,1,0:T(8,128)(2,1)S(1)}, bf16[2,200,256]{2,1,0:T(8,128)(2,1)S(1)}, u32[]{:S(2)}, u32[]{:S(2)}) %collective-permute-start.4) | collective-permute-done | bytes 204832 | tf_op jit(solution)/shard_map/ppermute | solution.py:47
  15.6 0.0 copy-done.2
  15.6 0.0 copy-done.3
  15.6 6.2 %attention_0.1 = (bf16[256,1024]{1,0:T(8,128)(2,1)}, bf16[256,1024]{1,0:T(8,128)(2,1)}, bf16[2,200,512]{2,1,0:T(8,128)(2,1)S(1)}, bf16[2,200,512]{2,1,0:T(8,128)...) custom-call(s32[2,256]{1,0:T(2,128)S(1)} %subtract_bitcast_fusion.refs_0_, bf16[256,1024]{1,0:T(8,128)(2,1)S(1)} %copy-done.2, ...), custom_call_target="tpu_custom_call" | custom-call | flops 8556380160 | bytes 5373952 | tf_op jit(solution)/shard_map/attention_0/pallas_call | solution.py:324
  21.8 0.1 collective-permute-start.7
  21.9 3.6 %collective-permute-start.8 = (bf16[2,200,512]{2,1,0:T(8,128)(2,1)S(1)}, bf16[2,200,512]{2,1,0:T(8,128)(2,1)S(1)}, u32[]{:S(2)}, u32[]{:S(2)}) collective-permute-start(bf16[2,200,512]{2,1,0:T(8,128)(2,1)S(1)} %get-tuple-element.45), channel_id=1, source_target_pairs={{1,2},{3,4},{5,6},{7,8},{9,10},{11,12},{13,14},{2,1},{4,3},{6,5},{... | collective-permute-start | bytes 1228808 | tf_op jit(solution)/shard_map/ppermute | solution.py:47
  25.5 0.0 collective-permute-done.3.refs_7_
  25.6 6.2 %attention_1.1 = (bf16[256,1024]{1,0:T(8,128)(2,1)}, bf16[256,1024]{1,0:T(8,128)(2,1)}, bf16[2,200,512]{2,1,0:T(8,128)(2,1)S(1)}, bf16[2,200,512]{2,1,0:T(8,128)...) custom-call(s32[2,256]{1,0:T(2,128)S(1)} %subtract_bitcast_fusion.refs_0_, ...), custom_call_target="tpu_custom_call", output_to_operand_aliasing={{0}: (8, {}), {1}: (9, {})} | custom-call | flops 8556380160 | bytes 5373952 | tf_op jit(solution)/shard_map/attention_1/pallas_call | solution.py:324
  31.8 0.4 collective-permute-start.5
  32.2 3.0 %collective-permute-start.6 = (bf16[2,200,512]{2,1,0:T(8,128)(2,1)S(1)}, bf16[2,200,512]{2,1,0:T(8,128)(2,1)S(1)}, u32[]{:S(2)}, u32[]{:S(2)}) collective-permute-start(bf16[2,200,512]{2,1,0:T(8,128)(2,1)S(1)} %get-tuple-element.41), channel_id=1, source_target_pairs={{1,2},{3,4},{5,6},{7,8},{9,10},{11,12},{13,14},{2,1},{4,3},{6,5},{... | collective-permute-start | bytes 1228808 | tf_op jit(solution)/shard_map/ppermute | solution.py:47
  35.3 0.0 collective-permute-done.7.refs_2_
  35.3 0.3 collective-permute-done.8.refs_3_
  35.6 1.1 %gradient_sums_0.1 = (bf16[256,1024]{1,0:T(8,128)(2,1)}, bf16[256,1024]{1,0:T(8,128)(2,1)}) custom-call(f32[256,512]{1,0:T(8,128)S(1)} %get-tuple-element.42.refs_0_, f32[256,512]{1,0:T(8,128)S(1)} %get-tuple-element.43.refs_1_, bf16[2,200,512]{2,1,0:T(8,128)(2,1)S(1)} %collective-permute-done.7.refs_2_, bf16[2,200,512]{2,1,0:T(8,128)(2,1)S(1)} %collective-permute-done.8.refs_3_), custom_call_target="tpu_custom_call" | custom-call | flops 786432 | bytes 2621440 | tf_op jit(solution)/shard_map/gradient_sums_0/pallas_call | solution.py:324
  36.6 0.0 collective-permute-done.5.refs_2_
  36.6 9.2 %collective-permute-done.6.refs_3_ = bf16[2,200,512]{2,1,0:T(8,128)(2,1)S(1)} collective-permute-done((bf16[2,200,512]{2,1,0:T(8,128)(2,1)S(1)}, bf16[2,200,512]{2,1,0:T(8,128)(2,1)S(1)}, u32[]{:S(2)}, u32[]{:S(2)}) %collective-permute-start.6) | collective-permute-done | bytes 409632 | tf_op jit(solution)/shard_map/ppermute | solution.py:47
  45.9 1.1 %gradient_sums_1.1 = (bf16[256,1024]{1,0:T(8,128)(2,1)}, bf16[256,1024]{1,0:T(8,128)(2,1)}) custom-call(f32[256,512]{1,0:T(8,128)S(1)} %get-tuple-element.38.refs_0_, f32[256,512]{1,0:T(8,128)S(1)} %get-tuple-element.39.refs_1_, bf16[2,200,512]{2,1,0:T(8,128)(2,1)S(1)} %collective-permute-done.5.refs_2_, ...), custom_call_target="tpu_custom_call", output_to_operand_aliasing={{0}: (4, {}), {1}: (5, {})} | custom-call | flops 786432 | bytes 2621440 | tf_op jit(solution)/shard_map/gradient_sums_1/pallas_call | solution.py:324
  (7 shorter events, 0.2 us)
Async XLA Ops:
  0.6 4.9 %copy-start = (bf16[256,1024]{1,0:T(8,128)(2,1)S(1)}, bf16[256,1024]{1,0:T(8,128)(2,1)}, u32[]{:S(2)}) copy-start(bf16[256,1024]{1,0:T(8,128)(2,1)} %refs_3_.3) | copy-start | bytes 1572868
  0.7 5.0 %copy-start.1 = (bf16[256,1024]{1,0:T(8,128)(2,1)S(1)}, bf16[256,1024]{1,0:T(8,128)(2,1)}, u32[]{:S(2)}) copy-start(bf16[256,1024]{1,0:T(8,128)(2,1)} %refs_4_.3) | copy-start | bytes 1572868
  1.9 9.3 %collective-permute-start.2 = (bf16[2,200,256]{2,1,0:T(8,128)(2,1)S(1)}, bf16[2,200,256]{2,1,0:T(8,128)(2,1)S(1)}, u32[]{:S(2)}, u32[]{:S(2)}) collective-permute-start(bf16[2,200,256]{2,1,0:T(8,128)(2,1)S(1)} %maximum_select_fusion.1), channel_id=1, source_target_pairs={{1,2},{3,4},{5,6},{7,8},{9,10},{11,12},{13,14},{2,1},{4,3},{6,5},{... | collective-permute-start | bytes 614408 | tf_op jit(solution)/shard_map/ppermute | solution.py:47
  5.6 3.8 %collective-permute-start = (bf16[256,1024]{1,0:T(8,128)(2,1)S(1)}, bf16[256,1024]{1,0:T(8,128)(2,1)S(1)}, u32[]{:S(2)}, u32[]{:S(2)}) collective-permute-start(bf16[256,1024]{1,0:T(8,128)(2,1)S(1)} %copy-done), channel_id=1, source_target_pairs={{0,1},{2,3},{4,5},{6,7},{8,9},{10,11},{12,13},{14,15},{1,0},{3,2},... | collective-permute-start | bytes 1572872 | tf_op jit(solution)/shard_map/ppermute | solution.py:47
  5.7 3.8 %collective-permute-start.1 = (bf16[256,1024]{1,0:T(8,128)(2,1)S(1)}, bf16[256,1024]{1,0:T(8,128)(2,1)S(1)}, u32[]{:S(2)}, u32[]{:S(2)}) collective-permute-start(bf16[256,1024]{1,0:T(8,128)(2,1)S(1)} %copy-done.1), channel_id=1, source_target_pairs={{0,1},{2,3},{4,5},{6,7},{8,9},{10,11},{12,13},{14,15},{1,0},{3,2},... | collective-permute-start | bytes 1572872 | tf_op jit(solution)/shard_map/ppermute | solution.py:47
  6.2 3.2 %copy-start.4 = (s32[256,2]{0,1:T(2,128)S(1)}, s32[256,2]{0,1:T(2,128)}, u32[]{:S(2)}) copy-start(s32[256,2]{0,1:T(2,128)} %param.9) | copy-start | bytes 6148
  6.3 9.3 %collective-permute-start.4 = (bf16[2,200,256]{2,1,0:T(8,128)(2,1)S(1)}, bf16[2,200,256]{2,1,0:T(8,128)(2,1)S(1)}, u32[]{:S(2)}, u32[]{:S(2)}) collective-permute-start(bf16[2,200,256]{2,1,0:T(8,128)(2,1)S(1)} %maximum_select_fusion.2), channel_id=1, source_target_pairs={{1,2},{3,4},{5,6},{7,8},{9,10},{11,12},{13,14},{2,1},{4,3},{6,5},{... | collective-permute-start | bytes 614408 | tf_op jit(solution)/shard_map/ppermute | solution.py:47
  9.5 6.1 %copy-start.2 = (bf16[256,1024]{1,0:T(8,128)(2,1)S(1)}, bf16[256,1024]{1,0:T(8,128)(2,1)}, u32[]{:S(2)}) copy-start(bf16[256,1024]{1,0:T(8,128)(2,1)} %refs_1_.3) | copy-start | bytes 1572868
  9.5 6.1 %copy-start.3 = (bf16[256,1024]{1,0:T(8,128)(2,1)S(1)}, bf16[256,1024]{1,0:T(8,128)(2,1)}, u32[]{:S(2)}) copy-start(bf16[256,1024]{1,0:T(8,128)(2,1)} %refs_2_.3) | copy-start | bytes 1572868
  11.2 14.3 %collective-permute-start.3 = (bf16[2,200,512]{2,1,0:T(8,128)(2,1)S(1)}, bf16[2,200,512]{2,1,0:T(8,128)(2,1)S(1)}, u32[]{:S(2)}, u32[]{:S(2)}) collective-permute-start(bf16[2,200,512]{2,1,0:T(8,128)(2,1)S(1)} %maximum_select_fusion), channel_id=1, source_target_pairs={{1,2},{3,4},{5,6},{7,8},{9,10},{11,12},{13,14},{2,1},{4,3},{6,5},{... | collective-permute-start | bytes 1228808 | tf_op jit(solution)/shard_map/ppermute | solution.py:47
  21.8 13.4 %collective-permute-start.7 = (bf16[2,200,512]{2,1,0:T(8,128)(2,1)S(1)}, bf16[2,200,512]{2,1,0:T(8,128)(2,1)S(1)}, u32[]{:S(2)}, u32[]{:S(2)}) collective-permute-start(bf16[2,200,512]{2,1,0:T(8,128)(2,1)S(1)} %get-tuple-element.44), channel_id=1, source_target_pairs={{0,1},{2,3},{4,5},{6,7},{8,9},{10,11},{12,13},{14,15},{1,0},{3,2},... | collective-permute-start | bytes 1228808 | tf_op jit(solution)/shard_map/ppermute | solution.py:47
  21.9 13.7 %collective-permute-start.8 = (bf16[2,200,512]{2,1,0:T(8,128)(2,1)S(1)}, bf16[2,200,512]{2,1,0:T(8,128)(2,1)S(1)}, u32[]{:S(2)}, u32[]{:S(2)}) collective-permute-start(bf16[2,200,512]{2,1,0:T(8,128)(2,1)S(1)} %get-tuple-element.45), channel_id=1, source_target_pairs={{1,2},{3,4},{5,6},{7,8},{9,10},{11,12},{13,14},{2,1},{4,3},{6,5},{... | collective-permute-start | bytes 1228808 | tf_op jit(solution)/shard_map/ppermute | solution.py:47
  31.8 4.9 %collective-permute-start.5 = (bf16[2,200,512]{2,1,0:T(8,128)(2,1)S(1)}, bf16[2,200,512]{2,1,0:T(8,128)(2,1)S(1)}, u32[]{:S(2)}, u32[]{:S(2)}) collective-permute-start(bf16[2,200,512]{2,1,0:T(8,128)(2,1)S(1)} %get-tuple-element.40), channel_id=1, source_target_pairs={{0,1},{2,3},{4,5},{6,7},{8,9},{10,11},{12,13},{14,15},{1,0},{3,2},... | collective-permute-start | bytes 1228808 | tf_op jit(solution)/shard_map/ppermute | solution.py:47
  32.2 13.6 %collective-permute-start.6 = (bf16[2,200,512]{2,1,0:T(8,128)(2,1)S(1)}, bf16[2,200,512]{2,1,0:T(8,128)(2,1)S(1)}, u32[]{:S(2)}, u32[]{:S(2)}) collective-permute-start(bf16[2,200,512]{2,1,0:T(8,128)(2,1)S(1)} %get-tuple-element.41), channel_id=1, source_target_pairs={{1,2},{3,4},{5,6},{7,8},{9,10},{11,12},{13,14},{2,1},{4,3},{6,5},{... | collective-permute-start | bytes 1228808 | tf_op jit(solution)/shard_map/ppermute | solution.py:47

commit v10 on v8

--- a/solution.py
+++ b/solution.py
@@ -17,9 +17,11 @@
 SCALE = HEAD_DIM**-0.5
 LOG2_E = math.log2(math.e)
 BLOCK = 32
+COST = 120
 OUTSIDE = -1e30
 CHUNKS = (0, 4, 8)
 NEXT_CHUNKS = (0, 2, 4, 8)
+CALLS = (0, 2, 4, 8)
 
 
 def reach_sizes(points, count):
@@ -79,7 +81,7 @@
     return (rows + 15) // 16 * 16
 
 
-def attention_kernel(rim_width, lengths, points, low_pair, next_pairs, carried, *refs):
+def attention_kernel(rim_width, lengths, points, low_pair, next_pairs, earlier, carried, *refs):
     far = len(lengths) // 2 - 1
     near = lengths[far]
     half = points // 2
@@ -91,7 +93,8 @@
     next_refs = refs[7 : 7 + len(next_pairs)]
     refs = refs[7 + len(next_pairs) :]
     far_refs = refs[: 2 * far]
-    outs = refs[2 * far + carried :]
+    before_refs = refs[2 * far : 2 * far + (1 if earlier else 0)]
+    outs = refs[2 * far + len(before_refs) + carried :]
     att_out, dq_out, to_partner_ref, to_next_ref, dk_ref, dv_ref = outs[:6]
     to_far_refs = outs[6 : 6 + 2 * far]
     (bias_ref, keys_ref, turned_ref, exps_ref, probs_ref, dscores_ref, att_ref, dq_ref, sems) = outs[-9:]
@@ -115,6 +118,9 @@
     if rim > rim_width:
         for gap in (slice(rim - 16, rim), slice(wide - 16, wide)):
             keys_ref[:, :, gap, :] = jnp.zeros((2, 2, 16, PAIR), jnp.bfloat16)
+
+    if earlier:
+        to_next_ref[:, :, : earlier * PAIR] = before_refs[0][...]
 
     where_next = [
         (chunk, at) for chunk, count in enumerate(next_pairs) for at in range(count)
@@ -219,24 +225,30 @@
 
     copies = []
 
-    def backward_outputs(pair):
-        for part in range(2):
-            dq = both(dot_nn(turned_ref[pair % 2, 0, :, spans_of[part]], dscores_ref[pair % 2, part]))
-            dq_ref[pair, owns[part], :] = jnp.concatenate(
-                [(x * SCALE).astype(jnp.bfloat16) for x in dq], axis=0
-            ).T
-        for slot, (scores_ref, own_both, own_ref) in enumerate(
-            [(dscores_ref, q_both, dk_ref), (probs_ref, g_both, dv_ref)]
-        ):
-            low_scores, high_scores = (scores_ref.at[pair % 2, part] for part in range(2))
-            low, high = (own_both(pair, part) for part in range(2))
-            shared = jnp.concatenate([low_scores[half:, :], high_scores[: reached - half, :]], axis=1)
-            sums = [
-                dot_nn(low_scores[:half, :], low),
-                dot_nn(shared, jnp.concatenate([low, high], axis=0)),
-                dot_nn(high_scores[reached - half :, :], high),
-            ]
-            send_out(pair, slot, own_ref, sums)
+    def backward_queries(pair, part):
+        dq = both(dot_nn(turned_ref[pair % 2, 0, :, spans_of[part]], dscores_ref[pair % 2, part]))
+        dq_ref[pair, owns[part], :] = jnp.concatenate(
+            [(x * SCALE).astype(jnp.bfloat16) for x in dq], axis=0
+        ).T
+        if part == 1:
+            for at, (ref, out) in enumerate([(att_ref, att_out), (dq_ref, dq_out)]):
+                copy = pltpu.make_async_copy(
+                    ref.at[pair], out.at[:, columns_of(pair)], sems.at[at, pair]
+                )
+                copy.start()
+                copies.append(copy)
+
+    def backward_keys(pair, slot):
+        scores_ref, own_both, own_ref = [(dscores_ref, q_both, dk_ref), (probs_ref, g_both, dv_ref)][slot]
+        low_scores, high_scores = (scores_ref.at[pair % 2, part] for part in range(2))
+        low, high = (own_both(pair, part) for part in range(2))
+        shared = jnp.concatenate([low_scores[half:, :], high_scores[: reached - half, :]], axis=1)
+        sums = [
+            dot_nn(low_scores[:half, :], low),
+            dot_nn(shared, jnp.concatenate([low, high], axis=0)),
+            dot_nn(high_scores[reached - half :, :], high),
+        ]
+        send_out(pair, slot, own_ref, sums)
 
     def send_out(pair, slot, own_ref, sums):
         columns = local_columns(pair)
@@ -254,7 +266,7 @@
         near_low = rows(rim_width - near, rim_width).astype(jnp.bfloat16)
         near_high = rows(rim + points, rim + points + near).astype(jnp.bfloat16)
         to_partner_ref[slot, :, columns] = jnp.where(even, near_high, near_low)
-        to_next_ref[slot, :, columns] = jnp.where(even, near_low, near_high)
+        to_next_ref[slot, :, local_columns(earlier + pair)] = jnp.where(even, near_low, near_high)
         start = 0
         for at in range(far):
             to_far_refs[at][slot, :, columns] = rows(start, start + lengths[at]).astype(jnp.bfloat16)
@@ -265,50 +277,52 @@
             to_far_refs[at][slot, :, columns] = rows(start, start + size).astype(jnp.bfloat16)
             start += size
 
-    def finish(pair):
-        backward_outputs(pair)
-        for at, (ref, out) in enumerate([(att_ref, att_out), (dq_ref, dq_out)]):
-            copy = pltpu.make_async_copy(ref.at[pair], out.at[:, columns_of(pair)], sems.at[at, pair])
-            copy.start()
-            copies.append(copy)
-
     units = [(pair, part) for pair in range(pairs) for part in range(2)]
     gather_keys(0)
     tops = {units[0]: forward_scores(*units[0])}
     for at, unit in enumerate(units):
+        pair, part = unit
         if at + 1 < len(units):
             following = units[at + 1]
             if following[1] == 0:
                 gather_keys(following[0])
             tops[following] = forward_scores(*following)
-        if unit[1] == 0 and unit[0] > 0:
-            finish(unit[0] - 1)
+        if at > 0:
+            backward_queries(*units[at - 1])
+        if pair > 0:
+            backward_keys(pair - 1, part)
         inverse = forward_probs(*unit, tops.pop(unit))
         delta = forward_outputs(*unit)
         backward_scores(*unit, inverse, delta)
-    finish(units[-1][0])
+    backward_queries(*units[-1])
+    backward_keys(pairs - 1, 0)
+    backward_keys(pairs - 1, 1)
     for copy in copies:
         copy.wait()
 
 
-def sum_kernel(far_lengths, points, low, high, carried, *refs):
+def sum_kernel(far_lengths, points, low, high, parts, carried, *refs):
     far = len(far_lengths) // 2
-    own_refs, partner_ref, next_ref = refs[:2], refs[2], refs[3]
-    far_refs = refs[4 : 4 + 2 * far]
-    outs = refs[4 + 2 * far + carried :]
+    part_refs, refs = [refs[3 * at : 3 * at + 3] for at in range(len(parts))], refs[3 * len(parts) :]
+    far_refs, refs = [refs[2 * far * at : 2 * far * (at + 1)] for at in range(len(parts))], refs[2 * far * len(parts) :]
+    next_ref, outs = refs[0], refs[1 + carried :]
     total, low_ref, sems = outs[-3:]
-    near = partner_ref.shape[1]
+    near = next_ref.shape[1]
     first = pl.multiple_of(jnp.where(is_even(), points - near, 0), 8)
-    starts = (first, points - near - first)
+    partner_rows = pl.ds(first, near)
+    next_rows = pl.ds(pl.multiple_of(points - near - first, 8), near)
     copies = []
     for slot in range(2):
-        total[...] = own_refs[slot][...]
-        for at, ref in enumerate((partner_ref, next_ref)):
-            rows = pl.ds(pl.multiple_of(starts[at], 8), near)
-            total[rows, :] += ref[slot].astype(jnp.float32)
-        for at, (ref, length) in enumerate(zip(far_refs, far_lengths)):
-            rows = slice(points - length, points) if at < far else slice(0, length)
-            total[rows, :] += ref[slot].astype(jnp.float32)
+        start = 0
+        for pairs, part, fars in zip(parts, part_refs, far_refs):
+            columns = slice(start * PAIR, (start + pairs) * PAIR)
+            start += pairs
+            total[:, columns] = part[slot][...]
+            total[partner_rows, columns] += part[2][slot].astype(jnp.float32)
+            for at, (ref, length) in enumerate(zip(fars, far_lengths)):
+                rows = slice(points - length, points) if at < far else slice(0, length)
+                total[rows, columns] += ref[slot].astype(jnp.float32)
+        total[next_rows, :] += next_ref[slot].astype(jnp.float32)
         low_ref[slot] = total[...].astype(jnp.bfloat16)
         copy = pltpu.make_async_copy(
             low_ref.at[slot], outs[slot].at[:, low * PAIR : high * PAIR], sems.at[slot]
@@ -352,8 +366,6 @@
         piece = pack(ready, near, low, high)
         to_next.append(piece)
         ready = lax.optimization_barrier((*ready, piece))[:2]
-        if chunk > 1:
-            piece = lax.optimization_barrier((piece, from_next[chunk - 2]))[0]
         from_next.append(swapped(piece, 1))
         if chunk == 0:
             from_partner = [swapped(field, 0) for field in ready]
@@ -365,10 +377,15 @@
         from_far.append(passed_along(jnp.stack([keys[part], values[part]]), -d))
 
     whole = jax.ShapeDtypeStruct((points, width), jnp.bfloat16)
-    outs, own_terms, back_partner, back_next, back_far = [], [], [], [], []
-    for chunk, (low, high) in enumerate(spans(CHUNKS)):
+    outs, own_terms, back_next = [], [[] for _ in spans(CHUNKS)], []
+    back_far = [[] for _ in spans(CHUNKS)]
+    for call, (low, high) in enumerate(spans(CALLS)):
         count = high - low
-        chunk_width = count * PAIR
+        call_width = count * PAIR
+        chunk, (first_pair, last_pair) = next(
+            (at, bounds) for at, bounds in enumerate(spans(CHUNKS)) if bounds[0] <= low < bounds[1]
+        )
+        earlier = low - first_pair
         parts = [
             (at, last - first)
             for at, (first, last) in enumerate(spans(NEXT_CHUNKS))
@@ -377,16 +394,22 @@
         next_pairs = [size for _, size in parts]
         assert sum(next_pairs) == count
         outs = chunk_call(
-            functools.partial(attention_kernel, rim_width, lengths, points, low, next_pairs),
+            functools.partial(
+                attention_kernel, rim_width, lengths, points, low, next_pairs, earlier
+            ),
             [relative, queries, grad_out, keys, values, *from_partner]
             + [from_next[at] for at, _ in parts]
-            + from_far,
+            + from_far
+            + ([outs[3]] if earlier else []),
             outs[:2],
             2,
             [whole] * 2
-            + [jax.ShapeDtypeStruct((2, near, chunk_width), jnp.bfloat16)] * 2
-            + [jax.ShapeDtypeStruct((points, chunk_width), jnp.float32)] * 2
-            + [jax.ShapeDtypeStruct((2, size, chunk_width), jnp.bfloat16) for size in far_sizes],
+            + [
+                jax.ShapeDtypeStruct((2, near, call_width), jnp.bfloat16),
+                jax.ShapeDtypeStruct((2, near, call_width + earlier * PAIR), jnp.bfloat16),
+            ]
+            + [jax.ShapeDtypeStruct((points, call_width), jnp.float32)] * 2
+            + [jax.ShapeDtypeStruct((2, size, call_width), jnp.bfloat16) for size in far_sizes],
             48 * wide * points + 12 * 2**20,
             scratch_shapes=[
                 pltpu.VMEM((2, reached, points), jnp.float32),
@@ -400,23 +423,24 @@
                 pltpu.SemaphoreType.DMA((2, count)),
             ],
             cost_estimate=pl.CostEstimate(
-                flops=count * 120 * reached * points * PAIR,
+                flops=count * COST * reached * points * PAIR,
                 bytes_accessed=count * PAIR * (20 * points + 8 * wide),
                 transcendentals=2 * count * points * reached,
             ),
-            name=f"attention_{chunk}",
+            name=f"attention_{call}",
         )
-        own_terms.append(outs[4:6])
-        back_partner.append(swapped(outs[2], 0))
-        back_next.append(swapped(outs[3], 1))
-        back_far.append([passed_along(term, d) for term, d in zip(outs[6:], far)])
+        own_terms[chunk] += [outs[4], outs[5], swapped(outs[2], 0)]
+        back_far[chunk] += [passed_along(term, d) for term, d in zip(outs[6:], far)]
+        if high == last_pair:
+            back_next.append(swapped(outs[3], 1))
 
     grads = []
     for chunk, (low, high) in enumerate(spans(CHUNKS)):
         chunk_width = (high - low) * PAIR
+        parts = [last - first for first, last in spans(CALLS) if low <= first and last <= high]
         grads = chunk_call(
-            functools.partial(sum_kernel, far_sizes, points, low, high),
-            [*own_terms[chunk], back_partner[chunk], back_next[chunk], *back_far[chunk]],
+            functools.partial(sum_kernel, far_sizes, points, low, high, parts),
+            [*own_terms[chunk], *back_far[chunk], back_next[chunk]],
             grads,
             2,
             [whole] * 2,

time: 45.2 us -> 45.9 us (1.015)
  starting transfers between devices: 18.5 us -> 16.2 us
  Pallas kernels: 12.6 us -> 14.3 us
  waiting for transfers between devices: 11.6 us -> 12.8 us
    ppermute x9 -> x10, starting transfers between devices: 18.5 us -> 16.2 us  [swapped(): lax.ppermute(value, 'band', pairs + [(high, low) for low, high in pairs])]
    pallas_call x4 -> x5, Pallas kernels: 12.6 us -> 14.3 us  [chunk_call(): pl.pallas_call(functools.partial(kernel, len(carried)), in_specs=[vmem] *...]
    ppermute x9 -> x10, waiting for transfers between devices: 11.6 us -> 12.8 us  [swapped(): lax.ppermute(value, 'band', pairs + [(high, low) for low, high in pairs])]
  transfers between devices with their start and end apart: 9 -> 10, of which waited for: 4 -> 4; matrix products, arithmetic and copies ran while one was open for 0% -> 0% of each run, Pallas kernels for 26% -> 29%
where the time goes in v10:
time: 45.9 us; the launch traced here: 45.6 us
  starting transfers between devices  16.2 us (35%)
  Pallas kernels  14.3 us (31%)
  waiting for transfers between devices  12.8 us (28%)
  local copies, waits for them, and re-layouts  1.28 us (3%)
  between operations  0.92 us (2%)
    ppermute x10, starting transfers between devices, swapped(): lax.ppermute(value, 'band', pairs + [(high, low) for low, high in pairs])  16.2 us
    pallas_call x5, Pallas kernels, chunk_call(): pl.pallas_call(functools.partial(kernel, len(carried)), in_specs=[vmem] *...  14.3 us
    ppermute x10, waiting for transfers between devices, swapped(): lax.ppermute(value, 'band', pairs + [(high, low) for low, high in pairs])  12.8 us
    another operation x5, local copies, waits for them, and re-layouts, pack(): last = jnp.stack([field[points - rows:, columns] for field in sources])  1.26 us
  transfers between devices with their start and end apart: 10, of which 4 were waited for; matrix products, arithmetic and copies ran while one was open for 0% of the time, Pallas kernels for 29%

profile of v10, /device:TPU:9, one launch (start us, length us, event | category | flops | bytes accessed | tf_op | source)
XLA Modules:
  0.0 45.6 jit_solution(4957999442851045687)
XLA Ops:
  0.6 0.0 copy-start
  0.7 0.0 copy-start.1
  0.7 1.2 %slice_bitcast_fusion.8 = (bf16[1,200,256]{2,1,0:T(8,128)(2,1)S(1)}, bf16[1,200,256]{2,1,0:T(8,128)(2,1)S(1)}, bf16[1,200,256]{2,1,0:T(8,128)(2,1)S(1)}, bf16[1,200,256]{2,1,0:T(8,128)(2,1)S(1)}) fusion(bf16[256,1024]{1,0:T(8,128)(2,1)} %refs_4_.5, bf16[256,1024]{1,0:T(8,128)(2,1)} %refs_3_.5), kind=kLoop, calls=%fused_computation.11 | loop fusion | bytes 819200 | tf_op jit(solution)/shard_map/stack | solution.py:76
  1.9 3.7 %collective-permute-start.4 = (bf16[2,200,256]{2,1,0:T(8,128)(2,1)S(1)}, bf16[2,200,256]{2,1,0:T(8,128)(2,1)S(1)}, u32[]{:S(2)}, u32[]{:S(2)}) collective-permute-start(bf16[2,200,256]{2,1,0:T(8,128)(2,1)S(1)} %maximum_select_fusion.1), channel_id=1, source_target_pairs={{1,2},{3,4},{5,6},{7,8},{9,10},{11,12},{13,14},{2,1},{4,3},{6,5},{... | collective-permute-start | bytes 614408 | tf_op jit(solution)/shard_map/ppermute | solution.py:49
  5.6 0.0 copy-done
  5.6 0.1 collective-permute-start
  5.7 0.0 copy-done.1
  5.7 0.5 %collective-permute-start.1 = (bf16[256,1024]{1,0:T(8,128)(2,1)S(1)}, bf16[256,1024]{1,0:T(8,128)(2,1)S(1)}, u32[]{:S(2)}, u32[]{:S(2)}) collective-permute-start(bf16[256,1024]{1,0:T(8,128)(2,1)S(1)} %copy-done.1), channel_id=1, source_target_pairs={{0,1},{2,3},{4,5},{6,7},{8,9},{10,11},{12,13},{14,15},{1,0},{3,2},... | collective-permute-start | bytes 1572872 | tf_op jit(solution)/shard_map/ppermute | solution.py:49
  6.2 0.0 copy-start.4
  6.3 3.1 %collective-permute-start.3 = (bf16[2,200,256]{2,1,0:T(8,128)(2,1)S(1)}, bf16[2,200,256]{2,1,0:T(8,128)(2,1)S(1)}, u32[]{:S(2)}, u32[]{:S(2)}) collective-permute-start(bf16[2,200,256]{2,1,0:T(8,128)(2,1)S(1)} %maximum_select_fusion.2), channel_id=1, source_target_pairs={{1,2},{3,4},{5,6},{7,8},{9,10},{11,12},{13,14},{2,1},{4,3},{6,5},{... | collective-permute-start | bytes 614408 | tf_op jit(solution)/shard_map/ppermute | solution.py:49
  9.4 0.0 copy-done.4
  9.4 0.0 collective-permute-done.refs_5_
  9.4 0.0 collective-permute-done.1.refs_6_
  9.5 0.0 copy-start.2
  9.5 0.0 copy-start.3
  9.6 0.1 maximum_select_fusion
  9.6 2.6 %collective-permute-start.2 = (bf16[2,200,512]{2,1,0:T(8,128)(2,1)S(1)}, bf16[2,200,512]{2,1,0:T(8,128)(2,1)S(1)}, u32[]{:S(2)}, u32[]{:S(2)}) collective-permute-start(bf16[2,200,512]{2,1,0:T(8,128)(2,1)S(1)} %maximum_select_fusion), channel_id=1, source_target_pairs={{1,2},{3,4},{5,6},{7,8},{9,10},{11,12},{13,14},{2,1},{4,3},{6,5},{... | collective-permute-start | bytes 1228808 | tf_op jit(solution)/shard_map/ppermute | solution.py:49
  12.2 0.0 collective-permute-done.4.refs_7_
  12.2 0.0 copy-done.2
  12.2 0.0 copy-done.3
  12.3 3.2 %attention_0.1 = (bf16[256,1024]{1,0:T(8,128)(2,1)}, bf16[256,1024]{1,0:T(8,128)(2,1)}, bf16[2,200,256]{2,1,0:T(8,128)(2,1)S(1)}, bf16[2,200,256]{2,1,0:T(8,128)...) custom-call(s32[2,256]{1,0:T(2,128)S(1)} %subtract_bitcast_fusion.refs_0_, bf16[256,1024]{1,0:T(8,128)(2,1)S(1)} %copy-done.2, ...), custom_call_target="tpu_custom_call" | custom-call | flops 4278190080 | bytes 2686976 | tf_op jit(solution)/shard_map/attention_0/pallas_call | solution.py:339
  15.5 4.5 %collective-permute-done.3.refs_7_ = bf16[2,200,256]{2,1,0:T(8,128)(2,1)S(1)} collective-permute-done((bf16[2,200,256]{2,1,0:T(8,128)(2,1)S(1)}, bf16[2,200,256]{2,1,0:T(8,128)(2,1)S(1)}, u32[]{:S(2)}, u32[]{:S(2)}) %collective-permute-start.3) | collective-permute-done | bytes 204832 | tf_op jit(solution)/shard_map/ppermute | solution.py:49
  20.0 3.3 %attention_1.1 = (bf16[256,1024]{1,0:T(8,128)(2,1)}, bf16[256,1024]{1,0:T(8,128)(2,1)}, bf16[2,200,256]{2,1,0:T(8,128)(2,1)S(1)}, bf16[2,200,512]{2,1,0:T(8,128)...) custom-call(s32[2,256]{1,0:T(2,128)S(1)} %subtract_bitcast_fusion.refs_0, ...), custom_call_target="tpu_custom_call", output_to_operand_aliasing={{0}: (9, {}), {1}: (10, {})} | custom-call | flops 4278190080 | bytes 2686976 | tf_op jit(solution)/shard_map/attention_1/pallas_call | solution.py:339
  23.3 1.9 %collective-permute-start.9 = (bf16[2,200,512]{2,1,0:T(8,128)(2,1)S(1)}, bf16[2,200,512]{2,1,0:T(8,128)(2,1)S(1)}, u32[]{:S(2)}, u32[]{:S(2)}) collective-permute-start(bf16[2,200,512]{2,1,0:T(8,128)(2,1)S(1)} %get-tuple-element.55), channel_id=1, source_target_pairs={{1,2},{3,4},{5,6},{7,8},{9,10},{11,12},{13,14},{2,1},{4,3},{6,5},{... | collective-permute-start | bytes 1228808 | tf_op jit(solution)/shard_map/ppermute | solution.py:49
  25.2 0.0 collective-permute-done.2.refs_7_
  25.2 5.6 %attention_2.1 = (bf16[256,1024]{1,0:T(8,128)(2,1)}, bf16[256,1024]{1,0:T(8,128)(2,1)}, bf16[2,200,512]{2,1,0:T(8,128)(2,1)S(1)}, bf16[2,200,512]{2,1,0:T(8,128)...) custom-call(s32[2,256]{1,0:T(2,128)S(1)} %subtract_bitcast_fusion.refs_0_, ...), custom_call_target="tpu_custom_call", output_to_operand_aliasing={{0}: (8, {}), {1}: (9, {})} | custom-call | flops 8556380160 | bytes 5373952 | tf_op jit(solution)/shard_map/attention_2/pallas_call | solution.py:339
  30.8 0.1 collective-permute-start.5
  30.9 3.6 %collective-permute-start.6 = (bf16[2,200,512]{2,1,0:T(8,128)(2,1)S(1)}, bf16[2,200,512]{2,1,0:T(8,128)(2,1)S(1)}, u32[]{:S(2)}, u32[]{:S(2)}) collective-permute-start(bf16[2,200,512]{2,1,0:T(8,128)(2,1)S(1)} %get-tuple-element.48), channel_id=1, source_target_pairs={{1,2},{3,4},{5,6},{7,8},{9,10},{11,12},{13,14},{2,1},{4,3},{6,5},{... | collective-permute-start | bytes 1228808 | tf_op jit(solution)/shard_map/ppermute | solution.py:49
  34.5 0.1 collective-permute-start.8
  34.6 0.5 %collective-permute-start.7 = (bf16[2,200,256]{2,1,0:T(8,128)(2,1)S(1)}, bf16[2,200,256]{2,1,0:T(8,128)(2,1)S(1)}, u32[]{:S(2)}, u32[]{:S(2)}) collective-permute-start(bf16[2,200,256]{2,1,0:T(8,128)(2,1)S(1)} %get-tuple-element.51), channel_id=1, source_target_pairs={{0,1},{2,3},{4,5},{6,7},{8,9},{10,11},{12,13},{14,15},{1,0},{3,2},... | collective-permute-start | bytes 614408 | tf_op jit(solution)/shard_map/ppermute | solution.py:49
  35.1 0.9 %collective-permute-done.8.refs_5_ = bf16[2,200,256]{2,1,0:T(8,128)(2,1)S(1)} collective-permute-done((bf16[2,200,256]{2,1,0:T(8,128)(2,1)S(1)}, bf16[2,200,256]{2,1,0:T(8,128)(2,1)S(1)}, u32[]{:S(2)}, u32[]{:S(2)}) %collective-permute-start.8) | collective-permute-done | bytes 204832 | tf_op jit(solution)/shard_map/ppermute | solution.py:49
  36.1 0.3 collective-permute-done.7.refs_2_
  36.4 0.0 collective-permute-done.9.refs_6_
  36.4 1.1 %gradient_sums_0.1 = (bf16[256,1024]{1,0:T(8,128)(2,1)}, bf16[256,1024]{1,0:T(8,128)(2,1)}) custom-call(f32[256,256]{1,0:T(8,128)S(1)} %get-tuple-element.49.refs_0_, f32[256,256]{1,0:T(8,128)S(1)} %get-tuple-element.50.refs_1_, bf16[2,200,256]{2,1,0:T(8,128)(2,1)S(1)} %collective-permute-done.7.refs_2_, f32[256,256]{1,0:T(8,128)S(1)} %get-tuple-element.52.refs_3_, ...), custom_call_target="tpu_custom_call" | custom-call | flops 786432 | bytes 2621440 | tf_op jit(solution)/shard_map/gradient_sums_0/pallas_call | solution.py:339
  37.5 0.0 collective-permute-done.5.refs_2_
  37.5 7.1 %collective-permute-done.6.refs_3_ = bf16[2,200,512]{2,1,0:T(8,128)(2,1)S(1)} collective-permute-done((bf16[2,200,512]{2,1,0:T(8,128)(2,1)S(1)}, bf16[2,200,512]{2,1,0:T(8,128)(2,1)S(1)}, u32[]{:S(2)}, u32[]{:S(2)}) %collective-permute-start.6) | collective-permute-done | bytes 409632 | tf_op jit(solution)/shard_map/ppermute | solution.py:49
  44.5 1.1 %gradient_sums_1.1 = (bf16[256,1024]{1,0:T(8,128)(2,1)}, bf16[256,1024]{1,0:T(8,128)(2,1)}) custom-call(f32[256,512]{1,0:T(8,128)S(1)} %get-tuple-element.45.refs_0_, f32[256,512]{1,0:T(8,128)S(1)} %get-tuple-element.46.refs_1_, bf16[2,200,512]{2,1,0:T(8,128)(2,1)S(1)} %collective-permute-done.5.refs_2_, ...), custom_call_target="tpu_custom_call", output_to_operand_aliasing={{0}: (4, {}), {1}: (5, {})} | custom-call | flops 786432 | bytes 2621440 | tf_op jit(solution)/shard_map/gradient_sums_1/pallas_call | solution.py:339
  (7 shorter events, 0.2 us)
Async XLA Ops:
  0.6 4.9 %copy-start = (bf16[256,1024]{1,0:T(8,128)(2,1)S(1)}, bf16[256,1024]{1,0:T(8,128)(2,1)}, u32[]{:S(2)}) copy-start(bf16[256,1024]{1,0:T(8,128)(2,1)} %refs_3_.5) | copy-start | bytes 1572868
  0.7 5.0 %copy-start.1 = (bf16[256,1024]{1,0:T(8,128)(2,1)S(1)}, bf16[256,1024]{1,0:T(8,128)(2,1)}, u32[]{:S(2)}) copy-start(bf16[256,1024]{1,0:T(8,128)(2,1)} %refs_4_.5) | copy-start | bytes 1572868
  1.9 10.4 %collective-permute-start.4 = (bf16[2,200,256]{2,1,0:T(8,128)(2,1)S(1)}, bf16[2,200,256]{2,1,0:T(8,128)(2,1)S(1)}, u32[]{:S(2)}, u32[]{:S(2)}) collective-permute-start(bf16[2,200,256]{2,1,0:T(8,128)(2,1)S(1)} %maximum_select_fusion.1), channel_id=1, source_target_pairs={{1,2},{3,4},{5,6},{7,8},{9,10},{11,12},{13,14},{2,1},{4,3},{6,5},{... | collective-permute-start | bytes 614408 | tf_op jit(solution)/shard_map/ppermute | solution.py:49
  5.6 3.8 %collective-permute-start = (bf16[256,1024]{1,0:T(8,128)(2,1)S(1)}, bf16[256,1024]{1,0:T(8,128)(2,1)S(1)}, u32[]{:S(2)}, u32[]{:S(2)}) collective-permute-start(bf16[256,1024]{1,0:T(8,128)(2,1)S(1)} %copy-done), channel_id=1, source_target_pairs={{0,1},{2,3},{4,5},{6,7},{8,9},{10,11},{12,13},{14,15},{1,0},{3,2},... | collective-permute-start | bytes 1572872 | tf_op jit(solution)/shard_map/ppermute | solution.py:49
  5.7 3.8 %collective-permute-start.1 = (bf16[256,1024]{1,0:T(8,128)(2,1)S(1)}, bf16[256,1024]{1,0:T(8,128)(2,1)S(1)}, u32[]{:S(2)}, u32[]{:S(2)}) collective-permute-start(bf16[256,1024]{1,0:T(8,128)(2,1)S(1)} %copy-done.1), channel_id=1, source_target_pairs={{0,1},{2,3},{4,5},{6,7},{8,9},{10,11},{12,13},{14,15},{1,0},{3,2},... | collective-permute-start | bytes 1572872 | tf_op jit(solution)/shard_map/ppermute | solution.py:49
  6.2 3.2 %copy-start.4 = (s32[256,2]{0,1:T(2,128)S(1)}, s32[256,2]{0,1:T(2,128)}, u32[]{:S(2)}) copy-start(s32[256,2]{0,1:T(2,128)} %param.9) | copy-start | bytes 6148
  6.3 13.7 %collective-permute-start.3 = (bf16[2,200,256]{2,1,0:T(8,128)(2,1)S(1)}, bf16[2,200,256]{2,1,0:T(8,128)(2,1)S(1)}, u32[]{:S(2)}, u32[]{:S(2)}) collective-permute-start(bf16[2,200,256]{2,1,0:T(8,128)(2,1)S(1)} %maximum_select_fusion.2), channel_id=1, source_target_pairs={{1,2},{3,4},{5,6},{7,8},{9,10},{11,12},{13,14},{2,1},{4,3},{6,5},{... | collective-permute-start | bytes 614408 | tf_op jit(solution)/shard_map/ppermute | solution.py:49
  9.5 2.7 %copy-start.2 = (bf16[256,1024]{1,0:T(8,128)(2,1)S(1)}, bf16[256,1024]{1,0:T(8,128)(2,1)}, u32[]{:S(2)}) copy-start(bf16[256,1024]{1,0:T(8,128)(2,1)} %refs_1_.5) | copy-start | bytes 1572868
  9.5 2.7 %copy-start.3 = (bf16[256,1024]{1,0:T(8,128)(2,1)S(1)}, bf16[256,1024]{1,0:T(8,128)(2,1)}, u32[]{:S(2)}) copy-start(bf16[256,1024]{1,0:T(8,128)(2,1)} %refs_2_.5) | copy-start | bytes 1572868
  9.6 15.6 %collective-permute-start.2 = (bf16[2,200,512]{2,1,0:T(8,128)(2,1)S(1)}, bf16[2,200,512]{2,1,0:T(8,128)(2,1)S(1)}, u32[]{:S(2)}, u32[]{:S(2)}) collective-permute-start(bf16[2,200,512]{2,1,0:T(8,128)(2,1)S(1)} %maximum_select_fusion), channel_id=1, source_target_pairs={{1,2},{3,4},{5,6},{7,8},{9,10},{11,12},{13,14},{2,1},{4,3},{6,5},{... | collective-permute-start | bytes 1228808 | tf_op jit(solution)/shard_map/ppermute | solution.py:49
  23.3 13.1 %collective-permute-start.9 = (bf16[2,200,512]{2,1,0:T(8,128)(2,1)S(1)}, bf16[2,200,512]{2,1,0:T(8,128)(2,1)S(1)}, u32[]{:S(2)}, u32[]{:S(2)}) collective-permute-start(bf16[2,200,512]{2,1,0:T(8,128)(2,1)S(1)} %get-tuple-element.55), channel_id=1, source_target_pairs={{1,2},{3,4},{5,6},{7,8},{9,10},{11,12},{13,14},{2,1},{4,3},{6,5},{... | collective-permute-start | bytes 1228808 | tf_op jit(solution)/shard_map/ppermute | solution.py:49
  30.8 6.7 %collective-permute-start.5 = (bf16[2,200,512]{2,1,0:T(8,128)(2,1)S(1)}, bf16[2,200,512]{2,1,0:T(8,128)(2,1)S(1)}, u32[]{:S(2)}, u32[]{:S(2)}) collective-permute-start(bf16[2,200,512]{2,1,0:T(8,128)(2,1)S(1)} %get-tuple-element.47), channel_id=1, source_target_pairs={{0,1},{2,3},{4,5},{6,7},{8,9},{10,11},{12,13},{14,15},{1,0},{3,2},... | collective-permute-start | bytes 1228808 | tf_op jit(solution)/shard_map/ppermute | solution.py:49
  30.9 13.7 %collective-permute-start.6 = (bf16[2,200,512]{2,1,0:T(8,128)(2,1)S(1)}, bf16[2,200,512]{2,1,0:T(8,128)(2,1)S(1)}, u32[]{:S(2)}, u32[]{:S(2)}) collective-permute-start(bf16[2,200,512]{2,1,0:T(8,128)(2,1)S(1)} %get-tuple-element.48), channel_id=1, source_target_pairs={{1,2},{3,4},{5,6},{7,8},{9,10},{11,12},{13,14},{2,1},{4,3},{6,5},{... | collective-permute-start | bytes 1228808 | tf_op jit(solution)/shard_map/ppermute | solution.py:49
  34.5 1.5 %collective-permute-start.8 = (bf16[2,200,256]{2,1,0:T(8,128)(2,1)S(1)}, bf16[2,200,256]{2,1,0:T(8,128)(2,1)S(1)}, u32[]{:S(2)}, u32[]{:S(2)}) collective-permute-start(bf16[2,200,256]{2,1,0:T(8,128)(2,1)S(1)} %get-tuple-element.54), channel_id=1, source_target_pairs={{0,1},{2,3},{4,5},{6,7},{8,9},{10,11},{12,13},{14,15},{1,0},{3,2},... | collective-permute-start | bytes 614408 | tf_op jit(solution)/shard_map/ppermute | solution.py:49
  34.6 1.7 %collective-permute-start.7 = (bf16[2,200,256]{2,1,0:T(8,128)(2,1)S(1)}, bf16[2,200,256]{2,1,0:T(8,128)(2,1)S(1)}, u32[]{:S(2)}, u32[]{:S(2)}) collective-permute-start(bf16[2,200,256]{2,1,0:T(8,128)(2,1)S(1)} %get-tuple-element.51), channel_id=1, source_target_pairs={{0,1},{2,3},{4,5},{6,7},{8,9},{10,11},{12,13},{14,15},{1,0},{3,2},... | collective-permute-start | bytes 614408 | tf_op jit(solution)/shard_map/ppermute | solution.py:49

commit v11 on v8

--- a/solution.py
+++ b/solution.py
@@ -16,7 +16,7 @@
 PAIRS = HEADS // 2
 SCALE = HEAD_DIM**-0.5
 LOG2_E = math.log2(math.e)
-BLOCK = 32
+BLOCK = 16
 OUTSIDE = -1e30
 CHUNKS = (0, 4, 8)
 NEXT_CHUNKS = (0, 2, 4, 8)

time: 45.2 us -> 45.3 us (level)
  no operation moved by 1% of the time
where the time goes in v11:
time: 45.3 us; the launch traced here: 45 us
  starting transfers between devices  18.4 us (41%)
  Pallas kernels  12.7 us (28%)
  waiting for transfers between devices  11.6 us (26%)
  local copies, waits for them, and re-layouts  1.28 us (3%)
  between operations  0.89 us (2%)
    ppermute x9, starting transfers between devices, swapped(): lax.ppermute(value, 'band', pairs + [(high, low) for low, high in pairs])  18.4 us
    pallas_call x4, Pallas kernels, chunk_call(): pl.pallas_call(functools.partial(kernel, len(carried)), in_specs=[vmem] *...  12.7 us
    ppermute x9, waiting for transfers between devices, swapped(): lax.ppermute(value, 'band', pairs + [(high, low) for low, high in pairs])  11.6 us
    another operation x5, local copies, waits for them, and re-layouts, pack(): last = jnp.stack([field[points - rows:, columns] for field in sources])  1.26 us
  transfers between devices with their start and end apart: 9, of which 4 were waited for; matrix products, arithmetic and copies ran while one was open for 0% of the time, Pallas kernels for 26%

profile of v11, /device:TPU:9, one launch (start us, length us, event | category | flops | bytes accessed | tf_op | source)
XLA Modules:
  0.0 45.0 jit_solution(2973783516494343632)
XLA Ops:
  0.6 0.0 copy-start
  0.7 0.0 copy-start.1
  0.7 1.2 %slice_bitcast_fusion.8 = (bf16[1,200,256]{2,1,0:T(8,128)(2,1)S(1)}, bf16[1,200,256]{2,1,0:T(8,128)(2,1)S(1)}, bf16[1,200,256]{2,1,0:T(8,128)(2,1)S(1)}, bf16[1,200,256]{2,1,0:T(8,128)(2,1)S(1)}) fusion(bf16[256,1024]{1,0:T(8,128)(2,1)} %refs_4_.3, bf16[256,1024]{1,0:T(8,128)(2,1)} %refs_3_.3), kind=kLoop, calls=%fused_computation.11 | loop fusion | bytes 819200 | tf_op jit(solution)/shard_map/stack | solution.py:74
  1.9 3.7 %collective-permute-start.2 = (bf16[2,200,256]{2,1,0:T(8,128)(2,1)S(1)}, bf16[2,200,256]{2,1,0:T(8,128)(2,1)S(1)}, u32[]{:S(2)}, u32[]{:S(2)}) collective-permute-start(bf16[2,200,256]{2,1,0:T(8,128)(2,1)S(1)} %maximum_select_fusion.1), channel_id=1, source_target_pairs={{1,2},{3,4},{5,6},{7,8},{9,10},{11,12},{13,14},{2,1},{4,3},{6,5},{... | collective-permute-start | bytes 614408 | tf_op jit(solution)/shard_map/ppermute | solution.py:47
  5.6 0.0 copy-done
  5.6 0.1 collective-permute-start
  5.7 0.0 copy-done.1
  5.7 0.5 %collective-permute-start.1 = (bf16[256,1024]{1,0:T(8,128)(2,1)S(1)}, bf16[256,1024]{1,0:T(8,128)(2,1)S(1)}, u32[]{:S(2)}, u32[]{:S(2)}) collective-permute-start(bf16[256,1024]{1,0:T(8,128)(2,1)S(1)} %copy-done.1), channel_id=1, source_target_pairs={{0,1},{2,3},{4,5},{6,7},{8,9},{10,11},{12,13},{14,15},{1,0},{3,2},... | collective-permute-start | bytes 1572872 | tf_op jit(solution)/shard_map/ppermute | solution.py:47
  6.2 0.0 copy-start.4
  6.3 3.1 %collective-permute-start.4 = (bf16[2,200,256]{2,1,0:T(8,128)(2,1)S(1)}, bf16[2,200,256]{2,1,0:T(8,128)(2,1)S(1)}, u32[]{:S(2)}, u32[]{:S(2)}) collective-permute-start(bf16[2,200,256]{2,1,0:T(8,128)(2,1)S(1)} %maximum_select_fusion.2), channel_id=1, source_target_pairs={{1,2},{3,4},{5,6},{7,8},{9,10},{11,12},{13,14},{2,1},{4,3},{6,5},{... | collective-permute-start | bytes 614408 | tf_op jit(solution)/shard_map/ppermute | solution.py:47
  9.4 0.0 copy-done.4
  9.4 0.0 collective-permute-done.refs_5_
  9.4 0.0 collective-permute-done.1.refs_6_
  9.5 0.0 copy-start.2
  9.5 0.0 copy-start.3
  9.6 0.1 maximum_select_fusion
  9.6 1.6 %collective-permute-done.2.refs_7_ = bf16[2,200,256]{2,1,0:T(8,128)(2,1)S(1)} collective-permute-done((bf16[2,200,256]{2,1,0:T(8,128)(2,1)S(1)}, bf16[2,200,256]{2,1,0:T(8,128)(2,1)S(1)}, u32[]{:S(2)}, u32[]{:S(2)}) %collective-permute-start.2) | collective-permute-done | bytes 204832 | tf_op jit(solution)/shard_map/ppermute | solution.py:47
  11.2 3.6 %collective-permute-start.3 = (bf16[2,200,512]{2,1,0:T(8,128)(2,1)S(1)}, bf16[2,200,512]{2,1,0:T(8,128)(2,1)S(1)}, u32[]{:S(2)}, u32[]{:S(2)}) collective-permute-start(bf16[2,200,512]{2,1,0:T(8,128)(2,1)S(1)} %maximum_select_fusion), channel_id=1, source_target_pairs={{1,2},{3,4},{5,6},{7,8},{9,10},{11,12},{13,14},{2,1},{4,3},{6,5},{... | collective-permute-start | bytes 1228808 | tf_op jit(solution)/shard_map/ppermute | solution.py:47
  14.9 0.8 %collective-permute-done.4.refs_8_ = bf16[2,200,256]{2,1,0:T(8,128)(2,1)S(1)} collective-permute-done((bf16[2,200,256]{2,1,0:T(8,128)(2,1)S(1)}, bf16[2,200,256]{2,1,0:T(8,128)(2,1)S(1)}, u32[]{:S(2)}, u32[]{:S(2)}) %collective-permute-start.4) | collective-permute-done | bytes 204832 | tf_op jit(solution)/shard_map/ppermute | solution.py:47
  15.6 0.0 copy-done.2
  15.6 0.0 copy-done.3
  15.6 5.2 %attention_0.1 = (bf16[256,1024]{1,0:T(8,128)(2,1)}, bf16[256,1024]{1,0:T(8,128)(2,1)}, bf16[2,200,512]{2,1,0:T(8,128)(2,1)S(1)}, bf16[2,200,512]{2,1,0:T(8,128)...) custom-call(s32[2,256]{1,0:T(2,128)S(1)} %subtract_bitcast_fusion.refs_0_, bf16[256,1024]{1,0:T(8,128)(2,1)S(1)} %copy-done.2, ...), custom_call_target="tpu_custom_call" | custom-call | flops 8556380160 | bytes 5373952 | tf_op jit(solution)/shard_map/attention_0/pallas_call | solution.py:325
  20.9 0.1 collective-permute-start.7
  20.9 3.7 %collective-permute-start.8 = (bf16[2,200,512]{2,1,0:T(8,128)(2,1)S(1)}, bf16[2,200,512]{2,1,0:T(8,128)(2,1)S(1)}, u32[]{:S(2)}, u32[]{:S(2)}) collective-permute-start(bf16[2,200,512]{2,1,0:T(8,128)(2,1)S(1)} %get-tuple-element.45), channel_id=1, source_target_pairs={{1,2},{3,4},{5,6},{7,8},{9,10},{11,12},{13,14},{2,1},{4,3},{6,5},{... | collective-permute-start | bytes 1228808 | tf_op jit(solution)/shard_map/ppermute | solution.py:47
  24.6 0.0 collective-permute-done.3.refs_7_
  24.6 5.3 %attention_1.1 = (bf16[256,1024]{1,0:T(8,128)(2,1)}, bf16[256,1024]{1,0:T(8,128)(2,1)}, bf16[2,200,512]{2,1,0:T(8,128)(2,1)S(1)}, bf16[2,200,512]{2,1,0:T(8,128)...) custom-call(s32[2,256]{1,0:T(2,128)S(1)} %subtract_bitcast_fusion.refs_0_, ...), custom_call_target="tpu_custom_call", output_to_operand_aliasing={{0}: (8, {}), {1}: (9, {})} | custom-call | flops 8556380160 | bytes 5373952 | tf_op jit(solution)/shard_map/attention_1/pallas_call | solution.py:325
  29.9 0.4 collective-permute-start.5
  30.3 3.3 %collective-permute-start.6 = (bf16[2,200,512]{2,1,0:T(8,128)(2,1)S(1)}, bf16[2,200,512]{2,1,0:T(8,128)(2,1)S(1)}, u32[]{:S(2)}, u32[]{:S(2)}) collective-permute-start(bf16[2,200,512]{2,1,0:T(8,128)(2,1)S(1)} %get-tuple-element.41), channel_id=1, source_target_pairs={{1,2},{3,4},{5,6},{7,8},{9,10},{11,12},{13,14},{2,1},{4,3},{6,5},{... | collective-permute-start | bytes 1228808 | tf_op jit(solution)/shard_map/ppermute | solution.py:47
  33.6 0.0 collective-permute-done.7.refs_2_
  33.6 1.0 %collective-permute-done.8.refs_3_ = bf16[2,200,512]{2,1,0:T(8,128)(2,1)S(1)} collective-permute-done((bf16[2,200,512]{2,1,0:T(8,128)(2,1)S(1)}, bf16[2,200,512]{2,1,0:T(8,128)(2,1)S(1)}, u32[]{:S(2)}, u32[]{:S(2)}) %collective-permute-start.8) | collective-permute-done | bytes 409632 | tf_op jit(solution)/shard_map/ppermute | solution.py:47
  34.6 1.1 %gradient_sums_0.1 = (bf16[256,1024]{1,0:T(8,128)(2,1)}, bf16[256,1024]{1,0:T(8,128)(2,1)}) custom-call(f32[256,512]{1,0:T(8,128)S(1)} %get-tuple-element.42.refs_0_, f32[256,512]{1,0:T(8,128)S(1)} %get-tuple-element.43.refs_1_, bf16[2,200,512]{2,1,0:T(8,128)(2,1)S(1)} %collective-permute-done.7.refs_2_, bf16[2,200,512]{2,1,0:T(8,128)(2,1)S(1)} %collective-permute-done.8.refs_3_), custom_call_target="tpu_custom_call" | custom-call | flops 786432 | bytes 2621440 | tf_op jit(solution)/shard_map/gradient_sums_0/pallas_call | solution.py:325
  35.7 0.0 collective-permute-done.5.refs_2_
  35.7 8.2 %collective-permute-done.6.refs_3_ = bf16[2,200,512]{2,1,0:T(8,128)(2,1)S(1)} collective-permute-done((bf16[2,200,512]{2,1,0:T(8,128)(2,1)S(1)}, bf16[2,200,512]{2,1,0:T(8,128)(2,1)S(1)}, u32[]{:S(2)}, u32[]{:S(2)}) %collective-permute-start.6) | collective-permute-done | bytes 409632 | tf_op jit(solution)/shard_map/ppermute | solution.py:47
  44.0 1.1 %gradient_sums_1.1 = (bf16[256,1024]{1,0:T(8,128)(2,1)}, bf16[256,1024]{1,0:T(8,128)(2,1)}) custom-call(f32[256,512]{1,0:T(8,128)S(1)} %get-tuple-element.38.refs_0_, f32[256,512]{1,0:T(8,128)S(1)} %get-tuple-element.39.refs_1_, bf16[2,200,512]{2,1,0:T(8,128)(2,1)S(1)} %collective-permute-done.5.refs_2_, ...), custom_call_target="tpu_custom_call", output_to_operand_aliasing={{0}: (4, {}), {1}: (5, {})} | custom-call | flops 786432 | bytes 2621440 | tf_op jit(solution)/shard_map/gradient_sums_1/pallas_call | solution.py:325
  (7 shorter events, 0.2 us)
Async XLA Ops:
  0.6 4.9 %copy-start = (bf16[256,1024]{1,0:T(8,128)(2,1)S(1)}, bf16[256,1024]{1,0:T(8,128)(2,1)}, u32[]{:S(2)}) copy-start(bf16[256,1024]{1,0:T(8,128)(2,1)} %refs_3_.3) | copy-start | bytes 1572868
  0.7 5.0 %copy-start.1 = (bf16[256,1024]{1,0:T(8,128)(2,1)S(1)}, bf16[256,1024]{1,0:T(8,128)(2,1)}, u32[]{:S(2)}) copy-start(bf16[256,1024]{1,0:T(8,128)(2,1)} %refs_4_.3) | copy-start | bytes 1572868
  1.9 9.3 %collective-permute-start.2 = (bf16[2,200,256]{2,1,0:T(8,128)(2,1)S(1)}, bf16[2,200,256]{2,1,0:T(8,128)(2,1)S(1)}, u32[]{:S(2)}, u32[]{:S(2)}) collective-permute-start(bf16[2,200,256]{2,1,0:T(8,128)(2,1)S(1)} %maximum_select_fusion.1), channel_id=1, source_target_pairs={{1,2},{3,4},{5,6},{7,8},{9,10},{11,12},{13,14},{2,1},{4,3},{6,5},{... | collective-permute-start | bytes 614408 | tf_op jit(solution)/shard_map/ppermute | solution.py:47
  5.6 3.8 %collective-permute-start = (bf16[256,1024]{1,0:T(8,128)(2,1)S(1)}, bf16[256,1024]{1,0:T(8,128)(2,1)S(1)}, u32[]{:S(2)}, u32[]{:S(2)}) collective-permute-start(bf16[256,1024]{1,0:T(8,128)(2,1)S(1)} %copy-done), channel_id=1, source_target_pairs={{0,1},{2,3},{4,5},{6,7},{8,9},{10,11},{12,13},{14,15},{1,0},{3,2},... | collective-permute-start | bytes 1572872 | tf_op jit(solution)/shard_map/ppermute | solution.py:47
  5.7 3.8 %collective-permute-start.1 = (bf16[256,1024]{1,0:T(8,128)(2,1)S(1)}, bf16[256,1024]{1,0:T(8,128)(2,1)S(1)}, u32[]{:S(2)}, u32[]{:S(2)}) collective-permute-start(bf16[256,1024]{1,0:T(8,128)(2,1)S(1)} %copy-done.1), channel_id=1, source_target_pairs={{0,1},{2,3},{4,5},{6,7},{8,9},{10,11},{12,13},{14,15},{1,0},{3,2},... | collective-permute-start | bytes 1572872 | tf_op jit(solution)/shard_map/ppermute | solution.py:47
  6.2 3.2 %copy-start.4 = (s32[256,2]{0,1:T(2,128)S(1)}, s32[256,2]{0,1:T(2,128)}, u32[]{:S(2)}) copy-start(s32[256,2]{0,1:T(2,128)} %param.9) | copy-start | bytes 6148
  6.3 9.3 %collective-permute-start.4 = (bf16[2,200,256]{2,1,0:T(8,128)(2,1)S(1)}, bf16[2,200,256]{2,1,0:T(8,128)(2,1)S(1)}, u32[]{:S(2)}, u32[]{:S(2)}) collective-permute-start(bf16[2,200,256]{2,1,0:T(8,128)(2,1)S(1)} %maximum_select_fusion.2), channel_id=1, source_target_pairs={{1,2},{3,4},{5,6},{7,8},{9,10},{11,12},{13,14},{2,1},{4,3},{6,5},{... | collective-permute-start | bytes 614408 | tf_op jit(solution)/shard_map/ppermute | solution.py:47
  9.5 6.1 %copy-start.2 = (bf16[256,1024]{1,0:T(8,128)(2,1)S(1)}, bf16[256,1024]{1,0:T(8,128)(2,1)}, u32[]{:S(2)}) copy-start(bf16[256,1024]{1,0:T(8,128)(2,1)} %refs_1_.3) | copy-start | bytes 1572868
  9.5 6.1 %copy-start.3 = (bf16[256,1024]{1,0:T(8,128)(2,1)S(1)}, bf16[256,1024]{1,0:T(8,128)(2,1)}, u32[]{:S(2)}) copy-start(bf16[256,1024]{1,0:T(8,128)(2,1)} %refs_2_.3) | copy-start | bytes 1572868
  11.2 13.4 %collective-permute-start.3 = (bf16[2,200,512]{2,1,0:T(8,128)(2,1)S(1)}, bf16[2,200,512]{2,1,0:T(8,128)(2,1)S(1)}, u32[]{:S(2)}, u32[]{:S(2)}) collective-permute-start(bf16[2,200,512]{2,1,0:T(8,128)(2,1)S(1)} %maximum_select_fusion), channel_id=1, source_target_pairs={{1,2},{3,4},{5,6},{7,8},{9,10},{11,12},{13,14},{2,1},{4,3},{6,5},{... | collective-permute-start | bytes 1228808 | tf_op jit(solution)/shard_map/ppermute | solution.py:47
  20.9 12.7 %collective-permute-start.7 = (bf16[2,200,512]{2,1,0:T(8,128)(2,1)S(1)}, bf16[2,200,512]{2,1,0:T(8,128)(2,1)S(1)}, u32[]{:S(2)}, u32[]{:S(2)}) collective-permute-start(bf16[2,200,512]{2,1,0:T(8,128)(2,1)S(1)} %get-tuple-element.44), channel_id=1, source_target_pairs={{0,1},{2,3},{4,5},{6,7},{8,9},{10,11},{12,13},{14,15},{1,0},{3,2},... | collective-permute-start | bytes 1228808 | tf_op jit(solution)/shard_map/ppermute | solution.py:47
  20.9 13.7 %collective-permute-start.8 = (bf16[2,200,512]{2,1,0:T(8,128)(2,1)S(1)}, bf16[2,200,512]{2,1,0:T(8,128)(2,1)S(1)}, u32[]{:S(2)}, u32[]{:S(2)}) collective-permute-start(bf16[2,200,512]{2,1,0:T(8,128)(2,1)S(1)} %get-tuple-element.45), channel_id=1, source_target_pairs={{1,2},{3,4},{5,6},{7,8},{9,10},{11,12},{13,14},{2,1},{4,3},{6,5},{... | collective-permute-start | bytes 1228808 | tf_op jit(solution)/shard_map/ppermute | solution.py:47
  29.9 5.8 %collective-permute-start.5 = (bf16[2,200,512]{2,1,0:T(8,128)(2,1)S(1)}, bf16[2,200,512]{2,1,0:T(8,128)(2,1)S(1)}, u32[]{:S(2)}, u32[]{:S(2)}) collective-permute-start(bf16[2,200,512]{2,1,0:T(8,128)(2,1)S(1)} %get-tuple-element.40), channel_id=1, source_target_pairs={{0,1},{2,3},{4,5},{6,7},{8,9},{10,11},{12,13},{14,15},{1,0},{3,2},... | collective-permute-start | bytes 1228808 | tf_op jit(solution)/shard_map/ppermute | solution.py:47
  30.3 13.6 %collective-permute-start.6 = (bf16[2,200,512]{2,1,0:T(8,128)(2,1)S(1)}, bf16[2,200,512]{2,1,0:T(8,128)(2,1)S(1)}, u32[]{:S(2)}, u32[]{:S(2)}) collective-permute-start(bf16[2,200,512]{2,1,0:T(8,128)(2,1)S(1)} %get-tuple-element.41), channel_id=1, source_target_pairs={{1,2},{3,4},{5,6},{7,8},{9,10},{11,12},{13,14},{2,1},{4,3},{6,5},{... | collective-permute-start | bytes 1228808 | tf_op jit(solution)/shard_map/ppermute | solution.py:47

commit v12 on v8

--- a/solution.py
+++ b/solution.py
@@ -79,7 +79,16 @@
     return (rows + 15) // 16 * 16
 
 
-def attention_kernel(rim_width, lengths, points, low_pair, next_pairs, carried, *refs):
+def head_blocks(turned, half):
+    return [turned[:HEAD_DIM, :half], turned[HEAD_DIM:, half:]]
+
+
+def query_gradient(turned_keys, dscores, half):
+    dq = head_blocks(dot_nn(turned_keys, dscores), half)
+    return jnp.concatenate([(x * SCALE).astype(jnp.bfloat16) for x in dq], axis=0).T
+
+
+def attention_kernel(rim_width, lengths, points, low_pair, next_pairs, deferred, carried, *refs):
     far = len(lengths) // 2 - 1
     near = lengths[far]
     half = points // 2
@@ -95,6 +104,7 @@
     att_out, dq_out, to_partner_ref, to_next_ref, dk_ref, dv_ref = outs[:6]
     to_far_refs = outs[6 : 6 + 2 * far]
     (bias_ref, keys_ref, turned_ref, exps_ref, probs_ref, dscores_ref, att_ref, dq_ref, sems) = outs[-9:]
+    kept_scores, kept_keys = outs[6 + 2 * far : 8 + 2 * far] if deferred else (None, None)
     even = is_even()
     owns = [slice(part * half, (part + 1) * half) for part in range(2)]
     spans_of = [slice(part * half, part * half + reached) for part in range(2)]
@@ -148,7 +158,10 @@
             for at in range(far, 2 * far):
                 into[slot, start : start + lengths[at + 2], :] = far_refs[at][slot, :, columns]
                 start += lengths[at + 2]
-            turned_ref[pair % 2, slot] = into[slot].T
+            if deferred and slot == 0:
+                kept_keys[pair] = into[slot].T
+            else:
+                turned_ref[pair % 2, slot] = into[slot].T
 
     def fold(op, total, block):
         for row in range(0, BLOCK, 8):
@@ -156,7 +169,13 @@
         return total
 
     def both(turned):
-        return [turned[:HEAD_DIM, :half], turned[HEAD_DIM:, half:]]
+        return head_blocks(turned, half)
+
+    def dscores_of(pair, part):
+        return kept_scores.at[pair, part] if deferred else dscores_ref.at[pair % 2, part]
+
+    def probs_of(pair, part):
+        return probs_ref.at[pair % 2, part]
 
     def q_both(pair, part):
         q = q_ref[owns[part], columns_of(pair)]
@@ -215,20 +234,19 @@
         dprobs = dot_nt(keys_ref[pair % 2, 1, spans_of[part], :], g_both(pair, part))
         for block in blocks:
             probs = exps_ref[pair % 2, part, block, :] * inverse
-            dscores_ref[pair % 2, part, block, :] = (probs * (dprobs[block] - delta)).astype(jnp.bfloat16)
+            dscores_of(pair, part)[block, :] = (probs * (dprobs[block] - delta)).astype(jnp.bfloat16)
 
     copies = []
 
     def backward_outputs(pair):
-        for part in range(2):
-            dq = both(dot_nn(turned_ref[pair % 2, 0, :, spans_of[part]], dscores_ref[pair % 2, part]))
-            dq_ref[pair, owns[part], :] = jnp.concatenate(
-                [(x * SCALE).astype(jnp.bfloat16) for x in dq], axis=0
-            ).T
-        for slot, (scores_ref, own_both, own_ref) in enumerate(
-            [(dscores_ref, q_both, dk_ref), (probs_ref, g_both, dv_ref)]
+        for part in range(0 if deferred else 2):
+            dq_ref[pair, owns[part], :] = query_gradient(
+                turned_ref[pair % 2, 0, :, spans_of[part]], dscores_of(pair, part)[...], half
+            )
+        for slot, (scores_of, own_both, own_ref) in enumerate(
+            [(dscores_of, q_both, dk_ref), (probs_of, g_both, dv_ref)]
         ):
-            low_scores, high_scores = (scores_ref.at[pair % 2, part] for part in range(2))
+            low_scores, high_scores = (scores_of(pair, part) for part in range(2))
             low, high = (own_both(pair, part) for part in range(2))
             shared = jnp.concatenate([low_scores[half:, :], high_scores[: reached - half, :]], axis=1)
             sums = [
@@ -267,7 +285,8 @@
 
     def finish(pair):
         backward_outputs(pair)
-        for at, (ref, out) in enumerate([(att_ref, att_out), (dq_ref, dq_out)]):
+        sent = [(att_ref, att_out)] + ([] if deferred else [(dq_ref, dq_out)])
+        for at, (ref, out) in enumerate(sent):
             copy = pltpu.make_async_copy(ref.at[pair], out.at[:, columns_of(pair)], sems.at[at, pair])
             copy.start()
             copies.append(copy)
@@ -287,6 +306,24 @@
         delta = forward_outputs(*unit)
         backward_scores(*unit, inverse, delta)
     finish(units[-1][0])
+    for copy in copies:
+        copy.wait()
+
+
+def query_kernel(points, low_pair, reached, carried, *refs):
+    scores_ref, keys_ref = refs[:2]
+    dq_out, dq_ref, sems = refs[2 + carried :]
+    half = points // 2
+    copies = []
+    for pair in range(scores_ref.shape[0]):
+        for part in range(2):
+            span = slice(part * half, part * half + reached)
+            dq_ref[pair, part * half : (part + 1) * half, :] = query_gradient(
+                keys_ref[pair, :, span], scores_ref[pair, part], half
+            )
+        columns = slice((low_pair + pair) * PAIR, (low_pair + pair + 1) * PAIR)
+        copies.append(pltpu.make_async_copy(dq_ref.at[pair], dq_out.at[:, columns], sems.at[pair]))
+        copies[-1].start()
     for copy in copies:
         copy.wait()
 
@@ -369,6 +406,10 @@
     for chunk, (low, high) in enumerate(spans(CHUNKS)):
         count = high - low
         chunk_width = count * PAIR
+        kept_shapes = [
+            jax.ShapeDtypeStruct((count, 2, reached, points), jnp.bfloat16),
+            jax.ShapeDtypeStruct((count, PAIR, wide), jnp.bfloat16),
+        ]
         parts = [
             (at, last - first)
             for at, (first, last) in enumerate(spans(NEXT_CHUNKS))
@@ -377,7 +418,9 @@
         next_pairs = [size for _, size in parts]
         assert sum(next_pairs) == count
         outs = chunk_call(
-            functools.partial(attention_kernel, rim_width, lengths, points, low, next_pairs),
+            functools.partial(
+                attention_kernel, rim_width, lengths, points, low, next_pairs, chunk == 0
+            ),
             [relative, queries, grad_out, keys, values, *from_partner]
             + [from_next[at] for at, _ in parts]
             + from_far,
@@ -386,7 +429,8 @@
             [whole] * 2
             + [jax.ShapeDtypeStruct((2, near, chunk_width), jnp.bfloat16)] * 2
             + [jax.ShapeDtypeStruct((points, chunk_width), jnp.float32)] * 2
-            + [jax.ShapeDtypeStruct((2, size, chunk_width), jnp.bfloat16) for size in far_sizes],
+            + [jax.ShapeDtypeStruct((2, size, chunk_width), jnp.bfloat16) for size in far_sizes]
+            + (kept_shapes if chunk == 0 else []),
             48 * wide * points + 12 * 2**20,
             scratch_shapes=[
                 pltpu.VMEM((2, reached, points), jnp.float32),
@@ -407,9 +451,31 @@
             name=f"attention_{chunk}",
         )
         own_terms.append(outs[4:6])
+        if chunk == 0:
+            kept = outs[6 + len(far) :]
         back_partner.append(swapped(outs[2], 0))
         back_next.append(swapped(outs[3], 1))
-        back_far.append([passed_along(term, d) for term, d in zip(outs[6:], far)])
+        back_far.append([passed_along(term, d) for term, d in zip(outs[6 : 6 + len(far)], far)])
+
+    first_pairs = CHUNKS[1]
+    grad_q = chunk_call(
+        functools.partial(query_kernel, points, 0, reached),
+        kept,
+        [outs[1]],
+        1,
+        [whole],
+        16 * wide * points + 8 * 2**20,
+        scratch_shapes=[
+            pltpu.VMEM((first_pairs, points, PAIR), jnp.bfloat16),
+            pltpu.SemaphoreType.DMA((first_pairs,)),
+        ],
+        cost_estimate=pl.CostEstimate(
+            flops=first_pairs * 4 * reached * points * PAIR,
+            bytes_accessed=first_pairs * 4 * reached * points,
+            transcendentals=0,
+        ),
+        name="query_gradients",
+    )[0]
 
     grads = []
     for chunk, (low, high) in enumerate(spans(CHUNKS)):
@@ -433,7 +499,7 @@
             ),
             name=f"gradient_sums_{chunk}",
         )
-    return (outs[0], outs[1], grads[0], grads[1])
+    return (outs[0], grad_q, grads[0], grads[1])
 
 
 def solution(mesh):

time: 45.2 us -> 48.3 us (1.069)
  other arithmetic: 0.16 us -> 2.2 us
  starting transfers between devices: 18.5 us -> 16.5 us
  local copies, waits for them, and re-layouts: 1.28 us -> 3.21 us
  Pallas kernels: 12.6 us -> 13.6 us
    ppermute x9, starting transfers between devices: 18.5 us -> 16.5 us  [swapped(): lax.ppermute(value, 'band', pairs + [(high, low) for low, high in pairs])]
    another operation x5, local copies, waits for them, and re-layouts: 1.26 us -> 3.19 us  [pack(): last = jnp.stack([field[points - rows:, columns] for field in sources])]
    select_n x3, other arithmetic: 0.15 us -> 1.51 us  [pack(): return jnp.where(is_even(), first, last)]
    pallas_call x4 -> x5, Pallas kernels: 12.6 us -> 13.6 us  [chunk_call(): pl.pallas_call(functools.partial(kernel, len(carried)), in_specs=[vmem] *...]
    transpose x1, other arithmetic: 0.01 us -> 0.69 us  [per_device(): relative = (windows - band * points).T]
  transfers between devices with their start and end apart: 9 -> 9, of which waited for: 4 -> 4; matrix products, arithmetic and copies ran while one was open for 0% -> 7% of each run, Pallas kernels for 26% -> 26%
where the time goes in v12:
time: 48.3 us; the launch traced here: 48 us
  starting transfers between devices  16.5 us (34%)
  Pallas kernels  13.6 us (28%)
  waiting for transfers between devices  11.6 us (24%)
  local copies, waits for them, and re-layouts  3.21 us (7%)
  other arithmetic  2.2 us (5%)
  between operations  0.83 us (2%)
    ppermute x9, starting transfers between devices, swapped(): lax.ppermute(value, 'band', pairs + [(high, low) for low, high in pairs])  16.5 us
    pallas_call x5, Pallas kernels, chunk_call(): pl.pallas_call(functools.partial(kernel, len(carried)), in_specs=[vmem] *...  13.6 us
    ppermute x9, waiting for transfers between devices, swapped(): lax.ppermute(value, 'band', pairs + [(high, low) for low, high in pairs])  11.6 us
    another operation x5, local copies, waits for them, and re-layouts, pack(): last = jnp.stack([field[points - rows:, columns] for field in sources])  3.19 us
    select_n x3, other arithmetic, pack(): return jnp.where(is_even(), first, last)  1.51 us
  transfers between devices with their start and end apart: 9, of which 4 were waited for; matrix products, arithmetic and copies ran while one was open for 7% of the time, Pallas kernels for 26%

profile of v12, /device:TPU:9, one launch (start us, length us, event | category | flops | bytes accessed | tf_op | source)
XLA Modules:
  0.0 48.0 jit_solution(16974248569703845796)
XLA Ops:
  0.6 0.0 copy-start
  0.6 0.0 copy-start.1
  0.7 1.2 %slice_bitcast_fusion.8 = (bf16[1,200,256]{2,1,0:T(8,128)(2,1)S(1)}, bf16[1,200,256]{2,1,0:T(8,128)(2,1)S(1)}, bf16[1,200,256]{2,1,0:T(8,128)(2,1)S(1)}, bf16[1,200,256]{2,1,0:T(8,128)(2,1)S(1)}) fusion(bf16[256,1024]{1,0:T(8,128)(2,1)} %refs_4_.3, bf16[256,1024]{1,0:T(8,128)(2,1)} %refs_3_.3), kind=kLoop, calls=%fused_computation.11 | loop fusion | bytes 819200 | tf_op jit(solution)/shard_map/stack | solution.py:74
  1.8 0.7 %maximum_select_fusion.1 = bf16[2,200,256]{2,1,0:T(8,128)(2,1)} fusion(bf16[1,200,256]{2,1,0:T(8,128)(2,1)S(1)} %get-tuple-element.65, bf16[1,200,256]{2,1,0:T(8,128)(2,1)S(1)} %get-tuple-element.66, bf16[1,200,256]{2,1,0:T(8,128)(2,1)S(1)} %get-tuple-element.64, bf16[1,200,256]{2,1,0:T(8,128)(2,1)S(1)} %get-tuple-element.67, pred[]{:T(512)S(6)} %eq.9), kind=kLoop, calls=%fused_computation.1 | loop fusion | flops 307200 | bytes 614401 | tf_op jit(solution)/shard_map/jit(_where)/select_n | solution.py:75
  2.5 0.0 copy-start.2
  2.6 0.0 copy-start.3
  2.6 3.8 %collective-permute-start.2 = (bf16[2,200,256]{2,1,0:T(8,128)(2,1)}, bf16[2,200,256]{2,1,0:T(8,128)(2,1)S(1)}, u32[]{:S(2)}, u32[]{:S(2)}) collective-permute-start(bf16[2,200,256]{2,1,0:T(8,128)(2,1)} %maximum_select_fusion.1), channel_id=1, source_target_pairs={{1,2},{3,4},{5,6},{7,8},{9,10},{11,12},{13,14},{2,1},{4,3},{6,5},{... | collective-permute-start | bytes 614408 | tf_op jit(solution)/shard_map/ppermute | solution.py:47
  6.4 0.1 collective-permute-start
  6.5 0.5 %collective-permute-start.1 = (bf16[256,1024]{1,0:T(8,128)(2,1)}, bf16[256,1024]{1,0:T(8,128)(2,1)S(1)}, u32[]{:S(2)}, u32[]{:S(2)}) collective-permute-start(bf16[256,1024]{1,0:T(8,128)(2,1)} %refs_4_.3), channel_id=1, source_target_pairs={{0,1},{2,3},{4,5},{6,7},{8,9},{10,11},{12,13},{14,15},{1,0},{3,2},... | collective-permute-start | bytes 1572872 | tf_op jit(solution)/shard_map/ppermute | solution.py:47
  7.0 1.0 %slice_bitcast_fusion.5 = (bf16[1,200,256]{2,1,0:T(8,128)(2,1)S(1)}, bf16[1,200,256]{2,1,0:T(8,128)(2,1)S(1)}) fusion(bf16[256,1024]{1,0:T(8,128)(2,1)} %refs_3_.3), kind=kLoop, calls=%fused_computation.8 | loop fusion | bytes 409600 | tf_op jit(solution)/shard_map/stack | solution.py:74
  8.0 1.0 %slice_bitcast_fusion.4 = (bf16[1,200,256]{2,1,0:T(8,128)(2,1)S(1)}, bf16[1,200,256]{2,1,0:T(8,128)(2,1)S(1)}) fusion(bf16[256,1024]{1,0:T(8,128)(2,1)} %refs_4_.3), kind=kLoop, calls=%fused_computation.7 | loop fusion | bytes 409600 | tf_op jit(solution)/shard_map/stack | solution.py:74
  8.9 0.7 %maximum_select_fusion.2 = bf16[2,200,256]{2,1,0:T(8,128)(2,1)} fusion(bf16[1,200,256]{2,1,0:T(8,128)(2,1)S(1)} %get-tuple-element.61, bf16[1,200,256]{2,1,0:T(8,128)(2,1)S(1)} %get-tuple-element.59, bf16[1,200,256]{2,1,0:T(8,128)(2,1)S(1)} %get-tuple-element.60, bf16[1,200,256]{2,1,0:T(8,128)(2,1)S(1)} %get-tuple-element.58, pred[]{:T(512)S(6)} %eq.9), kind=kLoop, calls=%fused_computation.2 | loop fusion | flops 307200 | bytes 614401 | tf_op jit(solution)/shard_map/jit(_where)/select_n | solution.py:75
  9.7 3.1 %collective-permute-start.4 = (bf16[2,200,256]{2,1,0:T(8,128)(2,1)}, bf16[2,200,256]{2,1,0:T(8,128)(2,1)S(1)}, u32[]{:S(2)}, u32[]{:S(2)}) collective-permute-start(bf16[2,200,256]{2,1,0:T(8,128)(2,1)} %maximum_select_fusion.2), channel_id=1, source_target_pairs={{1,2},{3,4},{5,6},{7,8},{9,10},{11,12},{13,14},{2,1},{4,3},{6,5},{... | collective-permute-start | bytes 614408 | tf_op jit(solution)/shard_map/ppermute | solution.py:47
  12.8 0.7 %subtract_bitcast_fusion.refs_0_ = s32[2,256]{1,0:T(2,128)S(1)} fusion(s32[256,2]{0,1:T(2,128)} %param.9, s32[]{:T(128)S(6)} %mul.3), kind=kLoop, calls=%fused_computation.15 | loop fusion | flops 512 | bytes 4100 | tf_op jit(solution)/shard_map/transpose | solution.py:384
  13.5 0.0 collective-permute-done.refs_5_
  13.5 0.0 collective-permute-done.1.refs_6_
  13.5 0.0 copy-done
  13.5 0.0 copy-done.1
  13.6 0.1 maximum_select_fusion
  13.6 0.0 collective-permute-done.2.refs_7_
  13.7 2.4 %collective-permute-start.3 = (bf16[2,200,512]{2,1,0:T(8,128)(2,1)S(1)}, bf16[2,200,512]{2,1,0:T(8,128)(2,1)S(1)}, u32[]{:S(2)}, u32[]{:S(2)}) collective-permute-start(bf16[2,200,512]{2,1,0:T(8,128)(2,1)S(1)} %maximum_select_fusion), channel_id=1, source_target_pairs={{1,2},{3,4},{5,6},{7,8},{9,10},{11,12},{13,14},{2,1},{4,3},{6,5},{... | collective-permute-start | bytes 1228808 | tf_op jit(solution)/shard_map/ppermute | solution.py:47
  16.1 3.3 %collective-permute-done.4.refs_8_ = bf16[2,200,256]{2,1,0:T(8,128)(2,1)S(1)} collective-permute-done((bf16[2,200,256]{2,1,0:T(8,128)(2,1)}, bf16[2,200,256]{2,1,0:T(8,128)(2,1)S(1)}, u32[]{:S(2)}, u32[]{:S(2)}) %collective-permute-start.4) | collective-permute-done | bytes 204832 | tf_op jit(solution)/shard_map/ppermute | solution.py:47
  19.4 0.0 copy-done.2
  19.4 0.0 copy-done.3
  19.4 4.9 %attention_0.1 = (bf16[256,1024]{1,0:T(8,128)(2,1)}, bf16[256,1024]{1,0:T(8,128)(2,1)}, bf16[2,200,512]{2,1,0:T(8,128)(2,1)S(1)}, bf16[2,200,512]{2,1,0:T(8,128)...) custom-call(s32[2,256]{1,0:T(2,128)S(1)} %subtract_bitcast_fusion.re, ...), custom_call_target="tpu_custom_call" | custom-call | flops 8556380160 | bytes 5373952 | tf_op jit(solution)/shard_map/attention_0/pallas_call | solution.py:362
  24.4 0.1 collective-permute-start.7
  24.5 2.8 %collective-permute-start.8 = (bf16[2,200,512]{2,1,0:T(8,128)(2,1)S(1)}, bf16[2,200,512]{2,1,0:T(8,128)(2,1)S(1)}, u32[]{:S(2)}, u32[]{:S(2)}) collective-permute-start(bf16[2,200,512]{2,1,0:T(8,128)(2,1)S(1)} %get-tuple-element.49), channel_id=1, source_target_pairs={{1,2},{3,4},{5,6},{7,8},{9,10},{11,12},{13,14},{2,1},{4,3},{6,5},{... | collective-permute-start | bytes 1228808 | tf_op jit(solution)/shard_map/ppermute | solution.py:47
  27.3 0.6 %collective-permute-done.3.refs_7_ = bf16[2,200,512]{2,1,0:T(8,128)(2,1)S(1)} collective-permute-done((bf16[2,200,512]{2,1,0:T(8,128)(2,1)S(1)}, bf16[2,200,512]{2,1,0:T(8,128)(2,1)S(1)}, u32[]{:S(2)}, u32[]{:S(2)}) %collective-permute-start.3) | collective-permute-done | bytes 409632 | tf_op jit(solution)/shard_map/ppermute | solution.py:47
  27.9 5.2 %attention_1.1 = (bf16[256,1024]{1,0:T(8,128)(2,1)}, bf16[256,1024]{1,0:T(8,128)(2,1)}, bf16[2,200,512]{2,1,0:T(8,128)(2,1)S(1)}, bf16[2,200,512]{2,1,0:T(8,128)...) custom-call(s32[2,256]{1,0:T(2,128)S(1)} %subtract_bitcast_fusion.refs_0_, ...), custom_call_target="tpu_custom_call", output_to_operand_aliasing={{0}: (8, {}), {1}: (9, {})} | custom-call | flops 8556380160 | bytes 5373952 | tf_op jit(solution)/shard_map/attention_1/pallas_call | solution.py:362
  33.1 0.1 collective-permute-start.5
  33.2 3.6 %collective-permute-start.6 = (bf16[2,200,512]{2,1,0:T(8,128)(2,1)S(1)}, bf16[2,200,512]{2,1,0:T(8,128)(2,1)S(1)}, u32[]{:S(2)}, u32[]{:S(2)}) collective-permute-start(bf16[2,200,512]{2,1,0:T(8,128)(2,1)S(1)} %get-tuple-element.45), channel_id=1, source_target_pairs={{1,2},{3,4},{5,6},{7,8},{9,10},{11,12},{13,14},{2,1},{4,3},{6,5},{... | collective-permute-start | bytes 1228808 | tf_op jit(solution)/shard_map/ppermute | solution.py:47
  36.8 0.0 collective-permute-done.7.refs_2_
  36.9 1.3 %collective-permute-done.8.refs_3_ = bf16[2,200,512]{2,1,0:T(8,128)(2,1)S(1)} collective-permute-done((bf16[2,200,512]{2,1,0:T(8,128)(2,1)S(1)}, bf16[2,200,512]{2,1,0:T(8,128)(2,1)S(1)}, u32[]{:S(2)}, u32[]{:S(2)}) %collective-permute-start.8) | collective-permute-done | bytes 409632 | tf_op jit(solution)/shard_map/ppermute | solution.py:47
  38.1 1.1 %gradient_sums_0.1 = (bf16[256,1024]{1,0:T(8,128)(2,1)}, bf16[256,1024]{1,0:T(8,128)(2,1)}) custom-call(f32[256,512]{1,0:T(8,128)S(1)} %get-tuple-element.46.refs_0_, f32[256,512]{1,0:T(8,128)S(1)} %get-tuple-element.47.refs_1_, bf16[2,200,512]{2,1,0:T(8,128)(2,1)S(1)} %collective-permute-done.7.refs_2_, bf16[2,200,512]{2,1,0:T(8,128)(2,1)S(1)} %collective-permute-done.8.refs_3_), custom_call_target="tpu_custom_call" | custom-call | flops 786432 | bytes 2621440 | tf_op jit(solution)/shard_map/gradient_sums_0/pallas_call | solution.py:362
  39.2 1.3 %query_gradients.1 = bf16[256,1024]{1,0:T(8,128)(2,1)} custom-call(bf16[4,2,544,256]{3,2,1,0:T(8,128)(2,1)S(1)} %get-tuple-element.39.refs_0_, bf16[4,128,672]{2,1,0:T(8,128)(2,1)S(1)} %get-tuple-element.40.refs_1_, bf16[256,1024]{1,0:T(8,128)(2,1)} %get-tuple-element.41.refs_2_), custom_call_target="tpu_custom_call", output_to_operand_aliasing={{}: (2, {})} | custom-call | flops 285212672 | bytes 2228224 | tf_op jit(solution)/shard_map/query_gradients/pallas_call | solution.py:362
  40.5 0.0 collective-permute-done.5.refs_2_
  40.5 6.4 %collective-permute-done.6.refs_3_ = bf16[2,200,512]{2,1,0:T(8,128)(2,1)S(1)} collective-permute-done((bf16[2,200,512]{2,1,0:T(8,128)(2,1)S(1)}, bf16[2,200,512]{2,1,0:T(8,128)(2,1)S(1)}, u32[]{:S(2)}, u32[]{:S(2)}) %collective-permute-start.6) | collective-permute-done | bytes 409632 | tf_op jit(solution)/shard_map/ppermute | solution.py:47
  46.9 1.1 %gradient_sums_1.1 = (bf16[256,1024]{1,0:T(8,128)(2,1)}, bf16[256,1024]{1,0:T(8,128)(2,1)}) custom-call(f32[256,512]{1,0:T(8,128)S(1)} %get-tuple-element.42.refs_0_, f32[256,512]{1,0:T(8,128)S(1)} %get-tuple-element.43.refs_1_, bf16[2,200,512]{2,1,0:T(8,128)(2,1)S(1)} %collective-permute-done.5.refs_2_, ...), custom_call_target="tpu_custom_call", output_to_operand_aliasing={{0}: (4, {}), {1}: (5, {})} | custom-call | flops 786432 | bytes 2621440 | tf_op jit(solution)/shard_map/gradient_sums_1/pallas_call | solution.py:362
  (2 shorter events, 0.1 us)
Async XLA Ops:
  0.6 12.8 %copy-start = (bf16[256,1024]{1,0:T(8,128)(2,1)S(1)}, bf16[256,1024]{1,0:T(8,128)(2,1)}, u32[]{:S(2)}) copy-start(bf16[256,1024]{1,0:T(8,128)(2,1)} %refs_3_.3) | copy-start | bytes 1572868
  0.6 12.9 %copy-start.1 = (bf16[256,1024]{1,0:T(8,128)(2,1)S(1)}, bf16[256,1024]{1,0:T(8,128)(2,1)}, u32[]{:S(2)}) copy-start(bf16[256,1024]{1,0:T(8,128)(2,1)} %refs_4_.3) | copy-start | bytes 1572868
  2.5 16.9 %copy-start.2 = (bf16[256,1024]{1,0:T(8,128)(2,1)S(1)}, bf16[256,1024]{1,0:T(8,128)(2,1)}, u32[]{:S(2)}) copy-start(bf16[256,1024]{1,0:T(8,128)(2,1)} %refs_1_.3) | copy-start | bytes 1572868
  2.6 16.9 %copy-start.3 = (bf16[256,1024]{1,0:T(8,128)(2,1)S(1)}, bf16[256,1024]{1,0:T(8,128)(2,1)}, u32[]{:S(2)}) copy-start(bf16[256,1024]{1,0:T(8,128)(2,1)} %refs_2_.3) | copy-start | bytes 1572868
  2.6 11.1 %collective-permute-start.2 = (bf16[2,200,256]{2,1,0:T(8,128)(2,1)}, bf16[2,200,256]{2,1,0:T(8,128)(2,1)S(1)}, u32[]{:S(2)}, u32[]{:S(2)}) collective-permute-start(bf16[2,200,256]{2,1,0:T(8,128)(2,1)} %maximum_select_fusion.1), channel_id=1, source_target_pairs={{1,2},{3,4},{5,6},{7,8},{9,10},{11,12},{13,14},{2,1},{4,3},{6,5},{... | collective-permute-start | bytes 614408 | tf_op jit(solution)/shard_map/ppermute | solution.py:47
  6.4 7.1 %collective-permute-start = (bf16[256,1024]{1,0:T(8,128)(2,1)}, bf16[256,1024]{1,0:T(8,128)(2,1)S(1)}, u32[]{:S(2)}, u32[]{:S(2)}) collective-permute-start(bf16[256,1024]{1,0:T(8,128)(2,1)} %refs_3_.3), channel_id=1, source_target_pairs={{0,1},{2,3},{4,5},{6,7},{8,9},{10,11},{12,13},{14,15},{1,0},{3,2},... | collective-permute-start | bytes 1572872 | tf_op jit(solution)/shard_map/ppermute | solution.py:47
  6.5 7.0 %collective-permute-start.1 = (bf16[256,1024]{1,0:T(8,128)(2,1)}, bf16[256,1024]{1,0:T(8,128)(2,1)S(1)}, u32[]{:S(2)}, u32[]{:S(2)}) collective-permute-start(bf16[256,1024]{1,0:T(8,128)(2,1)} %refs_4_.3), channel_id=1, source_target_pairs={{0,1},{2,3},{4,5},{6,7},{8,9},{10,11},{12,13},{14,15},{1,0},{3,2},... | collective-permute-start | bytes 1572872 | tf_op jit(solution)/shard_map/ppermute | solution.py:47
  9.7 9.8 %collective-permute-start.4 = (bf16[2,200,256]{2,1,0:T(8,128)(2,1)}, bf16[2,200,256]{2,1,0:T(8,128)(2,1)S(1)}, u32[]{:S(2)}, u32[]{:S(2)}) collective-permute-start(bf16[2,200,256]{2,1,0:T(8,128)(2,1)} %maximum_select_fusion.2), channel_id=1, source_target_pairs={{1,2},{3,4},{5,6},{7,8},{9,10},{11,12},{13,14},{2,1},{4,3},{6,5},{... | collective-permute-start | bytes 614408 | tf_op jit(solution)/shard_map/ppermute | solution.py:47
  13.7 14.3 %collective-permute-start.3 = (bf16[2,200,512]{2,1,0:T(8,128)(2,1)S(1)}, bf16[2,200,512]{2,1,0:T(8,128)(2,1)S(1)}, u32[]{:S(2)}, u32[]{:S(2)}) collective-permute-start(bf16[2,200,512]{2,1,0:T(8,128)(2,1)S(1)} %maximum_select_fusion), channel_id=1, source_target_pairs={{1,2},{3,4},{5,6},{7,8},{9,10},{11,12},{13,14},{2,1},{4,3},{6,5},{... | collective-permute-start | bytes 1228808 | tf_op jit(solution)/shard_map/ppermute | solution.py:47
  24.4 12.4 %collective-permute-start.7 = (bf16[2,200,512]{2,1,0:T(8,128)(2,1)S(1)}, bf16[2,200,512]{2,1,0:T(8,128)(2,1)S(1)}, u32[]{:S(2)}, u32[]{:S(2)}) collective-permute-start(bf16[2,200,512]{2,1,0:T(8,128)(2,1)S(1)} %get-tuple-element.48), channel_id=1, source_target_pairs={{0,1},{2,3},{4,5},{6,7},{8,9},{10,11},{12,13},{14,15},{1,0},{3,2},... | collective-permute-start | bytes 1228808 | tf_op jit(solution)/shard_map/ppermute | solution.py:47
  24.5 13.7 %collective-permute-start.8 = (bf16[2,200,512]{2,1,0:T(8,128)(2,1)S(1)}, bf16[2,200,512]{2,1,0:T(8,128)(2,1)S(1)}, u32[]{:S(2)}, u32[]{:S(2)}) collective-permute-start(bf16[2,200,512]{2,1,0:T(8,128)(2,1)S(1)} %get-tuple-element.49), channel_id=1, source_target_pairs={{1,2},{3,4},{5,6},{7,8},{9,10},{11,12},{13,14},{2,1},{4,3},{6,5},{... | collective-permute-start | bytes 1228808 | tf_op jit(solution)/shard_map/ppermute | solution.py:47
  33.1 7.4 %collective-permute-start.5 = (bf16[2,200,512]{2,1,0:T(8,128)(2,1)S(1)}, bf16[2,200,512]{2,1,0:T(8,128)(2,1)S(1)}, u32[]{:S(2)}, u32[]{:S(2)}) collective-permute-start(bf16[2,200,512]{2,1,0:T(8,128)(2,1)S(1)} %get-tuple-element.44), channel_id=1, source_target_pairs={{0,1},{2,3},{4,5},{6,7},{8,9},{10,11},{12,13},{14,15},{1,0},{3,2},... | collective-permute-start | bytes 1228808 | tf_op jit(solution)/shard_map/ppermute | solution.py:47
  33.2 13.7 %collective-permute-start.6 = (bf16[2,200,512]{2,1,0:T(8,128)(2,1)S(1)}, bf16[2,200,512]{2,1,0:T(8,128)(2,1)S(1)}, u32[]{:S(2)}, u32[]{:S(2)}) collective-permute-start(bf16[2,200,512]{2,1,0:T(8,128)(2,1)S(1)} %get-tuple-element.45), channel_id=1, source_target_pairs={{1,2},{3,4},{5,6},{7,8},{9,10},{11,12},{13,14},{2,1},{4,3},{6,5},{... | collective-permute-start | bytes 1228808 | tf_op jit(solution)/shard_map/ppermute | solution.py:47

commit v13 on v12

--- a/solution.py
+++ b/solution.py
@@ -431,7 +431,7 @@
             + [jax.ShapeDtypeStruct((points, chunk_width), jnp.float32)] * 2
             + [jax.ShapeDtypeStruct((2, size, chunk_width), jnp.bfloat16) for size in far_sizes]
             + (kept_shapes if chunk == 0 else []),
-            48 * wide * points + 12 * 2**20,
+            48 * wide * points + 5 * 2**20,
             scratch_shapes=[
                 pltpu.VMEM((2, reached, points), jnp.float32),
                 pltpu.VMEM((2, 2, wide, PAIR), jnp.bfloat16),
@@ -464,7 +464,7 @@
         [outs[1]],
         1,
         [whole],
-        16 * wide * points + 8 * 2**20,
+        16 * wide * points + 3 * 2**20,
         scratch_shapes=[
             pltpu.VMEM((first_pairs, points, PAIR), jnp.bfloat16),
             pltpu.SemaphoreType.DMA((first_pairs,)),
@@ -486,7 +486,7 @@
             grads,
             2,
             [whole] * 2,
-            12 * 2**20,
+            7 * 2**20,
             scratch_shapes=[
                 pltpu.VMEM((points, chunk_width), jnp.float32),
                 pltpu.VMEM((2, points, chunk_width), jnp.bfloat16),

time: 48.3 us -> 48.3 us (level)
  no operation moved by 1% of the time
where the time goes in v13:
time: 48.3 us; the launch traced here: 48 us
  starting transfers between devices  16.5 us (34%)
  Pallas kernels  13.6 us (28%)
  waiting for transfers between devices  11.6 us (24%)
  local copies, waits for them, and re-layouts  3.21 us (7%)
  other arithmetic  2.2 us (5%)
  between operations  0.83 us (2%)
    ppermute x9, starting transfers between devices, swapped(): lax.ppermute(value, 'band', pairs + [(high, low) for low, high in pairs])  16.5 us
    pallas_call x5, Pallas kernels, chunk_call(): pl.pallas_call(functools.partial(kernel, len(carried)), in_specs=[vmem] *...  13.6 us
    ppermute x9, waiting for transfers between devices, swapped(): lax.ppermute(value, 'band', pairs + [(high, low) for low, high in pairs])  11.6 us
    another operation x5, local copies, waits for them, and re-layouts, pack(): last = jnp.stack([field[points - rows:, columns] for field in sources])  3.19 us
    select_n x3, other arithmetic, pack(): return jnp.where(is_even(), first, last)  1.51 us
  transfers between devices with their start and end apart: 9, of which 4 were waited for; matrix products, arithmetic and copies ran while one was open for 7% of the time, Pallas kernels for 26%

profile of v13, /device:TPU:9, one launch (start us, length us, event | category | flops | bytes accessed | tf_op | source)
XLA Modules:
  0.0 48.0 jit_solution(10776442043117225264)
XLA Ops:
  0.6 0.0 copy-start
  0.6 0.0 copy-start.1
  0.7 1.2 %slice_bitcast_fusion.8 = (bf16[1,200,256]{2,1,0:T(8,128)(2,1)S(1)}, bf16[1,200,256]{2,1,0:T(8,128)(2,1)S(1)}, bf16[1,200,256]{2,1,0:T(8,128)(2,1)S(1)}, bf16[1,200,256]{2,1,0:T(8,128)(2,1)S(1)}) fusion(bf16[256,1024]{1,0:T(8,128)(2,1)} %refs_4_.3, bf16[256,1024]{1,0:T(8,128)(2,1)} %refs_3_.3), kind=kLoop, calls=%fused_computation.11 | loop fusion | bytes 819200 | tf_op jit(solution)/shard_map/stack | solution.py:74
  1.8 0.7 %maximum_select_fusion.1 = bf16[2,200,256]{2,1,0:T(8,128)(2,1)} fusion(bf16[1,200,256]{2,1,0:T(8,128)(2,1)S(1)} %get-tuple-element.65, bf16[1,200,256]{2,1,0:T(8,128)(2,1)S(1)} %get-tuple-element.66, bf16[1,200,256]{2,1,0:T(8,128)(2,1)S(1)} %get-tuple-element.64, bf16[1,200,256]{2,1,0:T(8,128)(2,1)S(1)} %get-tuple-element.67, pred[]{:T(512)S(6)} %eq.9), kind=kLoop, calls=%fused_computation.1 | loop fusion | flops 307200 | bytes 614401 | tf_op jit(solution)/shard_map/jit(_where)/select_n | solution.py:75
  2.5 0.0 copy-start.2
  2.6 0.0 copy-start.3
  2.6 3.8 %collective-permute-start.2 = (bf16[2,200,256]{2,1,0:T(8,128)(2,1)}, bf16[2,200,256]{2,1,0:T(8,128)(2,1)S(1)}, u32[]{:S(2)}, u32[]{:S(2)}) collective-permute-start(bf16[2,200,256]{2,1,0:T(8,128)(2,1)} %maximum_select_fusion.1), channel_id=1, source_target_pairs={{1,2},{3,4},{5,6},{7,8},{9,10},{11,12},{13,14},{2,1},{4,3},{6,5},{... | collective-permute-start | bytes 614408 | tf_op jit(solution)/shard_map/ppermute | solution.py:47
  6.4 0.1 collective-permute-start
  6.5 0.5 %collective-permute-start.1 = (bf16[256,1024]{1,0:T(8,128)(2,1)}, bf16[256,1024]{1,0:T(8,128)(2,1)S(1)}, u32[]{:S(2)}, u32[]{:S(2)}) collective-permute-start(bf16[256,1024]{1,0:T(8,128)(2,1)} %refs_4_.3), channel_id=1, source_target_pairs={{0,1},{2,3},{4,5},{6,7},{8,9},{10,11},{12,13},{14,15},{1,0},{3,2},... | collective-permute-start | bytes 1572872 | tf_op jit(solution)/shard_map/ppermute | solution.py:47
  7.0 1.0 %slice_bitcast_fusion.5 = (bf16[1,200,256]{2,1,0:T(8,128)(2,1)S(1)}, bf16[1,200,256]{2,1,0:T(8,128)(2,1)S(1)}) fusion(bf16[256,1024]{1,0:T(8,128)(2,1)} %refs_3_.3), kind=kLoop, calls=%fused_computation.8 | loop fusion | bytes 409600 | tf_op jit(solution)/shard_map/stack | solution.py:74
  8.0 1.0 %slice_bitcast_fusion.4 = (bf16[1,200,256]{2,1,0:T(8,128)(2,1)S(1)}, bf16[1,200,256]{2,1,0:T(8,128)(2,1)S(1)}) fusion(bf16[256,1024]{1,0:T(8,128)(2,1)} %refs_4_.3), kind=kLoop, calls=%fused_computation.7 | loop fusion | bytes 409600 | tf_op jit(solution)/shard_map/stack | solution.py:74
  8.9 0.7 %maximum_select_fusion.2 = bf16[2,200,256]{2,1,0:T(8,128)(2,1)} fusion(bf16[1,200,256]{2,1,0:T(8,128)(2,1)S(1)} %get-tuple-element.61, bf16[1,200,256]{2,1,0:T(8,128)(2,1)S(1)} %get-tuple-element.59, bf16[1,200,256]{2,1,0:T(8,128)(2,1)S(1)} %get-tuple-element.60, bf16[1,200,256]{2,1,0:T(8,128)(2,1)S(1)} %get-tuple-element.58, pred[]{:T(512)S(6)} %eq.9), kind=kLoop, calls=%fused_computation.2 | loop fusion | flops 307200 | bytes 614401 | tf_op jit(solution)/shard_map/jit(_where)/select_n | solution.py:75
  9.7 3.1 %collective-permute-start.4 = (bf16[2,200,256]{2,1,0:T(8,128)(2,1)}, bf16[2,200,256]{2,1,0:T(8,128)(2,1)S(1)}, u32[]{:S(2)}, u32[]{:S(2)}) collective-permute-start(bf16[2,200,256]{2,1,0:T(8,128)(2,1)} %maximum_select_fusion.2), channel_id=1, source_target_pairs={{1,2},{3,4},{5,6},{7,8},{9,10},{11,12},{13,14},{2,1},{4,3},{6,5},{... | collective-permute-start | bytes 614408 | tf_op jit(solution)/shard_map/ppermute | solution.py:47
  12.8 0.7 %subtract_bitcast_fusion.refs_0_ = s32[2,256]{1,0:T(2,128)S(1)} fusion(s32[256,2]{0,1:T(2,128)} %param.9, s32[]{:T(128)S(6)} %mul.3), kind=kLoop, calls=%fused_computation.15 | loop fusion | flops 512 | bytes 4100 | tf_op jit(solution)/shard_map/transpose | solution.py:384
  13.5 0.0 collective-permute-done.refs_5_
  13.5 0.0 collective-permute-done.1.refs_6_
  13.5 0.0 copy-done
  13.5 0.0 copy-done.1
  13.6 0.1 maximum_select_fusion
  13.6 0.0 collective-permute-done.2.refs_7_
  13.7 2.4 %collective-permute-start.3 = (bf16[2,200,512]{2,1,0:T(8,128)(2,1)S(1)}, bf16[2,200,512]{2,1,0:T(8,128)(2,1)S(1)}, u32[]{:S(2)}, u32[]{:S(2)}) collective-permute-start(bf16[2,200,512]{2,1,0:T(8,128)(2,1)S(1)} %maximum_select_fusion), channel_id=1, source_target_pairs={{1,2},{3,4},{5,6},{7,8},{9,10},{11,12},{13,14},{2,1},{4,3},{6,5},{... | collective-permute-start | bytes 1228808 | tf_op jit(solution)/shard_map/ppermute | solution.py:47
  16.1 3.3 %collective-permute-done.4.refs_8_ = bf16[2,200,256]{2,1,0:T(8,128)(2,1)S(1)} collective-permute-done((bf16[2,200,256]{2,1,0:T(8,128)(2,1)}, bf16[2,200,256]{2,1,0:T(8,128)(2,1)S(1)}, u32[]{:S(2)}, u32[]{:S(2)}) %collective-permute-start.4) | collective-permute-done | bytes 204832 | tf_op jit(solution)/shard_map/ppermute | solution.py:47
  19.4 0.0 copy-done.2
  19.4 0.0 copy-done.3
  19.4 4.9 %attention_0.1 = (bf16[256,1024]{1,0:T(8,128)(2,1)}, bf16[256,1024]{1,0:T(8,128)(2,1)}, bf16[2,200,512]{2,1,0:T(8,128)(2,1)S(1)}, bf16[2,200,512]{2,1,0:T(8,128)...) custom-call(s32[2,256]{1,0:T(2,128)S(1)} %subtract_bitcast_fusion.re, ...), custom_call_target="tpu_custom_call" | custom-call | flops 8556380160 | bytes 5373952 | tf_op jit(solution)/shard_map/attention_0/pallas_call | solution.py:362
  24.4 0.1 collective-permute-start.7
  24.5 2.8 %collective-permute-start.8 = (bf16[2,200,512]{2,1,0:T(8,128)(2,1)S(1)}, bf16[2,200,512]{2,1,0:T(8,128)(2,1)S(1)}, u32[]{:S(2)}, u32[]{:S(2)}) collective-permute-start(bf16[2,200,512]{2,1,0:T(8,128)(2,1)S(1)} %get-tuple-element.49), channel_id=1, source_target_pairs={{1,2},{3,4},{5,6},{7,8},{9,10},{11,12},{13,14},{2,1},{4,3},{6,5},{... | collective-permute-start | bytes 1228808 | tf_op jit(solution)/shard_map/ppermute | solution.py:47
  27.3 0.6 %collective-permute-done.3.refs_7_ = bf16[2,200,512]{2,1,0:T(8,128)(2,1)S(1)} collective-permute-done((bf16[2,200,512]{2,1,0:T(8,128)(2,1)S(1)}, bf16[2,200,512]{2,1,0:T(8,128)(2,1)S(1)}, u32[]{:S(2)}, u32[]{:S(2)}) %collective-permute-start.3) | collective-permute-done | bytes 409632 | tf_op jit(solution)/shard_map/ppermute | solution.py:47
  27.9 5.2 %attention_1.1 = (bf16[256,1024]{1,0:T(8,128)(2,1)}, bf16[256,1024]{1,0:T(8,128)(2,1)}, bf16[2,200,512]{2,1,0:T(8,128)(2,1)S(1)}, bf16[2,200,512]{2,1,0:T(8,128)...) custom-call(s32[2,256]{1,0:T(2,128)S(1)} %subtract_bitcast_fusion.refs_0_, ...), custom_call_target="tpu_custom_call", output_to_operand_aliasing={{0}: (8, {}), {1}: (9, {})} | custom-call | flops 8556380160 | bytes 5373952 | tf_op jit(solution)/shard_map/attention_1/pallas_call | solution.py:362
  33.1 0.1 collective-permute-start.5
  33.2 3.6 %collective-permute-start.6 = (bf16[2,200,512]{2,1,0:T(8,128)(2,1)S(1)}, bf16[2,200,512]{2,1,0:T(8,128)(2,1)S(1)}, u32[]{:S(2)}, u32[]{:S(2)}) collective-permute-start(bf16[2,200,512]{2,1,0:T(8,128)(2,1)S(1)} %get-tuple-element.45), channel_id=1, source_target_pairs={{1,2},{3,4},{5,6},{7,8},{9,10},{11,12},{13,14},{2,1},{4,3},{6,5},{... | collective-permute-start | bytes 1228808 | tf_op jit(solution)/shard_map/ppermute | solution.py:47
  36.8 0.0 collective-permute-done.7.refs_2_
  36.9 1.3 %collective-permute-done.8.refs_3_ = bf16[2,200,512]{2,1,0:T(8,128)(2,1)S(1)} collective-permute-done((bf16[2,200,512]{2,1,0:T(8,128)(2,1)S(1)}, bf16[2,200,512]{2,1,0:T(8,128)(2,1)S(1)}, u32[]{:S(2)}, u32[]{:S(2)}) %collective-permute-start.8) | collective-permute-done | bytes 409632 | tf_op jit(solution)/shard_map/ppermute | solution.py:47
  38.1 1.1 %gradient_sums_0.1 = (bf16[256,1024]{1,0:T(8,128)(2,1)}, bf16[256,1024]{1,0:T(8,128)(2,1)}) custom-call(f32[256,512]{1,0:T(8,128)S(1)} %get-tuple-element.46.refs_0_, f32[256,512]{1,0:T(8,128)S(1)} %get-tuple-element.47.refs_1_, bf16[2,200,512]{2,1,0:T(8,128)(2,1)S(1)} %collective-permute-done.7.refs_2_, bf16[2,200,512]{2,1,0:T(8,128)(2,1)S(1)} %collective-permute-done.8.refs_3_), custom_call_target="tpu_custom_call" | custom-call | flops 786432 | bytes 2621440 | tf_op jit(solution)/shard_map/gradient_sums_0/pallas_call | solution.py:362
  39.2 1.3 %query_gradients.1 = bf16[256,1024]{1,0:T(8,128)(2,1)} custom-call(bf16[4,2,544,256]{3,2,1,0:T(8,128)(2,1)S(1)} %get-tuple-element.39.refs_0_, bf16[4,128,672]{2,1,0:T(8,128)(2,1)S(1)} %get-tuple-element.40.refs_1_, bf16[256,1024]{1,0:T(8,128)(2,1)} %get-tuple-element.41.refs_2_), custom_call_target="tpu_custom_call", output_to_operand_aliasing={{}: (2, {})} | custom-call | flops 285212672 | bytes 2228224 | tf_op jit(solution)/shard_map/query_gradients/pallas_call | solution.py:362
  40.5 0.0 collective-permute-done.5.refs_2_
  40.5 6.4 %collective-permute-done.6.refs_3_ = bf16[2,200,512]{2,1,0:T(8,128)(2,1)S(1)} collective-permute-done((bf16[2,200,512]{2,1,0:T(8,128)(2,1)S(1)}, bf16[2,200,512]{2,1,0:T(8,128)(2,1)S(1)}, u32[]{:S(2)}, u32[]{:S(2)}) %collective-permute-start.6) | collective-permute-done | bytes 409632 | tf_op jit(solution)/shard_map/ppermute | solution.py:47
  46.9 1.1 %gradient_sums_1.1 = (bf16[256,1024]{1,0:T(8,128)(2,1)}, bf16[256,1024]{1,0:T(8,128)(2,1)}) custom-call(f32[256,512]{1,0:T(8,128)S(1)} %get-tuple-element.42.refs_0_, f32[256,512]{1,0:T(8,128)S(1)} %get-tuple-element.43.refs_1_, bf16[2,200,512]{2,1,0:T(8,128)(2,1)S(1)} %collective-permute-done.5.refs_2_, ...), custom_call_target="tpu_custom_call", output_to_operand_aliasing={{0}: (4, {}), {1}: (5, {})} | custom-call | flops 786432 | bytes 2621440 | tf_op jit(solution)/shard_map/gradient_sums_1/pallas_call | solution.py:362
  (2 shorter events, 0.1 us)
Async XLA Ops:
  0.6 12.8 %copy-start = (bf16[256,1024]{1,0:T(8,128)(2,1)S(1)}, bf16[256,1024]{1,0:T(8,128)(2,1)}, u32[]{:S(2)}) copy-start(bf16[256,1024]{1,0:T(8,128)(2,1)} %refs_3_.3) | copy-start | bytes 1572868
  0.6 12.9 %copy-start.1 = (bf16[256,1024]{1,0:T(8,128)(2,1)S(1)}, bf16[256,1024]{1,0:T(8,128)(2,1)}, u32[]{:S(2)}) copy-start(bf16[256,1024]{1,0:T(8,128)(2,1)} %refs_4_.3) | copy-start | bytes 1572868
  2.5 16.9 %copy-start.2 = (bf16[256,1024]{1,0:T(8,128)(2,1)S(1)}, bf16[256,1024]{1,0:T(8,128)(2,1)}, u32[]{:S(2)}) copy-start(bf16[256,1024]{1,0:T(8,128)(2,1)} %refs_1_.3) | copy-start | bytes 1572868
  2.6 16.9 %copy-start.3 = (bf16[256,1024]{1,0:T(8,128)(2,1)S(1)}, bf16[256,1024]{1,0:T(8,128)(2,1)}, u32[]{:S(2)}) copy-start(bf16[256,1024]{1,0:T(8,128)(2,1)} %refs_2_.3) | copy-start | bytes 1572868
  2.6 11.1 %collective-permute-start.2 = (bf16[2,200,256]{2,1,0:T(8,128)(2,1)}, bf16[2,200,256]{2,1,0:T(8,128)(2,1)S(1)}, u32[]{:S(2)}, u32[]{:S(2)}) collective-permute-start(bf16[2,200,256]{2,1,0:T(8,128)(2,1)} %maximum_select_fusion.1), channel_id=1, source_target_pairs={{1,2},{3,4},{5,6},{7,8},{9,10},{11,12},{13,14},{2,1},{4,3},{6,5},{... | collective-permute-start | bytes 614408 | tf_op jit(solution)/shard_map/ppermute | solution.py:47
  6.4 7.1 %collective-permute-start = (bf16[256,1024]{1,0:T(8,128)(2,1)}, bf16[256,1024]{1,0:T(8,128)(2,1)S(1)}, u32[]{:S(2)}, u32[]{:S(2)}) collective-permute-start(bf16[256,1024]{1,0:T(8,128)(2,1)} %refs_3_.3), channel_id=1, source_target_pairs={{0,1},{2,3},{4,5},{6,7},{8,9},{10,11},{12,13},{14,15},{1,0},{3,2},... | collective-permute-start | bytes 1572872 | tf_op jit(solution)/shard_map/ppermute | solution.py:47
  6.5 7.0 %collective-permute-start.1 = (bf16[256,1024]{1,0:T(8,128)(2,1)}, bf16[256,1024]{1,0:T(8,128)(2,1)S(1)}, u32[]{:S(2)}, u32[]{:S(2)}) collective-permute-start(bf16[256,1024]{1,0:T(8,128)(2,1)} %refs_4_.3), channel_id=1, source_target_pairs={{0,1},{2,3},{4,5},{6,7},{8,9},{10,11},{12,13},{14,15},{1,0},{3,2},... | collective-permute-start | bytes 1572872 | tf_op jit(solution)/shard_map/ppermute | solution.py:47
  9.7 9.8 %collective-permute-start.4 = (bf16[2,200,256]{2,1,0:T(8,128)(2,1)}, bf16[2,200,256]{2,1,0:T(8,128)(2,1)S(1)}, u32[]{:S(2)}, u32[]{:S(2)}) collective-permute-start(bf16[2,200,256]{2,1,0:T(8,128)(2,1)} %maximum_select_fusion.2), channel_id=1, source_target_pairs={{1,2},{3,4},{5,6},{7,8},{9,10},{11,12},{13,14},{2,1},{4,3},{6,5},{... | collective-permute-start | bytes 614408 | tf_op jit(solution)/shard_map/ppermute | solution.py:47
  13.7 14.3 %collective-permute-start.3 = (bf16[2,200,512]{2,1,0:T(8,128)(2,1)S(1)}, bf16[2,200,512]{2,1,0:T(8,128)(2,1)S(1)}, u32[]{:S(2)}, u32[]{:S(2)}) collective-permute-start(bf16[2,200,512]{2,1,0:T(8,128)(2,1)S(1)} %maximum_select_fusion), channel_id=1, source_target_pairs={{1,2},{3,4},{5,6},{7,8},{9,10},{11,12},{13,14},{2,1},{4,3},{6,5},{... | collective-permute-start | bytes 1228808 | tf_op jit(solution)/shard_map/ppermute | solution.py:47
  24.4 12.4 %collective-permute-start.7 = (bf16[2,200,512]{2,1,0:T(8,128)(2,1)S(1)}, bf16[2,200,512]{2,1,0:T(8,128)(2,1)S(1)}, u32[]{:S(2)}, u32[]{:S(2)}) collective-permute-start(bf16[2,200,512]{2,1,0:T(8,128)(2,1)S(1)} %get-tuple-element.48), channel_id=1, source_target_pairs={{0,1},{2,3},{4,5},{6,7},{8,9},{10,11},{12,13},{14,15},{1,0},{3,2},... | collective-permute-start | bytes 1228808 | tf_op jit(solution)/shard_map/ppermute | solution.py:47
  24.5 13.7 %collective-permute-start.8 = (bf16[2,200,512]{2,1,0:T(8,128)(2,1)S(1)}, bf16[2,200,512]{2,1,0:T(8,128)(2,1)S(1)}, u32[]{:S(2)}, u32[]{:S(2)}) collective-permute-start(bf16[2,200,512]{2,1,0:T(8,128)(2,1)S(1)} %get-tuple-element.49), channel_id=1, source_target_pairs={{1,2},{3,4},{5,6},{7,8},{9,10},{11,12},{13,14},{2,1},{4,3},{6,5},{... | collective-permute-start | bytes 1228808 | tf_op jit(solution)/shard_map/ppermute | solution.py:47
  33.1 7.4 %collective-permute-start.5 = (bf16[2,200,512]{2,1,0:T(8,128)(2,1)S(1)}, bf16[2,200,512]{2,1,0:T(8,128)(2,1)S(1)}, u32[]{:S(2)}, u32[]{:S(2)}) collective-permute-start(bf16[2,200,512]{2,1,0:T(8,128)(2,1)S(1)} %get-tuple-element.44), channel_id=1, source_target_pairs={{0,1},{2,3},{4,5},{6,7},{8,9},{10,11},{12,13},{14,15},{1,0},{3,2},... | collective-permute-start | bytes 1228808 | tf_op jit(solution)/shard_map/ppermute | solution.py:47
  33.2 13.7 %collective-permute-start.6 = (bf16[2,200,512]{2,1,0:T(8,128)(2,1)S(1)}, bf16[2,200,512]{2,1,0:T(8,128)(2,1)S(1)}, u32[]{:S(2)}, u32[]{:S(2)}) collective-permute-start(bf16[2,200,512]{2,1,0:T(8,128)(2,1)S(1)} %get-tuple-element.45), channel_id=1, source_target_pairs={{1,2},{3,4},{5,6},{7,8},{9,10},{11,12},{13,14},{2,1},{4,3},{6,5},{... | collective-permute-start | bytes 1228808 | tf_op jit(solution)/shard_map/ppermute | solution.py:47

commit v14 on v8

--- a/solution.py
+++ b/solution.py
@@ -276,13 +276,13 @@
     gather_keys(0)
     tops = {units[0]: forward_scores(*units[0])}
     for at, unit in enumerate(units):
+        if unit[1] == 0 and unit[0] > 0:
+            finish(unit[0] - 1)
         if at + 1 < len(units):
             following = units[at + 1]
             if following[1] == 0:
                 gather_keys(following[0])
             tops[following] = forward_scores(*following)
-        if unit[1] == 0 and unit[0] > 0:
-            finish(unit[0] - 1)
         inverse = forward_probs(*unit, tops.pop(unit))
         delta = forward_outputs(*unit)
         backward_scores(*unit, inverse, delta)

time: 45.2 us -> 46.3 us (1.024)
  Pallas kernels: 12.6 us -> 13.7 us
    pallas_call x4, Pallas kernels: 12.6 us -> 13.7 us  [chunk_call(): pl.pallas_call(functools.partial(kernel, len(carried)), in_specs=[vmem] *...]
  transfers between devices with their start and end apart: 9 -> 9, of which waited for: 4 -> 4; matrix products, arithmetic and copies ran while one was open for 0% -> 0% of each run, Pallas kernels for 26% -> 27%
where the time goes in v14:
time: 46.3 us; the launch traced here: 46.1 us
  starting transfers between devices  18.2 us (39%)
  Pallas kernels  13.7 us (30%)
  waiting for transfers between devices  11.8 us (25%)
  local copies, waits for them, and re-layouts  1.28 us (3%)
  between operations  0.89 us (2%)
    ppermute x9, starting transfers between devices, swapped(): lax.ppermute(value, 'band', pairs + [(high, low) for low, high in pairs])  18.2 us
    pallas_call x4, Pallas kernels, chunk_call(): pl.pallas_call(functools.partial(kernel, len(carried)), in_specs=[vmem] *...  13.7 us
    ppermute x9, waiting for transfers between devices, swapped(): lax.ppermute(value, 'band', pairs + [(high, low) for low, high in pairs])  11.8 us
    another operation x5, local copies, waits for them, and re-layouts, pack(): last = jnp.stack([field[points - rows:, columns] for field in sources])  1.26 us
  transfers between devices with their start and end apart: 9, of which 4 were waited for; matrix products, arithmetic and copies ran while one was open for 0% of the time, Pallas kernels for 27%

profile of v14, /device:TPU:9, one launch (start us, length us, event | category | flops | bytes accessed | tf_op | source)
XLA Modules:
  0.0 46.1 jit_solution(13607418714063224615)
XLA Ops:
  0.6 0.0 copy-start
  0.7 0.0 copy-start.1
  0.7 1.2 %slice_bitcast_fusion.8 = (bf16[1,200,256]{2,1,0:T(8,128)(2,1)S(1)}, bf16[1,200,256]{2,1,0:T(8,128)(2,1)S(1)}, bf16[1,200,256]{2,1,0:T(8,128)(2,1)S(1)}, bf16[1,200,256]{2,1,0:T(8,128)(2,1)S(1)}) fusion(bf16[256,1024]{1,0:T(8,128)(2,1)} %refs_4_.3, bf16[256,1024]{1,0:T(8,128)(2,1)} %refs_3_.3), kind=kLoop, calls=%fused_computation.11 | loop fusion | bytes 819200 | tf_op jit(solution)/shard_map/stack | solution.py:74
  1.9 3.7 %collective-permute-start.2 = (bf16[2,200,256]{2,1,0:T(8,128)(2,1)S(1)}, bf16[2,200,256]{2,1,0:T(8,128)(2,1)S(1)}, u32[]{:S(2)}, u32[]{:S(2)}) collective-permute-start(bf16[2,200,256]{2,1,0:T(8,128)(2,1)S(1)} %maximum_select_fusion.1), channel_id=1, source_target_pairs={{1,2},{3,4},{5,6},{7,8},{9,10},{11,12},{13,14},{2,1},{4,3},{6,5},{... | collective-permute-start | bytes 614408 | tf_op jit(solution)/shard_map/ppermute | solution.py:47
  5.6 0.0 copy-done
  5.6 0.1 collective-permute-start
  5.7 0.0 copy-done.1
  5.7 0.5 %collective-permute-start.1 = (bf16[256,1024]{1,0:T(8,128)(2,1)S(1)}, bf16[256,1024]{1,0:T(8,128)(2,1)S(1)}, u32[]{:S(2)}, u32[]{:S(2)}) collective-permute-start(bf16[256,1024]{1,0:T(8,128)(2,1)S(1)} %copy-done.1), channel_id=1, source_target_pairs={{0,1},{2,3},{4,5},{6,7},{8,9},{10,11},{12,13},{14,15},{1,0},{3,2},... | collective-permute-start | bytes 1572872 | tf_op jit(solution)/shard_map/ppermute | solution.py:47
  6.2 0.0 copy-start.4
  6.3 3.1 %collective-permute-start.4 = (bf16[2,200,256]{2,1,0:T(8,128)(2,1)S(1)}, bf16[2,200,256]{2,1,0:T(8,128)(2,1)S(1)}, u32[]{:S(2)}, u32[]{:S(2)}) collective-permute-start(bf16[2,200,256]{2,1,0:T(8,128)(2,1)S(1)} %maximum_select_fusion.2), channel_id=1, source_target_pairs={{1,2},{3,4},{5,6},{7,8},{9,10},{11,12},{13,14},{2,1},{4,3},{6,5},{... | collective-permute-start | bytes 614408 | tf_op jit(solution)/shard_map/ppermute | solution.py:47
  9.4 0.0 copy-done.4
  9.4 0.0 collective-permute-done.refs_5_
  9.4 0.0 collective-permute-done.1.refs_6_
  9.5 0.0 copy-start.2
  9.5 0.0 copy-start.3
  9.6 0.1 maximum_select_fusion
  9.6 1.6 %collective-permute-done.2.refs_7_ = bf16[2,200,256]{2,1,0:T(8,128)(2,1)S(1)} collective-permute-done((bf16[2,200,256]{2,1,0:T(8,128)(2,1)S(1)}, bf16[2,200,256]{2,1,0:T(8,128)(2,1)S(1)}, u32[]{:S(2)}, u32[]{:S(2)}) %collective-permute-start.2) | collective-permute-done | bytes 204832 | tf_op jit(solution)/shard_map/ppermute | solution.py:47
  11.2 3.6 %collective-permute-start.3 = (bf16[2,200,512]{2,1,0:T(8,128)(2,1)S(1)}, bf16[2,200,512]{2,1,0:T(8,128)(2,1)S(1)}, u32[]{:S(2)}, u32[]{:S(2)}) collective-permute-start(bf16[2,200,512]{2,1,0:T(8,128)(2,1)S(1)} %maximum_select_fusion), channel_id=1, source_target_pairs={{1,2},{3,4},{5,6},{7,8},{9,10},{11,12},{13,14},{2,1},{4,3},{6,5},{... | collective-permute-start | bytes 1228808 | tf_op jit(solution)/shard_map/ppermute | solution.py:47
  14.9 0.8 %collective-permute-done.4.refs_8_ = bf16[2,200,256]{2,1,0:T(8,128)(2,1)S(1)} collective-permute-done((bf16[2,200,256]{2,1,0:T(8,128)(2,1)S(1)}, bf16[2,200,256]{2,1,0:T(8,128)(2,1)S(1)}, u32[]{:S(2)}, u32[]{:S(2)}) %collective-permute-start.4) | collective-permute-done | bytes 204832 | tf_op jit(solution)/shard_map/ppermute | solution.py:47
  15.6 0.0 copy-done.2
  15.6 0.0 copy-done.3
  15.6 5.8 %attention_0.1 = (bf16[256,1024]{1,0:T(8,128)(2,1)}, bf16[256,1024]{1,0:T(8,128)(2,1)}, bf16[2,200,512]{2,1,0:T(8,128)(2,1)S(1)}, bf16[2,200,512]{2,1,0:T(8,128)...) custom-call(s32[2,256]{1,0:T(2,128)S(1)} %subtract_bitcast_fusion.refs_0_, bf16[256,1024]{1,0:T(8,128)(2,1)S(1)} %copy-done.2, ...), custom_call_target="tpu_custom_call" | custom-call | flops 8556380160 | bytes 5373952 | tf_op jit(solution)/shard_map/attention_0/pallas_call | solution.py:325
  21.4 0.1 collective-permute-start.7
  21.4 3.6 %collective-permute-start.8 = (bf16[2,200,512]{2,1,0:T(8,128)(2,1)S(1)}, bf16[2,200,512]{2,1,0:T(8,128)(2,1)S(1)}, u32[]{:S(2)}, u32[]{:S(2)}) collective-permute-start(bf16[2,200,512]{2,1,0:T(8,128)(2,1)S(1)} %get-tuple-element.45), channel_id=1, source_target_pairs={{1,2},{3,4},{5,6},{7,8},{9,10},{11,12},{13,14},{2,1},{4,3},{6,5},{... | collective-permute-start | bytes 1228808 | tf_op jit(solution)/shard_map/ppermute | solution.py:47
  25.1 0.0 collective-permute-done.3.refs_7_
  25.1 5.8 %attention_1.1 = (bf16[256,1024]{1,0:T(8,128)(2,1)}, bf16[256,1024]{1,0:T(8,128)(2,1)}, bf16[2,200,512]{2,1,0:T(8,128)(2,1)S(1)}, bf16[2,200,512]{2,1,0:T(8,128)...) custom-call(s32[2,256]{1,0:T(2,128)S(1)} %subtract_bitcast_fusion.refs_0_, ...), custom_call_target="tpu_custom_call", output_to_operand_aliasing={{0}: (8, {}), {1}: (9, {})} | custom-call | flops 8556380160 | bytes 5373952 | tf_op jit(solution)/shard_map/attention_1/pallas_call | solution.py:325
  30.9 0.4 collective-permute-start.5
  31.3 3.0 %collective-permute-start.6 = (bf16[2,200,512]{2,1,0:T(8,128)(2,1)S(1)}, bf16[2,200,512]{2,1,0:T(8,128)(2,1)S(1)}, u32[]{:S(2)}, u32[]{:S(2)}) collective-permute-start(bf16[2,200,512]{2,1,0:T(8,128)(2,1)S(1)} %get-tuple-element.41), channel_id=1, source_target_pairs={{1,2},{3,4},{5,6},{7,8},{9,10},{11,12},{13,14},{2,1},{4,3},{6,5},{... | collective-permute-start | bytes 1228808 | tf_op jit(solution)/shard_map/ppermute | solution.py:47
  34.4 0.0 collective-permute-done.7.refs_2_
  34.4 0.7 %collective-permute-done.8.refs_3_ = bf16[2,200,512]{2,1,0:T(8,128)(2,1)S(1)} collective-permute-done((bf16[2,200,512]{2,1,0:T(8,128)(2,1)S(1)}, bf16[2,200,512]{2,1,0:T(8,128)(2,1)S(1)}, u32[]{:S(2)}, u32[]{:S(2)}) %collective-permute-start.8) | collective-permute-done | bytes 409632 | tf_op jit(solution)/shard_map/ppermute | solution.py:47
  35.1 1.1 %gradient_sums_0.1 = (bf16[256,1024]{1,0:T(8,128)(2,1)}, bf16[256,1024]{1,0:T(8,128)(2,1)}) custom-call(f32[256,512]{1,0:T(8,128)S(1)} %get-tuple-element.42.refs_0_, f32[256,512]{1,0:T(8,128)S(1)} %get-tuple-element.43.refs_1_, bf16[2,200,512]{2,1,0:T(8,128)(2,1)S(1)} %collective-permute-done.7.refs_2_, bf16[2,200,512]{2,1,0:T(8,128)(2,1)S(1)} %collective-permute-done.8.refs_3_), custom_call_target="tpu_custom_call" | custom-call | flops 786432 | bytes 2621440 | tf_op jit(solution)/shard_map/gradient_sums_0/pallas_call | solution.py:325
  36.2 0.0 collective-permute-done.5.refs_2_
  36.2 8.8 %collective-permute-done.6.refs_3_ = bf16[2,200,512]{2,1,0:T(8,128)(2,1)S(1)} collective-permute-done((bf16[2,200,512]{2,1,0:T(8,128)(2,1)S(1)}, bf16[2,200,512]{2,1,0:T(8,128)(2,1)S(1)}, u32[]{:S(2)}, u32[]{:S(2)}) %collective-permute-start.6) | collective-permute-done | bytes 409632 | tf_op jit(solution)/shard_map/ppermute | solution.py:47
  45.0 1.1 %gradient_sums_1.1 = (bf16[256,1024]{1,0:T(8,128)(2,1)}, bf16[256,1024]{1,0:T(8,128)(2,1)}) custom-call(f32[256,512]{1,0:T(8,128)S(1)} %get-tuple-element.38.refs_0_, f32[256,512]{1,0:T(8,128)S(1)} %get-tuple-element.39.refs_1_, bf16[2,200,512]{2,1,0:T(8,128)(2,1)S(1)} %collective-permute-done.5.refs_2_, ...), custom_call_target="tpu_custom_call", output_to_operand_aliasing={{0}: (4, {}), {1}: (5, {})} | custom-call | flops 786432 | bytes 2621440 | tf_op jit(solution)/shard_map/gradient_sums_1/pallas_call | solution.py:325
  (7 shorter events, 0.2 us)
Async XLA Ops:
  0.6 4.9 %copy-start = (bf16[256,1024]{1,0:T(8,128)(2,1)S(1)}, bf16[256,1024]{1,0:T(8,128)(2,1)}, u32[]{:S(2)}) copy-start(bf16[256,1024]{1,0:T(8,128)(2,1)} %refs_3_.3) | copy-start | bytes 1572868
  0.7 5.0 %copy-start.1 = (bf16[256,1024]{1,0:T(8,128)(2,1)S(1)}, bf16[256,1024]{1,0:T(8,128)(2,1)}, u32[]{:S(2)}) copy-start(bf16[256,1024]{1,0:T(8,128)(2,1)} %refs_4_.3) | copy-start | bytes 1572868
  1.9 9.3 %collective-permute-start.2 = (bf16[2,200,256]{2,1,0:T(8,128)(2,1)S(1)}, bf16[2,200,256]{2,1,0:T(8,128)(2,1)S(1)}, u32[]{:S(2)}, u32[]{:S(2)}) collective-permute-start(bf16[2,200,256]{2,1,0:T(8,128)(2,1)S(1)} %maximum_select_fusion.1), channel_id=1, source_target_pairs={{1,2},{3,4},{5,6},{7,8},{9,10},{11,12},{13,14},{2,1},{4,3},{6,5},{... | collective-permute-start | bytes 614408 | tf_op jit(solution)/shard_map/ppermute | solution.py:47
  5.6 3.8 %collective-permute-start = (bf16[256,1024]{1,0:T(8,128)(2,1)S(1)}, bf16[256,1024]{1,0:T(8,128)(2,1)S(1)}, u32[]{:S(2)}, u32[]{:S(2)}) collective-permute-start(bf16[256,1024]{1,0:T(8,128)(2,1)S(1)} %copy-done), channel_id=1, source_target_pairs={{0,1},{2,3},{4,5},{6,7},{8,9},{10,11},{12,13},{14,15},{1,0},{3,2},... | collective-permute-start | bytes 1572872 | tf_op jit(solution)/shard_map/ppermute | solution.py:47
  5.7 3.8 %collective-permute-start.1 = (bf16[256,1024]{1,0:T(8,128)(2,1)S(1)}, bf16[256,1024]{1,0:T(8,128)(2,1)S(1)}, u32[]{:S(2)}, u32[]{:S(2)}) collective-permute-start(bf16[256,1024]{1,0:T(8,128)(2,1)S(1)} %copy-done.1), channel_id=1, source_target_pairs={{0,1},{2,3},{4,5},{6,7},{8,9},{10,11},{12,13},{14,15},{1,0},{3,2},... | collective-permute-start | bytes 1572872 | tf_op jit(solution)/shard_map/ppermute | solution.py:47
  6.2 3.2 %copy-start.4 = (s32[256,2]{0,1:T(2,128)S(1)}, s32[256,2]{0,1:T(2,128)}, u32[]{:S(2)}) copy-start(s32[256,2]{0,1:T(2,128)} %param.9) | copy-start | bytes 6148
  6.3 9.3 %collective-permute-start.4 = (bf16[2,200,256]{2,1,0:T(8,128)(2,1)S(1)}, bf16[2,200,256]{2,1,0:T(8,128)(2,1)S(1)}, u32[]{:S(2)}, u32[]{:S(2)}) collective-permute-start(bf16[2,200,256]{2,1,0:T(8,128)(2,1)S(1)} %maximum_select_fusion.2), channel_id=1, source_target_pairs={{1,2},{3,4},{5,6},{7,8},{9,10},{11,12},{13,14},{2,1},{4,3},{6,5},{... | collective-permute-start | bytes 614408 | tf_op jit(solution)/shard_map/ppermute | solution.py:47
  9.5 6.1 %copy-start.2 = (bf16[256,1024]{1,0:T(8,128)(2,1)S(1)}, bf16[256,1024]{1,0:T(8,128)(2,1)}, u32[]{:S(2)}) copy-start(bf16[256,1024]{1,0:T(8,128)(2,1)} %refs_1_.3) | copy-start | bytes 1572868
  9.5 6.1 %copy-start.3 = (bf16[256,1024]{1,0:T(8,128)(2,1)S(1)}, bf16[256,1024]{1,0:T(8,128)(2,1)}, u32[]{:S(2)}) copy-start(bf16[256,1024]{1,0:T(8,128)(2,1)} %refs_2_.3) | copy-start | bytes 1572868
  11.2 13.9 %collective-permute-start.3 = (bf16[2,200,512]{2,1,0:T(8,128)(2,1)S(1)}, bf16[2,200,512]{2,1,0:T(8,128)(2,1)S(1)}, u32[]{:S(2)}, u32[]{:S(2)}) collective-permute-start(bf16[2,200,512]{2,1,0:T(8,128)(2,1)S(1)} %maximum_select_fusion), channel_id=1, source_target_pairs={{1,2},{3,4},{5,6},{7,8},{9,10},{11,12},{13,14},{2,1},{4,3},{6,5},{... | collective-permute-start | bytes 1228808 | tf_op jit(solution)/shard_map/ppermute | solution.py:47
  21.4 13.0 %collective-permute-start.7 = (bf16[2,200,512]{2,1,0:T(8,128)(2,1)S(1)}, bf16[2,200,512]{2,1,0:T(8,128)(2,1)S(1)}, u32[]{:S(2)}, u32[]{:S(2)}) collective-permute-start(bf16[2,200,512]{2,1,0:T(8,128)(2,1)S(1)} %get-tuple-element.44), channel_id=1, source_target_pairs={{0,1},{2,3},{4,5},{6,7},{8,9},{10,11},{12,13},{14,15},{1,0},{3,2},... | collective-permute-start | bytes 1228808 | tf_op jit(solution)/shard_map/ppermute | solution.py:47
  21.4 13.7 %collective-permute-start.8 = (bf16[2,200,512]{2,1,0:T(8,128)(2,1)S(1)}, bf16[2,200,512]{2,1,0:T(8,128)(2,1)S(1)}, u32[]{:S(2)}, u32[]{:S(2)}) collective-permute-start(bf16[2,200,512]{2,1,0:T(8,128)(2,1)S(1)} %get-tuple-element.45), channel_id=1, source_target_pairs={{1,2},{3,4},{5,6},{7,8},{9,10},{11,12},{13,14},{2,1},{4,3},{6,5},{... | collective-permute-start | bytes 1228808 | tf_op jit(solution)/shard_map/ppermute | solution.py:47
  30.9 5.3 %collective-permute-start.5 = (bf16[2,200,512]{2,1,0:T(8,128)(2,1)S(1)}, bf16[2,200,512]{2,1,0:T(8,128)(2,1)S(1)}, u32[]{:S(2)}, u32[]{:S(2)}) collective-permute-start(bf16[2,200,512]{2,1,0:T(8,128)(2,1)S(1)} %get-tuple-element.40), channel_id=1, source_target_pairs={{0,1},{2,3},{4,5},{6,7},{8,9},{10,11},{12,13},{14,15},{1,0},{3,2},... | collective-permute-start | bytes 1228808 | tf_op jit(solution)/shard_map/ppermute | solution.py:47
  31.3 13.6 %collective-permute-start.6 = (bf16[2,200,512]{2,1,0:T(8,128)(2,1)S(1)}, bf16[2,200,512]{2,1,0:T(8,128)(2,1)S(1)}, u32[]{:S(2)}, u32[]{:S(2)}) collective-permute-start(bf16[2,200,512]{2,1,0:T(8,128)(2,1)S(1)} %get-tuple-element.41), channel_id=1, source_target_pairs={{1,2},{3,4},{5,6},{7,8},{9,10},{11,12},{13,14},{2,1},{4,3},{6,5},{... | collective-permute-start | bytes 1228808 | tf_op jit(solution)/shard_map/ppermute | solution.py:47
